TPU v7x, 32 devices: a whole 2x2x4 slice. The times are simulated.
32 devices in a mesh: blk: 8 (over y, x, core), head: 4 (over z).
Axes of the slice: x: 2, y: 2, z: 4, core: 2. Of those that a mesh axis runs over, the one named last changes fastest.
Arguments:
- query_states: bfloat16 [8, 2, 64, 2048], P('blk', None, 'head'), may hold values from -24 to 24
- key_states: bfloat16 [8, 2, 64, 512], P('blk', None, None, 'head'), may hold values from -6 to 6
- value_states: bfloat16 [8, 2, 64, 512], P('blk', None, None, 'head'), may hold values from -6 to 6
- doc_lengths: int32 [3], replicated, may hold values from 1 to 768, 1024 in all
- page_slot: int32 [8, 2, 4], replicated, may hold values from 0 to 127, as said below
Outputs:
- attended: bfloat16 [8, 2, 64, 2048], P('blk', None, None, 'head')
- kv_cache: bfloat16 [128, 4, 16, 256], P('blk', 'head')
Inputs may be any that keep to these rules, and one draw needn't show every extreme that they name: `page_slot`: all entries differ. The busiest owners hold 16 pages, the least busy 4.
All inputs are finite; a program needn't handle non-finite values.
Results may differ from a plain program's by a relative error of at most 0.007.
Values may be sent and summed in bfloat16 or wider, within the bound.
No kernel may reach another device: no remote copies, remote signals or barrier semaphores. Data moves between devices by JAX's collectives and lax.ppermute only.
A program may use at most 64 MiB of HBM per device.

v0:
```python
import jax
import jax.numpy as jnp
from jax import lax
from jax.experimental import pallas as pl
from jax.experimental.pallas import tpu as pltpu
from jax.sharding import PartitionSpec as P

PAGE = 16
LOG2E = 1.4426950408889634
HEAD_DIM = 128


def gather_queries(own, across, beside, q_rows):
    my_head = lax.axis_index("head")
    width = beside.shape[-1]
    sub_tok = own.shape[2]
    group = width // HEAD_DIM
    block_tok = q_rows.shape[1] // group
    for half in range(2):
        for g in range(group):
            lane = g * HEAD_DIM
            mine = pl.multiple_of(my_head * width + lane, HEAD_DIM)
            low = pl.multiple_of((my_head % 2) * width + lane, HEAD_DIM)
            parts = (
                own[0, half, :, pl.ds(mine, HEAD_DIM)],
                beside[0, half, :, lane : lane + HEAD_DIM],
                across[0, half, :, pl.ds(low, HEAD_DIM)],
                beside[1, half, :, lane : lane + HEAD_DIM],
            )
            for d, part in enumerate(parts):
                row = pl.multiple_of(g * block_tok + (my_head ^ d) * sub_tok, sub_tok)
                q_rows[half, pl.ds(row, sub_tok), :] = part


def key_bias(my_blk, doc_lengths, chips, block_tok, half, core):
    blk_count = 2 * chips
    sides = half + 1
    cols = chips * sides * block_tok
    col = lax.broadcasted_iota(jnp.int32, (1, cols), 1)
    owner = (my_blk ^ core) ^ (2 * (col // (sides * block_tok)))
    block = owner
    if half == 1:
        block = jnp.where((col // block_tok) % 2 == 1, 2 * blk_count - 1 - owner, owner)
    k_pos = block * block_tok + col % block_tok
    my_block = my_blk if half == 0 else 2 * blk_count - 1 - my_blk
    q_pos = my_block * block_tok + lax.broadcasted_iota(jnp.int32, (block_tok, 1), 0)
    first = jnp.zeros_like(q_pos)
    bound = 0
    for k in range(doc_lengths.shape[0] - 1):
        bound = bound + doc_lengths[k]
        first = jnp.where(q_pos >= bound, bound, first)
    return jnp.where((k_pos <= q_pos) & (k_pos >= first), 0.0, -1e30)


def page_targets(my_blk, page_slot, chips, block_tok, slot_count, core):
    pages_blk = block_tok // PAGE
    cols = chips * 2 * block_tok
    col = lax.broadcasted_iota(jnp.int32, (1, cols), 1)
    slots = jnp.zeros((1, cols), jnp.int32)
    for m in range(chips):
        owner = (my_blk ^ core) ^ (2 * m)
        for half in range(2):
            for n in range(pages_blk):
                slot = page_slot[half, n, owner]
                slots = jnp.where(col // PAGE == (m * 2 + half) * pages_blk + n, slot, slots)
    return (slots - my_blk * slot_count) * PAGE + col % PAGE


def place_pages(targets, pairs, slot_count):
    rows = pairs[...].reshape(-1, pairs.shape[-1])
    row = lax.broadcasted_iota(jnp.int32, (slot_count * PAGE, rows.shape[0]), 0)
    chosen = jnp.where(row == targets, 1.0, 0.0).astype(jnp.bfloat16)
    return jnp.dot(chosen, rows, preferred_element_type=jnp.float32)


def score_part(q_rows, pairs, half):
    keys = pairs[:, : half + 1].reshape(-1, 2 * HEAD_DIM)[:, :HEAD_DIM]
    return lax.dot_general(q_rows[half], keys, (((1,), (1,)), ((), ())), preferred_element_type=jnp.float32)


def weigh_part(scores, bias, pairs, half):
    values = pairs[:, : half + 1].reshape(-1, 2 * HEAD_DIM)[:, HEAD_DIM:]
    block_tok, cols = bias.shape
    scores = scores.reshape(-1, block_tok, cols) * (HEAD_DIM**-0.5 * LOG2E) + bias[None]
    scores = scores.reshape(-1, cols)
    top = jnp.max(scores, axis=1, keepdims=True)
    weights = jnp.exp2(scores - top)
    total = jnp.sum(weights, axis=1, keepdims=True)
    out = jnp.dot(weights.astype(jnp.bfloat16), values, preferred_element_type=jnp.float32)
    return top, total, out


def near_kernel(
    doc_hbm, slot_hbm, own, across, beside, near, q_rows, top_ref, total_ref, out_ref, pages_ref, far_bias_a,
    far_bias_b, far_targets, doc_lengths, page_slot, sems,
):
    chips, _, block_tok, _ = near.shape
    slot_count = pages_ref.shape[0] // PAGE
    my_blk = lax.axis_index("blk")
    fetch_doc = pltpu.make_async_copy(doc_hbm, doc_lengths, sems.at[0])
    fetch_slot = pltpu.make_async_copy(slot_hbm, page_slot, sems.at[1])
    fetch_doc.start()
    fetch_slot.start()
    gather_queries(own, across, beside, q_rows)
    scores = [score_part(q_rows, near, half) for half in range(2)]
    fetch_doc.wait()
    fetch_slot.wait()
    for half in range(2):
        bias = key_bias(my_blk, doc_lengths, chips, block_tok, half, 0)
        top, total, out = weigh_part(scores[half], bias, near, half)
        top_ref[half] = top
        total_ref[half] = total
        out_ref[half] = out
    pages_ref[...] = place_pages(
        page_targets(my_blk, page_slot, chips, block_tok, slot_count, 0), near, slot_count
    ).astype(jnp.bfloat16)
    far_bias_a[...] = key_bias(my_blk, doc_lengths, chips, block_tok, 0, 1)
    far_bias_b[...] = key_bias(my_blk, doc_lengths, chips, block_tok, 1, 1)
    far_targets[...] = page_targets(my_blk, page_slot, chips, block_tok, slot_count, 1)


def far_kernel(
    far, q_rows, top_ref, total_ref, out_ref, pages_ref, far_bias_a, far_bias_b, far_targets, attended, kv_cache,
    pages, result, sems,
):
    block_tok = far.shape[2]
    slot_count = kv_cache.shape[0]
    moved = place_pages(far_targets[...], far, slot_count) + pages_ref[...].astype(jnp.float32)
    pages[...] = moved.astype(jnp.bfloat16).reshape(pages.shape)
    writes = [pltpu.make_async_copy(pages, kv_cache, sems.at[2])]
    writes[0].start()
    for half in (1, 0):
        bias = (far_bias_a, far_bias_b)[half][...]
        top, total, out = weigh_part(score_part(q_rows, far, half), bias, far, half)
        best = jnp.maximum(top, top_ref[half])
        here = jnp.exp2(top - best)
        there = jnp.exp2(top_ref[half] - best)
        total = total * here + total_ref[half] * there
        out = ((out * here + out_ref[half] * there) / total).astype(jnp.bfloat16)
        for g in range(out.shape[0] // block_tok):
            result[half, :, g * HEAD_DIM : (g + 1) * HEAD_DIM] = out[g * block_tok : (g + 1) * block_tok]
        writes.append(pltpu.make_async_copy(result.at[half], attended.at[0, half], sems.at[half]))
        writes[-1].start()
    for write in writes:
        write.wait()


def per_device(query_states, key_states, value_states, doc_lengths, page_slot):
    blk_count = lax.axis_size("blk")
    head_count = lax.axis_size("head")
    q_width = query_states.shape[3]
    block_tok = key_states.shape[2]
    width = q_width // head_count
    rows = width // HEAD_DIM * block_tok
    slot_count = 4 * (block_tok // PAGE)

    my_head = lax.axis_index("head")
    part = lax.dynamic_slice_in_dim(query_states, ((my_head ^ 2) // 2) * 2 * width, 2 * width, axis=3)
    across = lax.ppermute(part, "head", [(i, i ^ 2) for i in range(head_count)])
    pair = jnp.concatenate([key_states, value_states], axis=3)
    pair, _ = lax.optimization_barrier((pair, part))
    near = [
        lax.ppermute(pair, "blk", [(i, i ^ d) for i in range(blk_count)]) for d in range(2, blk_count, 2)
    ]
    beside = jnp.concatenate(
        [
            lax.dynamic_slice_in_dim(query_states, (my_head ^ 1) * width, width, axis=3),
            lax.dynamic_slice_in_dim(across, (1 - my_head % 2) * width, width, axis=3),
        ],
        axis=0,
    )
    near = lax.optimization_barrier((near[::-1], beside))[0][::-1]
    beside = lax.ppermute(beside, "head", [(i, i ^ 1) for i in range(head_count)])
    near = jnp.concatenate([pair] + near, axis=0)
    far = lax.ppermute(near, "blk", [(i, i ^ 1) for i in range(blk_count)])

    hbm = pl.BlockSpec(memory_space=pl.ANY)
    vmem = pl.BlockSpec(memory_space=pltpu.VMEM)
    params = pltpu.CompilerParams(vmem_limit_bytes=32 * 1024 * 1024)
    cost = pl.CostEstimate(flops=4_000_000_000, bytes_accessed=1_000_000, transcendentals=200_000)
    slots = page_slot.transpose(1, 2, 0)
    half_cols = blk_count // 2 * block_tok
    stats = pl.pallas_call(
        near_kernel,
        out_shape=(
            jax.ShapeDtypeStruct((2, rows, HEAD_DIM), jnp.bfloat16),
            jax.ShapeDtypeStruct((2, rows, 1), jnp.float32),
            jax.ShapeDtypeStruct((2, rows, 1), jnp.float32),
            jax.ShapeDtypeStruct((2, rows, HEAD_DIM), jnp.float32),
            jax.ShapeDtypeStruct((slot_count * PAGE, 2 * HEAD_DIM), jnp.bfloat16),
            jax.ShapeDtypeStruct((block_tok, half_cols), jnp.float32),
            jax.ShapeDtypeStruct((block_tok, 2 * half_cols), jnp.float32),
            jax.ShapeDtypeStruct((1, 2 * half_cols), jnp.int32),
        ),
        in_specs=[hbm] * 2 + [vmem] * 4,
        out_specs=(vmem,) * 8,
        scratch_shapes=[
            pltpu.SMEM(doc_lengths.shape, jnp.int32),
            pltpu.SMEM(slots.shape, jnp.int32),
            pltpu.SemaphoreType.DMA((2,)),
        ],
        compiler_params=params,
        cost_estimate=cost,
    )(doc_lengths, slots, query_states, across, beside, near)
    return pl.pallas_call(
        far_kernel,
        out_shape=(
            jax.ShapeDtypeStruct((1, 2, block_tok, width), jnp.bfloat16),
            jax.ShapeDtypeStruct((slot_count, 1, PAGE, 2 * HEAD_DIM), jnp.bfloat16),
        ),
        in_specs=[vmem] * 9,
        out_specs=(hbm, hbm),
        scratch_shapes=[
            pltpu.VMEM((slot_count, 1, PAGE, 2 * HEAD_DIM), jnp.bfloat16),
            pltpu.VMEM((2, block_tok, width), jnp.bfloat16),
            pltpu.SemaphoreType.DMA((3,)),
        ],
        compiler_params=params,
        cost_estimate=cost,
    )(far, *stats)


def per_device_long(query_states, key_states, value_states, doc_lengths, page_slot):
    q_local = lax.all_to_all(query_states, "head", split_axis=3, concat_axis=2, tiled=True)
    axis_count = lax.axis_size("blk")
    my_index = lax.axis_index("blk")
    block_tok = q_local.shape[2]
    head_dim = key_states.shape[3]
    group_size = q_local.shape[3] // head_dim
    query_rows = q_local.reshape(2 * block_tok, group_size, head_dim)
    offsets = jnp.arange(block_tok, dtype=jnp.int32)
    doc_bounds = jnp.cumsum(doc_lengths)[:-1]
    page_count = block_tok // PAGE
    slot_count = 4 * page_count
    slot_range = jnp.arange(slot_count, dtype=jnp.int32)
    score_scale = head_dim ** (-0.5)

    def group_positions(owner_ids):
        block_starts = jnp.stack([owner_ids, 2 * axis_count - 1 - owner_ids], axis=1) * block_tok
        return (block_starts[:, :, None] + offsets[None, None, :]).reshape(-1)

    def doc_of(positions):
        return jnp.sum((positions[:, None] >= doc_bounds[None, :]).astype(jnp.int32), axis=1)

    q_pos = group_positions(my_index.reshape(1))
    q_doc = doc_of(q_pos)

    def attend_group(attn_state, key_rows, value_rows, allowed):
        running_max, weight_sum, accum = attn_state
        scores = (
            jnp.einsum("qhd,kd->qhk", query_rows, key_rows, preferred_element_type=jnp.float32)
            * score_scale
        )
        masked = jnp.where(allowed[:, None, :], scores, -1e30)
        new_max = jnp.maximum(running_max, jnp.max(masked, axis=2))
        weights = jnp.where(allowed[:, None, :], jnp.exp(masked - new_max[..., None]), 0.0)
        factor = jnp.exp(running_max - new_max)
        weight_sum = weight_sum * factor + jnp.sum(weights, axis=2)
        update = jnp.einsum(
            "qhk,kd->qhd",
            weights.astype(jnp.bfloat16),
            value_rows,
            preferred_element_type=jnp.float32,
        )
        accum = accum * factor[..., None] + update
        return (new_max, weight_sum, accum)

    def visit_group(attn_state, key_group, value_group, owner_ids):
        key_rows = key_group.reshape(-1, head_dim)
        value_rows = value_group.reshape(-1, head_dim)
        k_pos = group_positions(owner_ids)
        allowed = (k_pos[None, :] <= q_pos[:, None]) & (doc_of(k_pos)[None, :] == q_doc[:, None])
        return attend_group(attn_state, key_rows, value_rows, allowed)

    def place_pages(page_store, key_group, value_group, owner_ids):
        page_rows = jnp.concatenate([key_group, value_group], axis=-1).reshape(
            -1, PAGE * 2 * head_dim
        )
        slot_ids = jnp.take(page_slot, owner_ids, axis=0).reshape(-1) - my_index * slot_count
        selector = (slot_range[:, None] == slot_ids[None, :]).astype(jnp.bfloat16)
        return page_store + jnp.dot(selector, page_rows, preferred_element_type=jnp.float32)

    def fold_groups(step_fn, carried, kv_piece):
        key_piece, value_piece = kv_piece
        piece_len = key_piece.shape[0]
        width = 4
        owner_ids = jnp.arange(piece_len, dtype=jnp.int32).reshape(piece_len // width, width)
        key_groups = key_piece.reshape(piece_len // width, width, 2, block_tok, head_dim)
        value_groups = value_piece.reshape(piece_len // width, width, 2, block_tok, head_dim)

        def visit_one(inner_state, entry_tuple):
            key_group, value_group, owners = entry_tuple
            return (step_fn(inner_state, key_group, value_group, owners), None)

        return lax.scan(visit_one, carried, (key_groups, value_groups, owner_ids))[0]

    empty_store = jnp.zeros((slot_count, PAGE * 2 * head_dim), jnp.float32)
    start_state = (
        jnp.full((2 * block_tok, group_size), -1e30, jnp.float32),
        jnp.zeros((2 * block_tok, group_size), jnp.float32),
        jnp.zeros((2 * block_tok, group_size, head_dim), jnp.float32),
    )
    final_state = fold_groups(
        visit_group,
        start_state,
        (
            lax.all_gather(key_states, "blk", axis=0, tiled=True),
            lax.all_gather(value_states, "blk", axis=0, tiled=True),
        ),
    )
    page_store = fold_groups(
        place_pages,
        empty_store,
        (
            lax.all_gather(key_states, "blk", axis=0, tiled=True),
            lax.all_gather(value_states, "blk", axis=0, tiled=True),
        ),
    )
    running_max, weight_sum, accum = final_state
    attended = (
        (accum / weight_sum[..., None])
        .astype(jnp.bfloat16)
        .reshape(1, 2, block_tok, group_size * head_dim)
    )
    kv_cache = page_store.astype(jnp.bfloat16).reshape(slot_count, 1, PAGE, 2 * head_dim)
    return (attended, kv_cache)


def solution(mesh):
    return jax.shard_map(
        per_device if mesh.shape["blk"] <= 8 else per_device_long,
        mesh=mesh,
        in_specs=(
            P("blk", None, "head", None),
            P("blk", None, None, "head"),
            P("blk", None, None, "head"),
            P(),
            P(),
        ),
        out_specs=(P("blk", None, None, "head"), P("blk", "head", None, None)),
        check_vma=False,
    )
```

profile of v0, /device:TPU:0, one launch (start us, length us, event | category | flops | bytes accessed | tf_op | source)
XLA Modules:
  0.0 17.1 jit_solution(9609956768364063022)
XLA Ops:
  0.7 0.0 copy-start.3
  0.7 0.0 copy-start.4
  0.7 0.9 %constant_dynamic-slice_fusion.2 = bf16[1,2,16,1024]{3,2,1,0:T(8,128)(2,1)S(1)} fusion(bf16[1,2,16,2048]{3,2,1,0:T(8,128)(2,1)} %own.1, s32[]{:T(128)S(6)} %select_n.21), kind=kLoop, calls=%fused_computation.8 | loop fusion | bytes 131076 | tf_op jit(solution)/shard_map/dynamic_slice | solution.py:158
  1.5 0.0 copy-start
  1.5 4.0 %collective-permute-start.3 = (bf16[1,2,16,1024]{3,2,1,0:T(8,128)(2,1)S(1)}, bf16[1,2,16,1024]{3,2,1,0:T(8,128)(2,1)S(1)}, u32[]{:S(2)}, u32[]{:S(2)}) collective-permute-start(bf16[1,2,16,1024]{3,2,1,0:T(8,128)(2,1)S(1)} %constant_dynamic-slice_fusion.2), channel_id=1, source_target_pairs={{0,2},{1,3},{2,0},{3,1},{4,6},{5,7},{6,4},{7,5},{8,10},{9,11},{10,... | collective-permute-start | bytes 196616 | tf_op jit(solution)/shard_map/ppermute | solution.py:159
  5.6 0.0 copy-done.3
  5.6 0.0 copy-done.4
  5.6 2.5 %collective-permute-start = (bf16[1,2,64,256]{3,2,1,0:T(8,128)(2,1)S(1)}, bf16[1,2,64,256]{3,2,1,0:T(8,128)(2,1)S(1)}, u32[]{:S(2)}, u32[]{:S(2)}) collective-permute-start(bf16[1,2,64,256]{3,2,1,0:T(8,128)(2,1)S(1)} %pad_maximum_fusion), channel_id=1, source_target_pairs={{0,24},{4,28},{8,16},{12,20},{16,8},{20,12},{24,0},{28,4},{1,25},{... | collective-permute-start | bytes 196616 | tf_op jit(solution)/shard_map/ppermute | solution.py:163
  8.1 0.5 %collective-permute-start.1 = (bf16[1,2,64,256]{3,2,1,0:T(8,128)(2,1)S(1)}, bf16[1,2,64,256]{3,2,1,0:T(8,128)(2,1)S(1)}, u32[]{:S(2)}, u32[]{:S(2)}) collective-permute-start(bf16[1,2,64,256]{3,2,1,0:T(8,128)(2,1)S(1)} %pad_maximum_fusion), channel_id=1, source_target_pairs={{0,16},{4,20},{8,24},{12,28},{16,0},{20,4},{24,8},{28,12},{1,17},{... | collective-permute-start | bytes 196616 | tf_op jit(solution)/shard_map/ppermute | solution.py:163
  8.6 0.5 %collective-permute-start.2 = (bf16[1,2,64,256]{3,2,1,0:T(8,128)(2,1)S(1)}, bf16[1,2,64,256]{3,2,1,0:T(8,128)(2,1)S(1)}, u32[]{:S(2)}, u32[]{:S(2)}) collective-permute-start(bf16[1,2,64,256]{3,2,1,0:T(8,128)(2,1)S(1)} %pad_maximum_fusion), channel_id=1, source_target_pairs={{0,8},{4,12},{8,0},{12,4},{16,24},{20,28},{24,16},{28,20},{1,9},{5... | collective-permute-start | bytes 196616 | tf_op jit(solution)/shard_map/ppermute | solution.py:163
  9.2 0.0 copy-done
  9.2 0.0 collective-permute-done.3.across
  9.2 1.6 %collective-permute-start.5 = (bf16[2,2,16,512]{3,2,1,0:T(8,128)(2,1)S(1)}, bf16[2,2,16,512]{3,2,1,0:T(8,128)(2,1)S(1)}, u32[]{:S(2)}, u32[]{:S(2)}) collective-permute-start(bf16[2,2,16,512]{3,2,1,0:T(8,128)(2,1)S(1)} %pad_maximum_fusion.1), channel_id=1, source_target_pairs={{0,1},{1,0},{2,3},{3,2},{4,5},{5,4},{6,7},{7,6},{8,9},{9,8},{10,11... | collective-permute-start | bytes 196616 | tf_op jit(solution)/shard_map/ppermute | solution.py:173
  10.9 0.1 collective-permute-done
  10.9 1.4 %collective-permute-done.1 = bf16[1,2,64,256]{3,2,1,0:T(8,128)(2,1)S(1)} collective-permute-done((bf16[1,2,64,256]{3,2,1,0:T(8,128)(2,1)S(1)}, bf16[1,2,64,256]{3,2,1,0:T(8,128)(2,1)S(1)}, u32[]{:S(2)}, u32[]{:S(2)}) %collective-permute-start.1) | collective-permute-done | bytes 65568 | tf_op jit(solution)/shard_map/ppermute | solution.py:163
  12.4 0.5 %collective-permute-done.2 = bf16[1,2,64,256]{3,2,1,0:T(8,128)(2,1)S(1)} collective-permute-done((bf16[1,2,64,256]{3,2,1,0:T(8,128)(2,1)S(1)}, bf16[1,2,64,256]{3,2,1,0:T(8,128)(2,1)S(1)}, u32[]{:S(2)}, u32[]{:S(2)}) %collective-permute-start.2) | collective-permute-done | bytes 65568 | tf_op jit(solution)/shard_map/ppermute | solution.py:163
  12.9 0.0 copy-start.1
  12.9 0.0 copy-start.2
  12.9 0.1 collective-permute-start.4
  13.0 0.6 %collective-permute-done.5.beside = bf16[2,2,16,512]{3,2,1,0:T(8,128)(2,1)S(1)} collective-permute-done((bf16[2,2,16,512]{3,2,1,0:T(8,128)(2,1)S(1)}, bf16[2,2,16,512]{3,2,1,0:T(8,128)(2,1)S(1)}, u32[]{:S(2)}, u32[]{:S(2)}) %collective-permute-start.5) | collective-permute-done | bytes 65568 | tf_op jit(solution)/shard_map/ppermute | solution.py:173
  13.6 0.0 copy-done.1
  13.6 0.0 copy-done.2
  13.6 1.2 %shard_map.68 = (bf16[2,256,128]{2,1,0:T(8,128)(2,1)S(1)}, f32[2,256,1]{2,1,0:T(8,128)S(1)}, f32[2,256,1]{2,1,0:T(8,128)S(1)}, f32[2,256,128]{2,1,0:T(8,128)S(1)...) custom-call(s32[3]{0:T(128)S(1)} %copy-done.2, ...), custom_call_target="tpu_custom_call" | custom-call | flops 4000000000 | bytes 1000000 | tf_op jit(solution)/shard_map/pallas_call | solution.py:183
  14.8 0.0 collective-permute-done.4.far
  14.8 2.3 %shard_map.69 = (bf16[1,2,64,512]{3,2,1,0:T(8,128)(2,1)}, bf16[16,1,16,256]{3,2,1,0:T(8,128)(2,1)}) custom-call(bf16[4,2,64,256]{3,2,1,0:T(8,128)(2,1)S(1)} %collective-permute-done.4.far, bf16[2,256,128]{2,1,0:T(8,128)(2,1)S(1)} %get-tuple-element.18.q_rows, f32[2,256,1]{2,1,0:T(8,128)S(1)} %get-tuple-element.19.top_ref, ...), custom_call_target="tpu_custom_call" | custom-call | flops 4000000000 | bytes 1000000 | tf_op jit(solution)/shard_map/pallas_call | solution.py:205
  (8 shorter events, 0.1 us)
Async XLA Ops:
  0.7 4.9 %copy-start.3 = (bf16[1,2,64,128]{3,2,1,0:T(8,128)(2,1)S(1)}, bf16[1,2,64,128]{3,2,1,0:T(8,128)(2,1)}, u32[]{:S(2)}) copy-start(bf16[1,2,64,128]{3,2,1,0:T(8,128)(2,1)} %param.7) | copy-start | bytes 98308
  0.7 4.9 %copy-start.4 = (bf16[1,2,64,128]{3,2,1,0:T(8,128)(2,1)S(1)}, bf16[1,2,64,128]{3,2,1,0:T(8,128)(2,1)}, u32[]{:S(2)}) copy-start(bf16[1,2,64,128]{3,2,1,0:T(8,128)(2,1)} %param.6) | copy-start | bytes 98308
  1.5 7.6 %copy-start = (bf16[1,2,16,2048]{3,2,1,0:T(8,128)(2,1)S(1)}, bf16[1,2,16,2048]{3,2,1,0:T(8,128)(2,1)}, u32[]{:S(2)}) copy-start(bf16[1,2,16,2048]{3,2,1,0:T(8,128)(2,1)} %own.1) | copy-start | bytes 393220
  1.5 7.7 %collective-permute-start.3 = (bf16[1,2,16,1024]{3,2,1,0:T(8,128)(2,1)S(1)}, bf16[1,2,16,1024]{3,2,1,0:T(8,128)(2,1)S(1)}, u32[]{:S(2)}, u32[]{:S(2)}) collective-permute-start(bf16[1,2,16,1024]{3,2,1,0:T(8,128)(2,1)S(1)} %constant_dynamic-slice_fusion.2), channel_id=1, source_target_pairs={{0,2},{1,3},{2,0},{3,1},{4,6},{5,7},{6,4},{7,5},{8,10},{9,11},{10,... | collective-permute-start | bytes 196616 | tf_op jit(solution)/shard_map/ppermute | solution.py:159
  5.6 5.3 %collective-permute-start = (bf16[1,2,64,256]{3,2,1,0:T(8,128)(2,1)S(1)}, bf16[1,2,64,256]{3,2,1,0:T(8,128)(2,1)S(1)}, u32[]{:S(2)}, u32[]{:S(2)}) collective-permute-start(bf16[1,2,64,256]{3,2,1,0:T(8,128)(2,1)S(1)} %pad_maximum_fusion), channel_id=1, source_target_pairs={{0,24},{4,28},{8,16},{12,20},{16,8},{20,12},{24,0},{28,4},{1,25},{... | collective-permute-start | bytes 196616 | tf_op jit(solution)/shard_map/ppermute | solution.py:163
  8.1 4.3 %collective-permute-start.1 = (bf16[1,2,64,256]{3,2,1,0:T(8,128)(2,1)S(1)}, bf16[1,2,64,256]{3,2,1,0:T(8,128)(2,1)S(1)}, u32[]{:S(2)}, u32[]{:S(2)}) collective-permute-start(bf16[1,2,64,256]{3,2,1,0:T(8,128)(2,1)S(1)} %pad_maximum_fusion), channel_id=1, source_target_pairs={{0,16},{4,20},{8,24},{12,28},{16,0},{20,4},{24,8},{28,12},{1,17},{... | collective-permute-start | bytes 196616 | tf_op jit(solution)/shard_map/ppermute | solution.py:163
  8.6 4.3 %collective-permute-start.2 = (bf16[1,2,64,256]{3,2,1,0:T(8,128)(2,1)S(1)}, bf16[1,2,64,256]{3,2,1,0:T(8,128)(2,1)S(1)}, u32[]{:S(2)}, u32[]{:S(2)}) collective-permute-start(bf16[1,2,64,256]{3,2,1,0:T(8,128)(2,1)S(1)} %pad_maximum_fusion), channel_id=1, source_target_pairs={{0,8},{4,12},{8,0},{12,4},{16,24},{20,28},{24,16},{28,20},{1,9},{5... | collective-permute-start | bytes 196616 | tf_op jit(solution)/shard_map/ppermute | solution.py:163
  9.2 4.3 %collective-permute-start.5 = (bf16[2,2,16,512]{3,2,1,0:T(8,128)(2,1)S(1)}, bf16[2,2,16,512]{3,2,1,0:T(8,128)(2,1)S(1)}, u32[]{:S(2)}, u32[]{:S(2)}) collective-permute-start(bf16[2,2,16,512]{3,2,1,0:T(8,128)(2,1)S(1)} %pad_maximum_fusion.1), channel_id=1, source_target_pairs={{0,1},{1,0},{2,3},{3,2},{4,5},{5,4},{6,7},{7,6},{8,9},{9,8},{10,11... | collective-permute-start | bytes 196616 | tf_op jit(solution)/shard_map/ppermute | solution.py:173
  12.9 0.7 %copy-start.1 = (s32[8,2,4]{0,2,1:T(4,128)S(1)}, s32[8,2,4]{0,2,1:T(4,128)}, u32[]{:S(2)}) copy-start(s32[8,2,4]{0,2,1:T(4,128)} %param.9) | copy-start | bytes 772
  12.9 0.7 %copy-start.2 = (s32[3]{0:T(128)S(1)}, s32[3]{0:T(128)}, u32[]{:S(2)}) copy-start(s32[3]{0:T(128)} %doc_hbm.1) | copy-start | bytes 40
  12.9 1.9 %collective-permute-start.4 = (bf16[4,2,64,256]{3,2,1,0:T(8,128)(2,1)S(1)}, bf16[4,2,64,256]{3,2,1,0:T(8,128)(2,1)S(1)}, u32[]{:S(2)}, u32[]{:S(2)}) collective-permute-start(bf16[4,2,64,256]{3,2,1,0:T(8,128)(2,1)S(1)} %constant_dynamic-update-slice_fusion.near), channel_id=1, source_target_pairs={{0,4},{4,0},{8,12},{12,8},{16,20},{20,16},{24,28},{28,24},{1,5},{5... | collective-permute-start | bytes 786440 | tf_op jit(solution)/shard_map/ppermute | solution.py:175
where the time goes:
time: 17.3 us; the launch traced here: 17.1 us
  starting transfers between devices  9.29 us (54%)
  Pallas kernels  3.52 us (20%)
  waiting for transfers between devices  2.61 us (15%)
  local copies, waits for them, and re-layouts  0.93 us (5%)
  between operations  0.76 us (4%)
    ppermute x1, starting transfers between devices, per_device(): across = lax.ppermute(part, 'head', [(i, i ^ 2) for i in range(head_count)])  4.04 us
    ppermute x3, starting transfers between devices, per_device(): lax.ppermute(pair, 'blk', [(i, i ^ d) for i in range(blk_count)])  3.55 us
    pallas_call x1, Pallas kernels, per_device(): pl.pallas_call(far_kernel, out_shape=(jax.ShapeDtypeStruct((1, 2, block_t...  2.3 us
    ppermute x3, waiting for transfers between devices, per_device(): lax.ppermute(pair, 'blk', [(i, i ^ d) for i in range(blk_count)])  2.01 us
    ppermute x1, starting transfers between devices, per_device(): lax.ppermute(beside, 'head', [(i, i ^ 1) for i in range(head_count)])  1.63 us
    pallas_call x1, Pallas kernels, per_device(): pl.pallas_call(near_kernel, out_shape=(jax.ShapeDtypeStruct((2, rows, HEA...  1.22 us
    dynamic_slice x1, local copies, waits for them, and re-layouts, per_device(): lax.dynamic_slice_in_dim(query_states, (my_head ^ 2) // 2 * 2 * width, 2...  0.86 us
    ppermute x1, waiting for transfers between devices, per_device(): lax.ppermute(beside, 'head', [(i, i ^ 1) for i in range(head_count)])  0.56 us
  transfers between devices with their start and end apart: 6, of which 4 were waited for; matrix products, arithmetic and copies ran while one was open for 0% of the time, Pallas kernels for 7%

commit v1 on v0

--- a/solution.py
+++ b/solution.py
@@ -8,6 +8,7 @@
 PAGE = 16
 LOG2E = 1.4426950408889634
 HEAD_DIM = 128
+LANES = 128
 
 
 def gather_queries(own, across, beside, q_rows):
@@ -34,36 +35,36 @@
 
 def key_bias(my_blk, doc_lengths, chips, block_tok, half, core):
     blk_count = 2 * chips
-    sides = half + 1
-    cols = chips * sides * block_tok
-    col = lax.broadcasted_iota(jnp.int32, (1, cols), 1)
-    owner = (my_blk ^ core) ^ (2 * (col // (sides * block_tok)))
-    block = owner
-    if half == 1:
-        block = jnp.where((col // block_tok) % 2 == 1, 2 * blk_count - 1 - owner, owner)
-    k_pos = block * block_tok + col % block_tok
+    shape = (block_tok, LANES)
     my_block = my_blk if half == 0 else 2 * blk_count - 1 - my_blk
-    q_pos = my_block * block_tok + lax.broadcasted_iota(jnp.int32, (block_tok, 1), 0)
+    q_pos = my_block * block_tok + lax.broadcasted_iota(jnp.int32, (1, LANES), 1) % block_tok
     first = jnp.zeros_like(q_pos)
     bound = 0
     for k in range(doc_lengths.shape[0] - 1):
         bound = bound + doc_lengths[k]
         first = jnp.where(q_pos >= bound, bound, first)
-    return jnp.where((k_pos <= q_pos) & (k_pos >= first), 0.0, -1e30)
+    row = lax.broadcasted_iota(jnp.int32, shape, 0)
+    parts = []
+    for m in range(chips):
+        owner = (my_blk ^ core) ^ (2 * m)
+        for side in range(half + 1):
+            start = (owner if side == 0 else 2 * blk_count - 1 - owner) * block_tok
+            parts.append(jnp.where((row <= q_pos - start) & (row >= first - start), 0.0, -1e30))
+    return jnp.concatenate(parts, axis=0)
 
 
 def page_targets(my_blk, page_slot, chips, block_tok, slot_count, core):
     pages_blk = block_tok // PAGE
-    cols = chips * 2 * block_tok
-    col = lax.broadcasted_iota(jnp.int32, (1, cols), 1)
-    slots = jnp.zeros((1, cols), jnp.int32)
+    col = lax.broadcasted_iota(jnp.int32, (1, 2 * block_tok), 1)
+    parts = []
     for m in range(chips):
         owner = (my_blk ^ core) ^ (2 * m)
+        slots = jnp.zeros_like(col)
         for half in range(2):
             for n in range(pages_blk):
-                slot = page_slot[half, n, owner]
-                slots = jnp.where(col // PAGE == (m * 2 + half) * pages_blk + n, slot, slots)
-    return (slots - my_blk * slot_count) * PAGE + col % PAGE
+                slots = jnp.where(col // PAGE == half * pages_blk + n, page_slot[half, n, owner], slots)
+        parts.append((slots - my_blk * slot_count) * PAGE + col % PAGE)
+    return jnp.concatenate(parts, axis=1)
 
 
 def place_pages(targets, pairs, slot_count):
@@ -75,18 +76,19 @@
 
 def score_part(q_rows, pairs, half):
     keys = pairs[:, : half + 1].reshape(-1, 2 * HEAD_DIM)[:, :HEAD_DIM]
-    return lax.dot_general(q_rows[half], keys, (((1,), (1,)), ((), ())), preferred_element_type=jnp.float32)
+    return lax.dot_general(keys, q_rows[half], (((1,), (1,)), ((), ())), preferred_element_type=jnp.float32)
 
 
 def weigh_part(scores, bias, pairs, half):
     values = pairs[:, : half + 1].reshape(-1, 2 * HEAD_DIM)[:, HEAD_DIM:]
-    block_tok, cols = bias.shape
-    scores = scores.reshape(-1, block_tok, cols) * (HEAD_DIM**-0.5 * LOG2E) + bias[None]
-    scores = scores.reshape(-1, cols)
-    top = jnp.max(scores, axis=1, keepdims=True)
+    bias = jnp.concatenate([bias] * (scores.shape[1] // LANES), axis=1)
+    scores = scores * (HEAD_DIM**-0.5 * LOG2E) + bias
+    top = jnp.max(scores, axis=0, keepdims=True)
     weights = jnp.exp2(scores - top)
-    total = jnp.sum(weights, axis=1, keepdims=True)
-    out = jnp.dot(weights.astype(jnp.bfloat16), values, preferred_element_type=jnp.float32)
+    total = jnp.sum(weights, axis=0, keepdims=True)
+    out = lax.dot_general(
+        values, weights.astype(jnp.bfloat16), (((0,), (0,)), ((), ())), preferred_element_type=jnp.float32
+    )
     return top, total, out
 
 
@@ -135,8 +137,8 @@
         best = jnp.maximum(top, top_ref[half])
         here = jnp.exp2(top - best)
         there = jnp.exp2(top_ref[half] - best)
-        total = total * here + total_ref[half] * there
-        out = ((out * here + out_ref[half] * there) / total).astype(jnp.bfloat16)
+        inverse = 1.0 / (total * here + total_ref[half] * there)
+        out = (out * (here * inverse) + out_ref[half] * (there * inverse)).T.astype(jnp.bfloat16)
         for g in range(out.shape[0] // block_tok):
             result[half, :, g * HEAD_DIM : (g + 1) * HEAD_DIM] = out[g * block_tok : (g + 1) * block_tok]
         writes.append(pltpu.make_async_copy(result.at[half], attended.at[0, half], sems.at[half]))
@@ -184,12 +186,12 @@
         near_kernel,
         out_shape=(
             jax.ShapeDtypeStruct((2, rows, HEAD_DIM), jnp.bfloat16),
-            jax.ShapeDtypeStruct((2, rows, 1), jnp.float32),
-            jax.ShapeDtypeStruct((2, rows, 1), jnp.float32),
-            jax.ShapeDtypeStruct((2, rows, HEAD_DIM), jnp.float32),
+            jax.ShapeDtypeStruct((2, 1, rows), jnp.float32),
+            jax.ShapeDtypeStruct((2, 1, rows), jnp.float32),
+            jax.ShapeDtypeStruct((2, HEAD_DIM, rows), jnp.float32),
             jax.ShapeDtypeStruct((slot_count * PAGE, 2 * HEAD_DIM), jnp.bfloat16),
-            jax.ShapeDtypeStruct((block_tok, half_cols), jnp.float32),
-            jax.ShapeDtypeStruct((block_tok, 2 * half_cols), jnp.float32),
+            jax.ShapeDtypeStruct((half_cols, LANES), jnp.float32),
+            jax.ShapeDtypeStruct((2 * half_cols, LANES), jnp.float32),
             jax.ShapeDtypeStruct((1, 2 * half_cols), jnp.int32),
         ),
         in_specs=[hbm] * 2 + [vmem] * 4,

time: 17.3 us -> 16.4 us (0.948)
  Pallas kernels: 3.52 us -> 2.63 us
    pallas_call x1, Pallas kernels: 2.3 us -> 1.37 us  [per_device(): pl.pallas_call(far_kernel, out_shape=(jax.ShapeDtypeStruct((1, 2, block_t...]
  transfers between devices with their start and end apart: 6 -> 6, of which waited for: 4 -> 4; matrix products, arithmetic and copies ran while one was open for 0% -> 0% of each run, Pallas kernels for 7% -> 8%
where the time goes in v1:
time: 16.4 us; the launch traced here: 16.2 us
  starting transfers between devices  9.29 us (57%)
  Pallas kernels  2.63 us (16%)
  waiting for transfers between devices  2.61 us (16%)
  local copies, waits for them, and re-layouts  0.93 us (6%)
  between operations  0.76 us (5%)
    ppermute x1, starting transfers between devices, per_device(): across = lax.ppermute(part, 'head', [(i, i ^ 2) for i in range(head_count)])  4.04 us
    ppermute x3, starting transfers between devices, per_device(): lax.ppermute(pair, 'blk', [(i, i ^ d) for i in range(blk_count)])  3.55 us
    ppermute x3, waiting for transfers between devices, per_device(): lax.ppermute(pair, 'blk', [(i, i ^ d) for i in range(blk_count)])  2.01 us
    ppermute x1, starting transfers between devices, per_device(): lax.ppermute(beside, 'head', [(i, i ^ 1) for i in range(head_count)])  1.63 us
    pallas_call x1, Pallas kernels, per_device(): pl.pallas_call(far_kernel, out_shape=(jax.ShapeDtypeStruct((1, 2, block_t...  1.37 us
    pallas_call x1, Pallas kernels, per_device(): pl.pallas_call(near_kernel, out_shape=(jax.ShapeDtypeStruct((2, rows, HEA...  1.26 us
    dynamic_slice x1, local copies, waits for them, and re-layouts, per_device(): lax.dynamic_slice_in_dim(query_states, (my_head ^ 2) // 2 * 2 * width, 2...  0.86 us
    ppermute x1, waiting for transfers between devices, per_device(): lax.ppermute(beside, 'head', [(i, i ^ 1) for i in range(head_count)])  0.56 us
  transfers between devices with their start and end apart: 6, of which 4 were waited for; matrix products, arithmetic and copies ran while one was open for 0% of the time, Pallas kernels for 8%

profile of v1, /device:TPU:0, one launch (start us, length us, event | category | flops | bytes accessed | tf_op | source)
XLA Modules:
  0.0 16.2 jit_solution(397034366822445218)
XLA Ops:
  0.7 0.0 copy-start.3
  0.7 0.0 copy-start.4
  0.7 0.9 %constant_dynamic-slice_fusion.2 = bf16[1,2,16,1024]{3,2,1,0:T(8,128)(2,1)S(1)} fusion(bf16[1,2,16,2048]{3,2,1,0:T(8,128)(2,1)} %own.1, s32[]{:T(128)S(6)} %select_n.21), kind=kLoop, calls=%fused_computation.8 | loop fusion | bytes 131076 | tf_op jit(solution)/shard_map/dynamic_slice | solution.py:160
  1.5 0.0 copy-start
  1.5 4.0 %collective-permute-start.3 = (bf16[1,2,16,1024]{3,2,1,0:T(8,128)(2,1)S(1)}, bf16[1,2,16,1024]{3,2,1,0:T(8,128)(2,1)S(1)}, u32[]{:S(2)}, u32[]{:S(2)}) collective-permute-start(bf16[1,2,16,1024]{3,2,1,0:T(8,128)(2,1)S(1)} %constant_dynamic-slice_fusion.2), channel_id=1, source_target_pairs={{0,2},{1,3},{2,0},{3,1},{4,6},{5,7},{6,4},{7,5},{8,10},{9,11},{10,... | collective-permute-start | bytes 196616 | tf_op jit(solution)/shard_map/ppermute | solution.py:161
  5.6 0.0 copy-done.3
  5.6 0.0 copy-done.4
  5.6 2.5 %collective-permute-start = (bf16[1,2,64,256]{3,2,1,0:T(8,128)(2,1)S(1)}, bf16[1,2,64,256]{3,2,1,0:T(8,128)(2,1)S(1)}, u32[]{:S(2)}, u32[]{:S(2)}) collective-permute-start(bf16[1,2,64,256]{3,2,1,0:T(8,128)(2,1)S(1)} %pad_maximum_fusion), channel_id=1, source_target_pairs={{0,24},{4,28},{8,16},{12,20},{16,8},{20,12},{24,0},{28,4},{1,25},{... | collective-permute-start | bytes 196616 | tf_op jit(solution)/shard_map/ppermute | solution.py:165
  8.1 0.5 %collective-permute-start.1 = (bf16[1,2,64,256]{3,2,1,0:T(8,128)(2,1)S(1)}, bf16[1,2,64,256]{3,2,1,0:T(8,128)(2,1)S(1)}, u32[]{:S(2)}, u32[]{:S(2)}) collective-permute-start(bf16[1,2,64,256]{3,2,1,0:T(8,128)(2,1)S(1)} %pad_maximum_fusion), channel_id=1, source_target_pairs={{0,16},{4,20},{8,24},{12,28},{16,0},{20,4},{24,8},{28,12},{1,17},{... | collective-permute-start | bytes 196616 | tf_op jit(solution)/shard_map/ppermute | solution.py:165
  8.6 0.5 %collective-permute-start.2 = (bf16[1,2,64,256]{3,2,1,0:T(8,128)(2,1)S(1)}, bf16[1,2,64,256]{3,2,1,0:T(8,128)(2,1)S(1)}, u32[]{:S(2)}, u32[]{:S(2)}) collective-permute-start(bf16[1,2,64,256]{3,2,1,0:T(8,128)(2,1)S(1)} %pad_maximum_fusion), channel_id=1, source_target_pairs={{0,8},{4,12},{8,0},{12,4},{16,24},{20,28},{24,16},{28,20},{1,9},{5... | collective-permute-start | bytes 196616 | tf_op jit(solution)/shard_map/ppermute | solution.py:165
  9.2 0.0 copy-done
  9.2 0.0 collective-permute-done.3.across
  9.2 1.6 %collective-permute-start.5 = (bf16[2,2,16,512]{3,2,1,0:T(8,128)(2,1)S(1)}, bf16[2,2,16,512]{3,2,1,0:T(8,128)(2,1)S(1)}, u32[]{:S(2)}, u32[]{:S(2)}) collective-permute-start(bf16[2,2,16,512]{3,2,1,0:T(8,128)(2,1)S(1)} %pad_maximum_fusion.1), channel_id=1, source_target_pairs={{0,1},{1,0},{2,3},{3,2},{4,5},{5,4},{6,7},{7,6},{8,9},{9,8},{10,11... | collective-permute-start | bytes 196616 | tf_op jit(solution)/shard_map/ppermute | solution.py:175
  10.9 0.1 collective-permute-done
  10.9 1.4 %collective-permute-done.1 = bf16[1,2,64,256]{3,2,1,0:T(8,128)(2,1)S(1)} collective-permute-done((bf16[1,2,64,256]{3,2,1,0:T(8,128)(2,1)S(1)}, bf16[1,2,64,256]{3,2,1,0:T(8,128)(2,1)S(1)}, u32[]{:S(2)}, u32[]{:S(2)}) %collective-permute-start.1) | collective-permute-done | bytes 65568 | tf_op jit(solution)/shard_map/ppermute | solution.py:165
  12.4 0.5 %collective-permute-done.2 = bf16[1,2,64,256]{3,2,1,0:T(8,128)(2,1)S(1)} collective-permute-done((bf16[1,2,64,256]{3,2,1,0:T(8,128)(2,1)S(1)}, bf16[1,2,64,256]{3,2,1,0:T(8,128)(2,1)S(1)}, u32[]{:S(2)}, u32[]{:S(2)}) %collective-permute-start.2) | collective-permute-done | bytes 65568 | tf_op jit(solution)/shard_map/ppermute | solution.py:165
  12.9 0.0 copy-start.1
  12.9 0.0 copy-start.2
  12.9 0.1 collective-permute-start.4
  13.0 0.6 %collective-permute-done.5.beside = bf16[2,2,16,512]{3,2,1,0:T(8,128)(2,1)S(1)} collective-permute-done((bf16[2,2,16,512]{3,2,1,0:T(8,128)(2,1)S(1)}, bf16[2,2,16,512]{3,2,1,0:T(8,128)(2,1)S(1)}, u32[]{:S(2)}, u32[]{:S(2)}) %collective-permute-start.5) | collective-permute-done | bytes 65568 | tf_op jit(solution)/shard_map/ppermute | solution.py:175
  13.6 0.0 copy-done.1
  13.6 0.0 copy-done.2
  13.6 1.3 %shard_map.68 = (bf16[2,256,128]{2,1,0:T(8,128)(2,1)S(1)}, f32[2,1,256]{2,1,0:T(1,128)S(1)}, f32[2,1,256]{2,1,0:T(1,128)S(1)}, f32[2,128,256]{2,1,0:T(8,128)S(1)...) custom-call(s32[3]{0:T(128)S(1)} %copy-done.2, ...), custom_call_target="tpu_custom_call" | custom-call | flops 4000000000 | bytes 1000000 | tf_op jit(solution)/shard_map/pallas_call | solution.py:185
  14.9 0.0 collective-permute-done.4.far
  14.9 1.4 %shard_map.69 = (bf16[1,2,64,512]{3,2,1,0:T(8,128)(2,1)}, bf16[16,1,16,256]{3,2,1,0:T(8,128)(2,1)}) custom-call(bf16[4,2,64,256]{3,2,1,0:T(8,128)(2,1)S(1)} %collective-permute-done.4.far, bf16[2,256,128]{2,1,0:T(8,128)(2,1)S(1)} %get-tuple-element.18.q_rows, f32[2,1,256]{2,1,0:T(1,128)S(1)} %get-tuple-element.19.top_ref, ...), custom_call_target="tpu_custom_call" | custom-call | flops 4000000000 | bytes 1000000 | tf_op jit(solution)/shard_map/pallas_call | solution.py:207
  (8 shorter events, 0.1 us)
Async XLA Ops:
  0.7 4.9 %copy-start.3 = (bf16[1,2,64,128]{3,2,1,0:T(8,128)(2,1)S(1)}, bf16[1,2,64,128]{3,2,1,0:T(8,128)(2,1)}, u32[]{:S(2)}) copy-start(bf16[1,2,64,128]{3,2,1,0:T(8,128)(2,1)} %param.7) | copy-start | bytes 98308
  0.7 4.9 %copy-start.4 = (bf16[1,2,64,128]{3,2,1,0:T(8,128)(2,1)S(1)}, bf16[1,2,64,128]{3,2,1,0:T(8,128)(2,1)}, u32[]{:S(2)}) copy-start(bf16[1,2,64,128]{3,2,1,0:T(8,128)(2,1)} %param.6) | copy-start | bytes 98308
  1.5 7.6 %copy-start = (bf16[1,2,16,2048]{3,2,1,0:T(8,128)(2,1)S(1)}, bf16[1,2,16,2048]{3,2,1,0:T(8,128)(2,1)}, u32[]{:S(2)}) copy-start(bf16[1,2,16,2048]{3,2,1,0:T(8,128)(2,1)} %own.1) | copy-start | bytes 393220
  1.5 7.7 %collective-permute-start.3 = (bf16[1,2,16,1024]{3,2,1,0:T(8,128)(2,1)S(1)}, bf16[1,2,16,1024]{3,2,1,0:T(8,128)(2,1)S(1)}, u32[]{:S(2)}, u32[]{:S(2)}) collective-permute-start(bf16[1,2,16,1024]{3,2,1,0:T(8,128)(2,1)S(1)} %constant_dynamic-slice_fusion.2), channel_id=1, source_target_pairs={{0,2},{1,3},{2,0},{3,1},{4,6},{5,7},{6,4},{7,5},{8,10},{9,11},{10,... | collective-permute-start | bytes 196616 | tf_op jit(solution)/shard_map/ppermute | solution.py:161
  5.6 5.3 %collective-permute-start = (bf16[1,2,64,256]{3,2,1,0:T(8,128)(2,1)S(1)}, bf16[1,2,64,256]{3,2,1,0:T(8,128)(2,1)S(1)}, u32[]{:S(2)}, u32[]{:S(2)}) collective-permute-start(bf16[1,2,64,256]{3,2,1,0:T(8,128)(2,1)S(1)} %pad_maximum_fusion), channel_id=1, source_target_pairs={{0,24},{4,28},{8,16},{12,20},{16,8},{20,12},{24,0},{28,4},{1,25},{... | collective-permute-start | bytes 196616 | tf_op jit(solution)/shard_map/ppermute | solution.py:165
  8.1 4.3 %collective-permute-start.1 = (bf16[1,2,64,256]{3,2,1,0:T(8,128)(2,1)S(1)}, bf16[1,2,64,256]{3,2,1,0:T(8,128)(2,1)S(1)}, u32[]{:S(2)}, u32[]{:S(2)}) collective-permute-start(bf16[1,2,64,256]{3,2,1,0:T(8,128)(2,1)S(1)} %pad_maximum_fusion), channel_id=1, source_target_pairs={{0,16},{4,20},{8,24},{12,28},{16,0},{20,4},{24,8},{28,12},{1,17},{... | collective-permute-start | bytes 196616 | tf_op jit(solution)/shard_map/ppermute | solution.py:165
  8.6 4.3 %collective-permute-start.2 = (bf16[1,2,64,256]{3,2,1,0:T(8,128)(2,1)S(1)}, bf16[1,2,64,256]{3,2,1,0:T(8,128)(2,1)S(1)}, u32[]{:S(2)}, u32[]{:S(2)}) collective-permute-start(bf16[1,2,64,256]{3,2,1,0:T(8,128)(2,1)S(1)} %pad_maximum_fusion), channel_id=1, source_target_pairs={{0,8},{4,12},{8,0},{12,4},{16,24},{20,28},{24,16},{28,20},{1,9},{5... | collective-permute-start | bytes 196616 | tf_op jit(solution)/shard_map/ppermute | solution.py:165
  9.2 4.3 %collective-permute-start.5 = (bf16[2,2,16,512]{3,2,1,0:T(8,128)(2,1)S(1)}, bf16[2,2,16,512]{3,2,1,0:T(8,128)(2,1)S(1)}, u32[]{:S(2)}, u32[]{:S(2)}) collective-permute-start(bf16[2,2,16,512]{3,2,1,0:T(8,128)(2,1)S(1)} %pad_maximum_fusion.1), channel_id=1, source_target_pairs={{0,1},{1,0},{2,3},{3,2},{4,5},{5,4},{6,7},{7,6},{8,9},{9,8},{10,11... | collective-permute-start | bytes 196616 | tf_op jit(solution)/shard_map/ppermute | solution.py:175
  12.9 0.7 %copy-start.1 = (s32[8,2,4]{0,2,1:T(4,128)S(1)}, s32[8,2,4]{0,2,1:T(4,128)}, u32[]{:S(2)}) copy-start(s32[8,2,4]{0,2,1:T(4,128)} %param.9) | copy-start | bytes 772
  12.9 0.7 %copy-start.2 = (s32[3]{0:T(128)S(1)}, s32[3]{0:T(128)}, u32[]{:S(2)}) copy-start(s32[3]{0:T(128)} %doc_hbm.1) | copy-start | bytes 40
  12.9 1.9 %collective-permute-start.4 = (bf16[4,2,64,256]{3,2,1,0:T(8,128)(2,1)S(1)}, bf16[4,2,64,256]{3,2,1,0:T(8,128)(2,1)S(1)}, u32[]{:S(2)}, u32[]{:S(2)}) collective-permute-start(bf16[4,2,64,256]{3,2,1,0:T(8,128)(2,1)S(1)} %constant_dynamic-update-slice_fusion.near), channel_id=1, source_target_pairs={{0,4},{4,0},{8,12},{12,8},{16,20},{20,16},{24,28},{28,24},{1,5},{5... | collective-permute-start | bytes 786440 | tf_op jit(solution)/shard_map/ppermute | solution.py:177

commit v2 on v1

--- a/solution.py
+++ b/solution.py
@@ -92,33 +92,37 @@
     return top, total, out
 
 
-def near_kernel(
-    doc_hbm, slot_hbm, own, across, beside, near, q_rows, top_ref, total_ref, out_ref, pages_ref, far_bias_a,
-    far_bias_b, far_targets, doc_lengths, page_slot, sems,
+def plan_kernel(
+    doc_hbm, slot_hbm, bias_a, bias_b, targets, far_bias_a, far_bias_b, far_targets, doc_lengths, page_slot, sems
 ):
-    chips, _, block_tok, _ = near.shape
-    slot_count = pages_ref.shape[0] // PAGE
-    my_blk = lax.axis_index("blk")
     fetch_doc = pltpu.make_async_copy(doc_hbm, doc_lengths, sems.at[0])
     fetch_slot = pltpu.make_async_copy(slot_hbm, page_slot, sems.at[1])
     fetch_doc.start()
     fetch_slot.start()
-    gather_queries(own, across, beside, q_rows)
-    scores = [score_part(q_rows, near, half) for half in range(2)]
     fetch_doc.wait()
     fetch_slot.wait()
-    for half in range(2):
-        bias = key_bias(my_blk, doc_lengths, chips, block_tok, half, 0)
-        top, total, out = weigh_part(scores[half], bias, near, half)
+    my_blk = lax.axis_index("blk")
+    chips = page_slot.shape[2] // 2
+    block_tok = bias_a.shape[0] // chips
+    slot_count = 4 * page_slot.shape[1]
+    for core, refs in enumerate(((bias_a, bias_b, targets), (far_bias_a, far_bias_b, far_targets))):
+        for half in range(2):
+            refs[half][...] = key_bias(my_blk, doc_lengths, chips, block_tok, half, core)
+        refs[2][...] = page_targets(my_blk, page_slot, chips, block_tok, slot_count, core)
+
+
+def near_kernel(
+    own, across, beside, near, bias_a, bias_b, targets, q_rows, top_ref, total_ref, out_ref, pages_ref
+):
+    slot_count = pages_ref.shape[0] // PAGE
+    gather_queries(own, across, beside, q_rows)
+    for half in (1, 0):
+        bias = (bias_a, bias_b)[half][...]
+        top, total, out = weigh_part(score_part(q_rows, near, half), bias, near, half)
         top_ref[half] = top
         total_ref[half] = total
         out_ref[half] = out
-    pages_ref[...] = place_pages(
-        page_targets(my_blk, page_slot, chips, block_tok, slot_count, 0), near, slot_count
-    ).astype(jnp.bfloat16)
-    far_bias_a[...] = key_bias(my_blk, doc_lengths, chips, block_tok, 0, 1)
-    far_bias_b[...] = key_bias(my_blk, doc_lengths, chips, block_tok, 1, 1)
-    far_targets[...] = page_targets(my_blk, page_slot, chips, block_tok, slot_count, 1)
+    pages_ref[...] = place_pages(targets[...], near, slot_count).astype(jnp.bfloat16)
 
 
 def far_kernel(
@@ -155,6 +159,10 @@
     width = q_width // head_count
     rows = width // HEAD_DIM * block_tok
     slot_count = 4 * (block_tok // PAGE)
+    hbm = pl.BlockSpec(memory_space=pl.ANY)
+    vmem = pl.BlockSpec(memory_space=pltpu.VMEM)
+    params = pltpu.CompilerParams(vmem_limit_bytes=32 * 1024 * 1024)
+    cost = pl.CostEstimate(flops=4_000_000_000, bytes_accessed=1_000_000, transcendentals=200_000)
 
     my_head = lax.axis_index("head")
     part = lax.dynamic_slice_in_dim(query_states, ((my_head ^ 2) // 2) * 2 * width, 2 * width, axis=3)
@@ -171,17 +179,33 @@
         ],
         axis=0,
     )
-    near = lax.optimization_barrier((near[::-1], beside))[0][::-1]
+    slots = page_slot.transpose(1, 2, 0)
+    doc_lengths, slots, _ = lax.optimization_barrier((doc_lengths, slots, across))
+    half_cols = blk_count // 2 * block_tok
+    plan = pl.pallas_call(
+        plan_kernel,
+        out_shape=(
+            jax.ShapeDtypeStruct((half_cols, LANES), jnp.float32),
+            jax.ShapeDtypeStruct((2 * half_cols, LANES), jnp.float32),
+            jax.ShapeDtypeStruct((1, 2 * half_cols), jnp.int32),
+        )
+        * 2,
+        in_specs=[hbm] * 2,
+        out_specs=(vmem,) * 6,
+        scratch_shapes=[
+            pltpu.SMEM(doc_lengths.shape, jnp.int32),
+            pltpu.SMEM(slots.shape, jnp.int32),
+            pltpu.SemaphoreType.DMA((2,)),
+        ],
+        compiler_params=params,
+        cost_estimate=pl.CostEstimate(flops=1000, bytes_accessed=1000, transcendentals=0),
+    )(doc_lengths, slots)
+    near, _ = lax.optimization_barrier((near[::-1], beside))
+    near = near[::-1]
     beside = lax.ppermute(beside, "head", [(i, i ^ 1) for i in range(head_count)])
     near = jnp.concatenate([pair] + near, axis=0)
     far = lax.ppermute(near, "blk", [(i, i ^ 1) for i in range(blk_count)])
 
-    hbm = pl.BlockSpec(memory_space=pl.ANY)
-    vmem = pl.BlockSpec(memory_space=pltpu.VMEM)
-    params = pltpu.CompilerParams(vmem_limit_bytes=32 * 1024 * 1024)
-    cost = pl.CostEstimate(flops=4_000_000_000, bytes_accessed=1_000_000, transcendentals=200_000)
-    slots = page_slot.transpose(1, 2, 0)
-    half_cols = blk_count // 2 * block_tok
     stats = pl.pallas_call(
         near_kernel,
         out_shape=(
@@ -190,20 +214,12 @@
             jax.ShapeDtypeStruct((2, 1, rows), jnp.float32),
             jax.ShapeDtypeStruct((2, HEAD_DIM, rows), jnp.float32),
             jax.ShapeDtypeStruct((slot_count * PAGE, 2 * HEAD_DIM), jnp.bfloat16),
-            jax.ShapeDtypeStruct((half_cols, LANES), jnp.float32),
-            jax.ShapeDtypeStruct((2 * half_cols, LANES), jnp.float32),
-            jax.ShapeDtypeStruct((1, 2 * half_cols), jnp.int32),
-        ),
-        in_specs=[hbm] * 2 + [vmem] * 4,
-        out_specs=(vmem,) * 8,
-        scratch_shapes=[
-            pltpu.SMEM(doc_lengths.shape, jnp.int32),
-            pltpu.SMEM(slots.shape, jnp.int32),
-            pltpu.SemaphoreType.DMA((2,)),
-        ],
+        ),
+        in_specs=[vmem] * 7,
+        out_specs=(vmem,) * 5,
         compiler_params=params,
         cost_estimate=cost,
-    )(doc_lengths, slots, query_states, across, beside, near)
+    )(query_states, across, beside, near, *plan[:3])
     return pl.pallas_call(
         far_kernel,
         out_shape=(
@@ -219,7 +235,7 @@
         ],
         compiler_params=params,
         cost_estimate=cost,
-    )(far, *stats)
+    )(far, *stats, *plan[3:])
 
 
 def per_device_long(query_states, key_states, value_states, doc_lengths, page_slot):

time: 16.4 us -> 16.9 us (1.030)
  local copies, waits for them, and re-layouts: 0.93 us -> 1.49 us
  waiting for transfers between devices: 2.61 us -> 2.06 us
  Pallas kernels: 2.63 us -> 3.09 us
    pallas_call x0 -> x1, Pallas kernels: none -> 0.77 us  [per_device(): pl.pallas_call(plan_kernel, out_shape=(jax.ShapeDtypeStruct((half_cols, L...]
    unnamed x13, local copies, waits for them, and re-layouts: 0.05 us -> 0.61 us
    ppermute x1, waiting for transfers between devices: 0.56 us -> 0.01 us  [per_device(): lax.ppermute(beside, 'head', [(i, i ^ 1) for i in range(head_count)])]
    pallas_call x1, Pallas kernels: 1.26 us -> 0.95 us  [per_device(): pl.pallas_call(near_kernel, out_shape=(jax.ShapeDtypeStruct((2, rows, HEA...]
  transfers between devices with their start and end apart: 6 -> 6, of which waited for: 4 -> 3; matrix products, arithmetic and copies ran while one was open for 0% -> 0% of each run, Pallas kernels for 8% -> 10%
where the time goes in v2:
time: 16.9 us; the launch traced here: 16.7 us
  starting transfers between devices  9.29 us (55%)
  Pallas kernels  3.09 us (18%)
  waiting for transfers between devices  2.06 us (12%)
  local copies, waits for them, and re-layouts  1.49 us (9%)
  between operations  0.77 us (5%)
    ppermute x1, starting transfers between devices, per_device(): across = lax.ppermute(part, 'head', [(i, i ^ 2) for i in range(head_count)])  4.04 us
    ppermute x3, starting transfers between devices, per_device(): lax.ppermute(pair, 'blk', [(i, i ^ d) for i in range(blk_count)])  3.55 us
    ppermute x3, waiting for transfers between devices, per_device(): lax.ppermute(pair, 'blk', [(i, i ^ d) for i in range(blk_count)])  2.01 us
    ppermute x1, starting transfers between devices, per_device(): lax.ppermute(beside, 'head', [(i, i ^ 1) for i in range(head_count)])  1.63 us
    pallas_call x1, Pallas kernels, per_device(): pl.pallas_call(far_kernel, out_shape=(jax.ShapeDtypeStruct((1, 2, block_t...  1.37 us
    pallas_call x1, Pallas kernels, per_device(): pl.pallas_call(near_kernel, out_shape=(jax.ShapeDtypeStruct((2, rows, HEA...  0.95 us
    dynamic_slice x1, local copies, waits for them, and re-layouts, per_device(): lax.dynamic_slice_in_dim(query_states, (my_head ^ 2) // 2 * 2 * width, 2...  0.86 us
    pallas_call x1, Pallas kernels, per_device(): pl.pallas_call(plan_kernel, out_shape=(jax.ShapeDtypeStruct((half_cols, L...  0.77 us
  transfers between devices with their start and end apart: 6, of which 3 were waited for; matrix products, arithmetic and copies ran while one was open for 0% of the time, Pallas kernels for 10%

profile of v2, /device:TPU:0, one launch (start us, length us, event | category | flops | bytes accessed | tf_op | source)
XLA Modules:
  0.0 16.7 jit_solution(17266004830692991929)
XLA Ops:
  0.7 0.0 copy-start.3
  0.7 0.0 copy-start.4
  0.7 0.9 %constant_dynamic-slice_fusion.2 = bf16[1,2,16,1024]{3,2,1,0:T(8,128)(2,1)S(1)} fusion(bf16[1,2,16,2048]{3,2,1,0:T(8,128)(2,1)} %own.1, s32[]{:T(128)S(6)} %select_n.21), kind=kLoop, calls=%fused_computation.8 | loop fusion | bytes 131076 | tf_op jit(solution)/shard_map/dynamic_slice | solution.py:168
  1.5 0.0 copy-start
  1.5 4.0 %collective-permute-start.3 = (bf16[1,2,16,1024]{3,2,1,0:T(8,128)(2,1)S(1)}, bf16[1,2,16,1024]{3,2,1,0:T(8,128)(2,1)S(1)}, u32[]{:S(2)}, u32[]{:S(2)}) collective-permute-start(bf16[1,2,16,1024]{3,2,1,0:T(8,128)(2,1)S(1)} %constant_dynamic-slice_fusion.2), channel_id=1, source_target_pairs={{0,2},{1,3},{2,0},{3,1},{4,6},{5,7},{6,4},{7,5},{8,10},{9,11},{10,... | collective-permute-start | bytes 196616 | tf_op jit(solution)/shard_map/ppermute | solution.py:169
  5.6 0.0 copy-done.3
  5.6 0.0 copy-done.4
  5.6 2.5 %collective-permute-start = (bf16[1,2,64,256]{3,2,1,0:T(8,128)(2,1)S(1)}, bf16[1,2,64,256]{3,2,1,0:T(8,128)(2,1)S(1)}, u32[]{:S(2)}, u32[]{:S(2)}) collective-permute-start(bf16[1,2,64,256]{3,2,1,0:T(8,128)(2,1)S(1)} %pad_maximum_fusion), channel_id=1, source_target_pairs={{0,24},{4,28},{8,16},{12,20},{16,8},{20,12},{24,0},{28,4},{1,25},{... | collective-permute-start | bytes 196616 | tf_op jit(solution)/shard_map/ppermute | solution.py:173
  8.1 0.5 %collective-permute-start.1 = (bf16[1,2,64,256]{3,2,1,0:T(8,128)(2,1)S(1)}, bf16[1,2,64,256]{3,2,1,0:T(8,128)(2,1)S(1)}, u32[]{:S(2)}, u32[]{:S(2)}) collective-permute-start(bf16[1,2,64,256]{3,2,1,0:T(8,128)(2,1)S(1)} %pad_maximum_fusion), channel_id=1, source_target_pairs={{0,16},{4,20},{8,24},{12,28},{16,0},{20,4},{24,8},{28,12},{1,17},{... | collective-permute-start | bytes 196616 | tf_op jit(solution)/shard_map/ppermute | solution.py:173
  8.6 0.5 %collective-permute-start.2 = (bf16[1,2,64,256]{3,2,1,0:T(8,128)(2,1)S(1)}, bf16[1,2,64,256]{3,2,1,0:T(8,128)(2,1)S(1)}, u32[]{:S(2)}, u32[]{:S(2)}) collective-permute-start(bf16[1,2,64,256]{3,2,1,0:T(8,128)(2,1)S(1)} %pad_maximum_fusion), channel_id=1, source_target_pairs={{0,8},{4,12},{8,0},{12,4},{16,24},{20,28},{24,16},{28,20},{1,9},{5... | collective-permute-start | bytes 196616 | tf_op jit(solution)/shard_map/ppermute | solution.py:173
  9.2 0.0 copy-done
  9.2 0.0 collective-permute-done.3.across
  9.2 1.6 %collective-permute-start.5 = (bf16[2,2,16,512]{3,2,1,0:T(8,128)(2,1)S(1)}, bf16[2,2,16,512]{3,2,1,0:T(8,128)(2,1)S(1)}, u32[]{:S(2)}, u32[]{:S(2)}) collective-permute-start(bf16[2,2,16,512]{3,2,1,0:T(8,128)(2,1)S(1)} %pad_maximum_fusion.1), channel_id=1, source_target_pairs={{0,1},{1,0},{2,3},{3,2},{4,5},{5,4},{6,7},{7,6},{8,9},{9,8},{10,11... | collective-permute-start | bytes 196616 | tf_op jit(solution)/shard_map/ppermute | solution.py:205
  10.9 0.1 collective-permute-done
  10.9 1.4 %collective-permute-done.1 = bf16[1,2,64,256]{3,2,1,0:T(8,128)(2,1)S(1)} collective-permute-done((bf16[1,2,64,256]{3,2,1,0:T(8,128)(2,1)S(1)}, bf16[1,2,64,256]{3,2,1,0:T(8,128)(2,1)S(1)}, u32[]{:S(2)}, u32[]{:S(2)}) %collective-permute-start.1) | collective-permute-done | bytes 65568 | tf_op jit(solution)/shard_map/ppermute | solution.py:173
  12.4 0.5 %collective-permute-done.2 = bf16[1,2,64,256]{3,2,1,0:T(8,128)(2,1)S(1)} collective-permute-done((bf16[1,2,64,256]{3,2,1,0:T(8,128)(2,1)S(1)}, bf16[1,2,64,256]{3,2,1,0:T(8,128)(2,1)S(1)}, u32[]{:S(2)}, u32[]{:S(2)}) %collective-permute-start.2) | collective-permute-done | bytes 65568 | tf_op jit(solution)/shard_map/ppermute | solution.py:173
  12.9 0.0 copy-start.1
  12.9 0.0 copy-start.2
  12.9 0.1 collective-permute-start.4
  13.0 0.6 %copy-done.1 = s32[8,2,4]{0,2,1:T(4,128)S(1)} copy-done((s32[8,2,4]{0,2,1:T(4,128)S(1)}, s32[8,2,4]{0,2,1:T(4,128)}, u32[]{:S(2)}) %copy-start.1) | copy-done | bytes 280
  13.6 0.0 copy-done.2
  13.6 0.8 %shard_map.68 = (f32[256,128]{1,0:T(8,128)S(1)}, f32[512,128]{1,0:T(8,128)S(1)}, s32[1,512]{1,0:T(1,128)S(1)}, f32[256,128]{1,0:T(8,128)S(1)}, f32[512,128]{1,0:T(8,128)S(1)}, /*index=5*/s32[1,512]{1,0:T(1,128)S(1)}) custom-call(s32[3]{0:T(128)S(1)} %copy-done.2, s32[2,4,8]{2,1,0:T(4,128)S(1)} %bitcast.1), custom_call_target="tpu_custom_call" | custom-call | flops 1000 | bytes 1000 | tf_op jit(solution)/shard_map/pallas_call | solution.py:185
  14.4 0.0 collective-permute-done.5.beside
  14.4 1.0 %shard_map.69 = (bf16[2,256,128]{2,1,0:T(8,128)(2,1)S(1)}, f32[2,1,256]{2,1,0:T(1,128)S(1)}, f32[2,1,256]{2,1,0:T(1,128)S(1)}, f32[2,128,256]{2,1,0:T(8,128)S(1)}, bf16[256,256]{1,0:T(8,128)(2,1)S(1)}) custom-call(bf16[1,2,16,2048]{3,2,1,0:T(8,128)(2,1)S(1)} %copy-done, bf16[1,2,16,1024]{3,2,1,0:T(8,128)(2,1)S(1)} %collective-permute-done.3.across, ...), custom_call_target="tpu_custom_call" | custom-call | flops 4000000000 | bytes 1000000 | tf_op jit(solution)/shard_map/pallas_call | solution.py:209
  15.3 0.0 collective-permute-done.4.far
  15.3 1.4 %shard_map.70 = (bf16[1,2,64,512]{3,2,1,0:T(8,128)(2,1)}, bf16[16,1,16,256]{3,2,1,0:T(8,128)(2,1)}) custom-call(bf16[4,2,64,256]{3,2,1,0:T(8,128)(2,1)S(1)} %collective-permute-done.4.far, bf16[2,256,128]{2,1,0:T(8,128)(2,1)S(1)} %get-tuple-element.28.q_rows, f32[2,1,256]{2,1,0:T(1,128)S(1)} %get-tuple-element.29.top_ref, ...), custom_call_target="tpu_custom_call" | custom-call | flops 4000000000 | bytes 1000000 | tf_op jit(solution)/shard_map/pallas_call | solution.py:223
  (8 shorter events, 0.1 us)
Async XLA Ops:
  0.7 4.9 %copy-start.3 = (bf16[1,2,64,128]{3,2,1,0:T(8,128)(2,1)S(1)}, bf16[1,2,64,128]{3,2,1,0:T(8,128)(2,1)}, u32[]{:S(2)}) copy-start(bf16[1,2,64,128]{3,2,1,0:T(8,128)(2,1)} %param.7) | copy-start | bytes 98308
  0.7 4.9 %copy-start.4 = (bf16[1,2,64,128]{3,2,1,0:T(8,128)(2,1)S(1)}, bf16[1,2,64,128]{3,2,1,0:T(8,128)(2,1)}, u32[]{:S(2)}) copy-start(bf16[1,2,64,128]{3,2,1,0:T(8,128)(2,1)} %param.6) | copy-start | bytes 98308
  1.5 7.6 %copy-start = (bf16[1,2,16,2048]{3,2,1,0:T(8,128)(2,1)S(1)}, bf16[1,2,16,2048]{3,2,1,0:T(8,128)(2,1)}, u32[]{:S(2)}) copy-start(bf16[1,2,16,2048]{3,2,1,0:T(8,128)(2,1)} %own.1) | copy-start | bytes 393220
  1.5 7.7 %collective-permute-start.3 = (bf16[1,2,16,1024]{3,2,1,0:T(8,128)(2,1)S(1)}, bf16[1,2,16,1024]{3,2,1,0:T(8,128)(2,1)S(1)}, u32[]{:S(2)}, u32[]{:S(2)}) collective-permute-start(bf16[1,2,16,1024]{3,2,1,0:T(8,128)(2,1)S(1)} %constant_dynamic-slice_fusion.2), channel_id=1, source_target_pairs={{0,2},{1,3},{2,0},{3,1},{4,6},{5,7},{6,4},{7,5},{8,10},{9,11},{10,... | collective-permute-start | bytes 196616 | tf_op jit(solution)/shard_map/ppermute | solution.py:169
  5.6 5.3 %collective-permute-start = (bf16[1,2,64,256]{3,2,1,0:T(8,128)(2,1)S(1)}, bf16[1,2,64,256]{3,2,1,0:T(8,128)(2,1)S(1)}, u32[]{:S(2)}, u32[]{:S(2)}) collective-permute-start(bf16[1,2,64,256]{3,2,1,0:T(8,128)(2,1)S(1)} %pad_maximum_fusion), channel_id=1, source_target_pairs={{0,24},{4,28},{8,16},{12,20},{16,8},{20,12},{24,0},{28,4},{1,25},{... | collective-permute-start | bytes 196616 | tf_op jit(solution)/shard_map/ppermute | solution.py:173
  8.1 4.3 %collective-permute-start.1 = (bf16[1,2,64,256]{3,2,1,0:T(8,128)(2,1)S(1)}, bf16[1,2,64,256]{3,2,1,0:T(8,128)(2,1)S(1)}, u32[]{:S(2)}, u32[]{:S(2)}) collective-permute-start(bf16[1,2,64,256]{3,2,1,0:T(8,128)(2,1)S(1)} %pad_maximum_fusion), channel_id=1, source_target_pairs={{0,16},{4,20},{8,24},{12,28},{16,0},{20,4},{24,8},{28,12},{1,17},{... | collective-permute-start | bytes 196616 | tf_op jit(solution)/shard_map/ppermute | solution.py:173
  8.6 4.3 %collective-permute-start.2 = (bf16[1,2,64,256]{3,2,1,0:T(8,128)(2,1)S(1)}, bf16[1,2,64,256]{3,2,1,0:T(8,128)(2,1)S(1)}, u32[]{:S(2)}, u32[]{:S(2)}) collective-permute-start(bf16[1,2,64,256]{3,2,1,0:T(8,128)(2,1)S(1)} %pad_maximum_fusion), channel_id=1, source_target_pairs={{0,8},{4,12},{8,0},{12,4},{16,24},{20,28},{24,16},{28,20},{1,9},{5... | collective-permute-start | bytes 196616 | tf_op jit(solution)/shard_map/ppermute | solution.py:173
  9.2 5.1 %collective-permute-start.5 = (bf16[2,2,16,512]{3,2,1,0:T(8,128)(2,1)S(1)}, bf16[2,2,16,512]{3,2,1,0:T(8,128)(2,1)S(1)}, u32[]{:S(2)}, u32[]{:S(2)}) collective-permute-start(bf16[2,2,16,512]{3,2,1,0:T(8,128)(2,1)S(1)} %pad_maximum_fusion.1), channel_id=1, source_target_pairs={{0,1},{1,0},{2,3},{3,2},{4,5},{5,4},{6,7},{7,6},{8,9},{9,8},{10,11... | collective-permute-start | bytes 196616 | tf_op jit(solution)/shard_map/ppermute | solution.py:205
  12.9 0.7 %copy-start.1 = (s32[8,2,4]{0,2,1:T(4,128)S(1)}, s32[8,2,4]{0,2,1:T(4,128)}, u32[]{:S(2)}) copy-start(s32[8,2,4]{0,2,1:T(4,128)} %param.9) | copy-start | bytes 772
  12.9 0.7 %copy-start.2 = (s32[3]{0:T(128)S(1)}, s32[3]{0:T(128)}, u32[]{:S(2)}) copy-start(s32[3]{0:T(128)} %doc_hbm) | copy-start | bytes 40
  12.9 2.4 %collective-permute-start.4 = (bf16[4,2,64,256]{3,2,1,0:T(8,128)(2,1)S(1)}, bf16[4,2,64,256]{3,2,1,0:T(8,128)(2,1)S(1)}, u32[]{:S(2)}, u32[]{:S(2)}) collective-permute-start(bf16[4,2,64,256]{3,2,1,0:T(8,128)(2,1)S(1)} %constant_dynamic-update-slice_fusion.near), channel_id=1, source_target_pairs={{0,4},{4,0},{8,12},{12,8},{16,20},{20,16},{24,28},{28,24},{1,5},{5... | collective-permute-start | bytes 786440 | tf_op jit(solution)/shard_map/ppermute | solution.py:207

commit v3 on v1

--- a/solution.py
+++ b/solution.py
@@ -1,3 +1,5 @@
+import functools
+
 import jax
 import jax.numpy as jnp
 from jax import lax
@@ -11,33 +13,13 @@
 LANES = 128
 
 
-def gather_queries(own, across, beside, q_rows):
-    my_head = lax.axis_index("head")
-    width = beside.shape[-1]
-    sub_tok = own.shape[2]
-    group = width // HEAD_DIM
-    block_tok = q_rows.shape[1] // group
-    for half in range(2):
-        for g in range(group):
-            lane = g * HEAD_DIM
-            mine = pl.multiple_of(my_head * width + lane, HEAD_DIM)
-            low = pl.multiple_of((my_head % 2) * width + lane, HEAD_DIM)
-            parts = (
-                own[0, half, :, pl.ds(mine, HEAD_DIM)],
-                beside[0, half, :, lane : lane + HEAD_DIM],
-                across[0, half, :, pl.ds(low, HEAD_DIM)],
-                beside[1, half, :, lane : lane + HEAD_DIM],
-            )
-            for d, part in enumerate(parts):
-                row = pl.multiple_of(g * block_tok + (my_head ^ d) * sub_tok, sub_tok)
-                q_rows[half, pl.ds(row, sub_tok), :] = part
-
-
-def key_bias(my_blk, doc_lengths, chips, block_tok, half, core):
+def key_bias(my_blk, doc_lengths, chips, block_tok, sub_tok, half, core, odd):
     blk_count = 2 * chips
     shape = (block_tok, LANES)
     my_block = my_blk if half == 0 else 2 * blk_count - 1 - my_blk
-    q_pos = my_block * block_tok + lax.broadcasted_iota(jnp.int32, (1, LANES), 1) % block_tok
+    lane = lax.broadcasted_iota(jnp.int32, (1, LANES), 1)
+    sender = (lax.axis_index("head") ^ odd) ^ (2 * (lane // sub_tok % 2))
+    q_pos = my_block * block_tok + sender * sub_tok + lane % sub_tok
     first = jnp.zeros_like(q_pos)
     bound = 0
     for k in range(doc_lengths.shape[0] - 1):
@@ -74,14 +56,13 @@
     return jnp.dot(chosen, rows, preferred_element_type=jnp.float32)
 
 
-def score_part(q_rows, pairs, half):
+def score_part(queries, pairs, half):
     keys = pairs[:, : half + 1].reshape(-1, 2 * HEAD_DIM)[:, :HEAD_DIM]
-    return lax.dot_general(keys, q_rows[half], (((1,), (1,)), ((), ())), preferred_element_type=jnp.float32)
+    return lax.dot_general(keys, queries, (((1,), (1,)), ((), ())), preferred_element_type=jnp.float32)
 
 
 def weigh_part(scores, bias, pairs, half):
     values = pairs[:, : half + 1].reshape(-1, 2 * HEAD_DIM)[:, HEAD_DIM:]
-    bias = jnp.concatenate([bias] * (scores.shape[1] // LANES), axis=1)
     scores = scores * (HEAD_DIM**-0.5 * LOG2E) + bias
     top = jnp.max(scores, axis=0, keepdims=True)
     weights = jnp.exp2(scores - top)
@@ -92,55 +73,90 @@
     return top, total, out
 
 
-def near_kernel(
-    doc_hbm, slot_hbm, own, across, beside, near, q_rows, top_ref, total_ref, out_ref, pages_ref, far_bias_a,
-    far_bias_b, far_targets, doc_lengths, page_slot, sems,
+def first_kernel(
+    doc_hbm, slot_hbm, own, across, near, q_ref, top_ref, total_ref, out_ref, bias_a, bias_b, far_bias_a, far_bias_b,
+    far_targets, pages_ref, doc_lengths, page_slot, sems,
 ):
     chips, _, block_tok, _ = near.shape
     slot_count = pages_ref.shape[0] // PAGE
+    width = across.shape[3] // 2
+    sub_tok = own.shape[2]
     my_blk = lax.axis_index("blk")
+    my_head = lax.axis_index("head")
     fetch_doc = pltpu.make_async_copy(doc_hbm, doc_lengths, sems.at[0])
     fetch_slot = pltpu.make_async_copy(slot_hbm, page_slot, sems.at[1])
     fetch_doc.start()
     fetch_slot.start()
-    gather_queries(own, across, beside, q_rows)
-    scores = [score_part(q_rows, near, half) for half in range(2)]
+    scores = []
+    for half in range(2):
+        parts = []
+        for lane in range(0, width, HEAD_DIM):
+            mine = pl.multiple_of(my_head * width + lane, HEAD_DIM)
+            low = pl.multiple_of((my_head % 2) * width + lane, HEAD_DIM)
+            parts.append(own[0, half, :, pl.ds(mine, HEAD_DIM)])
+            parts.append(across[0, half, :, pl.ds(low, HEAD_DIM)])
+        queries = jnp.concatenate(parts, axis=0)
+        q_ref[half] = queries
+        scores.append(score_part(queries, near, half))
     fetch_doc.wait()
     fetch_slot.wait()
-    for half in range(2):
-        bias = key_bias(my_blk, doc_lengths, chips, block_tok, half, 0)
-        top, total, out = weigh_part(scores[half], bias, near, half)
+    bias = functools.partial(key_bias, my_blk, doc_lengths, chips, block_tok, sub_tok)
+    for half in (1, 0):
+        top, total, out = weigh_part(scores[half], bias(half, 0, 0), near, half)
         top_ref[half] = top
         total_ref[half] = total
         out_ref[half] = out
-    pages_ref[...] = place_pages(
-        page_targets(my_blk, page_slot, chips, block_tok, slot_count, 0), near, slot_count
-    ).astype(jnp.bfloat16)
-    far_bias_a[...] = key_bias(my_blk, doc_lengths, chips, block_tok, 0, 1)
-    far_bias_b[...] = key_bias(my_blk, doc_lengths, chips, block_tok, 1, 1)
-    far_targets[...] = page_targets(my_blk, page_slot, chips, block_tok, slot_count, 1)
+        (bias_a, bias_b)[half][...] = bias(half, 0, 1)
+        for odd in range(2):
+            (far_bias_a, far_bias_b)[half][:, odd * LANES : (odd + 1) * LANES] = bias(half, 1, odd)
+    targets = functools.partial(page_targets, my_blk, page_slot, chips, block_tok, slot_count)
+    pages_ref[...] = place_pages(targets(0), near, slot_count).astype(jnp.bfloat16)
+    far_targets[...] = targets(1)
+
+
+def second_kernel(beside, near, bias_a, bias_b, q_ref, top_ref, total_ref, out_ref):
+    width = beside.shape[3]
+    for half in (1, 0):
+        queries = jnp.concatenate(
+            [beside[d, half, :, lane : lane + HEAD_DIM] for lane in range(0, width, HEAD_DIM) for d in range(2)], axis=0
+        )
+        q_ref[half] = queries
+        bias = (bias_a, bias_b)[half][...]
+        top, total, out = weigh_part(score_part(queries, near, half), bias, near, half)
+        top_ref[half] = top
+        total_ref[half] = total
+        out_ref[half] = out
 
 
 def far_kernel(
-    far, q_rows, top_ref, total_ref, out_ref, pages_ref, far_bias_a, far_bias_b, far_targets, attended, kv_cache,
-    pages, result, sems,
+    far, far_bias_a, far_bias_b, far_targets, pages_ref, q_even, top_even, total_even, out_even, q_odd, top_odd,
+    total_odd, out_odd, attended, kv_cache, pages, result, sems,
 ):
-    block_tok = far.shape[2]
     slot_count = kv_cache.shape[0]
+    my_head = lax.axis_index("head")
     moved = place_pages(far_targets[...], far, slot_count) + pages_ref[...].astype(jnp.float32)
     pages[...] = moved.astype(jnp.bfloat16).reshape(pages.shape)
     writes = [pltpu.make_async_copy(pages, kv_cache, sems.at[2])]
     writes[0].start()
     for half in (1, 0):
+        queries = jnp.concatenate([q_even[half], q_odd[half]], axis=0)
+        near_top = jnp.concatenate([top_even[half], top_odd[half]], axis=1)
+        near_total = jnp.concatenate([total_even[half], total_odd[half]], axis=1)
+        near_out = jnp.concatenate([out_even[half], out_odd[half]], axis=1)
         bias = (far_bias_a, far_bias_b)[half][...]
-        top, total, out = weigh_part(score_part(q_rows, far, half), bias, far, half)
-        best = jnp.maximum(top, top_ref[half])
+        top, total, out = weigh_part(score_part(queries, far, half), bias, far, half)
+        best = jnp.maximum(top, near_top)
         here = jnp.exp2(top - best)
-        there = jnp.exp2(top_ref[half] - best)
-        inverse = 1.0 / (total * here + total_ref[half] * there)
-        out = (out * (here * inverse) + out_ref[half] * (there * inverse)).T.astype(jnp.bfloat16)
-        for g in range(out.shape[0] // block_tok):
-            result[half, :, g * HEAD_DIM : (g + 1) * HEAD_DIM] = out[g * block_tok : (g + 1) * block_tok]
+        there = jnp.exp2(near_top - best)
+        inverse = 1.0 / (total * here + near_total * there)
+        out = (out * (here * inverse) + near_out * (there * inverse)).T.astype(jnp.bfloat16)
+        sub_tok = LANES * HEAD_DIM // (2 * result.shape[2])
+        for odd in range(2):
+            for g in range(result.shape[2] // HEAD_DIM):
+                for p in range(2):
+                    row = pl.multiple_of((my_head ^ (odd + 2 * p)) * sub_tok, sub_tok)
+                    start = odd * LANES + (2 * g + p) * sub_tok
+                    result[half, pl.ds(row, sub_tok), g * HEAD_DIM : (g + 1) * HEAD_DIM] = out[start : start + sub_tok]
         writes.append(pltpu.make_async_copy(result.at[half], attended.at[0, half], sems.at[half]))
         writes[-1].start()
     for write in writes:
@@ -153,7 +169,6 @@
     q_width = query_states.shape[3]
     block_tok = key_states.shape[2]
     width = q_width // head_count
-    rows = width // HEAD_DIM * block_tok
     slot_count = 4 * (block_tok // PAGE)
 
     my_head = lax.axis_index("head")
@@ -182,20 +197,25 @@
     cost = pl.CostEstimate(flops=4_000_000_000, bytes_accessed=1_000_000, transcendentals=200_000)
     slots = page_slot.transpose(1, 2, 0)
     half_cols = blk_count // 2 * block_tok
-    stats = pl.pallas_call(
-        near_kernel,
-        out_shape=(
-            jax.ShapeDtypeStruct((2, rows, HEAD_DIM), jnp.bfloat16),
-            jax.ShapeDtypeStruct((2, 1, rows), jnp.float32),
-            jax.ShapeDtypeStruct((2, 1, rows), jnp.float32),
-            jax.ShapeDtypeStruct((2, HEAD_DIM, rows), jnp.float32),
-            jax.ShapeDtypeStruct((slot_count * PAGE, 2 * HEAD_DIM), jnp.bfloat16),
+    stats = (
+        jax.ShapeDtypeStruct((2, LANES, HEAD_DIM), jnp.bfloat16),
+        jax.ShapeDtypeStruct((2, 1, LANES), jnp.float32),
+        jax.ShapeDtypeStruct((2, 1, LANES), jnp.float32),
+        jax.ShapeDtypeStruct((2, HEAD_DIM, LANES), jnp.float32),
+    )
+    *even, bias_a, bias_b, far_bias_a, far_bias_b, far_targets, pages = pl.pallas_call(
+        first_kernel,
+        out_shape=stats
+        + (
             jax.ShapeDtypeStruct((half_cols, LANES), jnp.float32),
             jax.ShapeDtypeStruct((2 * half_cols, LANES), jnp.float32),
+            jax.ShapeDtypeStruct((half_cols, 2 * LANES), jnp.float32),
+            jax.ShapeDtypeStruct((2 * half_cols, 2 * LANES), jnp.float32),
             jax.ShapeDtypeStruct((1, 2 * half_cols), jnp.int32),
-        ),
-        in_specs=[hbm] * 2 + [vmem] * 4,
-        out_specs=(vmem,) * 8,
+            jax.ShapeDtypeStruct((slot_count * PAGE, 2 * HEAD_DIM), jnp.bfloat16),
+        ),
+        in_specs=[hbm] * 2 + [vmem] * 3,
+        out_specs=(vmem,) * 10,
         scratch_shapes=[
             pltpu.SMEM(doc_lengths.shape, jnp.int32),
             pltpu.SMEM(slots.shape, jnp.int32),
@@ -203,14 +223,22 @@
         ],
         compiler_params=params,
         cost_estimate=cost,
-    )(doc_lengths, slots, query_states, across, beside, near)
+    )(doc_lengths, slots, query_states, across, near)
+    odd = pl.pallas_call(
+        second_kernel,
+        out_shape=stats,
+        in_specs=[vmem] * 4,
+        out_specs=(vmem,) * 4,
+        compiler_params=params,
+        cost_estimate=cost,
+    )(beside, near, bias_a, bias_b)
     return pl.pallas_call(
         far_kernel,
         out_shape=(
             jax.ShapeDtypeStruct((1, 2, block_tok, width), jnp.bfloat16),
             jax.ShapeDtypeStruct((slot_count, 1, PAGE, 2 * HEAD_DIM), jnp.bfloat16),
         ),
-        in_specs=[vmem] * 9,
+        in_specs=[vmem] * 13,
         out_specs=(hbm, hbm),
         scratch_shapes=[
             pltpu.VMEM((slot_count, 1, PAGE, 2 * HEAD_DIM), jnp.bfloat16),
@@ -219,7 +247,7 @@
         ],
         compiler_params=params,
         cost_estimate=cost,
-    )(far, *stats)
+    )(far, far_bias_a, far_bias_b, far_targets, pages, *even, *odd)
 
 
 def per_device_long(query_states, key_states, value_states, doc_lengths, page_slot):

time: 16.4 us -> 17.2 us (1.049)
  Pallas kernels: 2.63 us -> 3.41 us
  local copies, waits for them, and re-layouts: 0.93 us -> 1.49 us
  waiting for transfers between devices: 2.61 us -> 2.06 us
    pallas_call x1 -> x2, Pallas kernels: 1.26 us -> 2.02 us  [the longest x1 1.36 us: per_device(): pl.pallas_call(first_kernel, out_shape=stats + (jax.ShapeDtypeStruct((hal...]
    unnamed x13, local copies, waits for them, and re-layouts: 0.05 us -> 0.61 us
    ppermute x1, waiting for transfers between devices: 0.56 us -> 0.01 us  [per_device(): lax.ppermute(beside, 'head', [(i, i ^ 1) for i in range(head_count)])]
  transfers between devices with their start and end apart: 6 -> 6, of which waited for: 4 -> 3; matrix products, arithmetic and copies ran while one was open for 0% -> 0% of each run, Pallas kernels for 8% -> 12%
where the time goes in v3:
time: 17.2 us; the launch traced here: 17 us
  starting transfers between devices  9.29 us (54%)
  Pallas kernels  3.41 us (20%)
  waiting for transfers between devices  2.06 us (12%)
  local copies, waits for them, and re-layouts  1.49 us (9%)
  between operations  0.77 us (4%)
    ppermute x1, starting transfers between devices, per_device(): across = lax.ppermute(part, 'head', [(i, i ^ 2) for i in range(head_count)])  4.04 us
    ppermute x3, starting transfers between devices, per_device(): lax.ppermute(pair, 'blk', [(i, i ^ d) for i in range(blk_count)])  3.55 us
    ppermute x3, waiting for transfers between devices, per_device(): lax.ppermute(pair, 'blk', [(i, i ^ d) for i in range(blk_count)])  2.01 us
    ppermute x1, starting transfers between devices, per_device(): lax.ppermute(beside, 'head', [(i, i ^ 1) for i in range(head_count)])  1.63 us
    pallas_call x1, Pallas kernels, per_device(): pl.pallas_call(far_kernel, out_shape=(jax.ShapeDtypeStruct((1, 2, block_t...  1.39 us
    pallas_call x1, Pallas kernels, per_device(): pl.pallas_call(first_kernel, out_shape=stats + (jax.ShapeDtypeStruct((hal...  1.36 us
    dynamic_slice x1, local copies, waits for them, and re-layouts, per_device(): lax.dynamic_slice_in_dim(query_states, (my_head ^ 2) // 2 * 2 * width, 2...  0.86 us
    pallas_call x1, Pallas kernels, per_device(): pl.pallas_call(second_kernel, out_shape=stats, in_specs=[vmem] * 4, out_s...  0.66 us
  transfers between devices with their start and end apart: 6, of which 3 were waited for; matrix products, arithmetic and copies ran while one was open for 0% of the time, Pallas kernels for 12%

profile of v3, /device:TPU:0, one launch (start us, length us, event | category | flops | bytes accessed | tf_op | source)
XLA Modules:
  0.0 17.0 jit_solution(2881817398301112204)
XLA Ops:
  0.7 0.0 copy-start.3
  0.7 0.0 copy-start.4
  0.7 0.9 %constant_dynamic-slice_fusion.2 = bf16[1,2,16,1024]{3,2,1,0:T(8,128)(2,1)S(1)} fusion(bf16[1,2,16,2048]{3,2,1,0:T(8,128)(2,1)} %own.1, s32[]{:T(128)S(6)} %select_n.21), kind=kLoop, calls=%fused_computation.8 | loop fusion | bytes 131076 | tf_op jit(solution)/shard_map/dynamic_slice | solution.py:175
  1.5 0.0 copy-start
  1.5 4.0 %collective-permute-start.3 = (bf16[1,2,16,1024]{3,2,1,0:T(8,128)(2,1)S(1)}, bf16[1,2,16,1024]{3,2,1,0:T(8,128)(2,1)S(1)}, u32[]{:S(2)}, u32[]{:S(2)}) collective-permute-start(bf16[1,2,16,1024]{3,2,1,0:T(8,128)(2,1)S(1)} %constant_dynamic-slice_fusion.2), channel_id=1, source_target_pairs={{0,2},{1,3},{2,0},{3,1},{4,6},{5,7},{6,4},{7,5},{8,10},{9,11},{10,... | collective-permute-start | bytes 196616 | tf_op jit(solution)/shard_map/ppermute | solution.py:176
  5.6 0.0 copy-done.3
  5.6 0.0 copy-done.4
  5.6 2.5 %collective-permute-start = (bf16[1,2,64,256]{3,2,1,0:T(8,128)(2,1)S(1)}, bf16[1,2,64,256]{3,2,1,0:T(8,128)(2,1)S(1)}, u32[]{:S(2)}, u32[]{:S(2)}) collective-permute-start(bf16[1,2,64,256]{3,2,1,0:T(8,128)(2,1)S(1)} %pad_maximum_fusion), channel_id=1, source_target_pairs={{0,24},{4,28},{8,16},{12,20},{16,8},{20,12},{24,0},{28,4},{1,25},{... | collective-permute-start | bytes 196616 | tf_op jit(solution)/shard_map/ppermute | solution.py:180
  8.1 0.5 %collective-permute-start.1 = (bf16[1,2,64,256]{3,2,1,0:T(8,128)(2,1)S(1)}, bf16[1,2,64,256]{3,2,1,0:T(8,128)(2,1)S(1)}, u32[]{:S(2)}, u32[]{:S(2)}) collective-permute-start(bf16[1,2,64,256]{3,2,1,0:T(8,128)(2,1)S(1)} %pad_maximum_fusion), channel_id=1, source_target_pairs={{0,16},{4,20},{8,24},{12,28},{16,0},{20,4},{24,8},{28,12},{1,17},{... | collective-permute-start | bytes 196616 | tf_op jit(solution)/shard_map/ppermute | solution.py:180
  8.6 0.5 %collective-permute-start.2 = (bf16[1,2,64,256]{3,2,1,0:T(8,128)(2,1)S(1)}, bf16[1,2,64,256]{3,2,1,0:T(8,128)(2,1)S(1)}, u32[]{:S(2)}, u32[]{:S(2)}) collective-permute-start(bf16[1,2,64,256]{3,2,1,0:T(8,128)(2,1)S(1)} %pad_maximum_fusion), channel_id=1, source_target_pairs={{0,8},{4,12},{8,0},{12,4},{16,24},{20,28},{24,16},{28,20},{1,9},{5... | collective-permute-start | bytes 196616 | tf_op jit(solution)/shard_map/ppermute | solution.py:180
  9.2 0.0 copy-done
  9.2 0.0 collective-permute-done.3.across
  9.2 1.6 %collective-permute-start.5 = (bf16[2,2,16,512]{3,2,1,0:T(8,128)(2,1)S(1)}, bf16[2,2,16,512]{3,2,1,0:T(8,128)(2,1)S(1)}, u32[]{:S(2)}, u32[]{:S(2)}) collective-permute-start(bf16[2,2,16,512]{3,2,1,0:T(8,128)(2,1)S(1)} %pad_maximum_fusion.1), channel_id=1, source_target_pairs={{0,1},{1,0},{2,3},{3,2},{4,5},{5,4},{6,7},{7,6},{8,9},{9,8},{10,11... | collective-permute-start | bytes 196616 | tf_op jit(solution)/shard_map/ppermute | solution.py:190
  10.9 0.1 collective-permute-done
  10.9 1.4 %collective-permute-done.1 = bf16[1,2,64,256]{3,2,1,0:T(8,128)(2,1)S(1)} collective-permute-done((bf16[1,2,64,256]{3,2,1,0:T(8,128)(2,1)S(1)}, bf16[1,2,64,256]{3,2,1,0:T(8,128)(2,1)S(1)}, u32[]{:S(2)}, u32[]{:S(2)}) %collective-permute-start.1) | collective-permute-done | bytes 65568 | tf_op jit(solution)/shard_map/ppermute | solution.py:180
  12.4 0.5 %collective-permute-done.2 = bf16[1,2,64,256]{3,2,1,0:T(8,128)(2,1)S(1)} collective-permute-done((bf16[1,2,64,256]{3,2,1,0:T(8,128)(2,1)S(1)}, bf16[1,2,64,256]{3,2,1,0:T(8,128)(2,1)S(1)}, u32[]{:S(2)}, u32[]{:S(2)}) %collective-permute-start.2) | collective-permute-done | bytes 65568 | tf_op jit(solution)/shard_map/ppermute | solution.py:180
  12.9 0.0 copy-start.1
  12.9 0.0 copy-start.2
  12.9 0.1 collective-permute-start.4
  13.0 0.6 %copy-done.1 = s32[8,2,4]{0,2,1:T(4,128)S(1)} copy-done((s32[8,2,4]{0,2,1:T(4,128)S(1)}, s32[8,2,4]{0,2,1:T(4,128)}, u32[]{:S(2)}) %copy-start.1) | copy-done | bytes 280
  13.6 0.0 copy-done.2
  13.6 1.4 %shard_map.68 = (bf16[2,128,128]{2,1,0:T(8,128)(2,1)S(1)}, f32[2,1,128]{2,1,0:T(1,128)S(1)}, f32[2,1,128]{2,1,0:T(1,128)S(1)}, f32[2,128,128]{2,1,0:T(8,128)S(1)...) custom-call(s32[3]{0:T(128)S(1)} %copy-done.2, ...), custom_call_target="tpu_custom_call" | custom-call | flops 4000000000 | bytes 1000000 | tf_op jit(solution)/shard_map/pallas_call | solution.py:206
  15.0 0.0 collective-permute-done.5.beside
  15.0 0.7 %shard_map.69 = (bf16[2,128,128]{2,1,0:T(8,128)(2,1)S(1)}, f32[2,1,128]{2,1,0:T(1,128)S(1)}, f32[2,1,128]{2,1,0:T(1,128)S(1)}, f32[2,128,128]{2,1,0:T(8,128)S(1)}) custom-call(bf16[2,2,16,512]{3,2,1,0:T(8,128)(2,1)S(1)} %collective-permute-done.5.beside, bf16[4,2,64,256]{3,2,1,0:T(8,128)(2,1)S(1)} %constant_dynamic-update-slice_fusion.near, ...), custom_call_target="tpu_custom_call" | custom-call | flops 4000000000 | bytes 1000000 | tf_op jit(solution)/shard_map/pallas_call | solution.py:227
  15.6 0.0 collective-permute-done.4.far
  15.7 1.4 %shard_map.70 = (bf16[1,2,64,512]{3,2,1,0:T(8,128)(2,1)}, bf16[16,1,16,256]{3,2,1,0:T(8,128)(2,1)}) custom-call(bf16[4,2,64,256]{3,2,1,0:T(8,128)(2,1)S(1)} %collective-permute-done.4.far, f32[256,256]{1,0:T(8,128)S(1)} %get-tuple-element.24.far_bias_a, f32[512,256]{1,0:T(8,128)S(1)} %get-tuple-element.25.far_bias_b, ...), custom_call_target="tpu_custom_call" | custom-call | flops 4000000000 | bytes 1000000 | tf_op jit(solution)/shard_map/pallas_call | solution.py:235
  (8 shorter events, 0.1 us)
Async XLA Ops:
  0.7 4.9 %copy-start.3 = (bf16[1,2,64,128]{3,2,1,0:T(8,128)(2,1)S(1)}, bf16[1,2,64,128]{3,2,1,0:T(8,128)(2,1)}, u32[]{:S(2)}) copy-start(bf16[1,2,64,128]{3,2,1,0:T(8,128)(2,1)} %param.7) | copy-start | bytes 98308
  0.7 4.9 %copy-start.4 = (bf16[1,2,64,128]{3,2,1,0:T(8,128)(2,1)S(1)}, bf16[1,2,64,128]{3,2,1,0:T(8,128)(2,1)}, u32[]{:S(2)}) copy-start(bf16[1,2,64,128]{3,2,1,0:T(8,128)(2,1)} %param.6) | copy-start | bytes 98308
  1.5 7.6 %copy-start = (bf16[1,2,16,2048]{3,2,1,0:T(8,128)(2,1)S(1)}, bf16[1,2,16,2048]{3,2,1,0:T(8,128)(2,1)}, u32[]{:S(2)}) copy-start(bf16[1,2,16,2048]{3,2,1,0:T(8,128)(2,1)} %own.1) | copy-start | bytes 393220
  1.5 7.7 %collective-permute-start.3 = (bf16[1,2,16,1024]{3,2,1,0:T(8,128)(2,1)S(1)}, bf16[1,2,16,1024]{3,2,1,0:T(8,128)(2,1)S(1)}, u32[]{:S(2)}, u32[]{:S(2)}) collective-permute-start(bf16[1,2,16,1024]{3,2,1,0:T(8,128)(2,1)S(1)} %constant_dynamic-slice_fusion.2), channel_id=1, source_target_pairs={{0,2},{1,3},{2,0},{3,1},{4,6},{5,7},{6,4},{7,5},{8,10},{9,11},{10,... | collective-permute-start | bytes 196616 | tf_op jit(solution)/shard_map/ppermute | solution.py:176
  5.6 5.3 %collective-permute-start = (bf16[1,2,64,256]{3,2,1,0:T(8,128)(2,1)S(1)}, bf16[1,2,64,256]{3,2,1,0:T(8,128)(2,1)S(1)}, u32[]{:S(2)}, u32[]{:S(2)}) collective-permute-start(bf16[1,2,64,256]{3,2,1,0:T(8,128)(2,1)S(1)} %pad_maximum_fusion), channel_id=1, source_target_pairs={{0,24},{4,28},{8,16},{12,20},{16,8},{20,12},{24,0},{28,4},{1,25},{... | collective-permute-start | bytes 196616 | tf_op jit(solution)/shard_map/ppermute | solution.py:180
  8.1 4.3 %collective-permute-start.1 = (bf16[1,2,64,256]{3,2,1,0:T(8,128)(2,1)S(1)}, bf16[1,2,64,256]{3,2,1,0:T(8,128)(2,1)S(1)}, u32[]{:S(2)}, u32[]{:S(2)}) collective-permute-start(bf16[1,2,64,256]{3,2,1,0:T(8,128)(2,1)S(1)} %pad_maximum_fusion), channel_id=1, source_target_pairs={{0,16},{4,20},{8,24},{12,28},{16,0},{20,4},{24,8},{28,12},{1,17},{... | collective-permute-start | bytes 196616 | tf_op jit(solution)/shard_map/ppermute | solution.py:180
  8.6 4.3 %collective-permute-start.2 = (bf16[1,2,64,256]{3,2,1,0:T(8,128)(2,1)S(1)}, bf16[1,2,64,256]{3,2,1,0:T(8,128)(2,1)S(1)}, u32[]{:S(2)}, u32[]{:S(2)}) collective-permute-start(bf16[1,2,64,256]{3,2,1,0:T(8,128)(2,1)S(1)} %pad_maximum_fusion), channel_id=1, source_target_pairs={{0,8},{4,12},{8,0},{12,4},{16,24},{20,28},{24,16},{28,20},{1,9},{5... | collective-permute-start | bytes 196616 | tf_op jit(solution)/shard_map/ppermute | solution.py:180
  9.2 5.7 %collective-permute-start.5 = (bf16[2,2,16,512]{3,2,1,0:T(8,128)(2,1)S(1)}, bf16[2,2,16,512]{3,2,1,0:T(8,128)(2,1)S(1)}, u32[]{:S(2)}, u32[]{:S(2)}) collective-permute-start(bf16[2,2,16,512]{3,2,1,0:T(8,128)(2,1)S(1)} %pad_maximum_fusion.1), channel_id=1, source_target_pairs={{0,1},{1,0},{2,3},{3,2},{4,5},{5,4},{6,7},{7,6},{8,9},{9,8},{10,11... | collective-permute-start | bytes 196616 | tf_op jit(solution)/shard_map/ppermute | solution.py:190
  12.9 0.7 %copy-start.1 = (s32[8,2,4]{0,2,1:T(4,128)S(1)}, s32[8,2,4]{0,2,1:T(4,128)}, u32[]{:S(2)}) copy-start(s32[8,2,4]{0,2,1:T(4,128)} %param.9) | copy-start | bytes 772
  12.9 0.7 %copy-start.2 = (s32[3]{0:T(128)S(1)}, s32[3]{0:T(128)}, u32[]{:S(2)}) copy-start(s32[3]{0:T(128)} %doc_hbm.1) | copy-start | bytes 40
  12.9 2.7 %collective-permute-start.4 = (bf16[4,2,64,256]{3,2,1,0:T(8,128)(2,1)S(1)}, bf16[4,2,64,256]{3,2,1,0:T(8,128)(2,1)S(1)}, u32[]{:S(2)}, u32[]{:S(2)}) collective-permute-start(bf16[4,2,64,256]{3,2,1,0:T(8,128)(2,1)S(1)} %constant_dynamic-update-slice_fusion.near), channel_id=1, source_target_pairs={{0,4},{4,0},{8,12},{12,8},{16,20},{20,16},{24,28},{28,24},{1,5},{5... | collective-permute-start | bytes 786440 | tf_op jit(solution)/shard_map/ppermute | solution.py:192

commit v4 on v1

--- a/solution.py
+++ b/solution.py
@@ -1,3 +1,5 @@
+import functools
+
 import jax
 import jax.numpy as jnp
 from jax import lax
@@ -11,60 +13,66 @@
 LANES = 128
 
 
-def gather_queries(own, across, beside, q_rows):
+def gather_queries(own, across, beside, half):
     my_head = lax.axis_index("head")
     width = beside.shape[-1]
-    sub_tok = own.shape[2]
-    group = width // HEAD_DIM
-    block_tok = q_rows.shape[1] // group
-    for half in range(2):
-        for g in range(group):
-            lane = g * HEAD_DIM
-            mine = pl.multiple_of(my_head * width + lane, HEAD_DIM)
-            low = pl.multiple_of((my_head % 2) * width + lane, HEAD_DIM)
-            parts = (
-                own[0, half, :, pl.ds(mine, HEAD_DIM)],
-                beside[0, half, :, lane : lane + HEAD_DIM],
-                across[0, half, :, pl.ds(low, HEAD_DIM)],
-                beside[1, half, :, lane : lane + HEAD_DIM],
-            )
-            for d, part in enumerate(parts):
-                row = pl.multiple_of(g * block_tok + (my_head ^ d) * sub_tok, sub_tok)
-                q_rows[half, pl.ds(row, sub_tok), :] = part
-
-
-def key_bias(my_blk, doc_lengths, chips, block_tok, half, core):
+    parts = []
+    for lane in range(0, width, HEAD_DIM):
+        mine = pl.multiple_of(my_head * width + lane, HEAD_DIM)
+        low = pl.multiple_of((my_head % 2) * width + lane, HEAD_DIM)
+        parts.append(own[0, half, :, pl.ds(mine, HEAD_DIM)])
+        parts.append(beside[0, half, :, lane : lane + HEAD_DIM])
+        parts.append(across[0, half, :, pl.ds(low, HEAD_DIM)])
+        parts.append(beside[1, half, :, lane : lane + HEAD_DIM])
+    return jnp.concatenate(parts, axis=0)
+
+
+def key_bias(my_blk, lengths, chips, block_tok, sub_tok, half, core):
     blk_count = 2 * chips
-    shape = (block_tok, LANES)
     my_block = my_blk if half == 0 else 2 * blk_count - 1 - my_blk
-    q_pos = my_block * block_tok + lax.broadcasted_iota(jnp.int32, (1, LANES), 1) % block_tok
+    lane = lax.broadcasted_iota(jnp.int32, (1, LANES), 1)
+    sender = lax.axis_index("head") ^ (lane % block_tok // sub_tok)
+    q_pos = my_block * block_tok + sender * sub_tok + lane % sub_tok
     first = jnp.zeros_like(q_pos)
-    bound = 0
-    for k in range(doc_lengths.shape[0] - 1):
-        bound = bound + doc_lengths[k]
+    bound = jnp.zeros_like(lengths[:, :1])
+    for k in range(lengths.shape[1] - 1):
+        bound = bound + lengths[:, k : k + 1]
         first = jnp.where(q_pos >= bound, bound, first)
-    row = lax.broadcasted_iota(jnp.int32, shape, 0)
+    row = lax.broadcasted_iota(jnp.int32, (block_tok, LANES), 0)
     parts = []
     for m in range(chips):
         owner = (my_blk ^ core) ^ (2 * m)
         for side in range(half + 1):
-            start = (owner if side == 0 else 2 * blk_count - 1 - owner) * block_tok
-            parts.append(jnp.where((row <= q_pos - start) & (row >= first - start), 0.0, -1e30))
+            block = owner if side == 0 else 2 * blk_count - 1 - owner
+            if core == 0 and m == 0 and side == half:
+                allowed = (row <= q_pos - block * block_tok) & (row >= first - block * block_tok)
+            else:
+                allowed = row >= first - jnp.where(block < my_block, block * block_tok, -(2**28))
+            parts.append(jnp.where(allowed, 0.0, -1e30))
     return jnp.concatenate(parts, axis=0)
 
 
-def page_targets(my_blk, page_slot, chips, block_tok, slot_count, core):
-    pages_blk = block_tok // PAGE
-    col = lax.broadcasted_iota(jnp.int32, (1, 2 * block_tok), 1)
-    parts = []
-    for m in range(chips):
-        owner = (my_blk ^ core) ^ (2 * m)
-        slots = jnp.zeros_like(col)
-        for half in range(2):
-            for n in range(pages_blk):
-                slots = jnp.where(col // PAGE == half * pages_blk + n, page_slot[half, n, owner], slots)
-        parts.append((slots - my_blk * slot_count) * PAGE + col % PAGE)
-    return jnp.concatenate(parts, axis=1)
+def page_targets(my_blk, page_slot, chips, slot_count, core):
+    _, pages_blk, blk_count = page_slot.shape
+    chip = lax.broadcasted_iota(jnp.int32, (chips, blk_count), 0)
+    owner = (my_blk ^ core) ^ (2 * chip)
+    chosen = (owner == lax.broadcasted_iota(jnp.int32, (chips, blk_count), 1)).astype(jnp.float32).astype(jnp.bfloat16)
+    cols = 2 * pages_blk * PAGE
+    page = lax.broadcasted_iota(jnp.int32, (pages_blk, cols), 0)
+    col = lax.broadcasted_iota(jnp.int32, (pages_blk, cols), 1)
+    slots = 0.0
+    for half in range(2):
+        held = lax.dot_general(
+            chosen,
+            page_slot[half].astype(jnp.float32).astype(jnp.bfloat16),
+            (((1,), (1,)), ((), ())),
+            preferred_element_type=jnp.float32,
+        )
+        spread = (col // PAGE == page + half * pages_blk).astype(jnp.float32).astype(jnp.bfloat16)
+        slots = slots + jnp.dot(held.astype(jnp.bfloat16), spread, preferred_element_type=jnp.float32)
+    slots = slots.astype(jnp.int32) - my_blk * slot_count
+    rows = slots * PAGE + lax.broadcasted_iota(jnp.int32, slots.shape, 1) % PAGE
+    return jnp.concatenate([rows[m : m + 1] for m in range(chips)], axis=1)
 
 
 def place_pages(targets, pairs, slot_count):
@@ -74,9 +82,9 @@
     return jnp.dot(chosen, rows, preferred_element_type=jnp.float32)
 
 
-def score_part(q_rows, pairs, half):
+def score_part(queries, pairs, half):
     keys = pairs[:, : half + 1].reshape(-1, 2 * HEAD_DIM)[:, :HEAD_DIM]
-    return lax.dot_general(keys, q_rows[half], (((1,), (1,)), ((), ())), preferred_element_type=jnp.float32)
+    return lax.dot_general(keys, queries, (((1,), (1,)), ((), ())), preferred_element_type=jnp.float32)
 
 
 def weigh_part(scores, bias, pairs, half):
@@ -93,32 +101,24 @@
 
 
 def near_kernel(
-    doc_hbm, slot_hbm, own, across, beside, near, q_rows, top_ref, total_ref, out_ref, pages_ref, far_bias_a,
-    far_bias_b, far_targets, doc_lengths, page_slot, sems,
+    lengths, page_slot, own, across, beside, near, q_rows, top_ref, total_ref, out_ref, pages_ref, far_bias_a,
+    far_bias_b, far_targets,
 ):
     chips, _, block_tok, _ = near.shape
     slot_count = pages_ref.shape[0] // PAGE
     my_blk = lax.axis_index("blk")
-    fetch_doc = pltpu.make_async_copy(doc_hbm, doc_lengths, sems.at[0])
-    fetch_slot = pltpu.make_async_copy(slot_hbm, page_slot, sems.at[1])
-    fetch_doc.start()
-    fetch_slot.start()
-    gather_queries(own, across, beside, q_rows)
-    scores = [score_part(q_rows, near, half) for half in range(2)]
-    fetch_doc.wait()
-    fetch_slot.wait()
-    for half in range(2):
-        bias = key_bias(my_blk, doc_lengths, chips, block_tok, half, 0)
-        top, total, out = weigh_part(scores[half], bias, near, half)
+    bias = functools.partial(key_bias, my_blk, lengths[...], chips, block_tok, own.shape[2])
+    for half in (1, 0):
+        queries = gather_queries(own, across, beside, half)
+        q_rows[half] = queries
+        top, total, out = weigh_part(score_part(queries, near, half), bias(half, 0), near, half)
         top_ref[half] = top
         total_ref[half] = total
         out_ref[half] = out
-    pages_ref[...] = place_pages(
-        page_targets(my_blk, page_slot, chips, block_tok, slot_count, 0), near, slot_count
-    ).astype(jnp.bfloat16)
-    far_bias_a[...] = key_bias(my_blk, doc_lengths, chips, block_tok, 0, 1)
-    far_bias_b[...] = key_bias(my_blk, doc_lengths, chips, block_tok, 1, 1)
-    far_targets[...] = page_targets(my_blk, page_slot, chips, block_tok, slot_count, 1)
+        (far_bias_a, far_bias_b)[half][...] = bias(half, 1)
+    targets = functools.partial(page_targets, my_blk, page_slot, chips, slot_count)
+    pages_ref[...] = place_pages(targets(0), near, slot_count).astype(jnp.bfloat16)
+    far_targets[...] = targets(1)
 
 
 def far_kernel(
@@ -127,20 +127,25 @@
 ):
     block_tok = far.shape[2]
     slot_count = kv_cache.shape[0]
+    my_head = lax.axis_index("head")
+    sub_tok = block_tok // lax.axis_size("head")
     moved = place_pages(far_targets[...], far, slot_count) + pages_ref[...].astype(jnp.float32)
     pages[...] = moved.astype(jnp.bfloat16).reshape(pages.shape)
     writes = [pltpu.make_async_copy(pages, kv_cache, sems.at[2])]
     writes[0].start()
     for half in (1, 0):
         bias = (far_bias_a, far_bias_b)[half][...]
-        top, total, out = weigh_part(score_part(q_rows, far, half), bias, far, half)
+        top, total, out = weigh_part(score_part(q_rows[half], far, half), bias, far, half)
         best = jnp.maximum(top, top_ref[half])
         here = jnp.exp2(top - best)
         there = jnp.exp2(top_ref[half] - best)
         inverse = 1.0 / (total * here + total_ref[half] * there)
         out = (out * (here * inverse) + out_ref[half] * (there * inverse)).T.astype(jnp.bfloat16)
         for g in range(out.shape[0] // block_tok):
-            result[half, :, g * HEAD_DIM : (g + 1) * HEAD_DIM] = out[g * block_tok : (g + 1) * block_tok]
+            for d in range(block_tok // sub_tok):
+                row = pl.multiple_of((my_head ^ d) * sub_tok, sub_tok)
+                start = g * block_tok + d * sub_tok
+                result[half, pl.ds(row, sub_tok), g * HEAD_DIM : (g + 1) * HEAD_DIM] = out[start : start + sub_tok]
         writes.append(pltpu.make_async_copy(result.at[half], attended.at[0, half], sems.at[half]))
         writes[-1].start()
     for write in writes:
@@ -180,7 +185,6 @@
     vmem = pl.BlockSpec(memory_space=pltpu.VMEM)
     params = pltpu.CompilerParams(vmem_limit_bytes=32 * 1024 * 1024)
     cost = pl.CostEstimate(flops=4_000_000_000, bytes_accessed=1_000_000, transcendentals=200_000)
-    slots = page_slot.transpose(1, 2, 0)
     half_cols = blk_count // 2 * block_tok
     stats = pl.pallas_call(
         near_kernel,
@@ -194,16 +198,11 @@
             jax.ShapeDtypeStruct((2 * half_cols, LANES), jnp.float32),
             jax.ShapeDtypeStruct((1, 2 * half_cols), jnp.int32),
         ),
-        in_specs=[hbm] * 2 + [vmem] * 4,
+        in_specs=[vmem] * 6,
         out_specs=(vmem,) * 8,
-        scratch_shapes=[
-            pltpu.SMEM(doc_lengths.shape, jnp.int32),
-            pltpu.SMEM(slots.shape, jnp.int32),
-            pltpu.SemaphoreType.DMA((2,)),
-        ],
         compiler_params=params,
         cost_estimate=cost,
-    )(doc_lengths, slots, query_states, across, beside, near)
+    )(doc_lengths.reshape(1, -1), page_slot.transpose(1, 2, 0), query_states, across, beside, near)
     return pl.pallas_call(
         far_kernel,
         out_shape=(

time: 16.4 us -> 16.8 us (1.024)
  local copies, waits for them, and re-layouts: 0.93 us -> 1.56 us
  Pallas kernels: 2.63 us -> 2.36 us
    unnamed x13, local copies, waits for them, and re-layouts: 0.05 us -> 0.69 us
    pallas_call x1, Pallas kernels: 1.26 us -> 0.98 us  [per_device(): pl.pallas_call(near_kernel, out_shape=(jax.ShapeDtypeStruct((2, rows, HEA...]
  transfers between devices with their start and end apart: 6 -> 6, of which waited for: 4 -> 4; matrix products, arithmetic and copies ran while one was open for 0% -> 0% of each run, Pallas kernels for 8% -> 6%
where the time goes in v4:
time: 16.8 us; the launch traced here: 16.6 us
  starting transfers between devices  9.29 us (55%)
  waiting for transfers between devices  2.62 us (16%)
  Pallas kernels  2.36 us (14%)
  local copies, waits for them, and re-layouts  1.56 us (9%)
  between operations  0.75 us (4%)
    ppermute x1, starting transfers between devices, per_device(): across = lax.ppermute(part, 'head', [(i, i ^ 2) for i in range(head_count)])  4.04 us
    ppermute x3, starting transfers between devices, per_device(): lax.ppermute(pair, 'blk', [(i, i ^ d) for i in range(blk_count)])  3.55 us
    ppermute x3, waiting for transfers between devices, per_device(): lax.ppermute(pair, 'blk', [(i, i ^ d) for i in range(blk_count)])  2.01 us
    ppermute x1, starting transfers between devices, per_device(): lax.ppermute(beside, 'head', [(i, i ^ 1) for i in range(head_count)])  1.63 us
    pallas_call x1, Pallas kernels, per_device(): pl.pallas_call(far_kernel, out_shape=(jax.ShapeDtypeStruct((1, 2, block_t...  1.38 us
    pallas_call x1, Pallas kernels, per_device(): pl.pallas_call(near_kernel, out_shape=(jax.ShapeDtypeStruct((2, rows, HEA...  0.98 us
    dynamic_slice x1, local copies, waits for them, and re-layouts, per_device(): lax.dynamic_slice_in_dim(query_states, (my_head ^ 2) // 2 * 2 * width, 2...  0.86 us
    unnamed x13, local copies, waits for them, and re-layouts  0.69 us
  transfers between devices with their start and end apart: 6, of which 4 were waited for; matrix products, arithmetic and copies ran while one was open for 0% of the time, Pallas kernels for 6%

profile of v4, /device:TPU:0, one launch (start us, length us, event | category | flops | bytes accessed | tf_op | source)
XLA Modules:
  0.0 16.6 jit_solution(11048384823473265312)
XLA Ops:
  0.7 0.0 copy-start.3
  0.7 0.0 copy-start.4
  0.7 0.9 %constant_dynamic-slice_fusion.2 = bf16[1,2,16,1024]{3,2,1,0:T(8,128)(2,1)S(1)} fusion(bf16[1,2,16,2048]{3,2,1,0:T(8,128)(2,1)} %own.1, s32[]{:T(128)S(6)} %select_n.21), kind=kLoop, calls=%fused_computation.8 | loop fusion | bytes 131076 | tf_op jit(solution)/shard_map/dynamic_slice | solution.py:165
  1.5 0.0 copy-start
  1.5 4.0 %collective-permute-start.3 = (bf16[1,2,16,1024]{3,2,1,0:T(8,128)(2,1)S(1)}, bf16[1,2,16,1024]{3,2,1,0:T(8,128)(2,1)S(1)}, u32[]{:S(2)}, u32[]{:S(2)}) collective-permute-start(bf16[1,2,16,1024]{3,2,1,0:T(8,128)(2,1)S(1)} %constant_dynamic-slice_fusion.2), channel_id=1, source_target_pairs={{0,2},{1,3},{2,0},{3,1},{4,6},{5,7},{6,4},{7,5},{8,10},{9,11},{10,... | collective-permute-start | bytes 196616 | tf_op jit(solution)/shard_map/ppermute | solution.py:166
  5.6 0.0 copy-done.3
  5.6 0.0 copy-done.4
  5.6 2.5 %collective-permute-start = (bf16[1,2,64,256]{3,2,1,0:T(8,128)(2,1)S(1)}, bf16[1,2,64,256]{3,2,1,0:T(8,128)(2,1)S(1)}, u32[]{:S(2)}, u32[]{:S(2)}) collective-permute-start(bf16[1,2,64,256]{3,2,1,0:T(8,128)(2,1)S(1)} %pad_maximum_fusion), channel_id=1, source_target_pairs={{0,24},{4,28},{8,16},{12,20},{16,8},{20,12},{24,0},{28,4},{1,25},{... | collective-permute-start | bytes 196616 | tf_op jit(solution)/shard_map/ppermute | solution.py:170
  8.1 0.5 %collective-permute-start.1 = (bf16[1,2,64,256]{3,2,1,0:T(8,128)(2,1)S(1)}, bf16[1,2,64,256]{3,2,1,0:T(8,128)(2,1)S(1)}, u32[]{:S(2)}, u32[]{:S(2)}) collective-permute-start(bf16[1,2,64,256]{3,2,1,0:T(8,128)(2,1)S(1)} %pad_maximum_fusion), channel_id=1, source_target_pairs={{0,16},{4,20},{8,24},{12,28},{16,0},{20,4},{24,8},{28,12},{1,17},{... | collective-permute-start | bytes 196616 | tf_op jit(solution)/shard_map/ppermute | solution.py:170
  8.6 0.5 %collective-permute-start.2 = (bf16[1,2,64,256]{3,2,1,0:T(8,128)(2,1)S(1)}, bf16[1,2,64,256]{3,2,1,0:T(8,128)(2,1)S(1)}, u32[]{:S(2)}, u32[]{:S(2)}) collective-permute-start(bf16[1,2,64,256]{3,2,1,0:T(8,128)(2,1)S(1)} %pad_maximum_fusion), channel_id=1, source_target_pairs={{0,8},{4,12},{8,0},{12,4},{16,24},{20,28},{24,16},{28,20},{1,9},{5... | collective-permute-start | bytes 196616 | tf_op jit(solution)/shard_map/ppermute | solution.py:170
  9.2 0.0 copy-done
  9.2 0.0 collective-permute-done.3.across
  9.2 1.6 %collective-permute-start.5 = (bf16[2,2,16,512]{3,2,1,0:T(8,128)(2,1)S(1)}, bf16[2,2,16,512]{3,2,1,0:T(8,128)(2,1)S(1)}, u32[]{:S(2)}, u32[]{:S(2)}) collective-permute-start(bf16[2,2,16,512]{3,2,1,0:T(8,128)(2,1)S(1)} %pad_maximum_fusion.1), channel_id=1, source_target_pairs={{0,1},{1,0},{2,3},{3,2},{4,5},{5,4},{6,7},{7,6},{8,9},{9,8},{10,11... | collective-permute-start | bytes 196616 | tf_op jit(solution)/shard_map/ppermute | solution.py:180
  10.9 0.1 collective-permute-done
  10.9 1.4 %collective-permute-done.1 = bf16[1,2,64,256]{3,2,1,0:T(8,128)(2,1)S(1)} collective-permute-done((bf16[1,2,64,256]{3,2,1,0:T(8,128)(2,1)S(1)}, bf16[1,2,64,256]{3,2,1,0:T(8,128)(2,1)S(1)}, u32[]{:S(2)}, u32[]{:S(2)}) %collective-permute-start.1) | collective-permute-done | bytes 65568 | tf_op jit(solution)/shard_map/ppermute | solution.py:170
  12.4 0.5 %collective-permute-done.2 = bf16[1,2,64,256]{3,2,1,0:T(8,128)(2,1)S(1)} collective-permute-done((bf16[1,2,64,256]{3,2,1,0:T(8,128)(2,1)S(1)}, bf16[1,2,64,256]{3,2,1,0:T(8,128)(2,1)S(1)}, u32[]{:S(2)}, u32[]{:S(2)}) %collective-permute-start.2) | collective-permute-done | bytes 65568 | tf_op jit(solution)/shard_map/ppermute | solution.py:170
  12.9 0.0 copy-start.1
  12.9 0.1 collective-permute-start.4
  13.0 0.6 %collective-permute-done.5.beside = bf16[2,2,16,512]{3,2,1,0:T(8,128)(2,1)S(1)} collective-permute-done((bf16[2,2,16,512]{3,2,1,0:T(8,128)(2,1)S(1)}, bf16[2,2,16,512]{3,2,1,0:T(8,128)(2,1)S(1)}, u32[]{:S(2)}, u32[]{:S(2)}) %collective-permute-start.5) | collective-permute-done | bytes 65568 | tf_op jit(solution)/shard_map/ppermute | solution.py:180
  13.6 0.0 copy-start.2
  13.6 0.0 copy-done.1
  13.6 0.6 %copy-done.2 = s32[3]{0:T(128)S(1)} copy-done((s32[3]{0:T(128)S(1)}, s32[3]{0:T(128)}, u32[]{:S(2)}) %copy-start.2) | copy-done | bytes 36
  14.2 1.0 %shard_map.68 = (bf16[2,256,128]{2,1,0:T(8,128)(2,1)S(1)}, f32[2,1,256]{2,1,0:T(1,128)S(1)}, f32[2,1,256]{2,1,0:T(1,128)S(1)}, f32[2,128,256]{2,1,0:T(8,128)S(1)...) custom-call(s32[1,3]{1,0:T(1,128)S(1)} %bitcast.3, ...), custom_call_target="tpu_custom_call" | custom-call | flops 4000000000 | bytes 1000000 | tf_op jit(solution)/shard_map/pallas_call | solution.py:189
  15.2 0.0 collective-permute-done.4.far
  15.2 1.4 %shard_map.69 = (bf16[1,2,64,512]{3,2,1,0:T(8,128)(2,1)}, bf16[16,1,16,256]{3,2,1,0:T(8,128)(2,1)}) custom-call(bf16[4,2,64,256]{3,2,1,0:T(8,128)(2,1)S(1)} %collective-permute-done.4.far, bf16[2,256,128]{2,1,0:T(8,128)(2,1)S(1)} %get-tuple-element.18.q_rows, f32[2,1,256]{2,1,0:T(1,128)S(1)} %get-tuple-element.19.top_ref, ...), custom_call_target="tpu_custom_call" | custom-call | flops 4000000000 | bytes 1000000 | tf_op jit(solution)/shard_map/pallas_call | solution.py:206
  (8 shorter events, 0.1 us)
Async XLA Ops:
  0.7 4.9 %copy-start.3 = (bf16[1,2,64,128]{3,2,1,0:T(8,128)(2,1)S(1)}, bf16[1,2,64,128]{3,2,1,0:T(8,128)(2,1)}, u32[]{:S(2)}) copy-start(bf16[1,2,64,128]{3,2,1,0:T(8,128)(2,1)} %param.7) | copy-start | bytes 98308
  0.7 4.9 %copy-start.4 = (bf16[1,2,64,128]{3,2,1,0:T(8,128)(2,1)S(1)}, bf16[1,2,64,128]{3,2,1,0:T(8,128)(2,1)}, u32[]{:S(2)}) copy-start(bf16[1,2,64,128]{3,2,1,0:T(8,128)(2,1)} %param.6) | copy-start | bytes 98308
  1.5 7.6 %copy-start = (bf16[1,2,16,2048]{3,2,1,0:T(8,128)(2,1)S(1)}, bf16[1,2,16,2048]{3,2,1,0:T(8,128)(2,1)}, u32[]{:S(2)}) copy-start(bf16[1,2,16,2048]{3,2,1,0:T(8,128)(2,1)} %own.1) | copy-start | bytes 393220
  1.5 7.7 %collective-permute-start.3 = (bf16[1,2,16,1024]{3,2,1,0:T(8,128)(2,1)S(1)}, bf16[1,2,16,1024]{3,2,1,0:T(8,128)(2,1)S(1)}, u32[]{:S(2)}, u32[]{:S(2)}) collective-permute-start(bf16[1,2,16,1024]{3,2,1,0:T(8,128)(2,1)S(1)} %constant_dynamic-slice_fusion.2), channel_id=1, source_target_pairs={{0,2},{1,3},{2,0},{3,1},{4,6},{5,7},{6,4},{7,5},{8,10},{9,11},{10,... | collective-permute-start | bytes 196616 | tf_op jit(solution)/shard_map/ppermute | solution.py:166
  5.6 5.3 %collective-permute-start = (bf16[1,2,64,256]{3,2,1,0:T(8,128)(2,1)S(1)}, bf16[1,2,64,256]{3,2,1,0:T(8,128)(2,1)S(1)}, u32[]{:S(2)}, u32[]{:S(2)}) collective-permute-start(bf16[1,2,64,256]{3,2,1,0:T(8,128)(2,1)S(1)} %pad_maximum_fusion), channel_id=1, source_target_pairs={{0,24},{4,28},{8,16},{12,20},{16,8},{20,12},{24,0},{28,4},{1,25},{... | collective-permute-start | bytes 196616 | tf_op jit(solution)/shard_map/ppermute | solution.py:170
  8.1 4.3 %collective-permute-start.1 = (bf16[1,2,64,256]{3,2,1,0:T(8,128)(2,1)S(1)}, bf16[1,2,64,256]{3,2,1,0:T(8,128)(2,1)S(1)}, u32[]{:S(2)}, u32[]{:S(2)}) collective-permute-start(bf16[1,2,64,256]{3,2,1,0:T(8,128)(2,1)S(1)} %pad_maximum_fusion), channel_id=1, source_target_pairs={{0,16},{4,20},{8,24},{12,28},{16,0},{20,4},{24,8},{28,12},{1,17},{... | collective-permute-start | bytes 196616 | tf_op jit(solution)/shard_map/ppermute | solution.py:170
  8.6 4.3 %collective-permute-start.2 = (bf16[1,2,64,256]{3,2,1,0:T(8,128)(2,1)S(1)}, bf16[1,2,64,256]{3,2,1,0:T(8,128)(2,1)S(1)}, u32[]{:S(2)}, u32[]{:S(2)}) collective-permute-start(bf16[1,2,64,256]{3,2,1,0:T(8,128)(2,1)S(1)} %pad_maximum_fusion), channel_id=1, source_target_pairs={{0,8},{4,12},{8,0},{12,4},{16,24},{20,28},{24,16},{28,20},{1,9},{5... | collective-permute-start | bytes 196616 | tf_op jit(solution)/shard_map/ppermute | solution.py:170
  9.2 4.3 %collective-permute-start.5 = (bf16[2,2,16,512]{3,2,1,0:T(8,128)(2,1)S(1)}, bf16[2,2,16,512]{3,2,1,0:T(8,128)(2,1)S(1)}, u32[]{:S(2)}, u32[]{:S(2)}) collective-permute-start(bf16[2,2,16,512]{3,2,1,0:T(8,128)(2,1)S(1)} %pad_maximum_fusion.1), channel_id=1, source_target_pairs={{0,1},{1,0},{2,3},{3,2},{4,5},{5,4},{6,7},{7,6},{8,9},{9,8},{10,11... | collective-permute-start | bytes 196616 | tf_op jit(solution)/shard_map/ppermute | solution.py:180
  12.9 0.7 %copy-start.1 = (s32[8,2,4]{0,2,1:T(4,128)S(1)}, s32[8,2,4]{0,2,1:T(4,128)}, u32[]{:S(2)}) copy-start(s32[8,2,4]{0,2,1:T(4,128)} %param.9) | copy-start | bytes 772
  12.9 2.3 %collective-permute-start.4 = (bf16[4,2,64,256]{3,2,1,0:T(8,128)(2,1)S(1)}, bf16[4,2,64,256]{3,2,1,0:T(8,128)(2,1)S(1)}, u32[]{:S(2)}, u32[]{:S(2)}) collective-permute-start(bf16[4,2,64,256]{3,2,1,0:T(8,128)(2,1)S(1)} %constant_dynamic-update-slice_fusion.near), channel_id=1, source_target_pairs={{0,4},{4,0},{8,12},{12,8},{16,20},{20,16},{24,28},{28,24},{1,5},{5... | collective-permute-start | bytes 786440 | tf_op jit(solution)/shard_map/ppermute | solution.py:182
  13.6 0.7 %copy-start.2 = (s32[3]{0:T(128)S(1)}, s32[3]{0:T(128)}, u32[]{:S(2)}) copy-start(s32[3]{0:T(128)} %param.8) | copy-start | bytes 40

commit v5 on v4

--- a/solution.py
+++ b/solution.py
@@ -19,7 +19,7 @@
     parts = []
     for lane in range(0, width, HEAD_DIM):
         mine = pl.multiple_of(my_head * width + lane, HEAD_DIM)
-        low = pl.multiple_of((my_head % 2) * width + lane, HEAD_DIM)
+        low = pl.multiple_of((my_head & 1) * width + lane, HEAD_DIM)
         parts.append(own[0, half, :, pl.ds(mine, HEAD_DIM)])
         parts.append(beside[0, half, :, lane : lane + HEAD_DIM])
         parts.append(across[0, half, :, pl.ds(low, HEAD_DIM)])
@@ -107,7 +107,7 @@
     chips, _, block_tok, _ = near.shape
     slot_count = pages_ref.shape[0] // PAGE
     my_blk = lax.axis_index("blk")
-    bias = functools.partial(key_bias, my_blk, lengths[...], chips, block_tok, own.shape[2])
+    bias = functools.partial(key_bias, my_blk, lengths[...] - lax.axis_index("head"), chips, block_tok, own.shape[2])
     for half in (1, 0):
         queries = gather_queries(own, across, beside, half)
         q_rows[half] = queries
@@ -162,17 +162,18 @@
     slot_count = 4 * (block_tok // PAGE)
 
     my_head = lax.axis_index("head")
-    part = lax.dynamic_slice_in_dim(query_states, ((my_head ^ 2) // 2) * 2 * width, 2 * width, axis=3)
+    part = lax.dynamic_slice_in_dim(query_states, ((my_head & 2) ^ 2) * width, 2 * width, axis=3)
     across = lax.ppermute(part, "head", [(i, i ^ 2) for i in range(head_count)])
     pair = jnp.concatenate([key_states, value_states], axis=3)
-    pair, _ = lax.optimization_barrier((pair, part))
+    lengths = doc_lengths + my_head
+    pair, lengths, _ = lax.optimization_barrier((pair, lengths, part))
     near = [
         lax.ppermute(pair, "blk", [(i, i ^ d) for i in range(blk_count)]) for d in range(2, blk_count, 2)
     ]
     beside = jnp.concatenate(
         [
             lax.dynamic_slice_in_dim(query_states, (my_head ^ 1) * width, width, axis=3),
-            lax.dynamic_slice_in_dim(across, (1 - my_head % 2) * width, width, axis=3),
+            lax.dynamic_slice_in_dim(across, ((my_head & 1) ^ 1) * width, width, axis=3),
         ],
         axis=0,
     )
@@ -202,7 +203,7 @@
         out_specs=(vmem,) * 8,
         compiler_params=params,
         cost_estimate=cost,
-    )(doc_lengths.reshape(1, -1), page_slot.transpose(1, 2, 0), query_states, across, beside, near)
+    )(lengths.reshape(1, -1), page_slot.transpose(1, 2, 0), query_states, across, beside, near)
     return pl.pallas_call(
         far_kernel,
         out_shape=(

time: 16.8 us -> 16.2 us (0.964)
  local copies, waits for them, and re-layouts: 1.56 us -> 0.95 us
    unnamed x13, local copies, waits for them, and re-layouts: 0.69 us -> 0.07 us
where the time goes in v5:
time: 16.2 us; the launch traced here: 16 us
  starting transfers between devices  9.3 us (57%)
  waiting for transfers between devices  2.59 us (16%)
  Pallas kernels  2.37 us (15%)
  local copies, waits for them, and re-layouts  0.95 us (6%)
  between operations  0.76 us (5%)
    ppermute x1, starting transfers between devices, per_device(): across = lax.ppermute(part, 'head', [(i, i ^ 2) for i in range(head_count)])  4.04 us
    ppermute x3, starting transfers between devices, per_device(): lax.ppermute(pair, 'blk', [(i, i ^ d) for i in range(blk_count)])  3.55 us
    ppermute x3, waiting for transfers between devices, per_device(): lax.ppermute(pair, 'blk', [(i, i ^ d) for i in range(blk_count)])  2.01 us
    ppermute x1, starting transfers between devices, per_device(): lax.ppermute(beside, 'head', [(i, i ^ 1) for i in range(head_count)])  1.64 us
    pallas_call x1, Pallas kernels, per_device(): pl.pallas_call(far_kernel, out_shape=(jax.ShapeDtypeStruct((1, 2, block_t...  1.38 us
    pallas_call x1, Pallas kernels, per_device(): pl.pallas_call(near_kernel, out_shape=(jax.ShapeDtypeStruct((2, rows, HEA...  1 us
    dynamic_slice x1, local copies, waits for them, and re-layouts, per_device(): lax.dynamic_slice_in_dim(query_states, (my_head & 2 ^ 2) * width, 2 * wid...  0.86 us
    ppermute x1, waiting for transfers between devices, per_device(): lax.ppermute(beside, 'head', [(i, i ^ 1) for i in range(head_count)])  0.56 us
  transfers between devices with their start and end apart: 6, of which 4 were waited for; matrix products, arithmetic and copies ran while one was open for 0% of the time, Pallas kernels for 6%

profile of v5, /device:TPU:0, one launch (start us, length us, event | category | flops | bytes accessed | tf_op | source)
XLA Modules:
  0.0 16.0 jit_solution(3598857381625831075)
XLA Ops:
  0.6 0.0 copy-start.4
  0.7 0.0 copy-start.2
  0.7 0.0 copy-start.3
  0.7 0.9 %constant_dynamic-slice_fusion.2 = bf16[1,2,16,1024]{3,2,1,0:T(8,128)(2,1)S(1)} fusion(bf16[1,2,16,2048]{3,2,1,0:T(8,128)(2,1)} %own.1, s32[]{:T(128)S(6)} %select_n.9), kind=kLoop, calls=%fused_computation.8 | loop fusion | bytes 131076 | tf_op jit(solution)/shard_map/dynamic_slice | solution.py:165
  1.5 4.0 %collective-permute-start.3 = (bf16[1,2,16,1024]{3,2,1,0:T(8,128)(2,1)S(1)}, bf16[1,2,16,1024]{3,2,1,0:T(8,128)(2,1)S(1)}, u32[]{:S(2)}, u32[]{:S(2)}) collective-permute-start(bf16[1,2,16,1024]{3,2,1,0:T(8,128)(2,1)S(1)} %constant_dynamic-slice_fusion.2), channel_id=1, source_target_pairs={{0,2},{1,3},{2,0},{3,1},{4,6},{5,7},{6,4},{7,5},{8,10},{9,11},{10,... | collective-permute-start | bytes 196616 | tf_op jit(solution)/shard_map/ppermute | solution.py:166
  5.6 0.0 copy-done.4
  5.6 0.0 copy-done.2
  5.6 0.0 copy-done.3
  5.6 0.0 copy-start
  5.6 2.5 %collective-permute-start = (bf16[1,2,64,256]{3,2,1,0:T(8,128)(2,1)S(1)}, bf16[1,2,64,256]{3,2,1,0:T(8,128)(2,1)S(1)}, u32[]{:S(2)}, u32[]{:S(2)}) collective-permute-start(bf16[1,2,64,256]{3,2,1,0:T(8,128)(2,1)S(1)} %pad_maximum_fusion), channel_id=1, source_target_pairs={{0,24},{4,28},{8,16},{12,20},{16,8},{20,12},{24,0},{28,4},{1,25},{... | collective-permute-start | bytes 196616 | tf_op jit(solution)/shard_map/ppermute | solution.py:171
  8.1 0.5 %collective-permute-start.1 = (bf16[1,2,64,256]{3,2,1,0:T(8,128)(2,1)S(1)}, bf16[1,2,64,256]{3,2,1,0:T(8,128)(2,1)S(1)}, u32[]{:S(2)}, u32[]{:S(2)}) collective-permute-start(bf16[1,2,64,256]{3,2,1,0:T(8,128)(2,1)S(1)} %pad_maximum_fusion), channel_id=1, source_target_pairs={{0,16},{4,20},{8,24},{12,28},{16,0},{20,4},{24,8},{28,12},{1,17},{... | collective-permute-start | bytes 196616 | tf_op jit(solution)/shard_map/ppermute | solution.py:171
  8.6 0.5 %collective-permute-start.2 = (bf16[1,2,64,256]{3,2,1,0:T(8,128)(2,1)S(1)}, bf16[1,2,64,256]{3,2,1,0:T(8,128)(2,1)S(1)}, u32[]{:S(2)}, u32[]{:S(2)}) collective-permute-start(bf16[1,2,64,256]{3,2,1,0:T(8,128)(2,1)S(1)} %pad_maximum_fusion), channel_id=1, source_target_pairs={{0,8},{4,12},{8,0},{12,4},{16,24},{20,28},{24,16},{28,20},{1,9},{5... | collective-permute-start | bytes 196616 | tf_op jit(solution)/shard_map/ppermute | solution.py:171
  9.2 0.0 copy-done
  9.2 0.0 collective-permute-done.3.across
  9.2 1.6 %collective-permute-start.5 = (bf16[2,2,16,512]{3,2,1,0:T(8,128)(2,1)S(1)}, bf16[2,2,16,512]{3,2,1,0:T(8,128)(2,1)S(1)}, u32[]{:S(2)}, u32[]{:S(2)}) collective-permute-start(bf16[2,2,16,512]{3,2,1,0:T(8,128)(2,1)S(1)} %pad_maximum_fusion.1), channel_id=1, source_target_pairs={{0,1},{1,0},{2,3},{3,2},{4,5},{5,4},{6,7},{7,6},{8,9},{9,8},{10,11... | collective-permute-start | bytes 196616 | tf_op jit(solution)/shard_map/ppermute | solution.py:181
  10.9 0.1 collective-permute-done
  10.9 1.4 %collective-permute-done.1 = bf16[1,2,64,256]{3,2,1,0:T(8,128)(2,1)S(1)} collective-permute-done((bf16[1,2,64,256]{3,2,1,0:T(8,128)(2,1)S(1)}, bf16[1,2,64,256]{3,2,1,0:T(8,128)(2,1)S(1)}, u32[]{:S(2)}, u32[]{:S(2)}) %collective-permute-start.1) | collective-permute-done | bytes 65568 | tf_op jit(solution)/shard_map/ppermute | solution.py:171
  12.4 0.5 %collective-permute-done.2 = bf16[1,2,64,256]{3,2,1,0:T(8,128)(2,1)S(1)} collective-permute-done((bf16[1,2,64,256]{3,2,1,0:T(8,128)(2,1)S(1)}, bf16[1,2,64,256]{3,2,1,0:T(8,128)(2,1)S(1)}, u32[]{:S(2)}, u32[]{:S(2)}) %collective-permute-start.2) | collective-permute-done | bytes 65568 | tf_op jit(solution)/shard_map/ppermute | solution.py:171
  12.9 0.0 copy-start.1
  12.9 0.1 collective-permute-start.4
  13.0 0.6 %collective-permute-done.5.beside = bf16[2,2,16,512]{3,2,1,0:T(8,128)(2,1)S(1)} collective-permute-done((bf16[2,2,16,512]{3,2,1,0:T(8,128)(2,1)S(1)}, bf16[2,2,16,512]{3,2,1,0:T(8,128)(2,1)S(1)}, u32[]{:S(2)}, u32[]{:S(2)}) %collective-permute-start.5) | collective-permute-done | bytes 65568 | tf_op jit(solution)/shard_map/ppermute | solution.py:181
  13.6 0.0 copy-done.1
  13.6 1.0 %shard_map.68 = (bf16[2,256,128]{2,1,0:T(8,128)(2,1)S(1)}, f32[2,1,256]{2,1,0:T(1,128)S(1)}, f32[2,1,256]{2,1,0:T(1,128)S(1)}, f32[2,128,256]{2,1,0:T(8,128)S(1)...) custom-call(s32[1,3]{1,0:T(1,128)S(1)} %bitcast.3, ...), custom_call_target="tpu_custom_call" | custom-call | flops 4000000000 | bytes 1000000 | tf_op jit(solution)/shard_map/pallas_call | solution.py:190
  14.6 0.0 collective-permute-done.4.far
  14.6 1.4 %shard_map.69 = (bf16[1,2,64,512]{3,2,1,0:T(8,128)(2,1)}, bf16[16,1,16,256]{3,2,1,0:T(8,128)(2,1)}) custom-call(bf16[4,2,64,256]{3,2,1,0:T(8,128)(2,1)S(1)} %collective-permute-done.4.far, bf16[2,256,128]{2,1,0:T(8,128)(2,1)S(1)} %get-tuple-element.20.q_rows, f32[2,1,256]{2,1,0:T(1,128)S(1)} %get-tuple-element.21.top_ref, ...), custom_call_target="tpu_custom_call" | custom-call | flops 4000000000 | bytes 1000000 | tf_op jit(solution)/shard_map/pallas_call | solution.py:207
  (9 shorter events, 0.1 us)
Async XLA Ops:
  0.6 4.9 %copy-start.4 = (s32[3]{0:T(128)S(1)}, s32[3]{0:T(128)}, u32[]{:S(2)}) copy-start(s32[3]{0:T(128)} %param.8) | copy-start | bytes 40
  0.7 4.9 %copy-start.2 = (bf16[1,2,64,128]{3,2,1,0:T(8,128)(2,1)S(1)}, bf16[1,2,64,128]{3,2,1,0:T(8,128)(2,1)}, u32[]{:S(2)}) copy-start(bf16[1,2,64,128]{3,2,1,0:T(8,128)(2,1)} %param.7) | copy-start | bytes 98308
  0.7 4.9 %copy-start.3 = (bf16[1,2,64,128]{3,2,1,0:T(8,128)(2,1)S(1)}, bf16[1,2,64,128]{3,2,1,0:T(8,128)(2,1)}, u32[]{:S(2)}) copy-start(bf16[1,2,64,128]{3,2,1,0:T(8,128)(2,1)} %param.6) | copy-start | bytes 98308
  1.5 7.7 %collective-permute-start.3 = (bf16[1,2,16,1024]{3,2,1,0:T(8,128)(2,1)S(1)}, bf16[1,2,16,1024]{3,2,1,0:T(8,128)(2,1)S(1)}, u32[]{:S(2)}, u32[]{:S(2)}) collective-permute-start(bf16[1,2,16,1024]{3,2,1,0:T(8,128)(2,1)S(1)} %constant_dynamic-slice_fusion.2), channel_id=1, source_target_pairs={{0,2},{1,3},{2,0},{3,1},{4,6},{5,7},{6,4},{7,5},{8,10},{9,11},{10,... | collective-permute-start | bytes 196616 | tf_op jit(solution)/shard_map/ppermute | solution.py:166
  5.6 3.6 %copy-start = (bf16[1,2,16,2048]{3,2,1,0:T(8,128)(2,1)S(1)}, bf16[1,2,16,2048]{3,2,1,0:T(8,128)(2,1)}, u32[]{:S(2)}) copy-start(bf16[1,2,16,2048]{3,2,1,0:T(8,128)(2,1)} %own.1) | copy-start | bytes 393220
  5.6 5.3 %collective-permute-start = (bf16[1,2,64,256]{3,2,1,0:T(8,128)(2,1)S(1)}, bf16[1,2,64,256]{3,2,1,0:T(8,128)(2,1)S(1)}, u32[]{:S(2)}, u32[]{:S(2)}) collective-permute-start(bf16[1,2,64,256]{3,2,1,0:T(8,128)(2,1)S(1)} %pad_maximum_fusion), channel_id=1, source_target_pairs={{0,24},{4,28},{8,16},{12,20},{16,8},{20,12},{24,0},{28,4},{1,25},{... | collective-permute-start | bytes 196616 | tf_op jit(solution)/shard_map/ppermute | solution.py:171
  8.1 4.3 %collective-permute-start.1 = (bf16[1,2,64,256]{3,2,1,0:T(8,128)(2,1)S(1)}, bf16[1,2,64,256]{3,2,1,0:T(8,128)(2,1)S(1)}, u32[]{:S(2)}, u32[]{:S(2)}) collective-permute-start(bf16[1,2,64,256]{3,2,1,0:T(8,128)(2,1)S(1)} %pad_maximum_fusion), channel_id=1, source_target_pairs={{0,16},{4,20},{8,24},{12,28},{16,0},{20,4},{24,8},{28,12},{1,17},{... | collective-permute-start | bytes 196616 | tf_op jit(solution)/shard_map/ppermute | solution.py:171
  8.6 4.3 %collective-permute-start.2 = (bf16[1,2,64,256]{3,2,1,0:T(8,128)(2,1)S(1)}, bf16[1,2,64,256]{3,2,1,0:T(8,128)(2,1)S(1)}, u32[]{:S(2)}, u32[]{:S(2)}) collective-permute-start(bf16[1,2,64,256]{3,2,1,0:T(8,128)(2,1)S(1)} %pad_maximum_fusion), channel_id=1, source_target_pairs={{0,8},{4,12},{8,0},{12,4},{16,24},{20,28},{24,16},{28,20},{1,9},{5... | collective-permute-start | bytes 196616 | tf_op jit(solution)/shard_map/ppermute | solution.py:171
  9.2 4.3 %collective-permute-start.5 = (bf16[2,2,16,512]{3,2,1,0:T(8,128)(2,1)S(1)}, bf16[2,2,16,512]{3,2,1,0:T(8,128)(2,1)S(1)}, u32[]{:S(2)}, u32[]{:S(2)}) collective-permute-start(bf16[2,2,16,512]{3,2,1,0:T(8,128)(2,1)S(1)} %pad_maximum_fusion.1), channel_id=1, source_target_pairs={{0,1},{1,0},{2,3},{3,2},{4,5},{5,4},{6,7},{7,6},{8,9},{9,8},{10,11... | collective-permute-start | bytes 196616 | tf_op jit(solution)/shard_map/ppermute | solution.py:181
  12.9 0.7 %copy-start.1 = (s32[8,2,4]{0,2,1:T(4,128)S(1)}, s32[8,2,4]{0,2,1:T(4,128)}, u32[]{:S(2)}) copy-start(s32[8,2,4]{0,2,1:T(4,128)} %param.9) | copy-start | bytes 772
  12.9 1.7 %collective-permute-start.4 = (bf16[4,2,64,256]{3,2,1,0:T(8,128)(2,1)S(1)}, bf16[4,2,64,256]{3,2,1,0:T(8,128)(2,1)S(1)}, u32[]{:S(2)}, u32[]{:S(2)}) collective-permute-start(bf16[4,2,64,256]{3,2,1,0:T(8,128)(2,1)S(1)} %constant_dynamic-update-slice_fusion.near), channel_id=1, source_target_pairs={{0,4},{4,0},{8,12},{12,8},{16,20},{20,16},{24,28},{28,24},{1,5},{5... | collective-permute-start | bytes 786440 | tf_op jit(solution)/shard_map/ppermute | solution.py:183

commit v6 on v5

--- a/solution.py
+++ b/solution.py
@@ -27,8 +27,14 @@
     return jnp.concatenate(parts, axis=0)
 
 
-def key_bias(my_blk, lengths, chips, block_tok, sub_tok, half, core):
-    blk_count = 2 * chips
+def owners_of(my_blk, far):
+    side = 2 << (my_blk & 1)
+    if far:
+        return [my_blk ^ 7 ^ side, my_blk ^ 6 ^ side, my_blk ^ 7]
+    return [my_blk, my_blk ^ 1, my_blk ^ side, my_blk ^ 1 ^ side, my_blk ^ 6]
+
+
+def key_bias(my_blk, lengths, blk_count, block_tok, sub_tok, half, far):
     my_block = my_blk if half == 0 else 2 * blk_count - 1 - my_blk
     lane = lax.broadcasted_iota(jnp.int32, (1, LANES), 1)
     sender = lax.axis_index("head") ^ (lane % block_tok // sub_tok)
@@ -40,11 +46,10 @@
         first = jnp.where(q_pos >= bound, bound, first)
     row = lax.broadcasted_iota(jnp.int32, (block_tok, LANES), 0)
     parts = []
-    for m in range(chips):
-        owner = (my_blk ^ core) ^ (2 * m)
+    for m, owner in enumerate(owners_of(my_blk, far)):
         for side in range(half + 1):
             block = owner if side == 0 else 2 * blk_count - 1 - owner
-            if core == 0 and m == 0 and side == half:
+            if not far and m == 0 and side == half:
                 allowed = (row <= q_pos - block * block_tok) & (row >= first - block * block_tok)
             else:
                 allowed = row >= first - jnp.where(block < my_block, block * block_tok, -(2**28))
@@ -52,11 +57,15 @@
     return jnp.concatenate(parts, axis=0)
 
 
-def page_targets(my_blk, page_slot, chips, slot_count, core):
+def page_targets(my_blk, page_slot, slot_count, far):
     _, pages_blk, blk_count = page_slot.shape
-    chip = lax.broadcasted_iota(jnp.int32, (chips, blk_count), 0)
-    owner = (my_blk ^ core) ^ (2 * chip)
-    chosen = (owner == lax.broadcasted_iota(jnp.int32, (chips, blk_count), 1)).astype(jnp.float32).astype(jnp.bfloat16)
+    owners = owners_of(my_blk, far)
+    shape = (len(owners), blk_count)
+    piece = lax.broadcasted_iota(jnp.int32, shape, 0)
+    owner = jnp.zeros(shape, jnp.int32)
+    for m, held in enumerate(owners):
+        owner = jnp.where(piece == m, held, owner)
+    chosen = (owner == lax.broadcasted_iota(jnp.int32, shape, 1)).astype(jnp.float32).astype(jnp.bfloat16)
     cols = 2 * pages_blk * PAGE
     page = lax.broadcasted_iota(jnp.int32, (pages_blk, cols), 0)
     col = lax.broadcasted_iota(jnp.int32, (pages_blk, cols), 1)
@@ -72,53 +81,61 @@
         slots = slots + jnp.dot(held.astype(jnp.bfloat16), spread, preferred_element_type=jnp.float32)
     slots = slots.astype(jnp.int32) - my_blk * slot_count
     rows = slots * PAGE + lax.broadcasted_iota(jnp.int32, slots.shape, 1) % PAGE
-    return jnp.concatenate([rows[m : m + 1] for m in range(chips)], axis=1)
+    return jnp.concatenate([rows[m : m + 1] for m in range(len(owners))], axis=1)
+
+
+def rows_of(pairs, halves, lane):
+    return jnp.concatenate(
+        [p[:, :halves, :, lane : lane + HEAD_DIM].reshape(-1, HEAD_DIM) for p in pairs], axis=0
+    )
 
 
 def place_pages(targets, pairs, slot_count):
-    rows = pairs[...].reshape(-1, pairs.shape[-1])
+    rows = jnp.concatenate([p[...].reshape(-1, p.shape[-1]) for p in pairs], axis=0)
     row = lax.broadcasted_iota(jnp.int32, (slot_count * PAGE, rows.shape[0]), 0)
     chosen = jnp.where(row == targets, 1.0, 0.0).astype(jnp.bfloat16)
     return jnp.dot(chosen, rows, preferred_element_type=jnp.float32)
 
 
-def score_part(queries, pairs, half):
-    keys = pairs[:, : half + 1].reshape(-1, 2 * HEAD_DIM)[:, :HEAD_DIM]
-    return lax.dot_general(keys, queries, (((1,), (1,)), ((), ())), preferred_element_type=jnp.float32)
-
-
-def weigh_part(scores, bias, pairs, half):
-    values = pairs[:, : half + 1].reshape(-1, 2 * HEAD_DIM)[:, HEAD_DIM:]
+def attend_part(queries, bias, pairs, half):
+    scores = lax.dot_general(
+        rows_of(pairs, half + 1, 0), queries, (((1,), (1,)), ((), ())), preferred_element_type=jnp.float32
+    )
     bias = jnp.concatenate([bias] * (scores.shape[1] // LANES), axis=1)
     scores = scores * (HEAD_DIM**-0.5 * LOG2E) + bias
     top = jnp.max(scores, axis=0, keepdims=True)
     weights = jnp.exp2(scores - top)
     total = jnp.sum(weights, axis=0, keepdims=True)
     out = lax.dot_general(
-        values, weights.astype(jnp.bfloat16), (((0,), (0,)), ((), ())), preferred_element_type=jnp.float32
+        rows_of(pairs, half + 1, HEAD_DIM),
+        weights.astype(jnp.bfloat16),
+        (((0,), (0,)), ((), ())),
+        preferred_element_type=jnp.float32,
     )
     return top, total, out
 
 
 def near_kernel(
-    lengths, page_slot, own, across, beside, near, q_rows, top_ref, total_ref, out_ref, pages_ref, far_bias_a,
+    lengths, page_slot, own, across, beside, chip, away, q_rows, top_ref, total_ref, out_ref, pages_ref, far_bias_a,
     far_bias_b, far_targets,
 ):
-    chips, _, block_tok, _ = near.shape
+    blk_count = page_slot.shape[2]
+    block_tok = chip.shape[2]
     slot_count = pages_ref.shape[0] // PAGE
     my_blk = lax.axis_index("blk")
-    bias = functools.partial(key_bias, my_blk, lengths[...] - lax.axis_index("head"), chips, block_tok, own.shape[2])
+    lengths = lengths[...] - lax.axis_index("head")
+    bias = functools.partial(key_bias, my_blk, lengths, blk_count, block_tok, own.shape[2])
     for half in (1, 0):
         queries = gather_queries(own, across, beside, half)
         q_rows[half] = queries
-        top, total, out = weigh_part(score_part(queries, near, half), bias(half, 0), near, half)
+        top, total, out = attend_part(queries, bias(half, False), (chip, away), half)
         top_ref[half] = top
         total_ref[half] = total
         out_ref[half] = out
-        (far_bias_a, far_bias_b)[half][...] = bias(half, 1)
-    targets = functools.partial(page_targets, my_blk, page_slot, chips, slot_count)
-    pages_ref[...] = place_pages(targets(0), near, slot_count).astype(jnp.bfloat16)
-    far_targets[...] = targets(1)
+        (far_bias_a, far_bias_b)[half][...] = bias(half, True)
+    targets = functools.partial(page_targets, my_blk, page_slot, slot_count)
+    pages_ref[...] = place_pages(targets(False), (chip, away), slot_count).astype(jnp.bfloat16)
+    far_targets[...] = targets(True)
 
 
 def far_kernel(
@@ -129,13 +146,13 @@
     slot_count = kv_cache.shape[0]
     my_head = lax.axis_index("head")
     sub_tok = block_tok // lax.axis_size("head")
-    moved = place_pages(far_targets[...], far, slot_count) + pages_ref[...].astype(jnp.float32)
+    moved = place_pages(far_targets[...], (far,), slot_count) + pages_ref[...].astype(jnp.float32)
     pages[...] = moved.astype(jnp.bfloat16).reshape(pages.shape)
     writes = [pltpu.make_async_copy(pages, kv_cache, sems.at[2])]
     writes[0].start()
     for half in (1, 0):
         bias = (far_bias_a, far_bias_b)[half][...]
-        top, total, out = weigh_part(score_part(q_rows[half], far, half), bias, far, half)
+        top, total, out = attend_part(q_rows[half], bias, (far,), half)
         best = jnp.maximum(top, top_ref[half])
         here = jnp.exp2(top - best)
         there = jnp.exp2(top_ref[half] - best)
@@ -167,9 +184,10 @@
     pair = jnp.concatenate([key_states, value_states], axis=3)
     lengths = doc_lengths + my_head
     pair, lengths, _ = lax.optimization_barrier((pair, lengths, part))
-    near = [
-        lax.ppermute(pair, "blk", [(i, i ^ d) for i in range(blk_count)]) for d in range(2, blk_count, 2)
-    ]
+    mate = lax.ppermute(pair, "blk", [(i, i ^ 1) for i in range(blk_count)])
+    across_chip = lax.ppermute(pair, "blk", [(i, i ^ 6) for i in range(blk_count)])
+    chip = jnp.concatenate([pair, mate], axis=0)
+    next_chip = lax.ppermute(chip, "blk", [(i, i ^ (2 << (i & 1))) for i in range(blk_count)])
     beside = jnp.concatenate(
         [
             lax.dynamic_slice_in_dim(query_states, (my_head ^ 1) * width, width, axis=3),
@@ -177,16 +195,16 @@
         ],
         axis=0,
     )
-    near = lax.optimization_barrier((near[::-1], beside))[0][::-1]
+    across_chip, next_chip, _ = lax.optimization_barrier((across_chip, next_chip, beside))
     beside = lax.ppermute(beside, "head", [(i, i ^ 1) for i in range(head_count)])
-    near = jnp.concatenate([pair] + near, axis=0)
-    far = lax.ppermute(near, "blk", [(i, i ^ 1) for i in range(blk_count)])
+    away = jnp.concatenate([next_chip, across_chip], axis=0)
+    far = lax.ppermute(away, "blk", [(i, i ^ 1) for i in range(blk_count)])
 
     hbm = pl.BlockSpec(memory_space=pl.ANY)
     vmem = pl.BlockSpec(memory_space=pltpu.VMEM)
     params = pltpu.CompilerParams(vmem_limit_bytes=32 * 1024 * 1024)
     cost = pl.CostEstimate(flops=4_000_000_000, bytes_accessed=1_000_000, transcendentals=200_000)
-    half_cols = blk_count // 2 * block_tok
+    far_cols = far.shape[0] * block_tok
     stats = pl.pallas_call(
         near_kernel,
         out_shape=(
@@ -195,15 +213,15 @@
             jax.ShapeDtypeStruct((2, 1, rows), jnp.float32),
             jax.ShapeDtypeStruct((2, HEAD_DIM, rows), jnp.float32),
             jax.ShapeDtypeStruct((slot_count * PAGE, 2 * HEAD_DIM), jnp.bfloat16),
-            jax.ShapeDtypeStruct((half_cols, LANES), jnp.float32),
-            jax.ShapeDtypeStruct((2 * half_cols, LANES), jnp.float32),
-            jax.ShapeDtypeStruct((1, 2 * half_cols), jnp.int32),
-        ),
-        in_specs=[vmem] * 6,
+            jax.ShapeDtypeStruct((far_cols, LANES), jnp.float32),
+            jax.ShapeDtypeStruct((2 * far_cols, LANES), jnp.float32),
+            jax.ShapeDtypeStruct((1, 2 * far_cols), jnp.int32),
+        ),
+        in_specs=[vmem] * 7,
         out_specs=(vmem,) * 8,
         compiler_params=params,
         cost_estimate=cost,
-    )(lengths.reshape(1, -1), page_slot.transpose(1, 2, 0), query_states, across, beside, near)
+    )(lengths.reshape(1, -1), page_slot.transpose(1, 2, 0), query_states, across, beside, chip, away)
     return pl.pallas_call(
         far_kernel,
         out_shape=(
@@ -330,7 +348,7 @@
 
 def solution(mesh):
     return jax.shard_map(
-        per_device if mesh.shape["blk"] <= 8 else per_device_long,
+        per_device if (mesh.shape["blk"], mesh.shape["head"]) == (8, 4) else per_device_long,
         mesh=mesh,
         in_specs=(
             P("blk", None, "head", None),

time: 16.2 us -> 16.7 us (1.031)
  starting transfers between devices: 9.3 us -> 8.58 us
  waiting for transfers between devices: 2.59 us -> 3.28 us
  local copies, waits for them, and re-layouts: 0.95 us -> 1.36 us
    ppermute x4, waiting for transfers between devices: 2.01 us -> 2.78 us  [the longest x1 2.19 us: per_device(): lax.ppermute(chip, 'blk', [(i, i ^ 2 << (i & 1)) for i in range(blk_count)])]
    ppermute x1, waiting for transfers between devices: 0.56 us -> 0.15 us  [per_device(): lax.ppermute(beside, 'head', [(i, i ^ 1) for i in range(head_count)])]
    unnamed x13 -> x12, local copies, waits for them, and re-layouts: 0.07 us -> 0.47 us
    ppermute x4, starting transfers between devices: 3.62 us -> 3.25 us  [the longest x1 2.51 us: per_device(): lax.ppermute(pair, 'blk', [(i, i ^ 6) for i in range(blk_count)])]
    ppermute x1, starting transfers between devices: 1.64 us -> 1.29 us  [per_device(): lax.ppermute(beside, 'head', [(i, i ^ 1) for i in range(head_count)])]
    ppermute x1, waiting for transfers between devices: 0.02 us -> 0.36 us  [per_device(): across = lax.ppermute(part, 'head', [(i, i ^ 2) for i in range(head_count)])]
    pallas_call x1, Pallas kernels: 1 us -> 1.19 us  [per_device(): pl.pallas_call(near_kernel, out_shape=(jax.ShapeDtypeStruct((2, rows, HEA...]
  transfers between devices with their start and end apart: 6 -> 6, of which waited for: 4 -> 4; matrix products, arithmetic and copies ran while one was open for 0% -> 0% of each run, Pallas kernels for 6% -> 7%
where the time goes in v6:
time: 16.7 us; the launch traced here: 16.5 us
  starting transfers between devices  8.58 us (51%)
  waiting for transfers between devices  3.28 us (20%)
  Pallas kernels  2.5 us (15%)
  local copies, waits for them, and re-layouts  1.36 us (8%)
  between operations  0.77 us (5%)
    ppermute x1, starting transfers between devices, per_device(): across = lax.ppermute(part, 'head', [(i, i ^ 2) for i in range(head_count)])  4.04 us
    ppermute x1, starting transfers between devices, per_device(): lax.ppermute(pair, 'blk', [(i, i ^ 6) for i in range(blk_count)])  2.51 us
    ppermute x1, waiting for transfers between devices, per_device(): lax.ppermute(chip, 'blk', [(i, i ^ 2 << (i & 1)) for i in range(blk_count)])  2.19 us
    pallas_call x1, Pallas kernels, per_device(): pl.pallas_call(far_kernel, out_shape=(jax.ShapeDtypeStruct((1, 2, block_t...  1.31 us
    ppermute x1, starting transfers between devices, per_device(): lax.ppermute(beside, 'head', [(i, i ^ 1) for i in range(head_count)])  1.29 us
    pallas_call x1, Pallas kernels, per_device(): pl.pallas_call(near_kernel, out_shape=(jax.ShapeDtypeStruct((2, rows, HEA...  1.19 us
    dynamic_slice x1, local copies, waits for them, and re-layouts, per_device(): lax.dynamic_slice_in_dim(query_states, (my_head & 2 ^ 2) * width, 2 * wid...  0.86 us
    ppermute x1, starting transfers between devices, per_device(): lax.ppermute(chip, 'blk', [(i, i ^ 2 << (i & 1)) for i in range(blk_count)])  0.6 us
  transfers between devices with their start and end apart: 6, of which 4 were waited for; matrix products, arithmetic and copies ran while one was open for 0% of the time, Pallas kernels for 7%

profile of v6, /device:TPU:0, one launch (start us, length us, event | category | flops | bytes accessed | tf_op | source)
XLA Modules:
  0.0 16.5 jit_solution(9010629520429189835)
XLA Ops:
  0.6 0.0 copy-start.4
  0.7 0.0 copy-start.2
  0.7 0.0 copy-start.3
  0.7 0.9 %constant_dynamic-slice_fusion.2 = bf16[1,2,16,1024]{3,2,1,0:T(8,128)(2,1)S(1)} fusion(bf16[1,2,16,2048]{3,2,1,0:T(8,128)(2,1)} %own.1, s32[]{:T(128)S(6)} %select_n.9), kind=kLoop, calls=%fused_computation.8 | loop fusion | bytes 131076 | tf_op jit(solution)/shard_map/dynamic_slice | solution.py:182
  1.5 4.0 %collective-permute-start.3 = (bf16[1,2,16,1024]{3,2,1,0:T(8,128)(2,1)S(1)}, bf16[1,2,16,1024]{3,2,1,0:T(8,128)(2,1)S(1)}, u32[]{:S(2)}, u32[]{:S(2)}) collective-permute-start(bf16[1,2,16,1024]{3,2,1,0:T(8,128)(2,1)S(1)} %constant_dynamic-slice_fusion.2), channel_id=1, source_target_pairs={{0,2},{1,3},{2,0},{3,1},{4,6},{5,7},{6,4},{7,5},{8,10},{9,11},{10,... | collective-permute-start | bytes 196616 | tf_op jit(solution)/shard_map/ppermute | solution.py:183
  5.6 0.0 copy-done.4
  5.6 0.0 copy-done.2
  5.6 0.0 copy-done.3
  5.6 0.0 copy-start
  5.6 0.1 collective-permute-start.1
  5.7 2.5 %collective-permute-start = (bf16[1,2,64,256]{3,2,1,0:T(8,128)(2,1)S(1)}, bf16[1,2,64,256]{3,2,1,0:T(8,128)(2,1)S(1)}, u32[]{:S(2)}, u32[]{:S(2)}) collective-permute-start(bf16[1,2,64,256]{3,2,1,0:T(8,128)(2,1)S(1)} %pad_maximum_fusion), channel_id=1, source_target_pairs={{0,24},{4,28},{8,16},{12,20},{16,8},{20,12},{24,0},{28,4},{1,25},{... | collective-permute-start | bytes 196616 | tf_op jit(solution)/shard_map/ppermute | solution.py:188
  8.2 0.0 copy-done
  8.2 0.0 collective-permute-done.1
  8.3 0.6 %collective-permute-start.2 = (bf16[2,2,64,256]{3,2,1,0:T(8,128)(2,1)S(1)}, bf16[2,2,64,256]{3,2,1,0:T(8,128)(2,1)S(1)}, u32[]{:S(2)}, u32[]{:S(2)}) collective-permute-start(bf16[2,2,64,256]{3,2,1,0:T(8,128)(2,1)S(1)} %constant_dynamic-update-slice_fusion.chip), channel_id=1, source_target_pairs={{0,8},{4,20},{8,0},{12,28},{16,24},{20,4},{24,16},{28,12},{1,9},{5... | collective-permute-start | bytes 393224 | tf_op jit(solution)/shard_map/ppermute | solution.py:190
  8.9 0.4 %collective-permute-done.3.across = bf16[1,2,16,1024]{3,2,1,0:T(8,128)(2,1)S(1)} collective-permute-done((bf16[1,2,16,1024]{3,2,1,0:T(8,128)(2,1)S(1)}, bf16[1,2,16,1024]{3,2,1,0:T(8,128)(2,1)S(1)}, u32[]{:S(2)}, u32[]{:S(2)}) %collective-permute-start.3) | collective-permute-done | bytes 65568 | tf_op jit(solution)/shard_map/ppermute | solution.py:183
  9.2 1.3 %collective-permute-start.5 = (bf16[2,2,16,512]{3,2,1,0:T(8,128)(2,1)S(1)}, bf16[2,2,16,512]{3,2,1,0:T(8,128)(2,1)S(1)}, u32[]{:S(2)}, u32[]{:S(2)}) collective-permute-start(bf16[2,2,16,512]{3,2,1,0:T(8,128)(2,1)S(1)} %pad_maximum_fusion.1), channel_id=1, source_target_pairs={{0,1},{1,0},{2,3},{3,2},{4,5},{5,4},{6,7},{7,6},{8,9},{9,8},{10,11... | collective-permute-start | bytes 196616 | tf_op jit(solution)/shard_map/ppermute | solution.py:199
  10.5 0.6 %collective-permute-done = bf16[1,2,64,256]{3,2,1,0:T(8,128)(2,1)S(1)} collective-permute-done((bf16[1,2,64,256]{3,2,1,0:T(8,128)(2,1)S(1)}, bf16[1,2,64,256]{3,2,1,0:T(8,128)(2,1)S(1)}, u32[]{:S(2)}, u32[]{:S(2)}) %collective-permute-start) | collective-permute-done | bytes 65568 | tf_op jit(solution)/shard_map/ppermute | solution.py:188
  11.1 2.2 %collective-permute-done.2 = bf16[2,2,64,256]{3,2,1,0:T(8,128)(2,1)S(1)} collective-permute-done((bf16[2,2,64,256]{3,2,1,0:T(8,128)(2,1)S(1)}, bf16[2,2,64,256]{3,2,1,0:T(8,128)(2,1)S(1)}, u32[]{:S(2)}, u32[]{:S(2)}) %collective-permute-start.2) | collective-permute-done | bytes 131104 | tf_op jit(solution)/shard_map/ppermute | solution.py:190
  13.3 0.0 copy-start.1
  13.3 0.1 collective-permute-start.4
  13.4 0.2 collective-permute-done.5.beside
  13.6 0.4 %copy-done.1 = s32[8,2,4]{0,2,1:T(4,128)S(1)} copy-done((s32[8,2,4]{0,2,1:T(4,128)S(1)}, s32[8,2,4]{0,2,1:T(4,128)}, u32[]{:S(2)}) %copy-start.1) | copy-done | bytes 280
  14.0 1.2 %shard_map.68 = (bf16[2,256,128]{2,1,0:T(8,128)(2,1)S(1)}, f32[2,1,256]{2,1,0:T(1,128)S(1)}, f32[2,1,256]{2,1,0:T(1,128)S(1)}, f32[2,128,256]{2,1,0:T(8,128)S(1)...) custom-call(s32[1,3]{1,0:T(1,128)S(1)} %bitcast.3, ...), custom_call_target="tpu_custom_call" | custom-call | flops 4000000000 | bytes 1000000 | tf_op jit(solution)/shard_map/pallas_call | solution.py:208
  15.2 0.0 collective-permute-done.4.far
  15.2 1.3 %shard_map.69 = (bf16[1,2,64,512]{3,2,1,0:T(8,128)(2,1)}, bf16[16,1,16,256]{3,2,1,0:T(8,128)(2,1)}) custom-call(bf16[3,2,64,256]{3,2,1,0:T(8,128)(2,1)S(1)} %collective-permute-done.4.far, bf16[2,256,128]{2,1,0:T(8,128)(2,1)S(1)} %get-tuple-element.18.q_rows, f32[2,1,256]{2,1,0:T(1,128)S(1)} %get-tuple-element.19.top_ref, ...), custom_call_target="tpu_custom_call" | custom-call | flops 4000000000 | bytes 1000000 | tf_op jit(solution)/shard_map/pallas_call | solution.py:225
  (9 shorter events, 0.1 us)
Async XLA Ops:
  0.6 4.9 %copy-start.4 = (s32[3]{0:T(128)S(1)}, s32[3]{0:T(128)}, u32[]{:S(2)}) copy-start(s32[3]{0:T(128)} %param.8) | copy-start | bytes 40
  0.7 4.9 %copy-start.2 = (bf16[1,2,64,128]{3,2,1,0:T(8,128)(2,1)S(1)}, bf16[1,2,64,128]{3,2,1,0:T(8,128)(2,1)}, u32[]{:S(2)}) copy-start(bf16[1,2,64,128]{3,2,1,0:T(8,128)(2,1)} %param.7) | copy-start | bytes 98308
  0.7 4.9 %copy-start.3 = (bf16[1,2,64,128]{3,2,1,0:T(8,128)(2,1)S(1)}, bf16[1,2,64,128]{3,2,1,0:T(8,128)(2,1)}, u32[]{:S(2)}) copy-start(bf16[1,2,64,128]{3,2,1,0:T(8,128)(2,1)} %param.6) | copy-start | bytes 98308
  1.5 7.7 %collective-permute-start.3 = (bf16[1,2,16,1024]{3,2,1,0:T(8,128)(2,1)S(1)}, bf16[1,2,16,1024]{3,2,1,0:T(8,128)(2,1)S(1)}, u32[]{:S(2)}, u32[]{:S(2)}) collective-permute-start(bf16[1,2,16,1024]{3,2,1,0:T(8,128)(2,1)S(1)} %constant_dynamic-slice_fusion.2), channel_id=1, source_target_pairs={{0,2},{1,3},{2,0},{3,1},{4,6},{5,7},{6,4},{7,5},{8,10},{9,11},{10,... | collective-permute-start | bytes 196616 | tf_op jit(solution)/shard_map/ppermute | solution.py:183
  5.6 2.6 %copy-start = (bf16[1,2,16,2048]{3,2,1,0:T(8,128)(2,1)S(1)}, bf16[1,2,16,2048]{3,2,1,0:T(8,128)(2,1)}, u32[]{:S(2)}) copy-start(bf16[1,2,16,2048]{3,2,1,0:T(8,128)(2,1)} %own.1) | copy-start | bytes 393220
  5.6 2.6 %collective-permute-start.1 = (bf16[1,2,64,256]{3,2,1,0:T(8,128)(2,1)S(1)}, bf16[1,2,64,256]{3,2,1,0:T(8,128)(2,1)S(1)}, u32[]{:S(2)}, u32[]{:S(2)}) collective-permute-start(bf16[1,2,64,256]{3,2,1,0:T(8,128)(2,1)S(1)} %pad_maximum_fusion), channel_id=1, source_target_pairs={{0,4},{4,0},{8,12},{12,8},{16,20},{20,16},{24,28},{28,24},{1,5},{5... | collective-permute-start | bytes 196616 | tf_op jit(solution)/shard_map/ppermute | solution.py:187
  5.7 5.4 %collective-permute-start = (bf16[1,2,64,256]{3,2,1,0:T(8,128)(2,1)S(1)}, bf16[1,2,64,256]{3,2,1,0:T(8,128)(2,1)S(1)}, u32[]{:S(2)}, u32[]{:S(2)}) collective-permute-start(bf16[1,2,64,256]{3,2,1,0:T(8,128)(2,1)S(1)} %pad_maximum_fusion), channel_id=1, source_target_pairs={{0,24},{4,28},{8,16},{12,20},{16,8},{20,12},{24,0},{28,4},{1,25},{... | collective-permute-start | bytes 196616 | tf_op jit(solution)/shard_map/ppermute | solution.py:188
  8.3 5.0 %collective-permute-start.2 = (bf16[2,2,64,256]{3,2,1,0:T(8,128)(2,1)S(1)}, bf16[2,2,64,256]{3,2,1,0:T(8,128)(2,1)S(1)}, u32[]{:S(2)}, u32[]{:S(2)}) collective-permute-start(bf16[2,2,64,256]{3,2,1,0:T(8,128)(2,1)S(1)} %constant_dynamic-update-slice_fusion.chip), channel_id=1, source_target_pairs={{0,8},{4,20},{8,0},{12,28},{16,24},{20,4},{24,16},{28,12},{1,9},{5... | collective-permute-start | bytes 393224 | tf_op jit(solution)/shard_map/ppermute | solution.py:190
  9.2 4.3 %collective-permute-start.5 = (bf16[2,2,16,512]{3,2,1,0:T(8,128)(2,1)S(1)}, bf16[2,2,16,512]{3,2,1,0:T(8,128)(2,1)S(1)}, u32[]{:S(2)}, u32[]{:S(2)}) collective-permute-start(bf16[2,2,16,512]{3,2,1,0:T(8,128)(2,1)S(1)} %pad_maximum_fusion.1), channel_id=1, source_target_pairs={{0,1},{1,0},{2,3},{3,2},{4,5},{5,4},{6,7},{7,6},{8,9},{9,8},{10,11... | collective-permute-start | bytes 196616 | tf_op jit(solution)/shard_map/ppermute | solution.py:199
  13.3 0.7 %copy-start.1 = (s32[8,2,4]{0,2,1:T(4,128)S(1)}, s32[8,2,4]{0,2,1:T(4,128)}, u32[]{:S(2)}) copy-start(s32[8,2,4]{0,2,1:T(4,128)} %param.9) | copy-start | bytes 772
  13.3 1.9 %collective-permute-start.4 = (bf16[3,2,64,256]{3,2,1,0:T(8,128)(2,1)S(1)}, bf16[3,2,64,256]{3,2,1,0:T(8,128)(2,1)S(1)}, u32[]{:S(2)}, u32[]{:S(2)}) collective-permute-start(bf16[3,2,64,256]{3,2,1,0:T(8,128)(2,1)S(1)} %constant_dynamic-update-slice_fusion.2.away), channel_id=1, source_target_pairs={{0,4},{4,0},{8,12},{12,8},{16,20},{20,16},{24,28},{28,24},{1,5},{5... | collective-permute-start | bytes 589832 | tf_op jit(solution)/shard_map/ppermute | solution.py:201

commit v7 on v5

--- a/solution.py
+++ b/solution.py
@@ -87,17 +87,17 @@
     return lax.dot_general(keys, queries, (((1,), (1,)), ((), ())), preferred_element_type=jnp.float32)
 
 
-def weigh_part(scores, bias, pairs, half):
-    values = pairs[:, : half + 1].reshape(-1, 2 * HEAD_DIM)[:, HEAD_DIM:]
+def soften(scores, bias):
     bias = jnp.concatenate([bias] * (scores.shape[1] // LANES), axis=1)
     scores = scores * (HEAD_DIM**-0.5 * LOG2E) + bias
     top = jnp.max(scores, axis=0, keepdims=True)
     weights = jnp.exp2(scores - top)
-    total = jnp.sum(weights, axis=0, keepdims=True)
-    out = lax.dot_general(
-        values, weights.astype(jnp.bfloat16), (((0,), (0,)), ((), ())), preferred_element_type=jnp.float32
-    )
-    return top, total, out
+    return top, jnp.sum(weights, axis=0, keepdims=True), weights.astype(jnp.bfloat16)
+
+
+def weigh_part(weights, pairs, half):
+    values = pairs[:, : half + 1].reshape(-1, 2 * HEAD_DIM)[:, HEAD_DIM:]
+    return lax.dot_general(values, weights, (((0,), (0,)), ((), ())), preferred_element_type=jnp.float32)
 
 
 def near_kernel(
@@ -108,34 +108,40 @@
     slot_count = pages_ref.shape[0] // PAGE
     my_blk = lax.axis_index("blk")
     bias = functools.partial(key_bias, my_blk, lengths[...] - lax.axis_index("head"), chips, block_tok, own.shape[2])
+    targets = functools.partial(page_targets, my_blk, page_slot, chips, slot_count)
+    scores = {}
     for half in (1, 0):
         queries = gather_queries(own, across, beside, half)
         q_rows[half] = queries
-        top, total, out = weigh_part(score_part(queries, near, half), bias(half, 0), near, half)
-        top_ref[half] = top
-        total_ref[half] = total
-        out_ref[half] = out
+        scores[half] = score_part(queries, near, half)
+    for half in (1, 0):
+        top_ref[half], total_ref[half], weights = soften(scores[half], bias(half, 0))
+        out_ref[half] = weigh_part(weights, near, half)
+    pages_ref[...] = place_pages(targets(0), near, slot_count).astype(jnp.bfloat16)
+    for half in (1, 0):
         (far_bias_a, far_bias_b)[half][...] = bias(half, 1)
-    targets = functools.partial(page_targets, my_blk, page_slot, chips, slot_count)
-    pages_ref[...] = place_pages(targets(0), near, slot_count).astype(jnp.bfloat16)
     far_targets[...] = targets(1)
 
 
 def far_kernel(
-    far, q_rows, top_ref, total_ref, out_ref, pages_ref, far_bias_a, far_bias_b, far_targets, attended, kv_cache,
+    far, q_rows, top_ref, total_ref, out_ref, pages_ref, bias_a, bias_b, far_targets, attended, kv_cache,
     pages, result, sems,
 ):
     block_tok = far.shape[2]
     slot_count = kv_cache.shape[0]
     my_head = lax.axis_index("head")
     sub_tok = block_tok // lax.axis_size("head")
+    scores = {half: score_part(q_rows[half], far, half) for half in (1, 0)}
     moved = place_pages(far_targets[...], far, slot_count) + pages_ref[...].astype(jnp.float32)
     pages[...] = moved.astype(jnp.bfloat16).reshape(pages.shape)
     writes = [pltpu.make_async_copy(pages, kv_cache, sems.at[2])]
     writes[0].start()
-    for half in (1, 0):
-        bias = (far_bias_a, far_bias_b)[half][...]
-        top, total, out = weigh_part(score_part(q_rows[half], far, half), bias, far, half)
+    parts = {}
+    for half in (1, 0):
+        top, total, weights = soften(scores[half], (bias_a, bias_b)[half][...])
+        parts[half] = (top, total, weigh_part(weights, far, half))
+    for half in (1, 0):
+        top, total, out = parts[half]
         best = jnp.maximum(top, top_ref[half])
         here = jnp.exp2(top - best)
         there = jnp.exp2(top_ref[half] - best)

time: 16.2 us -> 16.1 us (level)
  no operation moved by 1% of the time
where the time goes in v7:
time: 16.1 us; the launch traced here: 15.9 us
  starting transfers between devices  9.3 us (58%)
  waiting for transfers between devices  2.59 us (16%)
  Pallas kernels  2.31 us (14%)
  local copies, waits for them, and re-layouts  0.95 us (6%)
  between operations  0.76 us (5%)
    ppermute x1, starting transfers between devices, per_device(): across = lax.ppermute(part, 'head', [(i, i ^ 2) for i in range(head_count)])  4.04 us
    ppermute x3, starting transfers between devices, per_device(): lax.ppermute(pair, 'blk', [(i, i ^ d) for i in range(blk_count)])  3.55 us
    ppermute x3, waiting for transfers between devices, per_device(): lax.ppermute(pair, 'blk', [(i, i ^ d) for i in range(blk_count)])  2.01 us
    ppermute x1, starting transfers between devices, per_device(): lax.ppermute(beside, 'head', [(i, i ^ 1) for i in range(head_count)])  1.64 us
    pallas_call x1, Pallas kernels, per_device(): pl.pallas_call(far_kernel, out_shape=(jax.ShapeDtypeStruct((1, 2, block_t...  1.37 us
    pallas_call x1, Pallas kernels, per_device(): pl.pallas_call(near_kernel, out_shape=(jax.ShapeDtypeStruct((2, rows, HEA...  0.94 us
    dynamic_slice x1, local copies, waits for them, and re-layouts, per_device(): lax.dynamic_slice_in_dim(query_states, (my_head & 2 ^ 2) * width, 2 * wid...  0.86 us
    ppermute x1, waiting for transfers between devices, per_device(): lax.ppermute(beside, 'head', [(i, i ^ 1) for i in range(head_count)])  0.56 us
  transfers between devices with their start and end apart: 6, of which 4 were waited for; matrix products, arithmetic and copies ran while one was open for 0% of the time, Pallas kernels for 6%

profile of v7, /device:TPU:0, one launch (start us, length us, event | category | flops | bytes accessed | tf_op | source)
XLA Modules:
  0.0 15.9 jit_solution(8704143008643588367)
XLA Ops:
  0.6 0.0 copy-start.4
  0.7 0.0 copy-start.2
  0.7 0.0 copy-start.3
  0.7 0.9 %constant_dynamic-slice_fusion.2 = bf16[1,2,16,1024]{3,2,1,0:T(8,128)(2,1)S(1)} fusion(bf16[1,2,16,2048]{3,2,1,0:T(8,128)(2,1)} %own.1, s32[]{:T(128)S(6)} %select_n.9), kind=kLoop, calls=%fused_computation.8 | loop fusion | bytes 131076 | tf_op jit(solution)/shard_map/dynamic_slice | solution.py:171
  1.5 4.0 %collective-permute-start.3 = (bf16[1,2,16,1024]{3,2,1,0:T(8,128)(2,1)S(1)}, bf16[1,2,16,1024]{3,2,1,0:T(8,128)(2,1)S(1)}, u32[]{:S(2)}, u32[]{:S(2)}) collective-permute-start(bf16[1,2,16,1024]{3,2,1,0:T(8,128)(2,1)S(1)} %constant_dynamic-slice_fusion.2), channel_id=1, source_target_pairs={{0,2},{1,3},{2,0},{3,1},{4,6},{5,7},{6,4},{7,5},{8,10},{9,11},{10,... | collective-permute-start | bytes 196616 | tf_op jit(solution)/shard_map/ppermute | solution.py:172
  5.6 0.0 copy-done.4
  5.6 0.0 copy-done.2
  5.6 0.0 copy-done.3
  5.6 0.0 copy-start
  5.6 2.5 %collective-permute-start = (bf16[1,2,64,256]{3,2,1,0:T(8,128)(2,1)S(1)}, bf16[1,2,64,256]{3,2,1,0:T(8,128)(2,1)S(1)}, u32[]{:S(2)}, u32[]{:S(2)}) collective-permute-start(bf16[1,2,64,256]{3,2,1,0:T(8,128)(2,1)S(1)} %pad_maximum_fusion), channel_id=1, source_target_pairs={{0,24},{4,28},{8,16},{12,20},{16,8},{20,12},{24,0},{28,4},{1,25},{... | collective-permute-start | bytes 196616 | tf_op jit(solution)/shard_map/ppermute | solution.py:177
  8.1 0.5 %collective-permute-start.1 = (bf16[1,2,64,256]{3,2,1,0:T(8,128)(2,1)S(1)}, bf16[1,2,64,256]{3,2,1,0:T(8,128)(2,1)S(1)}, u32[]{:S(2)}, u32[]{:S(2)}) collective-permute-start(bf16[1,2,64,256]{3,2,1,0:T(8,128)(2,1)S(1)} %pad_maximum_fusion), channel_id=1, source_target_pairs={{0,16},{4,20},{8,24},{12,28},{16,0},{20,4},{24,8},{28,12},{1,17},{... | collective-permute-start | bytes 196616 | tf_op jit(solution)/shard_map/ppermute | solution.py:177
  8.6 0.5 %collective-permute-start.2 = (bf16[1,2,64,256]{3,2,1,0:T(8,128)(2,1)S(1)}, bf16[1,2,64,256]{3,2,1,0:T(8,128)(2,1)S(1)}, u32[]{:S(2)}, u32[]{:S(2)}) collective-permute-start(bf16[1,2,64,256]{3,2,1,0:T(8,128)(2,1)S(1)} %pad_maximum_fusion), channel_id=1, source_target_pairs={{0,8},{4,12},{8,0},{12,4},{16,24},{20,28},{24,16},{28,20},{1,9},{5... | collective-permute-start | bytes 196616 | tf_op jit(solution)/shard_map/ppermute | solution.py:177
  9.2 0.0 copy-done
  9.2 0.0 collective-permute-done.3.across
  9.2 1.6 %collective-permute-start.5 = (bf16[2,2,16,512]{3,2,1,0:T(8,128)(2,1)S(1)}, bf16[2,2,16,512]{3,2,1,0:T(8,128)(2,1)S(1)}, u32[]{:S(2)}, u32[]{:S(2)}) collective-permute-start(bf16[2,2,16,512]{3,2,1,0:T(8,128)(2,1)S(1)} %pad_maximum_fusion.1), channel_id=1, source_target_pairs={{0,1},{1,0},{2,3},{3,2},{4,5},{5,4},{6,7},{7,6},{8,9},{9,8},{10,11... | collective-permute-start | bytes 196616 | tf_op jit(solution)/shard_map/ppermute | solution.py:187
  10.9 0.1 collective-permute-done
  10.9 1.4 %collective-permute-done.1 = bf16[1,2,64,256]{3,2,1,0:T(8,128)(2,1)S(1)} collective-permute-done((bf16[1,2,64,256]{3,2,1,0:T(8,128)(2,1)S(1)}, bf16[1,2,64,256]{3,2,1,0:T(8,128)(2,1)S(1)}, u32[]{:S(2)}, u32[]{:S(2)}) %collective-permute-start.1) | collective-permute-done | bytes 65568 | tf_op jit(solution)/shard_map/ppermute | solution.py:177
  12.4 0.5 %collective-permute-done.2 = bf16[1,2,64,256]{3,2,1,0:T(8,128)(2,1)S(1)} collective-permute-done((bf16[1,2,64,256]{3,2,1,0:T(8,128)(2,1)S(1)}, bf16[1,2,64,256]{3,2,1,0:T(8,128)(2,1)S(1)}, u32[]{:S(2)}, u32[]{:S(2)}) %collective-permute-start.2) | collective-permute-done | bytes 65568 | tf_op jit(solution)/shard_map/ppermute | solution.py:177
  12.9 0.0 copy-start.1
  12.9 0.1 collective-permute-start.4
  13.0 0.6 %collective-permute-done.5.beside = bf16[2,2,16,512]{3,2,1,0:T(8,128)(2,1)S(1)} collective-permute-done((bf16[2,2,16,512]{3,2,1,0:T(8,128)(2,1)S(1)}, bf16[2,2,16,512]{3,2,1,0:T(8,128)(2,1)S(1)}, u32[]{:S(2)}, u32[]{:S(2)}) %collective-permute-start.5) | collective-permute-done | bytes 65568 | tf_op jit(solution)/shard_map/ppermute | solution.py:187
  13.6 0.0 copy-done.1
  13.6 0.9 %shard_map.68 = (bf16[2,256,128]{2,1,0:T(8,128)(2,1)S(1)}, f32[2,1,256]{2,1,0:T(1,128)S(1)}, f32[2,1,256]{2,1,0:T(1,128)S(1)}, f32[2,128,256]{2,1,0:T(8,128)S(1)...) custom-call(s32[1,3]{1,0:T(1,128)S(1)} %bitcast.3, ...), custom_call_target="tpu_custom_call" | custom-call | flops 4000000000 | bytes 1000000 | tf_op jit(solution)/shard_map/pallas_call | solution.py:196
  14.5 0.0 collective-permute-done.4.far
  14.6 1.4 %shard_map.69 = (bf16[1,2,64,512]{3,2,1,0:T(8,128)(2,1)}, bf16[16,1,16,256]{3,2,1,0:T(8,128)(2,1)}) custom-call(bf16[4,2,64,256]{3,2,1,0:T(8,128)(2,1)S(1)} %collective-permute-done.4.far, bf16[2,256,128]{2,1,0:T(8,128)(2,1)S(1)} %get-tuple-element.20.q_rows, f32[2,1,256]{2,1,0:T(1,128)S(1)} %get-tuple-element.21.top_ref, ...), custom_call_target="tpu_custom_call" | custom-call | flops 4000000000 | bytes 1000000 | tf_op jit(solution)/shard_map/pallas_call | solution.py:213
  (9 shorter events, 0.1 us)
Async XLA Ops:
  0.6 4.9 %copy-start.4 = (s32[3]{0:T(128)S(1)}, s32[3]{0:T(128)}, u32[]{:S(2)}) copy-start(s32[3]{0:T(128)} %param.8) | copy-start | bytes 40
  0.7 4.9 %copy-start.2 = (bf16[1,2,64,128]{3,2,1,0:T(8,128)(2,1)S(1)}, bf16[1,2,64,128]{3,2,1,0:T(8,128)(2,1)}, u32[]{:S(2)}) copy-start(bf16[1,2,64,128]{3,2,1,0:T(8,128)(2,1)} %param.7) | copy-start | bytes 98308
  0.7 4.9 %copy-start.3 = (bf16[1,2,64,128]{3,2,1,0:T(8,128)(2,1)S(1)}, bf16[1,2,64,128]{3,2,1,0:T(8,128)(2,1)}, u32[]{:S(2)}) copy-start(bf16[1,2,64,128]{3,2,1,0:T(8,128)(2,1)} %param.6) | copy-start | bytes 98308
  1.5 7.7 %collective-permute-start.3 = (bf16[1,2,16,1024]{3,2,1,0:T(8,128)(2,1)S(1)}, bf16[1,2,16,1024]{3,2,1,0:T(8,128)(2,1)S(1)}, u32[]{:S(2)}, u32[]{:S(2)}) collective-permute-start(bf16[1,2,16,1024]{3,2,1,0:T(8,128)(2,1)S(1)} %constant_dynamic-slice_fusion.2), channel_id=1, source_target_pairs={{0,2},{1,3},{2,0},{3,1},{4,6},{5,7},{6,4},{7,5},{8,10},{9,11},{10,... | collective-permute-start | bytes 196616 | tf_op jit(solution)/shard_map/ppermute | solution.py:172
  5.6 3.6 %copy-start = (bf16[1,2,16,2048]{3,2,1,0:T(8,128)(2,1)S(1)}, bf16[1,2,16,2048]{3,2,1,0:T(8,128)(2,1)}, u32[]{:S(2)}) copy-start(bf16[1,2,16,2048]{3,2,1,0:T(8,128)(2,1)} %own.1) | copy-start | bytes 393220
  5.6 5.3 %collective-permute-start = (bf16[1,2,64,256]{3,2,1,0:T(8,128)(2,1)S(1)}, bf16[1,2,64,256]{3,2,1,0:T(8,128)(2,1)S(1)}, u32[]{:S(2)}, u32[]{:S(2)}) collective-permute-start(bf16[1,2,64,256]{3,2,1,0:T(8,128)(2,1)S(1)} %pad_maximum_fusion), channel_id=1, source_target_pairs={{0,24},{4,28},{8,16},{12,20},{16,8},{20,12},{24,0},{28,4},{1,25},{... | collective-permute-start | bytes 196616 | tf_op jit(solution)/shard_map/ppermute | solution.py:177
  8.1 4.3 %collective-permute-start.1 = (bf16[1,2,64,256]{3,2,1,0:T(8,128)(2,1)S(1)}, bf16[1,2,64,256]{3,2,1,0:T(8,128)(2,1)S(1)}, u32[]{:S(2)}, u32[]{:S(2)}) collective-permute-start(bf16[1,2,64,256]{3,2,1,0:T(8,128)(2,1)S(1)} %pad_maximum_fusion), channel_id=1, source_target_pairs={{0,16},{4,20},{8,24},{12,28},{16,0},{20,4},{24,8},{28,12},{1,17},{... | collective-permute-start | bytes 196616 | tf_op jit(solution)/shard_map/ppermute | solution.py:177
  8.6 4.3 %collective-permute-start.2 = (bf16[1,2,64,256]{3,2,1,0:T(8,128)(2,1)S(1)}, bf16[1,2,64,256]{3,2,1,0:T(8,128)(2,1)S(1)}, u32[]{:S(2)}, u32[]{:S(2)}) collective-permute-start(bf16[1,2,64,256]{3,2,1,0:T(8,128)(2,1)S(1)} %pad_maximum_fusion), channel_id=1, source_target_pairs={{0,8},{4,12},{8,0},{12,4},{16,24},{20,28},{24,16},{28,20},{1,9},{5... | collective-permute-start | bytes 196616 | tf_op jit(solution)/shard_map/ppermute | solution.py:177
  9.2 4.3 %collective-permute-start.5 = (bf16[2,2,16,512]{3,2,1,0:T(8,128)(2,1)S(1)}, bf16[2,2,16,512]{3,2,1,0:T(8,128)(2,1)S(1)}, u32[]{:S(2)}, u32[]{:S(2)}) collective-permute-start(bf16[2,2,16,512]{3,2,1,0:T(8,128)(2,1)S(1)} %pad_maximum_fusion.1), channel_id=1, source_target_pairs={{0,1},{1,0},{2,3},{3,2},{4,5},{5,4},{6,7},{7,6},{8,9},{9,8},{10,11... | collective-permute-start | bytes 196616 | tf_op jit(solution)/shard_map/ppermute | solution.py:187
  12.9 0.7 %copy-start.1 = (s32[8,2,4]{0,2,1:T(4,128)S(1)}, s32[8,2,4]{0,2,1:T(4,128)}, u32[]{:S(2)}) copy-start(s32[8,2,4]{0,2,1:T(4,128)} %param.9) | copy-start | bytes 772
  12.9 1.6 %collective-permute-start.4 = (bf16[4,2,64,256]{3,2,1,0:T(8,128)(2,1)S(1)}, bf16[4,2,64,256]{3,2,1,0:T(8,128)(2,1)S(1)}, u32[]{:S(2)}, u32[]{:S(2)}) collective-permute-start(bf16[4,2,64,256]{3,2,1,0:T(8,128)(2,1)S(1)} %constant_dynamic-update-slice_fusion.near), channel_id=1, source_target_pairs={{0,4},{4,0},{8,12},{12,8},{16,20},{20,16},{24,28},{28,24},{1,5},{5... | collective-permute-start | bytes 786440 | tf_op jit(solution)/shard_map/ppermute | solution.py:189

commit v8 on v6

--- a/solution.py
+++ b/solution.py
@@ -13,18 +13,17 @@
 LANES = 128
 
 
-def gather_queries(own, across, beside, half):
-    my_head = lax.axis_index("head")
-    width = beside.shape[-1]
-    parts = []
-    for lane in range(0, width, HEAD_DIM):
-        mine = pl.multiple_of(my_head * width + lane, HEAD_DIM)
-        low = pl.multiple_of((my_head & 1) * width + lane, HEAD_DIM)
-        parts.append(own[0, half, :, pl.ds(mine, HEAD_DIM)])
-        parts.append(beside[0, half, :, lane : lane + HEAD_DIM])
-        parts.append(across[0, half, :, pl.ds(low, HEAD_DIM)])
-        parts.append(beside[1, half, :, lane : lane + HEAD_DIM])
-    return jnp.concatenate(parts, axis=0)
+def gather_queries(q_all, half):
+    senders, rows, width = q_all.shape
+    sub_tok = rows // 2
+    return jnp.concatenate(
+        [
+            q_all[d, half * sub_tok : (half + 1) * sub_tok, lane : lane + HEAD_DIM]
+            for lane in range(0, width, HEAD_DIM)
+            for d in range(senders)
+        ],
+        axis=0,
+    )
 
 
 def owners_of(my_blk, far):
@@ -34,11 +33,9 @@
     return [my_blk, my_blk ^ 1, my_blk ^ side, my_blk ^ 1 ^ side, my_blk ^ 6]
 
 
-def key_bias(my_blk, lengths, blk_count, block_tok, sub_tok, half, far):
+def key_bias(my_blk, lengths, blk_count, block_tok, half, far):
     my_block = my_blk if half == 0 else 2 * blk_count - 1 - my_blk
-    lane = lax.broadcasted_iota(jnp.int32, (1, LANES), 1)
-    sender = lax.axis_index("head") ^ (lane % block_tok // sub_tok)
-    q_pos = my_block * block_tok + sender * sub_tok + lane % sub_tok
+    q_pos = my_block * block_tok + lax.broadcasted_iota(jnp.int32, (1, LANES), 1) % block_tok
     first = jnp.zeros_like(q_pos)
     bound = jnp.zeros_like(lengths[:, :1])
     for k in range(lengths.shape[1] - 1):
@@ -116,17 +113,16 @@
 
 
 def near_kernel(
-    lengths, page_slot, own, across, beside, chip, away, q_rows, top_ref, total_ref, out_ref, pages_ref, far_bias_a,
-    far_bias_b, far_targets,
+    lengths, page_slot, q_all, chip, away, q_rows, top_ref, total_ref, out_ref, pages_ref, far_bias_a, far_bias_b,
+    far_targets,
 ):
     blk_count = page_slot.shape[2]
     block_tok = chip.shape[2]
     slot_count = pages_ref.shape[0] // PAGE
     my_blk = lax.axis_index("blk")
-    lengths = lengths[...] - lax.axis_index("head")
-    bias = functools.partial(key_bias, my_blk, lengths, blk_count, block_tok, own.shape[2])
+    bias = functools.partial(key_bias, my_blk, lengths[...], blk_count, block_tok)
     for half in (1, 0):
-        queries = gather_queries(own, across, beside, half)
+        queries = gather_queries(q_all, half)
         q_rows[half] = queries
         top, total, out = attend_part(queries, bias(half, False), (chip, away), half)
         top_ref[half] = top
@@ -144,8 +140,6 @@
 ):
     block_tok = far.shape[2]
     slot_count = kv_cache.shape[0]
-    my_head = lax.axis_index("head")
-    sub_tok = block_tok // lax.axis_size("head")
     moved = place_pages(far_targets[...], (far,), slot_count) + pages_ref[...].astype(jnp.float32)
     pages[...] = moved.astype(jnp.bfloat16).reshape(pages.shape)
     writes = [pltpu.make_async_copy(pages, kv_cache, sems.at[2])]
@@ -159,10 +153,7 @@
         inverse = 1.0 / (total * here + total_ref[half] * there)
         out = (out * (here * inverse) + out_ref[half] * (there * inverse)).T.astype(jnp.bfloat16)
         for g in range(out.shape[0] // block_tok):
-            for d in range(block_tok // sub_tok):
-                row = pl.multiple_of((my_head ^ d) * sub_tok, sub_tok)
-                start = g * block_tok + d * sub_tok
-                result[half, pl.ds(row, sub_tok), g * HEAD_DIM : (g + 1) * HEAD_DIM] = out[start : start + sub_tok]
+            result[half, :, g * HEAD_DIM : (g + 1) * HEAD_DIM] = out[g * block_tok : (g + 1) * block_tok]
         writes.append(pltpu.make_async_copy(result.at[half], attended.at[0, half], sems.at[half]))
         writes[-1].start()
     for write in writes:
@@ -179,24 +170,21 @@
     slot_count = 4 * (block_tok // PAGE)
 
     my_head = lax.axis_index("head")
-    part = lax.dynamic_slice_in_dim(query_states, ((my_head & 2) ^ 2) * width, 2 * width, axis=3)
-    across = lax.ppermute(part, "head", [(i, i ^ 2) for i in range(head_count)])
     pair = jnp.concatenate([key_states, value_states], axis=3)
-    lengths = doc_lengths + my_head
-    pair, lengths, _ = lax.optimization_barrier((pair, lengths, part))
     mate = lax.ppermute(pair, "blk", [(i, i ^ 1) for i in range(blk_count)])
     across_chip = lax.ppermute(pair, "blk", [(i, i ^ 6) for i in range(blk_count)])
     chip = jnp.concatenate([pair, mate], axis=0)
     next_chip = lax.ppermute(chip, "blk", [(i, i ^ (2 << (i & 1))) for i in range(blk_count)])
-    beside = jnp.concatenate(
-        [
-            lax.dynamic_slice_in_dim(query_states, (my_head ^ 1) * width, width, axis=3),
-            lax.dynamic_slice_in_dim(across, ((my_head & 1) ^ 1) * width, width, axis=3),
-        ],
-        axis=0,
-    )
-    across_chip, next_chip, _ = lax.optimization_barrier((across_chip, next_chip, beside))
-    beside = lax.ppermute(beside, "head", [(i, i ^ 1) for i in range(head_count)])
+    query_states, chip = lax.optimization_barrier((query_states, chip))
+    q_flat = query_states.reshape(-1, query_states.shape[3])
+    q_split = jnp.stack([q_flat[:, h * width : (h + 1) * width] for h in range(head_count)])
+    q_all = lax.cond(
+        my_head < head_count,
+        lambda q: lax.all_to_all(q, "head", split_axis=0, concat_axis=0, tiled=True),
+        lambda q: q,
+        q_split,
+    )
+    across_chip, next_chip, q_all = lax.optimization_barrier((across_chip, next_chip, q_all))
     away = jnp.concatenate([next_chip, across_chip], axis=0)
     far = lax.ppermute(away, "blk", [(i, i ^ 1) for i in range(blk_count)])
 
@@ -217,11 +205,11 @@
             jax.ShapeDtypeStruct((2 * far_cols, LANES), jnp.float32),
             jax.ShapeDtypeStruct((1, 2 * far_cols), jnp.int32),
         ),
-        in_specs=[vmem] * 7,
+        in_specs=[vmem] * 5,
         out_specs=(vmem,) * 8,
         compiler_params=params,
         cost_estimate=cost,
-    )(lengths.reshape(1, -1), page_slot.transpose(1, 2, 0), query_states, across, beside, chip, away)
+    )(doc_lengths.reshape(1, -1), page_slot.transpose(1, 2, 0), q_all, chip, away)
     return pl.pallas_call(
         far_kernel,
         out_shape=(

time: 16.7 us -> 20.9 us (1.25)
  blocking collectives: 0 us -> 10.9 us
  starting transfers between devices: 8.58 us -> 4.71 us
  waiting for transfers between devices: 3.28 us -> 0.01 us
  local copies, waits for them, and re-layouts: 1.36 us -> 1.76 us
    all_to_all x0 -> x1, blocking collectives: none -> 10.9 us  [per_device(): lax.all_to_all(q, 'head', split_axis=0, concat_axis=0, tiled=True)]
    ppermute x2 -> x0, starting transfers between devices: 5.33 us -> none  [the longest x1 4.04 us: per_device(): across = lax.ppermute(part, 'head', [(i, i ^ 2) for i in range(head_count)])]
    ppermute x1, waiting for transfers between devices: 2.19 us -> 0.01 us  [per_device(): lax.ppermute(chip, 'blk', [(i, i ^ 2 << (i & 1)) for i in range(blk_count)])]
    unnamed x12 -> x10, local copies, waits for them, and re-layouts: 0.47 us -> 1.72 us
    ppermute x1, starting transfers between devices: 2.51 us -> 3.52 us  [per_device(): lax.ppermute(pair, 'blk', [(i, i ^ 6) for i in range(blk_count)])]
    dynamic_slice x3 -> x0, local copies, waits for them, and re-layouts: 0.88 us -> none  [the longest x1 0.86 us: per_device(): lax.dynamic_slice_in_dim(query_states, (my_head & 2 ^ 2) * width, 2 * wid...]
    ppermute x1, waiting for transfers between devices: 0.58 us -> 0.01 us  [per_device(): lax.ppermute(pair, 'blk', [(i, i ^ 6) for i in range(blk_count)])]
    ppermute x2 -> x0, waiting for transfers between devices: 0.51 us -> none  [the longest x1 0.36 us: per_device(): across = lax.ppermute(part, 'head', [(i, i ^ 2) for i in range(head_count)])]
  transfers between devices with their start and end apart: 6 -> 4, of which waited for: 4 -> 0; matrix products, arithmetic and copies ran while one was open for 0% -> 0% of each run, Pallas kernels for 7% -> 6%
where the time goes in v8:
time: 20.9 us; the launch traced here: 20.6 us
  blocking collectives  10.9 us (52%)
  starting transfers between devices  4.71 us (23%)
  Pallas kernels  2.47 us (12%)
  local copies, waits for them, and re-layouts  1.76 us (8%)
  between operations  0.72 us (3%)
    all_to_all x1, blocking collectives, per_device(): lax.all_to_all(q, 'head', split_axis=0, concat_axis=0, tiled=True)  10.9 us
    ppermute x1, starting transfers between devices, per_device(): lax.ppermute(pair, 'blk', [(i, i ^ 6) for i in range(blk_count)])  3.52 us
    unnamed x10, local copies, waits for them, and re-layouts  1.72 us
    pallas_call x1, Pallas kernels, per_device(): pl.pallas_call(far_kernel, out_shape=(jax.ShapeDtypeStruct((1, 2, block_t...  1.31 us
    pallas_call x1, Pallas kernels, per_device(): pl.pallas_call(near_kernel, out_shape=(jax.ShapeDtypeStruct((2, rows, HEA...  1.16 us
    ppermute x1, starting transfers between devices, per_device(): lax.ppermute(chip, 'blk', [(i, i ^ 2 << (i & 1)) for i in range(blk_count)])  0.6 us
    ppermute x1, starting transfers between devices, per_device(): mate = lax.ppermute(pair, 'blk', [(i, i ^ 1) for i in range(blk_count)])  0.52 us
  transfers between devices with their start and end apart: 4, of which 0 were waited for; matrix products, arithmetic and copies ran while one was open for 0% of the time, Pallas kernels for 6%

profile of v8, /device:TPU:0, one launch (start us, length us, event | category | flops | bytes accessed | tf_op | source)
XLA Modules:
  0.0 20.6 jit_solution(279975014745610227)
XLA Ops:
  0.6 0.0 copy-start.3
  0.6 0.8 %constant_dynamic-update-slice_fusion.1 = bf16[1,2,64,256]{3,2,1,0:T(8,128)(2,1)S(1)} fusion(bf16[1,2,64,128]{3,2,1,0:T(8,128)(2,1)} %param.8), kind=kLoop, calls=%fused_computation.7 | loop fusion | bytes 65536
  1.4 0.0 copy-done.3
  1.4 0.5 %collective-permute-start.1 = (bf16[1,2,64,256]{3,2,1,0:T(8,128)(2,1)S(1)}, bf16[1,2,64,256]{3,2,1,0:T(8,128)(2,1)S(1)}, u32[]{:S(2)}, u32[]{:S(2)}) collective-permute-start(bf16[1,2,64,256]{3,2,1,0:T(8,128)(2,1)S(1)} %constant_dynamic-update-slice_fusion), channel_id=1, source_target_pairs={{0,4},{4,0},{8,12},{12,8},{16,20},{20,16},{24,28},{28,24},{1,5},{5... | collective-permute-start | bytes 196616 | tf_op jit(solution)/shard_map/ppermute | solution.py:174
  2.0 3.5 %collective-permute-start = (bf16[1,2,64,256]{3,2,1,0:T(8,128)(2,1)S(1)}, bf16[1,2,64,256]{3,2,1,0:T(8,128)(2,1)S(1)}, u32[]{:S(2)}, u32[]{:S(2)}) collective-permute-start(bf16[1,2,64,256]{3,2,1,0:T(8,128)(2,1)S(1)} %constant_dynamic-update-slice_fusion), channel_id=1, source_target_pairs={{0,24},{4,28},{8,16},{12,20},{16,8},{20,12},{24,0},{28,4},{1,25},{... | collective-permute-start | bytes 196616 | tf_op jit(solution)/shard_map/ppermute | solution.py:175
  5.5 0.0 copy-start.2
  5.5 0.0 collective-permute-done.1
  5.5 0.6 %collective-permute-start.2 = (bf16[2,2,64,256]{3,2,1,0:T(8,128)(2,1)S(1)}, bf16[2,2,64,256]{3,2,1,0:T(8,128)(2,1)S(1)}, u32[]{:S(2)}, u32[]{:S(2)}) collective-permute-start(bf16[2,2,64,256]{3,2,1,0:T(8,128)(2,1)S(1)} %pad_maximum_fusion.chip), channel_id=1, source_target_pairs={{0,8},{4,20},{8,0},{12,28},{16,24},{20,4},{24,16},{28,12},{1,9},{5... | collective-permute-start | bytes 393224 | tf_op jit(solution)/shard_map/ppermute | solution.py:177
  6.1 0.3 %copy-done.2 = bf16[1,2,16,2048]{3,2,1,0:T(8,128)(2,1)S(1)} copy-done((bf16[1,2,16,2048]{3,2,1,0:T(8,128)(2,1)S(1)}, bf16[1,2,16,2048]{3,2,1,0:T(8,128)(2,1)}, u32[]{:S(2)}) %copy-start.2) | copy-done | bytes 131096
  6.4 10.9 %conditional.1 = (bf16[4,32,512]{2,1,0:T(8,128)(2,1)S(1)}) conditional(s32[]{:T(128)} %convert_element_type.3, bf16[4,32,512]{2,1,0:T(8,128)(2,1)S(1)} %pad_maximum_fusion.1, bf16[4,32,512]{2,1,0:T(8,128)(2,1)S(1)} %pad_maximum_fusion.1), branch_computations={%region_0.0_spmd, %region_1.0_spmd} | conditional | bytes 524296 | solution.py:181
  6.4 10.9 %all_to_all.4 = bf16[4,32,512]{2,1,0:T(8,128)(2,1)S(1)} all-to-all(bf16[4,32,512]{2,1,0:T(8,128)(2,1)S(1)} %copy.11), channel_id=1, replica_groups=mesh['blk'=8,'head'=4] {'head'}, dimensions={0} | all-to-all | bytes 262144 | tf_op jit(solution)/shard_map/cond/branch_1_fun/all_to_all | solution.py:183
  17.4 0.0 collective-permute-done
  17.4 0.0 collective-permute-done.2
  17.4 0.0 copy-start
  17.4 0.1 collective-permute-start.3
  17.5 0.0 copy-start.1
  17.5 0.6 %copy-done = s32[8,2,4]{0,2,1:T(4,128)S(1)} copy-done((s32[8,2,4]{0,2,1:T(4,128)S(1)}, s32[8,2,4]{0,2,1:T(4,128)}, u32[]{:S(2)}) %copy-start) | copy-done | bytes 280
  18.1 0.1 copy-done.1
  18.1 1.2 %shard_map.68 = (bf16[2,256,128]{2,1,0:T(8,128)(2,1)S(1)}, f32[2,1,256]{2,1,0:T(1,128)S(1)}, f32[2,1,256]{2,1,0:T(1,128)S(1)}, f32[2,128,256]{2,1,0:T(8,128)S(1)...) custom-call(s32[1,3]{1,0:T(1,128)S(1)} %bitcast.12, ...), custom_call_target="tpu_custom_call" | custom-call | flops 4000000000 | bytes 1000000 | tf_op jit(solution)/shard_map/pallas_call | solution.py:196
  19.3 0.0 collective-permute-done.3.far
  19.3 1.3 %shard_map.69 = (bf16[1,2,64,512]{3,2,1,0:T(8,128)(2,1)}, bf16[16,1,16,256]{3,2,1,0:T(8,128)(2,1)}) custom-call(bf16[3,2,64,256]{3,2,1,0:T(8,128)(2,1)S(1)} %collective-permute-done.3.far, bf16[2,256,128]{2,1,0:T(8,128)(2,1)S(1)} %get-tuple-element.25.q_rows, f32[2,1,256]{2,1,0:T(1,128)S(1)} %get-tuple-element.26.top_ref, ...), custom_call_target="tpu_custom_call" | custom-call | flops 4000000000 | bytes 1000000 | tf_op jit(solution)/shard_map/pallas_call | solution.py:213
  (7 shorter events, 0.1 us)
Async XLA Ops:
  0.6 0.8 %copy-start.3 = (bf16[1,2,64,128]{3,2,1,0:T(8,128)(2,1)S(1)}, bf16[1,2,64,128]{3,2,1,0:T(8,128)(2,1)}, u32[]{:S(2)}) copy-start(bf16[1,2,64,128]{3,2,1,0:T(8,128)(2,1)} %param.9) | copy-start | bytes 98308
  1.4 4.0 %collective-permute-start.1 = (bf16[1,2,64,256]{3,2,1,0:T(8,128)(2,1)S(1)}, bf16[1,2,64,256]{3,2,1,0:T(8,128)(2,1)S(1)}, u32[]{:S(2)}, u32[]{:S(2)}) collective-permute-start(bf16[1,2,64,256]{3,2,1,0:T(8,128)(2,1)S(1)} %constant_dynamic-update-slice_fusion), channel_id=1, source_target_pairs={{0,4},{4,0},{8,12},{12,8},{16,20},{20,16},{24,28},{28,24},{1,5},{5... | collective-permute-start | bytes 196616 | tf_op jit(solution)/shard_map/ppermute | solution.py:174
  2.0 15.4 %collective-permute-start = (bf16[1,2,64,256]{3,2,1,0:T(8,128)(2,1)S(1)}, bf16[1,2,64,256]{3,2,1,0:T(8,128)(2,1)S(1)}, u32[]{:S(2)}, u32[]{:S(2)}) collective-permute-start(bf16[1,2,64,256]{3,2,1,0:T(8,128)(2,1)S(1)} %constant_dynamic-update-slice_fusion), channel_id=1, source_target_pairs={{0,24},{4,28},{8,16},{12,20},{16,8},{20,12},{24,0},{28,4},{1,25},{... | collective-permute-start | bytes 196616 | tf_op jit(solution)/shard_map/ppermute | solution.py:175
  5.5 0.9 %copy-start.2 = (bf16[1,2,16,2048]{3,2,1,0:T(8,128)(2,1)S(1)}, bf16[1,2,16,2048]{3,2,1,0:T(8,128)(2,1)}, u32[]{:S(2)}) copy-start(bf16[1,2,16,2048]{3,2,1,0:T(8,128)(2,1)} %param.7) | copy-start | bytes 393220
  5.5 11.9 %collective-permute-start.2 = (bf16[2,2,64,256]{3,2,1,0:T(8,128)(2,1)S(1)}, bf16[2,2,64,256]{3,2,1,0:T(8,128)(2,1)S(1)}, u32[]{:S(2)}, u32[]{:S(2)}) collective-permute-start(bf16[2,2,64,256]{3,2,1,0:T(8,128)(2,1)S(1)} %pad_maximum_fusion.chip), channel_id=1, source_target_pairs={{0,8},{4,20},{8,0},{12,28},{16,24},{20,4},{24,16},{28,12},{1,9},{5... | collective-permute-start | bytes 393224 | tf_op jit(solution)/shard_map/ppermute | solution.py:177
  17.4 0.7 %copy-start = (s32[8,2,4]{0,2,1:T(4,128)S(1)}, s32[8,2,4]{0,2,1:T(4,128)}, u32[]{:S(2)}) copy-start(s32[8,2,4]{0,2,1:T(4,128)} %param.11) | copy-start | bytes 772
  17.4 1.9 %collective-permute-start.3 = (bf16[3,2,64,256]{3,2,1,0:T(8,128)(2,1)S(1)}, bf16[3,2,64,256]{3,2,1,0:T(8,128)(2,1)S(1)}, u32[]{:S(2)}, u32[]{:S(2)}) collective-permute-start(bf16[3,2,64,256]{3,2,1,0:T(8,128)(2,1)S(1)} %constant_dynamic-update-slice_fusion.2.away), channel_id=1, source_target_pairs={{0,4},{4,0},{8,12},{12,8},{16,20},{20,16},{24,28},{28,24},{1,5},{5... | collective-permute-start | bytes 589832 | tf_op jit(solution)/shard_map/ppermute | solution.py:189
  17.5 0.7 %copy-start.1 = (s32[3]{0:T(128)S(1)}, s32[3]{0:T(128)}, u32[]{:S(2)}) copy-start(s32[3]{0:T(128)} %param.10) | copy-start | bytes 40

commit v9 on v7

--- a/solution.py
+++ b/solution.py
@@ -100,6 +100,12 @@
     return lax.dot_general(values, weights, (((0,), (0,)), ((), ())), preferred_element_type=jnp.float32)
 
 
+def part_kernel(queries, part):
+    width = part.shape[3]
+    start = pl.multiple_of(((lax.axis_index("head") & 2) ^ 2) * (width // 2), width)
+    part[...] = queries[:, :, :, pl.ds(start, width)]
+
+
 def near_kernel(
     lengths, page_slot, own, across, beside, near, q_rows, top_ref, total_ref, out_ref, pages_ref, far_bias_a,
     far_bias_b, far_targets,
@@ -168,7 +174,15 @@
     slot_count = 4 * (block_tok // PAGE)
 
     my_head = lax.axis_index("head")
-    part = lax.dynamic_slice_in_dim(query_states, ((my_head & 2) ^ 2) * width, 2 * width, axis=3)
+    vmem = pl.BlockSpec(memory_space=pltpu.VMEM)
+    part = pl.pallas_call(
+        part_kernel,
+        out_shape=jax.ShapeDtypeStruct((*query_states.shape[:3], 2 * width), query_states.dtype),
+        in_specs=[vmem],
+        out_specs=vmem,
+        compiler_params=pltpu.CompilerParams(vmem_limit_bytes=4 * 1024 * 1024),
+        cost_estimate=pl.CostEstimate(flops=0, bytes_accessed=200_000, transcendentals=0),
+    )(query_states)
     across = lax.ppermute(part, "head", [(i, i ^ 2) for i in range(head_count)])
     pair = jnp.concatenate([key_states, value_states], axis=3)
     lengths = doc_lengths + my_head
@@ -189,7 +203,6 @@
     far = lax.ppermute(near, "blk", [(i, i ^ 1) for i in range(blk_count)])
 
     hbm = pl.BlockSpec(memory_space=pl.ANY)
-    vmem = pl.BlockSpec(memory_space=pltpu.VMEM)
     params = pltpu.CompilerParams(vmem_limit_bytes=32 * 1024 * 1024)
     cost = pl.CostEstimate(flops=4_000_000_000, bytes_accessed=1_000_000, transcendentals=200_000)
     half_cols = blk_count // 2 * block_tok

time: 16.1 us -> 16.9 us (1.050)
  local copies, waits for them, and re-layouts: 0.95 us -> 1.64 us
    unnamed x13 -> x15, local copies, waits for them, and re-layouts: 0.07 us -> 1.61 us
    dynamic_slice x1 -> x0, local copies, waits for them, and re-layouts: 0.86 us -> none  [per_device(): lax.dynamic_slice_in_dim(query_states, (my_head & 2 ^ 2) * width, 2 * wid...]
where the time goes in v9:
time: 16.9 us; the launch traced here: 16.7 us
  starting transfers between devices  9.37 us (55%)
  waiting for transfers between devices  2.57 us (15%)
  Pallas kernels  2.31 us (14%)
  local copies, waits for them, and re-layouts  1.64 us (10%)
  between operations  0.74 us (4%)
    ppermute x1, starting transfers between devices, per_device(): across = lax.ppermute(part, 'head', [(i, i ^ 2) for i in range(head_count)])  4.1 us
    ppermute x3, starting transfers between devices, per_device(): lax.ppermute(pair, 'blk', [(i, i ^ d) for i in range(blk_count)])  3.55 us
    ppermute x3, waiting for transfers between devices, per_device(): lax.ppermute(pair, 'blk', [(i, i ^ d) for i in range(blk_count)])  2.01 us
    ppermute x1, starting transfers between devices, per_device(): lax.ppermute(beside, 'head', [(i, i ^ 1) for i in range(head_count)])  1.64 us
    unnamed x15, local copies, waits for them, and re-layouts  1.61 us
    pallas_call x1, Pallas kernels, per_device(): pl.pallas_call(far_kernel, out_shape=(jax.ShapeDtypeStruct((1, 2, block_t...  1.37 us
    pallas_call x1, Pallas kernels, per_device(): pl.pallas_call(near_kernel, out_shape=(jax.ShapeDtypeStruct((2, rows, HEA...  0.93 us
    ppermute x1, waiting for transfers between devices, per_device(): lax.ppermute(beside, 'head', [(i, i ^ 1) for i in range(head_count)])  0.56 us
  transfers between devices with their start and end apart: 6, of which 4 were waited for; matrix products, arithmetic and copies ran while one was open for 0% of the time, Pallas kernels for 6%

profile of v9, /device:TPU:0, one launch (start us, length us, event | category | flops | bytes accessed | tf_op | source)
XLA Modules:
  0.0 16.7 jit_solution(17192711841218451383)
XLA Ops:
  0.6 0.0 copy-start
  0.6 0.9 %copy-done = bf16[1,2,16,2048]{3,2,1,0:T(8,128)(2,1)S(1)} copy-done((bf16[1,2,16,2048]{3,2,1,0:T(8,128)(2,1)S(1)}, bf16[1,2,16,2048]{3,2,1,0:T(8,128)(2,1)}, u32[]{:S(2)}) %copy-start) | copy-done | bytes 131096
  1.5 0.0 copy-start.3
  1.5 0.0 copy-start.4
  1.6 4.1 %collective-permute-start.3 = (bf16[1,2,16,1024]{3,2,1,0:T(8,128)(2,1)S(1)}, bf16[1,2,16,1024]{3,2,1,0:T(8,128)(2,1)S(1)}, u32[]{:S(2)}, u32[]{:S(2)}) collective-permute-start(bf16[1,2,16,1024]{3,2,1,0:T(8,128)(2,1)S(1)} %shard_map.68), channel_id=1, source_target_pairs={{0,2},{1,3},{2,0},{3,1},{4,6},{5,7},{6,4},{7,5},{8,10},{9,11},{10,... | collective-permute-start | bytes 196616 | tf_op jit(solution)/shard_map/ppermute | solution.py:186
  5.7 0.0 copy-start.5
  5.7 0.7 %copy-done.5 = s32[3]{0:T(128)S(1)} copy-done((s32[3]{0:T(128)S(1)}, s32[3]{0:T(128)}, u32[]{:S(2)}) %copy-start.5) | copy-done | bytes 36
  6.3 0.0 copy-done.3
  6.3 0.0 copy-done.4
  6.3 0.0 copy-start.1
  6.3 2.5 %collective-permute-start = (bf16[1,2,64,256]{3,2,1,0:T(8,128)(2,1)S(1)}, bf16[1,2,64,256]{3,2,1,0:T(8,128)(2,1)S(1)}, u32[]{:S(2)}, u32[]{:S(2)}) collective-permute-start(bf16[1,2,64,256]{3,2,1,0:T(8,128)(2,1)S(1)} %pad_maximum_fusion), channel_id=1, source_target_pairs={{0,24},{4,28},{8,16},{12,20},{16,8},{20,12},{24,0},{28,4},{1,25},{... | collective-permute-start | bytes 196616 | tf_op jit(solution)/shard_map/ppermute | solution.py:191
  8.9 0.5 %collective-permute-start.1 = (bf16[1,2,64,256]{3,2,1,0:T(8,128)(2,1)S(1)}, bf16[1,2,64,256]{3,2,1,0:T(8,128)(2,1)S(1)}, u32[]{:S(2)}, u32[]{:S(2)}) collective-permute-start(bf16[1,2,64,256]{3,2,1,0:T(8,128)(2,1)S(1)} %pad_maximum_fusion), channel_id=1, source_target_pairs={{0,16},{4,20},{8,24},{12,28},{16,0},{20,4},{24,8},{28,12},{1,17},{... | collective-permute-start | bytes 196616 | tf_op jit(solution)/shard_map/ppermute | solution.py:191
  9.4 0.5 %collective-permute-start.2 = (bf16[1,2,64,256]{3,2,1,0:T(8,128)(2,1)S(1)}, bf16[1,2,64,256]{3,2,1,0:T(8,128)(2,1)S(1)}, u32[]{:S(2)}, u32[]{:S(2)}) collective-permute-start(bf16[1,2,64,256]{3,2,1,0:T(8,128)(2,1)S(1)} %pad_maximum_fusion), channel_id=1, source_target_pairs={{0,8},{4,12},{8,0},{12,4},{16,24},{20,28},{24,16},{28,20},{1,9},{5... | collective-permute-start | bytes 196616 | tf_op jit(solution)/shard_map/ppermute | solution.py:191
  9.9 0.0 copy-done.1
  9.9 0.0 collective-permute-done.3.across
  10.0 1.6 %collective-permute-start.5 = (bf16[2,2,16,512]{3,2,1,0:T(8,128)(2,1)S(1)}, bf16[2,2,16,512]{3,2,1,0:T(8,128)(2,1)S(1)}, u32[]{:S(2)}, u32[]{:S(2)}) collective-permute-start(bf16[2,2,16,512]{3,2,1,0:T(8,128)(2,1)S(1)} %pad_maximum_fusion.1), channel_id=1, source_target_pairs={{0,1},{1,0},{2,3},{3,2},{4,5},{5,4},{6,7},{7,6},{8,9},{9,8},{10,11... | collective-permute-start | bytes 196616 | tf_op jit(solution)/shard_map/ppermute | solution.py:201
  11.6 0.1 collective-permute-done
  11.7 1.4 %collective-permute-done.1 = bf16[1,2,64,256]{3,2,1,0:T(8,128)(2,1)S(1)} collective-permute-done((bf16[1,2,64,256]{3,2,1,0:T(8,128)(2,1)S(1)}, bf16[1,2,64,256]{3,2,1,0:T(8,128)(2,1)S(1)}, u32[]{:S(2)}, u32[]{:S(2)}) %collective-permute-start.1) | collective-permute-done | bytes 65568 | tf_op jit(solution)/shard_map/ppermute | solution.py:191
  13.1 0.5 %collective-permute-done.2 = bf16[1,2,64,256]{3,2,1,0:T(8,128)(2,1)S(1)} collective-permute-done((bf16[1,2,64,256]{3,2,1,0:T(8,128)(2,1)S(1)}, bf16[1,2,64,256]{3,2,1,0:T(8,128)(2,1)S(1)}, u32[]{:S(2)}, u32[]{:S(2)}) %collective-permute-start.2) | collective-permute-done | bytes 65568 | tf_op jit(solution)/shard_map/ppermute | solution.py:191
  13.6 0.0 copy-start.2
  13.7 0.1 collective-permute-start.4
  13.7 0.6 %collective-permute-done.5.beside = bf16[2,2,16,512]{3,2,1,0:T(8,128)(2,1)S(1)} collective-permute-done((bf16[2,2,16,512]{3,2,1,0:T(8,128)(2,1)S(1)}, bf16[2,2,16,512]{3,2,1,0:T(8,128)(2,1)S(1)}, u32[]{:S(2)}, u32[]{:S(2)}) %collective-permute-start.5) | collective-permute-done | bytes 65568 | tf_op jit(solution)/shard_map/ppermute | solution.py:201
  14.3 0.0 copy-done.2
  14.3 0.9 %shard_map.69 = (bf16[2,256,128]{2,1,0:T(8,128)(2,1)S(1)}, f32[2,1,256]{2,1,0:T(1,128)S(1)}, f32[2,1,256]{2,1,0:T(1,128)S(1)}, f32[2,128,256]{2,1,0:T(8,128)S(1)...) custom-call(s32[1,3]{1,0:T(1,128)S(1)} %bitcast.3, ...), custom_call_target="tpu_custom_call" | custom-call | flops 4000000000 | bytes 1000000 | tf_op jit(solution)/shard_map/pallas_call | solution.py:209
  15.3 0.0 collective-permute-done.4.far
  15.3 1.4 %shard_map.70 = (bf16[1,2,64,512]{3,2,1,0:T(8,128)(2,1)}, bf16[16,1,16,256]{3,2,1,0:T(8,128)(2,1)}) custom-call(bf16[4,2,64,256]{3,2,1,0:T(8,128)(2,1)S(1)} %collective-permute-done.4.far, bf16[2,256,128]{2,1,0:T(8,128)(2,1)S(1)} %get-tuple-element.20.q_rows, f32[2,1,256]{2,1,0:T(1,128)S(1)} %get-tuple-element.21.top_ref, ...), custom_call_target="tpu_custom_call" | custom-call | flops 4000000000 | bytes 1000000 | tf_op jit(solution)/shard_map/pallas_call | solution.py:226
  (10 shorter events, 0.1 us)
Async XLA Ops:
  0.6 0.9 %copy-start = (bf16[1,2,16,2048]{3,2,1,0:T(8,128)(2,1)S(1)}, bf16[1,2,16,2048]{3,2,1,0:T(8,128)(2,1)}, u32[]{:S(2)}) copy-start(bf16[1,2,16,2048]{3,2,1,0:T(8,128)(2,1)} %own.1) | copy-start | bytes 393220
  1.5 4.8 %copy-start.3 = (bf16[1,2,64,128]{3,2,1,0:T(8,128)(2,1)S(1)}, bf16[1,2,64,128]{3,2,1,0:T(8,128)(2,1)}, u32[]{:S(2)}) copy-start(bf16[1,2,64,128]{3,2,1,0:T(8,128)(2,1)} %param.7) | copy-start | bytes 98308
  1.5 4.8 %copy-start.4 = (bf16[1,2,64,128]{3,2,1,0:T(8,128)(2,1)S(1)}, bf16[1,2,64,128]{3,2,1,0:T(8,128)(2,1)}, u32[]{:S(2)}) copy-start(bf16[1,2,64,128]{3,2,1,0:T(8,128)(2,1)} %param.6) | copy-start | bytes 98308
  1.6 8.4 %collective-permute-start.3 = (bf16[1,2,16,1024]{3,2,1,0:T(8,128)(2,1)S(1)}, bf16[1,2,16,1024]{3,2,1,0:T(8,128)(2,1)S(1)}, u32[]{:S(2)}, u32[]{:S(2)}) collective-permute-start(bf16[1,2,16,1024]{3,2,1,0:T(8,128)(2,1)S(1)} %shard_map.68), channel_id=1, source_target_pairs={{0,2},{1,3},{2,0},{3,1},{4,6},{5,7},{6,4},{7,5},{8,10},{9,11},{10,... | collective-permute-start | bytes 196616 | tf_op jit(solution)/shard_map/ppermute | solution.py:186
  5.7 0.7 %copy-start.5 = (s32[3]{0:T(128)S(1)}, s32[3]{0:T(128)}, u32[]{:S(2)}) copy-start(s32[3]{0:T(128)} %param.8) | copy-start | bytes 40
  6.3 3.6 %copy-start.1 = (bf16[1,2,16,2048]{3,2,1,0:T(8,128)(2,1)S(1)}, bf16[1,2,16,2048]{3,2,1,0:T(8,128)(2,1)}, u32[]{:S(2)}) copy-start(bf16[1,2,16,2048]{3,2,1,0:T(8,128)(2,1)} %own.1) | copy-start | bytes 393220
  6.3 5.3 %collective-permute-start = (bf16[1,2,64,256]{3,2,1,0:T(8,128)(2,1)S(1)}, bf16[1,2,64,256]{3,2,1,0:T(8,128)(2,1)S(1)}, u32[]{:S(2)}, u32[]{:S(2)}) collective-permute-start(bf16[1,2,64,256]{3,2,1,0:T(8,128)(2,1)S(1)} %pad_maximum_fusion), channel_id=1, source_target_pairs={{0,24},{4,28},{8,16},{12,20},{16,8},{20,12},{24,0},{28,4},{1,25},{... | collective-permute-start | bytes 196616 | tf_op jit(solution)/shard_map/ppermute | solution.py:191
  8.9 4.3 %collective-permute-start.1 = (bf16[1,2,64,256]{3,2,1,0:T(8,128)(2,1)S(1)}, bf16[1,2,64,256]{3,2,1,0:T(8,128)(2,1)S(1)}, u32[]{:S(2)}, u32[]{:S(2)}) collective-permute-start(bf16[1,2,64,256]{3,2,1,0:T(8,128)(2,1)S(1)} %pad_maximum_fusion), channel_id=1, source_target_pairs={{0,16},{4,20},{8,24},{12,28},{16,0},{20,4},{24,8},{28,12},{1,17},{... | collective-permute-start | bytes 196616 | tf_op jit(solution)/shard_map/ppermute | solution.py:191
  9.4 4.3 %collective-permute-start.2 = (bf16[1,2,64,256]{3,2,1,0:T(8,128)(2,1)S(1)}, bf16[1,2,64,256]{3,2,1,0:T(8,128)(2,1)S(1)}, u32[]{:S(2)}, u32[]{:S(2)}) collective-permute-start(bf16[1,2,64,256]{3,2,1,0:T(8,128)(2,1)S(1)} %pad_maximum_fusion), channel_id=1, source_target_pairs={{0,8},{4,12},{8,0},{12,4},{16,24},{20,28},{24,16},{28,20},{1,9},{5... | collective-permute-start | bytes 196616 | tf_op jit(solution)/shard_map/ppermute | solution.py:191
  10.0 4.3 %collective-permute-start.5 = (bf16[2,2,16,512]{3,2,1,0:T(8,128)(2,1)S(1)}, bf16[2,2,16,512]{3,2,1,0:T(8,128)(2,1)S(1)}, u32[]{:S(2)}, u32[]{:S(2)}) collective-permute-start(bf16[2,2,16,512]{3,2,1,0:T(8,128)(2,1)S(1)} %pad_maximum_fusion.1), channel_id=1, source_target_pairs={{0,1},{1,0},{2,3},{3,2},{4,5},{5,4},{6,7},{7,6},{8,9},{9,8},{10,11... | collective-permute-start | bytes 196616 | tf_op jit(solution)/shard_map/ppermute | solution.py:201
  13.6 0.7 %copy-start.2 = (s32[8,2,4]{0,2,1:T(4,128)S(1)}, s32[8,2,4]{0,2,1:T(4,128)}, u32[]{:S(2)}) copy-start(s32[8,2,4]{0,2,1:T(4,128)} %param.9) | copy-start | bytes 772
  13.7 1.6 %collective-permute-start.4 = (bf16[4,2,64,256]{3,2,1,0:T(8,128)(2,1)S(1)}, bf16[4,2,64,256]{3,2,1,0:T(8,128)(2,1)S(1)}, u32[]{:S(2)}, u32[]{:S(2)}) collective-permute-start(bf16[4,2,64,256]{3,2,1,0:T(8,128)(2,1)S(1)} %constant_dynamic-update-slice_fusion.near), channel_id=1, source_target_pairs={{0,4},{4,0},{8,12},{12,8},{16,20},{20,16},{24,28},{28,24},{1,5},{5... | collective-permute-start | bytes 786440 | tf_op jit(solution)/shard_map/ppermute | solution.py:203

commit v10 on v7

--- a/solution.py
+++ b/solution.py
@@ -52,38 +52,21 @@
     return jnp.concatenate(parts, axis=0)
 
 
-def page_targets(my_blk, page_slot, chips, slot_count, core):
-    _, pages_blk, blk_count = page_slot.shape
-    chip = lax.broadcasted_iota(jnp.int32, (chips, blk_count), 0)
-    owner = (my_blk ^ core) ^ (2 * chip)
-    chosen = (owner == lax.broadcasted_iota(jnp.int32, (chips, blk_count), 1)).astype(jnp.float32).astype(jnp.bfloat16)
-    cols = 2 * pages_blk * PAGE
-    page = lax.broadcasted_iota(jnp.int32, (pages_blk, cols), 0)
-    col = lax.broadcasted_iota(jnp.int32, (pages_blk, cols), 1)
-    slots = 0.0
-    for half in range(2):
-        held = lax.dot_general(
-            chosen,
-            page_slot[half].astype(jnp.float32).astype(jnp.bfloat16),
-            (((1,), (1,)), ((), ())),
-            preferred_element_type=jnp.float32,
-        )
-        spread = (col // PAGE == page + half * pages_blk).astype(jnp.float32).astype(jnp.bfloat16)
-        slots = slots + jnp.dot(held.astype(jnp.bfloat16), spread, preferred_element_type=jnp.float32)
-    slots = slots.astype(jnp.int32) - my_blk * slot_count
-    rows = slots * PAGE + lax.broadcasted_iota(jnp.int32, slots.shape, 1) % PAGE
-    return jnp.concatenate([rows[m : m + 1] for m in range(chips)], axis=1)
-
-
-def place_pages(targets, pairs, slot_count):
-    rows = pairs[...].reshape(-1, pairs.shape[-1])
-    row = lax.broadcasted_iota(jnp.int32, (slot_count * PAGE, rows.shape[0]), 0)
-    chosen = jnp.where(row == targets, 1.0, 0.0).astype(jnp.bfloat16)
-    return jnp.dot(chosen, rows, preferred_element_type=jnp.float32)
-
-
-def score_part(queries, pairs, half):
-    keys = pairs[:, : half + 1].reshape(-1, 2 * HEAD_DIM)[:, :HEAD_DIM]
+def move_pages(my_blk, page_slot, keys, values, slot_count, core, pages):
+    chips, halves, block_tok, _ = keys.shape
+    for m in range(chips):
+        owner = (my_blk ^ core) ^ (2 * m)
+        for half in range(halves):
+            for n in range(block_tok // PAGE):
+                slot = page_slot[half, n, owner] - my_blk * slot_count
+                slot = jnp.where((slot >= 0) & (slot < slot_count), slot, slot_count)
+                rows = pl.ds(pl.multiple_of(slot * PAGE, PAGE), PAGE)
+                pages[rows, :HEAD_DIM] = keys[m, half, n * PAGE : (n + 1) * PAGE, :]
+                pages[rows, HEAD_DIM:] = values[m, half, n * PAGE : (n + 1) * PAGE, :]
+
+
+def score_part(queries, keys, half):
+    keys = keys[:, : half + 1].reshape(-1, HEAD_DIM)
     return lax.dot_general(keys, queries, (((1,), (1,)), ((), ())), preferred_element_type=jnp.float32)
 
 
@@ -95,51 +78,57 @@
     return top, jnp.sum(weights, axis=0, keepdims=True), weights.astype(jnp.bfloat16)
 
 
-def weigh_part(weights, pairs, half):
-    values = pairs[:, : half + 1].reshape(-1, 2 * HEAD_DIM)[:, HEAD_DIM:]
+def weigh_part(weights, values, half):
+    values = values[:, : half + 1].reshape(-1, HEAD_DIM)
     return lax.dot_general(values, weights, (((0,), (0,)), ((), ())), preferred_element_type=jnp.float32)
 
 
 def near_kernel(
-    lengths, page_slot, own, across, beside, near, q_rows, top_ref, total_ref, out_ref, pages_ref, far_bias_a,
-    far_bias_b, far_targets,
+    lengths, page_slot, own, across, beside, near_k, near_v, q_rows, top_ref, total_ref, out_ref, pages_ref, far_bias_a,
+    far_bias_b, slots, sem,
 ):
-    chips, _, block_tok, _ = near.shape
-    slot_count = pages_ref.shape[0] // PAGE
+    chips, _, block_tok, _ = near_k.shape
+    slot_count = pages_ref.shape[0] // PAGE - 1
+    fetch = pltpu.make_async_copy(page_slot, slots, sem)
+    fetch.start()
     my_blk = lax.axis_index("blk")
     bias = functools.partial(key_bias, my_blk, lengths[...] - lax.axis_index("head"), chips, block_tok, own.shape[2])
-    targets = functools.partial(page_targets, my_blk, page_slot, chips, slot_count)
     scores = {}
     for half in (1, 0):
         queries = gather_queries(own, across, beside, half)
         q_rows[half] = queries
-        scores[half] = score_part(queries, near, half)
+        scores[half] = score_part(queries, near_k, half)
     for half in (1, 0):
         top_ref[half], total_ref[half], weights = soften(scores[half], bias(half, 0))
-        out_ref[half] = weigh_part(weights, near, half)
-    pages_ref[...] = place_pages(targets(0), near, slot_count).astype(jnp.bfloat16)
+        out_ref[half] = weigh_part(weights, near_v, half)
     for half in (1, 0):
         (far_bias_a, far_bias_b)[half][...] = bias(half, 1)
-    far_targets[...] = targets(1)
+    pages_ref[...] = jnp.zeros_like(pages_ref)
+    fetch.wait()
+    move_pages(my_blk, slots, near_k, near_v, slot_count, 0, pages_ref)
 
 
 def far_kernel(
-    far, q_rows, top_ref, total_ref, out_ref, pages_ref, bias_a, bias_b, far_targets, attended, kv_cache,
-    pages, result, sems,
+    page_slot, far_k, far_v, q_rows, top_ref, total_ref, out_ref, pages_ref, bias_a, bias_b, attended, kv_cache,
+    pages, result, slots, sems,
 ):
-    block_tok = far.shape[2]
-    slot_count = kv_cache.shape[0]
+    block_tok = far_k.shape[2]
+    slot_count = kv_cache.shape[0] // PAGE
     my_head = lax.axis_index("head")
     sub_tok = block_tok // lax.axis_size("head")
-    scores = {half: score_part(q_rows[half], far, half) for half in (1, 0)}
-    moved = place_pages(far_targets[...], far, slot_count) + pages_ref[...].astype(jnp.float32)
-    pages[...] = moved.astype(jnp.bfloat16).reshape(pages.shape)
-    writes = [pltpu.make_async_copy(pages, kv_cache, sems.at[2])]
+    my_blk = lax.axis_index("blk")
+    fetch = pltpu.make_async_copy(page_slot, slots, sems.at[3])
+    fetch.start()
+    scores = {half: score_part(q_rows[half], far_k, half) for half in (1, 0)}
+    parts = {}
+    for half in (1, 0):
+        top, total, weights = soften(scores[half], (bias_a, bias_b)[half][...])
+        parts[half] = (top, total, weigh_part(weights, far_v, half))
+    pages[...] = pages_ref[...]
+    fetch.wait()
+    move_pages(my_blk, slots, far_k, far_v, slot_count, 1, pages)
+    writes = [pltpu.make_async_copy(pages.at[: slot_count * PAGE], kv_cache, sems.at[2])]
     writes[0].start()
-    parts = {}
-    for half in (1, 0):
-        top, total, weights = soften(scores[half], (bias_a, bias_b)[half][...])
-        parts[half] = (top, total, weigh_part(weights, far, half))
     for half in (1, 0):
         top, total, out = parts[half]
         best = jnp.maximum(top, top_ref[half])
@@ -185,14 +174,17 @@
     )
     near = lax.optimization_barrier((near[::-1], beside))[0][::-1]
     beside = lax.ppermute(beside, "head", [(i, i ^ 1) for i in range(head_count)])
-    near = jnp.concatenate([pair] + near, axis=0)
-    far = lax.ppermute(near, "blk", [(i, i ^ 1) for i in range(blk_count)])
+    near = [pair] + near
+    near_k = jnp.concatenate([p[..., :HEAD_DIM] for p in near], axis=0)
+    near_v = jnp.concatenate([p[..., HEAD_DIM:] for p in near], axis=0)
+    far_k, far_v = (lax.ppermute(x, "blk", [(i, i ^ 1) for i in range(blk_count)]) for x in (near_k, near_v))
 
     hbm = pl.BlockSpec(memory_space=pl.ANY)
     vmem = pl.BlockSpec(memory_space=pltpu.VMEM)
     params = pltpu.CompilerParams(vmem_limit_bytes=32 * 1024 * 1024)
     cost = pl.CostEstimate(flops=4_000_000_000, bytes_accessed=1_000_000, transcendentals=200_000)
     half_cols = blk_count // 2 * block_tok
+    slots = page_slot.transpose(1, 2, 0)
     stats = pl.pallas_call(
         near_kernel,
         out_shape=(
@@ -200,32 +192,34 @@
             jax.ShapeDtypeStruct((2, 1, rows), jnp.float32),
             jax.ShapeDtypeStruct((2, 1, rows), jnp.float32),
             jax.ShapeDtypeStruct((2, HEAD_DIM, rows), jnp.float32),
-            jax.ShapeDtypeStruct((slot_count * PAGE, 2 * HEAD_DIM), jnp.bfloat16),
+            jax.ShapeDtypeStruct(((slot_count + 1) * PAGE, 2 * HEAD_DIM), jnp.bfloat16),
             jax.ShapeDtypeStruct((half_cols, LANES), jnp.float32),
             jax.ShapeDtypeStruct((2 * half_cols, LANES), jnp.float32),
-            jax.ShapeDtypeStruct((1, 2 * half_cols), jnp.int32),
-        ),
-        in_specs=[vmem] * 6,
-        out_specs=(vmem,) * 8,
+        ),
+        in_specs=[vmem, hbm] + [vmem] * 5,
+        out_specs=(vmem,) * 7,
+        scratch_shapes=[pltpu.SMEM(slots.shape, jnp.int32), pltpu.SemaphoreType.DMA],
         compiler_params=params,
         cost_estimate=cost,
-    )(lengths.reshape(1, -1), page_slot.transpose(1, 2, 0), query_states, across, beside, near)
-    return pl.pallas_call(
+    )(lengths.reshape(1, -1), slots, query_states, across, beside, near_k, near_v)
+    attended, kv_cache = pl.pallas_call(
         far_kernel,
         out_shape=(
             jax.ShapeDtypeStruct((1, 2, block_tok, width), jnp.bfloat16),
-            jax.ShapeDtypeStruct((slot_count, 1, PAGE, 2 * HEAD_DIM), jnp.bfloat16),
-        ),
-        in_specs=[vmem] * 9,
+            jax.ShapeDtypeStruct((slot_count * PAGE, 2 * HEAD_DIM), jnp.bfloat16),
+        ),
+        in_specs=[hbm] + [vmem] * 9,
         out_specs=(hbm, hbm),
         scratch_shapes=[
-            pltpu.VMEM((slot_count, 1, PAGE, 2 * HEAD_DIM), jnp.bfloat16),
+            pltpu.VMEM(((slot_count + 1) * PAGE, 2 * HEAD_DIM), jnp.bfloat16),
             pltpu.VMEM((2, block_tok, width), jnp.bfloat16),
-            pltpu.SemaphoreType.DMA((3,)),
+            pltpu.SMEM(slots.shape, jnp.int32),
+            pltpu.SemaphoreType.DMA((4,)),
         ],
         compiler_params=params,
         cost_estimate=cost,
-    )(far, *stats)
+    )(slots, far_k, far_v, *stats)
+    return attended, kv_cache.reshape(slot_count, 1, PAGE, 2 * HEAD_DIM)
 
 
 def per_device_long(query_states, key_states, value_states, doc_lengths, page_slot):

time: 16.1 us -> 16.5 us (1.025)
  waiting for transfers between devices: 2.59 us -> 1.99 us
  starting transfers between devices: 9.3 us -> 9.85 us
  Pallas kernels: 2.31 us -> 2.51 us
    ppermute x1, waiting for transfers between devices: 0.56 us -> 0.01 us  [per_device(): lax.ppermute(beside, 'head', [(i, i ^ 1) for i in range(head_count)])]
    ppermute x1 -> x2, starting transfers between devices: 0.07 us -> 0.62 us  [per_device(): lax.ppermute(x, 'blk', [(i, i ^ 1) for i in range(blk_count)])]
  transfers between devices with their start and end apart: 6 -> 7, of which waited for: 4 -> 2; matrix products, arithmetic and copies ran while one was open for 0% -> 1% of each run, Pallas kernels for 6% -> 6%
where the time goes in v10:
time: 16.5 us; the launch traced here: 16.3 us
  starting transfers between devices  9.85 us (60%)
  Pallas kernels  2.51 us (15%)
  waiting for transfers between devices  1.99 us (12%)
  local copies, waits for them, and re-layouts  1.06 us (6%)
  between operations  0.81 us (5%)
    ppermute x1, starting transfers between devices, per_device(): across = lax.ppermute(part, 'head', [(i, i ^ 2) for i in range(head_count)])  4.04 us
    ppermute x3, starting transfers between devices, per_device(): lax.ppermute(pair, 'blk', [(i, i ^ d) for i in range(blk_count)])  3.55 us
    ppermute x3, waiting for transfers between devices, per_device(): lax.ppermute(pair, 'blk', [(i, i ^ d) for i in range(blk_count)])  1.98 us
    ppermute x1, starting transfers between devices, per_device(): lax.ppermute(beside, 'head', [(i, i ^ 1) for i in range(head_count)])  1.64 us
    pallas_call x1, Pallas kernels, per_device(): pl.pallas_call(far_kernel, out_shape=(jax.ShapeDtypeStruct((1, 2, block_t...  1.47 us
    pallas_call x1, Pallas kernels, per_device(): pl.pallas_call(near_kernel, out_shape=(jax.ShapeDtypeStruct((2, rows, HEA...  1.03 us
    dynamic_slice x1, local copies, waits for them, and re-layouts, per_device(): lax.dynamic_slice_in_dim(query_states, (my_head & 2 ^ 2) * width, 2 * wid...  0.86 us
    ppermute x2, starting transfers between devices, per_device(): lax.ppermute(x, 'blk', [(i, i ^ 1) for i in range(blk_count)])  0.62 us
  transfers between devices with their start and end apart: 7, of which 2 were waited for; matrix products, arithmetic and copies ran while one was open for 1% of the time, Pallas kernels for 6%

profile of v10, /device:TPU:0, one launch (start us, length us, event | category | flops | bytes accessed | tf_op | source)
XLA Modules:
  0.0 16.3 jit_solution(5596248926986414944)
XLA Ops:
  0.6 0.0 copy-start.4
  0.7 0.0 copy-start.2
  0.7 0.0 copy-start.3
  0.7 0.9 %constant_dynamic-slice_fusion.2 = bf16[1,2,16,1024]{3,2,1,0:T(8,128)(2,1)S(1)} fusion(bf16[1,2,16,2048]{3,2,1,0:T(8,128)(2,1)} %own.1, s32[]{:T(128)S(6)} %select_n.9), kind=kLoop, calls=%fused_computation.6 | loop fusion | bytes 131076 | tf_op jit(solution)/shard_map/dynamic_slice | solution.py:160
  1.5 4.0 %collective-permute-start.3 = (bf16[1,2,16,1024]{3,2,1,0:T(8,128)(2,1)S(1)}, bf16[1,2,16,1024]{3,2,1,0:T(8,128)(2,1)S(1)}, u32[]{:S(2)}, u32[]{:S(2)}) collective-permute-start(bf16[1,2,16,1024]{3,2,1,0:T(8,128)(2,1)S(1)} %constant_dynamic-slice_fusion.2), channel_id=1, source_target_pairs={{0,2},{1,3},{2,0},{3,1},{4,6},{5,7},{6,4},{7,5},{8,10},{9,11},{10,... | collective-permute-start | bytes 196616 | tf_op jit(solution)/shard_map/ppermute | solution.py:161
  5.6 0.0 copy-done.4
  5.6 0.0 copy-done.2
  5.6 0.0 copy-done.3
  5.6 0.0 copy-start
  5.6 2.5 %collective-permute-start = (bf16[1,2,64,256]{3,2,1,0:T(8,128)(2,1)S(1)}, bf16[1,2,64,256]{3,2,1,0:T(8,128)(2,1)S(1)}, u32[]{:S(2)}, u32[]{:S(2)}) collective-permute-start(bf16[1,2,64,256]{3,2,1,0:T(8,128)(2,1)S(1)} %pad_maximum_fusion.2), channel_id=1, source_target_pairs={{0,24},{4,28},{8,16},{12,20},{16,8},{20,12},{24,0},{28,4},{1,25},{... | collective-permute-start | bytes 196616 | tf_op jit(solution)/shard_map/ppermute | solution.py:166
  8.1 0.5 %collective-permute-start.1 = (bf16[1,2,64,256]{3,2,1,0:T(8,128)(2,1)S(1)}, bf16[1,2,64,256]{3,2,1,0:T(8,128)(2,1)S(1)}, u32[]{:S(2)}, u32[]{:S(2)}) collective-permute-start(bf16[1,2,64,256]{3,2,1,0:T(8,128)(2,1)S(1)} %pad_maximum_fusion.2), channel_id=1, source_target_pairs={{0,16},{4,20},{8,24},{12,28},{16,0},{20,4},{24,8},{28,12},{1,17},{... | collective-permute-start | bytes 196616 | tf_op jit(solution)/shard_map/ppermute | solution.py:166
  8.6 0.5 %collective-permute-start.2 = (bf16[1,2,64,256]{3,2,1,0:T(8,128)(2,1)S(1)}, bf16[1,2,64,256]{3,2,1,0:T(8,128)(2,1)S(1)}, u32[]{:S(2)}, u32[]{:S(2)}) collective-permute-start(bf16[1,2,64,256]{3,2,1,0:T(8,128)(2,1)S(1)} %pad_maximum_fusion.2), channel_id=1, source_target_pairs={{0,8},{4,12},{8,0},{12,4},{16,24},{20,28},{24,16},{28,20},{1,9},{5... | collective-permute-start | bytes 196616 | tf_op jit(solution)/shard_map/ppermute | solution.py:166
  9.2 0.0 copy-done
  9.2 0.0 collective-permute-done.3.across
  9.3 1.6 %collective-permute-start.6 = (bf16[2,2,16,512]{3,2,1,0:T(8,128)(2,1)S(1)}, bf16[2,2,16,512]{3,2,1,0:T(8,128)(2,1)S(1)}, u32[]{:S(2)}, u32[]{:S(2)}) collective-permute-start(bf16[2,2,16,512]{3,2,1,0:T(8,128)(2,1)S(1)} %pad_maximum_fusion.3), channel_id=1, source_target_pairs={{0,1},{1,0},{2,3},{3,2},{4,5},{5,4},{6,7},{7,6},{8,9},{9,8},{10,11... | collective-permute-start | bytes 196616 | tf_op jit(solution)/shard_map/ppermute | solution.py:176
  10.9 0.0 collective-permute-done
  10.9 1.4 %collective-permute-done.1 = bf16[1,2,64,256]{3,2,1,0:T(8,128)(2,1)S(1)} collective-permute-done((bf16[1,2,64,256]{3,2,1,0:T(8,128)(2,1)S(1)}, bf16[1,2,64,256]{3,2,1,0:T(8,128)(2,1)S(1)}, u32[]{:S(2)}, u32[]{:S(2)}) %collective-permute-start.1) | collective-permute-done | bytes 65568 | tf_op jit(solution)/shard_map/ppermute | solution.py:166
  12.4 0.5 %collective-permute-done.2 = bf16[1,2,64,256]{3,2,1,0:T(8,128)(2,1)S(1)} collective-permute-done((bf16[1,2,64,256]{3,2,1,0:T(8,128)(2,1)S(1)}, bf16[1,2,64,256]{3,2,1,0:T(8,128)(2,1)S(1)}, u32[]{:S(2)}, u32[]{:S(2)}) %collective-permute-start.2) | collective-permute-done | bytes 65568 | tf_op jit(solution)/shard_map/ppermute | solution.py:166
  13.0 0.1 collective-permute-start.5
  13.1 0.0 copy-start.1
  13.1 0.5 %collective-permute-start.4 = (bf16[4,2,64,128]{3,2,1,0:T(8,128)(2,1)S(1)}, bf16[4,2,64,128]{3,2,1,0:T(8,128)(2,1)S(1)}, u32[]{:S(2)}, u32[]{:S(2)}) collective-permute-start(bf16[4,2,64,128]{3,2,1,0:T(8,128)(2,1)S(1)} %pad_maximum_fusion.near_k), channel_id=1, source_target_pairs={{0,4},{4,0},{8,12},{12,8},{16,20},{20,16},{24,28},{28,24},{1,5},{5... | collective-permute-start | bytes 393224 | tf_op jit(solution)/shard_map/ppermute | solution.py:180
  13.6 0.0 collective-permute-done.6.beside
  13.6 0.1 copy-done.1
  13.7 1.0 %shard_map.68 = (bf16[2,256,128]{2,1,0:T(8,128)(2,1)S(1)}, f32[2,1,256]{2,1,0:T(1,128)S(1)}, f32[2,1,256]{2,1,0:T(1,128)S(1)}, f32[2,128,256]{2,1,0:T(8,128)S(1)...) custom-call(s32[1,3]{1,0:T(1,128)S(1)} %bitcast.7, s32[2,4,8]{2,1,0:T(4,128)S(1)} %bitcast.5, ...), custom_call_target="tpu_custom_call" | custom-call | flops 4000000000 | bytes 1000000 | tf_op jit(solution)/shard_map/pallas_call | solution.py:188
  14.8 0.0 collective-permute-done.5.far_v
  14.8 0.0 collective-permute-done.4.far_k
  14.8 1.5 %shard_map.69 = (bf16[1,2,64,512]{3,2,1,0:T(8,128)(2,1)}, bf16[256,256]{1,0:T(8,128)(2,1)}) custom-call(s32[2,4,8]{2,1,0:T(4,128)S(1)} %bitcast.6, bf16[4,2,64,128]{3,2,1,0:T(8,128)(2,1)S(1)} %collective-permute-done.4.far_k, bf16[4,2,64,128]{3,2,1,0:T(8,128)(2,1)S(1)} %collective-permute-done.5.far_v, bf16[2,256,128]{2,1,0:T(8,128)(2,1)S(1)} %get-tuple-element.21.q_rows, ...), custom_call_target="tpu_custom_call" | custom-call | flops 4000000000 | bytes 1000000 | tf_op jit(solution)/shard_map/pallas_call | solution.py:205
  (10 shorter events, 0.1 us)
Async XLA Ops:
  0.6 4.9 %copy-start.4 = (s32[3]{0:T(128)S(1)}, s32[3]{0:T(128)}, u32[]{:S(2)}) copy-start(s32[3]{0:T(128)} %param.8) | copy-start | bytes 40
  0.7 4.9 %copy-start.2 = (bf16[1,2,64,128]{3,2,1,0:T(8,128)(2,1)S(1)}, bf16[1,2,64,128]{3,2,1,0:T(8,128)(2,1)}, u32[]{:S(2)}) copy-start(bf16[1,2,64,128]{3,2,1,0:T(8,128)(2,1)} %param.7) | copy-start | bytes 98308
  0.7 4.9 %copy-start.3 = (bf16[1,2,64,128]{3,2,1,0:T(8,128)(2,1)S(1)}, bf16[1,2,64,128]{3,2,1,0:T(8,128)(2,1)}, u32[]{:S(2)}) copy-start(bf16[1,2,64,128]{3,2,1,0:T(8,128)(2,1)} %param.6) | copy-start | bytes 98308
  1.5 7.7 %collective-permute-start.3 = (bf16[1,2,16,1024]{3,2,1,0:T(8,128)(2,1)S(1)}, bf16[1,2,16,1024]{3,2,1,0:T(8,128)(2,1)S(1)}, u32[]{:S(2)}, u32[]{:S(2)}) collective-permute-start(bf16[1,2,16,1024]{3,2,1,0:T(8,128)(2,1)S(1)} %constant_dynamic-slice_fusion.2), channel_id=1, source_target_pairs={{0,2},{1,3},{2,0},{3,1},{4,6},{5,7},{6,4},{7,5},{8,10},{9,11},{10,... | collective-permute-start | bytes 196616 | tf_op jit(solution)/shard_map/ppermute | solution.py:161
  5.6 3.6 %copy-start = (bf16[1,2,16,2048]{3,2,1,0:T(8,128)(2,1)S(1)}, bf16[1,2,16,2048]{3,2,1,0:T(8,128)(2,1)}, u32[]{:S(2)}) copy-start(bf16[1,2,16,2048]{3,2,1,0:T(8,128)(2,1)} %own.1) | copy-start | bytes 393220
  5.6 5.3 %collective-permute-start = (bf16[1,2,64,256]{3,2,1,0:T(8,128)(2,1)S(1)}, bf16[1,2,64,256]{3,2,1,0:T(8,128)(2,1)S(1)}, u32[]{:S(2)}, u32[]{:S(2)}) collective-permute-start(bf16[1,2,64,256]{3,2,1,0:T(8,128)(2,1)S(1)} %pad_maximum_fusion.2), channel_id=1, source_target_pairs={{0,24},{4,28},{8,16},{12,20},{16,8},{20,12},{24,0},{28,4},{1,25},{... | collective-permute-start | bytes 196616 | tf_op jit(solution)/shard_map/ppermute | solution.py:166
  8.1 4.3 %collective-permute-start.1 = (bf16[1,2,64,256]{3,2,1,0:T(8,128)(2,1)S(1)}, bf16[1,2,64,256]{3,2,1,0:T(8,128)(2,1)S(1)}, u32[]{:S(2)}, u32[]{:S(2)}) collective-permute-start(bf16[1,2,64,256]{3,2,1,0:T(8,128)(2,1)S(1)} %pad_maximum_fusion.2), channel_id=1, source_target_pairs={{0,16},{4,20},{8,24},{12,28},{16,0},{20,4},{24,8},{28,12},{1,17},{... | collective-permute-start | bytes 196616 | tf_op jit(solution)/shard_map/ppermute | solution.py:166
  8.6 4.3 %collective-permute-start.2 = (bf16[1,2,64,256]{3,2,1,0:T(8,128)(2,1)S(1)}, bf16[1,2,64,256]{3,2,1,0:T(8,128)(2,1)S(1)}, u32[]{:S(2)}, u32[]{:S(2)}) collective-permute-start(bf16[1,2,64,256]{3,2,1,0:T(8,128)(2,1)S(1)} %pad_maximum_fusion.2), channel_id=1, source_target_pairs={{0,8},{4,12},{8,0},{12,4},{16,24},{20,28},{24,16},{28,20},{1,9},{5... | collective-permute-start | bytes 196616 | tf_op jit(solution)/shard_map/ppermute | solution.py:166
  9.3 4.4 %collective-permute-start.6 = (bf16[2,2,16,512]{3,2,1,0:T(8,128)(2,1)S(1)}, bf16[2,2,16,512]{3,2,1,0:T(8,128)(2,1)S(1)}, u32[]{:S(2)}, u32[]{:S(2)}) collective-permute-start(bf16[2,2,16,512]{3,2,1,0:T(8,128)(2,1)S(1)} %pad_maximum_fusion.3), channel_id=1, source_target_pairs={{0,1},{1,0},{2,3},{3,2},{4,5},{5,4},{6,7},{7,6},{8,9},{9,8},{10,11... | collective-permute-start | bytes 196616 | tf_op jit(solution)/shard_map/ppermute | solution.py:176
  13.0 1.8 %collective-permute-start.5 = (bf16[4,2,64,128]{3,2,1,0:T(8,128)(2,1)S(1)}, bf16[4,2,64,128]{3,2,1,0:T(8,128)(2,1)S(1)}, u32[]{:S(2)}, u32[]{:S(2)}) collective-permute-start(bf16[4,2,64,128]{3,2,1,0:T(8,128)(2,1)S(1)} %pad_maximum_fusion.1.near_v), channel_id=1, source_target_pairs={{0,4},{4,0},{8,12},{12,8},{16,20},{20,16},{24,28},{28,24},{1,5},{5... | collective-permute-start | bytes 393224 | tf_op jit(solution)/shard_map/ppermute | solution.py:180
  13.1 0.7 %copy-start.1 = (s32[8,2,4]{0,2,1:T(4,128)S(1)}, s32[8,2,4]{0,2,1:T(4,128)}, u32[]{:S(2)}) copy-start(s32[8,2,4]{0,2,1:T(4,128)} %param.9) | copy-start | bytes 772
  13.1 1.7 %collective-permute-start.4 = (bf16[4,2,64,128]{3,2,1,0:T(8,128)(2,1)S(1)}, bf16[4,2,64,128]{3,2,1,0:T(8,128)(2,1)S(1)}, u32[]{:S(2)}, u32[]{:S(2)}) collective-permute-start(bf16[4,2,64,128]{3,2,1,0:T(8,128)(2,1)S(1)} %pad_maximum_fusion.near_k), channel_id=1, source_target_pairs={{0,4},{4,0},{8,12},{12,8},{16,20},{20,16},{24,28},{28,24},{1,5},{5... | collective-permute-start | bytes 393224 | tf_op jit(solution)/shard_map/ppermute | solution.py:180

commit v11 on v7

--- a/solution.py
+++ b/solution.py
@@ -75,15 +75,15 @@
     return jnp.concatenate([rows[m : m + 1] for m in range(chips)], axis=1)
 
 
-def place_pages(targets, pairs, slot_count):
-    rows = pairs[...].reshape(-1, pairs.shape[-1])
+def place_pages(targets, keys, values, slot_count):
+    rows = jnp.concatenate([keys[...].reshape(-1, HEAD_DIM), values[...].reshape(-1, HEAD_DIM)], axis=1)
     row = lax.broadcasted_iota(jnp.int32, (slot_count * PAGE, rows.shape[0]), 0)
     chosen = jnp.where(row == targets, 1.0, 0.0).astype(jnp.bfloat16)
     return jnp.dot(chosen, rows, preferred_element_type=jnp.float32)
 
 
-def score_part(queries, pairs, half):
-    keys = pairs[:, : half + 1].reshape(-1, 2 * HEAD_DIM)[:, :HEAD_DIM]
+def score_part(queries, keys, half):
+    keys = keys[:, : half + 1].reshape(-1, HEAD_DIM)
     return lax.dot_general(keys, queries, (((1,), (1,)), ((), ())), preferred_element_type=jnp.float32)
 
 
@@ -95,16 +95,16 @@
     return top, jnp.sum(weights, axis=0, keepdims=True), weights.astype(jnp.bfloat16)
 
 
-def weigh_part(weights, pairs, half):
-    values = pairs[:, : half + 1].reshape(-1, 2 * HEAD_DIM)[:, HEAD_DIM:]
+def weigh_part(weights, values, half):
+    values = values[:, : half + 1].reshape(-1, HEAD_DIM)
     return lax.dot_general(values, weights, (((0,), (0,)), ((), ())), preferred_element_type=jnp.float32)
 
 
 def near_kernel(
-    lengths, page_slot, own, across, beside, near, q_rows, top_ref, total_ref, out_ref, pages_ref, far_bias_a,
+    lengths, page_slot, own, across, beside, near_k, near_v, q_rows, top_ref, total_ref, out_ref, pages_ref, far_bias_a,
     far_bias_b, far_targets,
 ):
-    chips, _, block_tok, _ = near.shape
+    chips, _, block_tok, _ = near_k.shape
     slot_count = pages_ref.shape[0] // PAGE
     my_blk = lax.axis_index("blk")
     bias = functools.partial(key_bias, my_blk, lengths[...] - lax.axis_index("head"), chips, block_tok, own.shape[2])
@@ -113,33 +113,39 @@
     for half in (1, 0):
         queries = gather_queries(own, across, beside, half)
         q_rows[half] = queries
-        scores[half] = score_part(queries, near, half)
+        scores[half] = score_part(queries, near_k, half)
     for half in (1, 0):
         top_ref[half], total_ref[half], weights = soften(scores[half], bias(half, 0))
-        out_ref[half] = weigh_part(weights, near, half)
-    pages_ref[...] = place_pages(targets(0), near, slot_count).astype(jnp.bfloat16)
+        out_ref[half] = weigh_part(weights, near_v, half)
+    pages_ref[...] = place_pages(targets(0), near_k, near_v, slot_count).astype(jnp.bfloat16)
     for half in (1, 0):
         (far_bias_a, far_bias_b)[half][...] = bias(half, 1)
     far_targets[...] = targets(1)
 
 
 def far_kernel(
-    far, q_rows, top_ref, total_ref, out_ref, pages_ref, bias_a, bias_b, far_targets, attended, kv_cache,
+    far_k, far_v, q_rows, top_ref, total_ref, out_ref, pages_ref, bias_a, bias_b, far_targets, attended, kv_cache,
     pages, result, sems,
 ):
-    block_tok = far.shape[2]
+    block_tok = far_k.shape[2]
     slot_count = kv_cache.shape[0]
     my_head = lax.axis_index("head")
     sub_tok = block_tok // lax.axis_size("head")
-    scores = {half: score_part(q_rows[half], far, half) for half in (1, 0)}
-    moved = place_pages(far_targets[...], far, slot_count) + pages_ref[...].astype(jnp.float32)
+    scores = {half: score_part(q_rows[half], far_k, half) for half in (1, 0)}
+    moved = place_pages(far_targets[...], far_k, far_v, slot_count) + pages_ref[...].astype(jnp.float32)
     pages[...] = moved.astype(jnp.bfloat16).reshape(pages.shape)
-    writes = [pltpu.make_async_copy(pages, kv_cache, sems.at[2])]
-    writes[0].start()
+    writes = []
+
+    def write(source, target):
+        writes.append(pltpu.make_async_copy(source, target, sems.at[len(writes)]))
+        writes[-1].start()
+
+    for slot in range(0, slot_count, 4):
+        write(pages.at[slot : slot + 4], kv_cache.at[slot : slot + 4])
     parts = {}
     for half in (1, 0):
         top, total, weights = soften(scores[half], (bias_a, bias_b)[half][...])
-        parts[half] = (top, total, weigh_part(weights, far, half))
+        parts[half] = (top, total, weigh_part(weights, far_v, half))
     for half in (1, 0):
         top, total, out = parts[half]
         best = jnp.maximum(top, top_ref[half])
@@ -152,10 +158,10 @@
                 row = pl.multiple_of((my_head ^ d) * sub_tok, sub_tok)
                 start = g * block_tok + d * sub_tok
                 result[half, pl.ds(row, sub_tok), g * HEAD_DIM : (g + 1) * HEAD_DIM] = out[start : start + sub_tok]
-        writes.append(pltpu.make_async_copy(result.at[half], attended.at[0, half], sems.at[half]))
-        writes[-1].start()
-    for write in writes:
-        write.wait()
+        for row in range(0, block_tok, 32):
+            write(result.at[half, row : row + 32], attended.at[0, half, row : row + 32])
+    for copy in writes:
+        copy.wait()
 
 
 def per_device(query_states, key_states, value_states, doc_lengths, page_slot):
@@ -185,8 +191,10 @@
     )
     near = lax.optimization_barrier((near[::-1], beside))[0][::-1]
     beside = lax.ppermute(beside, "head", [(i, i ^ 1) for i in range(head_count)])
-    near = jnp.concatenate([pair] + near, axis=0)
-    far = lax.ppermute(near, "blk", [(i, i ^ 1) for i in range(blk_count)])
+    near = [pair] + near
+    near_k = jnp.concatenate([p[..., :HEAD_DIM] for p in near], axis=0)
+    near_v = jnp.concatenate([p[..., HEAD_DIM:] for p in near], axis=0)
+    far_k, far_v = (lax.ppermute(x, "blk", [(i, i ^ 1) for i in range(blk_count)]) for x in (near_k, near_v))
 
     hbm = pl.BlockSpec(memory_space=pl.ANY)
     vmem = pl.BlockSpec(memory_space=pltpu.VMEM)
@@ -205,27 +213,27 @@
             jax.ShapeDtypeStruct((2 * half_cols, LANES), jnp.float32),
             jax.ShapeDtypeStruct((1, 2 * half_cols), jnp.int32),
         ),
-        in_specs=[vmem] * 6,
+        in_specs=[vmem] * 7,
         out_specs=(vmem,) * 8,
         compiler_params=params,
         cost_estimate=cost,
-    )(lengths.reshape(1, -1), page_slot.transpose(1, 2, 0), query_states, across, beside, near)
+    )(lengths.reshape(1, -1), page_slot.transpose(1, 2, 0), query_states, across, beside, near_k, near_v)
     return pl.pallas_call(
         far_kernel,
         out_shape=(
             jax.ShapeDtypeStruct((1, 2, block_tok, width), jnp.bfloat16),
             jax.ShapeDtypeStruct((slot_count, 1, PAGE, 2 * HEAD_DIM), jnp.bfloat16),
         ),
-        in_specs=[vmem] * 9,
+        in_specs=[vmem] * 10,
         out_specs=(hbm, hbm),
         scratch_shapes=[
             pltpu.VMEM((slot_count, 1, PAGE, 2 * HEAD_DIM), jnp.bfloat16),
             pltpu.VMEM((2, block_tok, width), jnp.bfloat16),
-            pltpu.SemaphoreType.DMA((3,)),
+            pltpu.SemaphoreType.DMA((slot_count // 4 + 2 * (block_tok // 32),)),
         ],
         compiler_params=params,
         cost_estimate=cost,
-    )(far, *stats)
+    )(far_k, far_v, *stats)
 
 
 def per_device_long(query_states, key_states, value_states, doc_lengths, page_slot):

time: 16.1 us -> 16.4 us (1.019)
  waiting for transfers between devices: 2.59 us -> 1.99 us
  starting transfers between devices: 9.3 us -> 9.85 us
    ppermute x1, waiting for transfers between devices: 0.56 us -> 0.01 us  [per_device(): lax.ppermute(beside, 'head', [(i, i ^ 1) for i in range(head_count)])]
    ppermute x1 -> x2, starting transfers between devices: 0.07 us -> 0.62 us  [per_device(): lax.ppermute(x, 'blk', [(i, i ^ 1) for i in range(blk_count)])]
  transfers between devices with their start and end apart: 6 -> 7, of which waited for: 4 -> 2; matrix products, arithmetic and copies ran while one was open for 0% -> 1% of each run, Pallas kernels for 6% -> 6%
where the time goes in v11:
time: 16.4 us; the launch traced here: 16.1 us
  starting transfers between devices  9.85 us (60%)
  Pallas kernels  2.35 us (14%)
  waiting for transfers between devices  1.99 us (12%)
  local copies, waits for them, and re-layouts  1.06 us (6%)
  between operations  0.81 us (5%)
    ppermute x1, starting transfers between devices, per_device(): across = lax.ppermute(part, 'head', [(i, i ^ 2) for i in range(head_count)])  4.04 us
    ppermute x3, starting transfers between devices, per_device(): lax.ppermute(pair, 'blk', [(i, i ^ d) for i in range(blk_count)])  3.55 us
    ppermute x3, waiting for transfers between devices, per_device(): lax.ppermute(pair, 'blk', [(i, i ^ d) for i in range(blk_count)])  1.98 us
    ppermute x1, starting transfers between devices, per_device(): lax.ppermute(beside, 'head', [(i, i ^ 1) for i in range(head_count)])  1.64 us
    pallas_call x1, Pallas kernels, per_device(): pl.pallas_call(far_kernel, out_shape=(jax.ShapeDtypeStruct((1, 2, block_t...  1.41 us
    pallas_call x1, Pallas kernels, per_device(): pl.pallas_call(near_kernel, out_shape=(jax.ShapeDtypeStruct((2, rows, HEA...  0.94 us
    dynamic_slice x1, local copies, waits for them, and re-layouts, per_device(): lax.dynamic_slice_in_dim(query_states, (my_head & 2 ^ 2) * width, 2 * wid...  0.86 us
    ppermute x2, starting transfers between devices, per_device(): lax.ppermute(x, 'blk', [(i, i ^ 1) for i in range(blk_count)])  0.62 us
  transfers between devices with their start and end apart: 7, of which 2 were waited for; matrix products, arithmetic and copies ran while one was open for 1% of the time, Pallas kernels for 6%

profile of v11, /device:TPU:0, one launch (start us, length us, event | category | flops | bytes accessed | tf_op | source)
XLA Modules:
  0.0 16.1 jit_solution(4176894211310808541)
XLA Ops:
  0.6 0.0 copy-start.4
  0.7 0.0 copy-start.2
  0.7 0.0 copy-start.3
  0.7 0.9 %constant_dynamic-slice_fusion.2 = bf16[1,2,16,1024]{3,2,1,0:T(8,128)(2,1)S(1)} fusion(bf16[1,2,16,2048]{3,2,1,0:T(8,128)(2,1)} %own.1, s32[]{:T(128)S(6)} %select_n.9), kind=kLoop, calls=%fused_computation.6 | loop fusion | bytes 131076 | tf_op jit(solution)/shard_map/dynamic_slice | solution.py:177
  1.5 4.0 %collective-permute-start.3 = (bf16[1,2,16,1024]{3,2,1,0:T(8,128)(2,1)S(1)}, bf16[1,2,16,1024]{3,2,1,0:T(8,128)(2,1)S(1)}, u32[]{:S(2)}, u32[]{:S(2)}) collective-permute-start(bf16[1,2,16,1024]{3,2,1,0:T(8,128)(2,1)S(1)} %constant_dynamic-slice_fusion.2), channel_id=1, source_target_pairs={{0,2},{1,3},{2,0},{3,1},{4,6},{5,7},{6,4},{7,5},{8,10},{9,11},{10,... | collective-permute-start | bytes 196616 | tf_op jit(solution)/shard_map/ppermute | solution.py:178
  5.6 0.0 copy-done.4
  5.6 0.0 copy-done.2
  5.6 0.0 copy-done.3
  5.6 0.0 copy-start
  5.6 2.5 %collective-permute-start = (bf16[1,2,64,256]{3,2,1,0:T(8,128)(2,1)S(1)}, bf16[1,2,64,256]{3,2,1,0:T(8,128)(2,1)S(1)}, u32[]{:S(2)}, u32[]{:S(2)}) collective-permute-start(bf16[1,2,64,256]{3,2,1,0:T(8,128)(2,1)S(1)} %pad_maximum_fusion.2), channel_id=1, source_target_pairs={{0,24},{4,28},{8,16},{12,20},{16,8},{20,12},{24,0},{28,4},{1,25},{... | collective-permute-start | bytes 196616 | tf_op jit(solution)/shard_map/ppermute | solution.py:183
  8.1 0.5 %collective-permute-start.1 = (bf16[1,2,64,256]{3,2,1,0:T(8,128)(2,1)S(1)}, bf16[1,2,64,256]{3,2,1,0:T(8,128)(2,1)S(1)}, u32[]{:S(2)}, u32[]{:S(2)}) collective-permute-start(bf16[1,2,64,256]{3,2,1,0:T(8,128)(2,1)S(1)} %pad_maximum_fusion.2), channel_id=1, source_target_pairs={{0,16},{4,20},{8,24},{12,28},{16,0},{20,4},{24,8},{28,12},{1,17},{... | collective-permute-start | bytes 196616 | tf_op jit(solution)/shard_map/ppermute | solution.py:183
  8.6 0.5 %collective-permute-start.2 = (bf16[1,2,64,256]{3,2,1,0:T(8,128)(2,1)S(1)}, bf16[1,2,64,256]{3,2,1,0:T(8,128)(2,1)S(1)}, u32[]{:S(2)}, u32[]{:S(2)}) collective-permute-start(bf16[1,2,64,256]{3,2,1,0:T(8,128)(2,1)S(1)} %pad_maximum_fusion.2), channel_id=1, source_target_pairs={{0,8},{4,12},{8,0},{12,4},{16,24},{20,28},{24,16},{28,20},{1,9},{5... | collective-permute-start | bytes 196616 | tf_op jit(solution)/shard_map/ppermute | solution.py:183
  9.2 0.0 copy-done
  9.2 0.0 collective-permute-done.3.across
  9.3 1.6 %collective-permute-start.6 = (bf16[2,2,16,512]{3,2,1,0:T(8,128)(2,1)S(1)}, bf16[2,2,16,512]{3,2,1,0:T(8,128)(2,1)S(1)}, u32[]{:S(2)}, u32[]{:S(2)}) collective-permute-start(bf16[2,2,16,512]{3,2,1,0:T(8,128)(2,1)S(1)} %pad_maximum_fusion.3), channel_id=1, source_target_pairs={{0,1},{1,0},{2,3},{3,2},{4,5},{5,4},{6,7},{7,6},{8,9},{9,8},{10,11... | collective-permute-start | bytes 196616 | tf_op jit(solution)/shard_map/ppermute | solution.py:193
  10.9 0.0 collective-permute-done
  10.9 1.4 %collective-permute-done.1 = bf16[1,2,64,256]{3,2,1,0:T(8,128)(2,1)S(1)} collective-permute-done((bf16[1,2,64,256]{3,2,1,0:T(8,128)(2,1)S(1)}, bf16[1,2,64,256]{3,2,1,0:T(8,128)(2,1)S(1)}, u32[]{:S(2)}, u32[]{:S(2)}) %collective-permute-start.1) | collective-permute-done | bytes 65568 | tf_op jit(solution)/shard_map/ppermute | solution.py:183
  12.4 0.5 %collective-permute-done.2 = bf16[1,2,64,256]{3,2,1,0:T(8,128)(2,1)S(1)} collective-permute-done((bf16[1,2,64,256]{3,2,1,0:T(8,128)(2,1)S(1)}, bf16[1,2,64,256]{3,2,1,0:T(8,128)(2,1)S(1)}, u32[]{:S(2)}, u32[]{:S(2)}) %collective-permute-start.2) | collective-permute-done | bytes 65568 | tf_op jit(solution)/shard_map/ppermute | solution.py:183
  13.0 0.1 collective-permute-start.5
  13.1 0.0 copy-start.1
  13.1 0.5 %collective-permute-start.4 = (bf16[4,2,64,128]{3,2,1,0:T(8,128)(2,1)S(1)}, bf16[4,2,64,128]{3,2,1,0:T(8,128)(2,1)S(1)}, u32[]{:S(2)}, u32[]{:S(2)}) collective-permute-start(bf16[4,2,64,128]{3,2,1,0:T(8,128)(2,1)S(1)} %pad_maximum_fusion.near_k), channel_id=1, source_target_pairs={{0,4},{4,0},{8,12},{12,8},{16,20},{20,16},{24,28},{28,24},{1,5},{5... | collective-permute-start | bytes 393224 | tf_op jit(solution)/shard_map/ppermute | solution.py:197
  13.6 0.0 collective-permute-done.6.beside
  13.6 0.1 copy-done.1
  13.7 0.9 %shard_map.68 = (bf16[2,256,128]{2,1,0:T(8,128)(2,1)S(1)}, f32[2,1,256]{2,1,0:T(1,128)S(1)}, f32[2,1,256]{2,1,0:T(1,128)S(1)}, f32[2,128,256]{2,1,0:T(8,128)S(1)...) custom-call(s32[1,3]{1,0:T(1,128)S(1)} %bitcast.3, ...), custom_call_target="tpu_custom_call" | custom-call | flops 4000000000 | bytes 1000000 | tf_op jit(solution)/shard_map/pallas_call | solution.py:204
  14.7 0.0 collective-permute-done.5.far_v
  14.7 0.0 collective-permute-done.4.far_k
  14.7 1.4 %shard_map.69 = (bf16[1,2,64,512]{3,2,1,0:T(8,128)(2,1)}, bf16[16,1,16,256]{3,2,1,0:T(8,128)(2,1)}) custom-call(bf16[4,2,64,128]{3,2,1,0:T(8,128)(2,1)S(1)} %collective-permute-done.4.far_k, bf16[4,2,64,128]{3,2,1,0:T(8,128)(2,1)S(1)} %collective-permute-done.5.far_v, bf16[2,256,128]{2,1,0:T(8,128)(2,1)S(1)} %get-tuple-element.20.q_rows, ...), custom_call_target="tpu_custom_call" | custom-call | flops 4000000000 | bytes 1000000 | tf_op jit(solution)/shard_map/pallas_call | solution.py:221
  (10 shorter events, 0.1 us)
Async XLA Ops:
  0.6 4.9 %copy-start.4 = (s32[3]{0:T(128)S(1)}, s32[3]{0:T(128)}, u32[]{:S(2)}) copy-start(s32[3]{0:T(128)} %param.8) | copy-start | bytes 40
  0.7 4.9 %copy-start.2 = (bf16[1,2,64,128]{3,2,1,0:T(8,128)(2,1)S(1)}, bf16[1,2,64,128]{3,2,1,0:T(8,128)(2,1)}, u32[]{:S(2)}) copy-start(bf16[1,2,64,128]{3,2,1,0:T(8,128)(2,1)} %param.7) | copy-start | bytes 98308
  0.7 4.9 %copy-start.3 = (bf16[1,2,64,128]{3,2,1,0:T(8,128)(2,1)S(1)}, bf16[1,2,64,128]{3,2,1,0:T(8,128)(2,1)}, u32[]{:S(2)}) copy-start(bf16[1,2,64,128]{3,2,1,0:T(8,128)(2,1)} %param.6) | copy-start | bytes 98308
  1.5 7.7 %collective-permute-start.3 = (bf16[1,2,16,1024]{3,2,1,0:T(8,128)(2,1)S(1)}, bf16[1,2,16,1024]{3,2,1,0:T(8,128)(2,1)S(1)}, u32[]{:S(2)}, u32[]{:S(2)}) collective-permute-start(bf16[1,2,16,1024]{3,2,1,0:T(8,128)(2,1)S(1)} %constant_dynamic-slice_fusion.2), channel_id=1, source_target_pairs={{0,2},{1,3},{2,0},{3,1},{4,6},{5,7},{6,4},{7,5},{8,10},{9,11},{10,... | collective-permute-start | bytes 196616 | tf_op jit(solution)/shard_map/ppermute | solution.py:178
  5.6 3.6 %copy-start = (bf16[1,2,16,2048]{3,2,1,0:T(8,128)(2,1)S(1)}, bf16[1,2,16,2048]{3,2,1,0:T(8,128)(2,1)}, u32[]{:S(2)}) copy-start(bf16[1,2,16,2048]{3,2,1,0:T(8,128)(2,1)} %own.1) | copy-start | bytes 393220
  5.6 5.3 %collective-permute-start = (bf16[1,2,64,256]{3,2,1,0:T(8,128)(2,1)S(1)}, bf16[1,2,64,256]{3,2,1,0:T(8,128)(2,1)S(1)}, u32[]{:S(2)}, u32[]{:S(2)}) collective-permute-start(bf16[1,2,64,256]{3,2,1,0:T(8,128)(2,1)S(1)} %pad_maximum_fusion.2), channel_id=1, source_target_pairs={{0,24},{4,28},{8,16},{12,20},{16,8},{20,12},{24,0},{28,4},{1,25},{... | collective-permute-start | bytes 196616 | tf_op jit(solution)/shard_map/ppermute | solution.py:183
  8.1 4.3 %collective-permute-start.1 = (bf16[1,2,64,256]{3,2,1,0:T(8,128)(2,1)S(1)}, bf16[1,2,64,256]{3,2,1,0:T(8,128)(2,1)S(1)}, u32[]{:S(2)}, u32[]{:S(2)}) collective-permute-start(bf16[1,2,64,256]{3,2,1,0:T(8,128)(2,1)S(1)} %pad_maximum_fusion.2), channel_id=1, source_target_pairs={{0,16},{4,20},{8,24},{12,28},{16,0},{20,4},{24,8},{28,12},{1,17},{... | collective-permute-start | bytes 196616 | tf_op jit(solution)/shard_map/ppermute | solution.py:183
  8.6 4.3 %collective-permute-start.2 = (bf16[1,2,64,256]{3,2,1,0:T(8,128)(2,1)S(1)}, bf16[1,2,64,256]{3,2,1,0:T(8,128)(2,1)S(1)}, u32[]{:S(2)}, u32[]{:S(2)}) collective-permute-start(bf16[1,2,64,256]{3,2,1,0:T(8,128)(2,1)S(1)} %pad_maximum_fusion.2), channel_id=1, source_target_pairs={{0,8},{4,12},{8,0},{12,4},{16,24},{20,28},{24,16},{28,20},{1,9},{5... | collective-permute-start | bytes 196616 | tf_op jit(solution)/shard_map/ppermute | solution.py:183
  9.3 4.4 %collective-permute-start.6 = (bf16[2,2,16,512]{3,2,1,0:T(8,128)(2,1)S(1)}, bf16[2,2,16,512]{3,2,1,0:T(8,128)(2,1)S(1)}, u32[]{:S(2)}, u32[]{:S(2)}) collective-permute-start(bf16[2,2,16,512]{3,2,1,0:T(8,128)(2,1)S(1)} %pad_maximum_fusion.3), channel_id=1, source_target_pairs={{0,1},{1,0},{2,3},{3,2},{4,5},{5,4},{6,7},{7,6},{8,9},{9,8},{10,11... | collective-permute-start | bytes 196616 | tf_op jit(solution)/shard_map/ppermute | solution.py:193
  13.0 1.7 %collective-permute-start.5 = (bf16[4,2,64,128]{3,2,1,0:T(8,128)(2,1)S(1)}, bf16[4,2,64,128]{3,2,1,0:T(8,128)(2,1)S(1)}, u32[]{:S(2)}, u32[]{:S(2)}) collective-permute-start(bf16[4,2,64,128]{3,2,1,0:T(8,128)(2,1)S(1)} %pad_maximum_fusion.1.near_v), channel_id=1, source_target_pairs={{0,4},{4,0},{8,12},{12,8},{16,20},{20,16},{24,28},{28,24},{1,5},{5... | collective-permute-start | bytes 393224 | tf_op jit(solution)/shard_map/ppermute | solution.py:197
  13.1 0.7 %copy-start.1 = (s32[8,2,4]{0,2,1:T(4,128)S(1)}, s32[8,2,4]{0,2,1:T(4,128)}, u32[]{:S(2)}) copy-start(s32[8,2,4]{0,2,1:T(4,128)} %param.9) | copy-start | bytes 772
  13.1 1.6 %collective-permute-start.4 = (bf16[4,2,64,128]{3,2,1,0:T(8,128)(2,1)S(1)}, bf16[4,2,64,128]{3,2,1,0:T(8,128)(2,1)S(1)}, u32[]{:S(2)}, u32[]{:S(2)}) collective-permute-start(bf16[4,2,64,128]{3,2,1,0:T(8,128)(2,1)S(1)} %pad_maximum_fusion.near_k), channel_id=1, source_target_pairs={{0,4},{4,0},{8,12},{12,8},{16,20},{20,16},{24,28},{28,24},{1,5},{5... | collective-permute-start | bytes 393224 | tf_op jit(solution)/shard_map/ppermute | solution.py:197

commit v12 on v11

--- a/solution.py
+++ b/solution.py
@@ -100,31 +100,50 @@
     return lax.dot_general(values, weights, (((0,), (0,)), ((), ())), preferred_element_type=jnp.float32)
 
 
-def near_kernel(
-    lengths, page_slot, own, across, beside, near_k, near_v, q_rows, top_ref, total_ref, out_ref, pages_ref, far_bias_a,
-    far_bias_b, far_targets,
+def fetch_kernel(queries, lengths, page_slot, part, lengths_out, slots_out, sems):
+    _, halves, _, width = part.shape
+    start = ((lax.axis_index("head") & 2) ^ 2) * (width // 2)
+    pairs = [(lengths, lengths_out), (page_slot, slots_out)]
+    for half in range(halves):
+        for lane in range(0, width, width // 2):
+            lanes = pl.ds(pl.multiple_of(start + lane, width // 2), width // 2)
+            pairs.append((queries.at[0, half, :, lanes], part.at[0, half, :, lane : lane + width // 2]))
+    copies = [pltpu.make_async_copy(a, b, sems.at[k]) for k, (a, b) in enumerate(pairs)]
+    for copy in copies:
+        copy.start()
+    for copy in copies:
+        copy.wait()
+
+
+def plan_kernel(
+    lengths, page_slot, near_k, near_v, bias_a, bias_b, far_bias_a, far_bias_b, far_targets, pages_ref
 ):
     chips, _, block_tok, _ = near_k.shape
     slot_count = pages_ref.shape[0] // PAGE
+    sub_tok = block_tok // lax.axis_size("head")
     my_blk = lax.axis_index("blk")
-    bias = functools.partial(key_bias, my_blk, lengths[...] - lax.axis_index("head"), chips, block_tok, own.shape[2])
     targets = functools.partial(page_targets, my_blk, page_slot, chips, slot_count)
+    pages_ref[...] = place_pages(targets(0), near_k, near_v, slot_count).astype(jnp.bfloat16)
+    far_targets[...] = targets(1)
+    bias = functools.partial(key_bias, my_blk, lengths[...], chips, block_tok, sub_tok)
+    for half in range(2):
+        (bias_a, bias_b)[half][...] = bias(half, 0)
+        (far_bias_a, far_bias_b)[half][...] = bias(half, 1)
+
+
+def near_kernel(own, across, beside, near_k, near_v, bias_a, bias_b, q_rows, top_ref, total_ref, out_ref):
     scores = {}
     for half in (1, 0):
         queries = gather_queries(own, across, beside, half)
         q_rows[half] = queries
         scores[half] = score_part(queries, near_k, half)
     for half in (1, 0):
-        top_ref[half], total_ref[half], weights = soften(scores[half], bias(half, 0))
+        top_ref[half], total_ref[half], weights = soften(scores[half], (bias_a, bias_b)[half][...])
         out_ref[half] = weigh_part(weights, near_v, half)
-    pages_ref[...] = place_pages(targets(0), near_k, near_v, slot_count).astype(jnp.bfloat16)
-    for half in (1, 0):
-        (far_bias_a, far_bias_b)[half][...] = bias(half, 1)
-    far_targets[...] = targets(1)
 
 
 def far_kernel(
-    far_k, far_v, q_rows, top_ref, total_ref, out_ref, pages_ref, bias_a, bias_b, far_targets, attended, kv_cache,
+    far_k, far_v, bias_a, bias_b, far_targets, pages_ref, q_rows, top_ref, total_ref, out_ref, attended, kv_cache,
     pages, result, sems,
 ):
     block_tok = far_k.shape[2]
@@ -134,14 +153,8 @@
     scores = {half: score_part(q_rows[half], far_k, half) for half in (1, 0)}
     moved = place_pages(far_targets[...], far_k, far_v, slot_count) + pages_ref[...].astype(jnp.float32)
     pages[...] = moved.astype(jnp.bfloat16).reshape(pages.shape)
-    writes = []
-
-    def write(source, target):
-        writes.append(pltpu.make_async_copy(source, target, sems.at[len(writes)]))
-        writes[-1].start()
-
-    for slot in range(0, slot_count, 4):
-        write(pages.at[slot : slot + 4], kv_cache.at[slot : slot + 4])
+    writes = [pltpu.make_async_copy(pages, kv_cache, sems.at[2])]
+    writes[0].start()
     parts = {}
     for half in (1, 0):
         top, total, weights = soften(scores[half], (bias_a, bias_b)[half][...])
@@ -158,10 +171,10 @@
                 row = pl.multiple_of((my_head ^ d) * sub_tok, sub_tok)
                 start = g * block_tok + d * sub_tok
                 result[half, pl.ds(row, sub_tok), g * HEAD_DIM : (g + 1) * HEAD_DIM] = out[start : start + sub_tok]
-        for row in range(0, block_tok, 32):
-            write(result.at[half, row : row + 32], attended.at[0, half, row : row + 32])
-    for copy in writes:
-        copy.wait()
+        writes.append(pltpu.make_async_copy(result.at[half], attended.at[0, half], sems.at[half]))
+        writes[-1].start()
+    for write in writes:
+        write.wait()
 
 
 def per_device(query_states, key_states, value_states, doc_lengths, page_slot):
@@ -174,11 +187,24 @@
     slot_count = 4 * (block_tok // PAGE)
 
     my_head = lax.axis_index("head")
-    part = lax.dynamic_slice_in_dim(query_states, ((my_head & 2) ^ 2) * width, 2 * width, axis=3)
+    hbm = pl.BlockSpec(memory_space=pl.ANY)
+    vmem = pl.BlockSpec(memory_space=pltpu.VMEM)
+    fetched = [query_states, doc_lengths.reshape(1, -1), page_slot.transpose(1, 2, 0)]
+    part, lengths, slots = pl.pallas_call(
+        fetch_kernel,
+        out_shape=(
+            jax.ShapeDtypeStruct((*query_states.shape[:3], 2 * width), query_states.dtype),
+            *(jax.ShapeDtypeStruct(x.shape, x.dtype) for x in fetched[1:]),
+        ),
+        in_specs=[hbm] * 3,
+        out_specs=(vmem,) * 3,
+        scratch_shapes=[pltpu.SemaphoreType.DMA((6,))],
+        compiler_params=pltpu.CompilerParams(vmem_limit_bytes=4 * 1024 * 1024),
+        cost_estimate=pl.CostEstimate(flops=0, bytes_accessed=200_000, transcendentals=0),
+    )(*(pltpu.with_memory_space_constraint(x, pltpu.HBM) for x in fetched))
     across = lax.ppermute(part, "head", [(i, i ^ 2) for i in range(head_count)])
     pair = jnp.concatenate([key_states, value_states], axis=3)
-    lengths = doc_lengths + my_head
-    pair, lengths, _ = lax.optimization_barrier((pair, lengths, part))
+    pair, _ = lax.optimization_barrier((pair, part))
     near = [
         lax.ppermute(pair, "blk", [(i, i ^ d) for i in range(blk_count)]) for d in range(2, blk_count, 2)
     ]
@@ -196,11 +222,25 @@
     near_v = jnp.concatenate([p[..., HEAD_DIM:] for p in near], axis=0)
     far_k, far_v = (lax.ppermute(x, "blk", [(i, i ^ 1) for i in range(blk_count)]) for x in (near_k, near_v))
 
-    hbm = pl.BlockSpec(memory_space=pl.ANY)
-    vmem = pl.BlockSpec(memory_space=pltpu.VMEM)
     params = pltpu.CompilerParams(vmem_limit_bytes=32 * 1024 * 1024)
     cost = pl.CostEstimate(flops=4_000_000_000, bytes_accessed=1_000_000, transcendentals=200_000)
     half_cols = blk_count // 2 * block_tok
+    *bias, far_bias_a, far_bias_b, far_targets, pages = pl.pallas_call(
+        plan_kernel,
+        out_shape=(
+            jax.ShapeDtypeStruct((half_cols, LANES), jnp.float32),
+            jax.ShapeDtypeStruct((2 * half_cols, LANES), jnp.float32),
+        )
+        * 2
+        + (
+            jax.ShapeDtypeStruct((1, 2 * half_cols), jnp.int32),
+            jax.ShapeDtypeStruct((slot_count * PAGE, 2 * HEAD_DIM), jnp.bfloat16),
+        ),
+        in_specs=[vmem] * 4,
+        out_specs=(vmem,) * 6,
+        compiler_params=params,
+        cost_estimate=cost,
+    )(lengths, slots, near_k, near_v)
     stats = pl.pallas_call(
         near_kernel,
         out_shape=(
@@ -208,16 +248,12 @@
             jax.ShapeDtypeStruct((2, 1, rows), jnp.float32),
             jax.ShapeDtypeStruct((2, 1, rows), jnp.float32),
             jax.ShapeDtypeStruct((2, HEAD_DIM, rows), jnp.float32),
-            jax.ShapeDtypeStruct((slot_count * PAGE, 2 * HEAD_DIM), jnp.bfloat16),
-            jax.ShapeDtypeStruct((half_cols, LANES), jnp.float32),
-            jax.ShapeDtypeStruct((2 * half_cols, LANES), jnp.float32),
-            jax.ShapeDtypeStruct((1, 2 * half_cols), jnp.int32),
         ),
         in_specs=[vmem] * 7,
-        out_specs=(vmem,) * 8,
+        out_specs=(vmem,) * 4,
         compiler_params=params,
         cost_estimate=cost,
-    )(lengths.reshape(1, -1), page_slot.transpose(1, 2, 0), query_states, across, beside, near_k, near_v)
+    )(query_states, across, beside, near_k, near_v, *bias)
     return pl.pallas_call(
         far_kernel,
         out_shape=(
@@ -229,11 +265,11 @@
         scratch_shapes=[
             pltpu.VMEM((slot_count, 1, PAGE, 2 * HEAD_DIM), jnp.bfloat16),
             pltpu.VMEM((2, block_tok, width), jnp.bfloat16),
-            pltpu.SemaphoreType.DMA((slot_count // 4 + 2 * (block_tok // 32),)),
+            pltpu.SemaphoreType.DMA((3,)),
         ],
         compiler_params=params,
         cost_estimate=cost,
-    )(far_k, far_v, *stats)
+    )(far_k, far_v, far_bias_a, far_bias_b, far_targets, pages, *stats)
 
 
 def per_device_long(query_states, key_states, value_states, doc_lengths, page_slot):

time: 16.4 us -> 16.5 us (level)
  Pallas kernels: 2.35 us -> 3.43 us
  local copies, waits for them, and re-layouts: 1.06 us -> 0.08 us
    pallas_call x0 -> x2, Pallas kernels: none -> 1.45 us  [the longest x1 0.86 us: per_device(): pl.pallas_call(fetch_kernel, out_shape=(jax.ShapeDtypeStruct((*query_stat...]
    dynamic_slice x1 -> x0, local copies, waits for them, and re-layouts: 0.86 us -> none  [per_device(): lax.dynamic_slice_in_dim(query_states, (my_head & 2 ^ 2) * width, 2 * wid...]
    pallas_call x1, Pallas kernels: 0.94 us -> 0.6 us  [per_device(): pl.pallas_call(near_kernel, out_shape=(jax.ShapeDtypeStruct((2, rows, HEA...]
  transfers between devices with their start and end apart: 7 -> 7, of which waited for: 2 -> 2; matrix products, arithmetic and copies ran while one was open for 1% -> 1% of each run, Pallas kernels for 6% -> 7%
where the time goes in v12:
time: 16.5 us; the launch traced here: 16.3 us
  starting transfers between devices  9.92 us (60%)
  Pallas kernels  3.43 us (21%)
  waiting for transfers between devices  2.01 us (12%)
  between operations  0.79 us (5%)
    ppermute x1, starting transfers between devices, per_device(): across = lax.ppermute(part, 'head', [(i, i ^ 2) for i in range(head_count)])  4.1 us
    ppermute x3, starting transfers between devices, per_device(): lax.ppermute(pair, 'blk', [(i, i ^ d) for i in range(blk_count)])  3.55 us
    ppermute x3, waiting for transfers between devices, per_device(): lax.ppermute(pair, 'blk', [(i, i ^ d) for i in range(blk_count)])  1.98 us
    ppermute x1, starting transfers between devices, per_device(): lax.ppermute(beside, 'head', [(i, i ^ 1) for i in range(head_count)])  1.64 us
    pallas_call x1, Pallas kernels, per_device(): pl.pallas_call(far_kernel, out_shape=(jax.ShapeDtypeStruct((1, 2, block_t...  1.37 us
    pallas_call x1, Pallas kernels, per_device(): pl.pallas_call(fetch_kernel, out_shape=(jax.ShapeDtypeStruct((*query_stat...  0.86 us
    ppermute x2, starting transfers between devices, per_device(): lax.ppermute(x, 'blk', [(i, i ^ 1) for i in range(blk_count)])  0.63 us
    pallas_call x1, Pallas kernels, per_device(): pl.pallas_call(near_kernel, out_shape=(jax.ShapeDtypeStruct((2, rows, HEA...  0.6 us
  transfers between devices with their start and end apart: 7, of which 2 were waited for; matrix products, arithmetic and copies ran while one was open for 1% of the time, Pallas kernels for 7%

profile of v12, /device:TPU:0, one launch (start us, length us, event | category | flops | bytes accessed | tf_op | source)
XLA Modules:
  0.0 16.3 jit_solution(7914649441236769667)
XLA Ops:
  0.6 0.0 copy-start.1
  0.6 0.0 copy-start.2
  0.7 0.9 %shard_map.68 = (bf16[1,2,16,1024]{3,2,1,0:T(8,128)(2,1)S(1)}, s32[1,3]{1,0:T(1,128)S(1)}, s32[2,4,8]{2,1,0:T(4,128)S(1)}) custom-call(bf16[1,2,16,2048]{3,2,1,0:T(8,128)(2,1)} %own.1, s32[1,3]{1,0:T(1,128)} %bitcast.3, s32[2,4,8]{2,1,0:T(4,128)} %bitcast.2), custom_call_target="tpu_custom_call" | custom-call | bytes 200000 | tf_op jit(solution)/shard_map/pallas_call | solution.py:193
  1.5 0.0 copy-start
  1.5 4.1 %collective-permute-start.3 = (bf16[1,2,16,1024]{3,2,1,0:T(8,128)(2,1)S(1)}, bf16[1,2,16,1024]{3,2,1,0:T(8,128)(2,1)S(1)}, u32[]{:S(2)}, u32[]{:S(2)}) collective-permute-start(bf16[1,2,16,1024]{3,2,1,0:T(8,128)(2,1)S(1)} %get-tuple-element.19), channel_id=1, source_target_pairs={{0,2},{1,3},{2,0},{3,1},{4,6},{5,7},{6,4},{7,5},{8,10},{9,11},{10,... | collective-permute-start | bytes 196616 | tf_op jit(solution)/shard_map/ppermute | solution.py:205
  5.6 0.0 copy-done.1
  5.6 0.0 copy-done.2
  5.7 2.5 %collective-permute-start = (bf16[1,2,64,256]{3,2,1,0:T(8,128)(2,1)S(1)}, bf16[1,2,64,256]{3,2,1,0:T(8,128)(2,1)S(1)}, u32[]{:S(2)}, u32[]{:S(2)}) collective-permute-start(bf16[1,2,64,256]{3,2,1,0:T(8,128)(2,1)S(1)} %pad_maximum_fusion.2), channel_id=1, source_target_pairs={{0,24},{4,28},{8,16},{12,20},{16,8},{20,12},{24,0},{28,4},{1,25},{... | collective-permute-start | bytes 196616 | tf_op jit(solution)/shard_map/ppermute | solution.py:209
  8.2 0.5 %collective-permute-start.1 = (bf16[1,2,64,256]{3,2,1,0:T(8,128)(2,1)S(1)}, bf16[1,2,64,256]{3,2,1,0:T(8,128)(2,1)S(1)}, u32[]{:S(2)}, u32[]{:S(2)}) collective-permute-start(bf16[1,2,64,256]{3,2,1,0:T(8,128)(2,1)S(1)} %pad_maximum_fusion.2), channel_id=1, source_target_pairs={{0,16},{4,20},{8,24},{12,28},{16,0},{20,4},{24,8},{28,12},{1,17},{... | collective-permute-start | bytes 196616 | tf_op jit(solution)/shard_map/ppermute | solution.py:209
  8.7 0.5 %collective-permute-start.2 = (bf16[1,2,64,256]{3,2,1,0:T(8,128)(2,1)S(1)}, bf16[1,2,64,256]{3,2,1,0:T(8,128)(2,1)S(1)}, u32[]{:S(2)}, u32[]{:S(2)}) collective-permute-start(bf16[1,2,64,256]{3,2,1,0:T(8,128)(2,1)S(1)} %pad_maximum_fusion.2), channel_id=1, source_target_pairs={{0,8},{4,12},{8,0},{12,4},{16,24},{20,28},{24,16},{28,20},{1,9},{5... | collective-permute-start | bytes 196616 | tf_op jit(solution)/shard_map/ppermute | solution.py:209
  9.2 0.0 copy-done
  9.3 0.0 collective-permute-done.3.across
  9.3 1.6 %collective-permute-start.6 = (bf16[2,2,16,512]{3,2,1,0:T(8,128)(2,1)S(1)}, bf16[2,2,16,512]{3,2,1,0:T(8,128)(2,1)S(1)}, u32[]{:S(2)}, u32[]{:S(2)}) collective-permute-start(bf16[2,2,16,512]{3,2,1,0:T(8,128)(2,1)S(1)} %pad_maximum_fusion.3), channel_id=1, source_target_pairs={{0,1},{1,0},{2,3},{3,2},{4,5},{5,4},{6,7},{7,6},{8,9},{9,8},{10,11... | collective-permute-start | bytes 196616 | tf_op jit(solution)/shard_map/ppermute | solution.py:219
  11.0 0.0 collective-permute-done
  11.0 1.4 %collective-permute-done.1 = bf16[1,2,64,256]{3,2,1,0:T(8,128)(2,1)S(1)} collective-permute-done((bf16[1,2,64,256]{3,2,1,0:T(8,128)(2,1)S(1)}, bf16[1,2,64,256]{3,2,1,0:T(8,128)(2,1)S(1)}, u32[]{:S(2)}, u32[]{:S(2)}) %collective-permute-start.1) | collective-permute-done | bytes 65568 | tf_op jit(solution)/shard_map/ppermute | solution.py:209
  12.4 0.5 %collective-permute-done.2 = bf16[1,2,64,256]{3,2,1,0:T(8,128)(2,1)S(1)} collective-permute-done((bf16[1,2,64,256]{3,2,1,0:T(8,128)(2,1)S(1)}, bf16[1,2,64,256]{3,2,1,0:T(8,128)(2,1)S(1)}, u32[]{:S(2)}, u32[]{:S(2)}) %collective-permute-start.2) | collective-permute-done | bytes 65568 | tf_op jit(solution)/shard_map/ppermute | solution.py:209
  13.0 0.1 collective-permute-start.5
  13.1 0.6 %collective-permute-start.4 = (bf16[4,2,64,128]{3,2,1,0:T(8,128)(2,1)S(1)}, bf16[4,2,64,128]{3,2,1,0:T(8,128)(2,1)S(1)}, u32[]{:S(2)}, u32[]{:S(2)}) collective-permute-start(bf16[4,2,64,128]{3,2,1,0:T(8,128)(2,1)S(1)} %pad_maximum_fusion.near_k), channel_id=1, source_target_pairs={{0,4},{4,0},{8,12},{12,8},{16,20},{20,16},{24,28},{28,24},{1,5},{5... | collective-permute-start | bytes 393224 | tf_op jit(solution)/shard_map/ppermute | solution.py:223
  13.7 0.6 %shard_map.69 = (f32[256,128]{1,0:T(8,128)S(1)}, f32[512,128]{1,0:T(8,128)S(1)}, f32[256,128]{1,0:T(8,128)S(1)}, f32[512,128]{1,0:T(8,128)S(1)}, s32[1,512]{1,0:T(1,128)S(1)}, /*index=5*/bf16[256,256]{1,0:T(8,128)(2,1)S(1)}) custom-call(s32[1,3]{1,0:T(1,128)S(1)} %get-tuple-element.24.lengths, s32[2,4,8]{2,1,0:T(4,128)S(1)} %get-tuple-element.25.page_slot, ...), custom_call_target="tpu_custom_call" | custom-call | flops 4000000000 | bytes 1000000 | tf_op jit(solution)/shard_map/pallas_call | solution.py:228
  14.3 0.0 collective-permute-done.6.beside
  14.3 0.6 %shard_map.70 = (bf16[2,256,128]{2,1,0:T(8,128)(2,1)S(1)}, f32[2,1,256]{2,1,0:T(1,128)S(1)}, f32[2,1,256]{2,1,0:T(1,128)S(1)}, f32[2,128,256]{2,1,0:T(8,128)S(1)}) custom-call(bf16[1,2,16,2048]{3,2,1,0:T(8,128)(2,1)S(1)} %copy-done, bf16[1,2,16,1024]{3,2,1,0:T(8,128)(2,1)S(1)} %collective-permute-done.3.across, ...), custom_call_target="tpu_custom_call" | custom-call | flops 4000000000 | bytes 1000000 | tf_op jit(solution)/shard_map/pallas_call | solution.py:244
  14.9 0.0 collective-permute-done.5.far_v
  14.9 0.0 collective-permute-done.4.far_k
  14.9 1.4 %shard_map.71 = (bf16[1,2,64,512]{3,2,1,0:T(8,128)(2,1)}, bf16[16,1,16,256]{3,2,1,0:T(8,128)(2,1)}) custom-call(bf16[4,2,64,128]{3,2,1,0:T(8,128)(2,1)S(1)} %collective-permute-done.4.far_k, bf16[4,2,64,128]{3,2,1,0:T(8,128)(2,1)S(1)} %collective-permute-done.5.far_v, f32[256,128]{1,0:T(8,128)S(1)} %get-tuple-element.26.bias_a, ...), custom_call_target="tpu_custom_call" | custom-call | flops 4000000000 | bytes 1000000 | tf_op jit(solution)/shard_map/pallas_call | solution.py:257
  (9 shorter events, 0.1 us)
Async XLA Ops:
  0.6 5.0 %copy-start.1 = (bf16[1,2,64,128]{3,2,1,0:T(8,128)(2,1)S(1)}, bf16[1,2,64,128]{3,2,1,0:T(8,128)(2,1)}, u32[]{:S(2)}) copy-start(bf16[1,2,64,128]{3,2,1,0:T(8,128)(2,1)} %param.7) | copy-start | bytes 98308
  0.6 5.0 %copy-start.2 = (bf16[1,2,64,128]{3,2,1,0:T(8,128)(2,1)S(1)}, bf16[1,2,64,128]{3,2,1,0:T(8,128)(2,1)}, u32[]{:S(2)}) copy-start(bf16[1,2,64,128]{3,2,1,0:T(8,128)(2,1)} %param.6) | copy-start | bytes 98308
  1.5 7.7 %copy-start = (bf16[1,2,16,2048]{3,2,1,0:T(8,128)(2,1)S(1)}, bf16[1,2,16,2048]{3,2,1,0:T(8,128)(2,1)}, u32[]{:S(2)}) copy-start(bf16[1,2,16,2048]{3,2,1,0:T(8,128)(2,1)} %own.1) | copy-start | bytes 393220
  1.5 7.8 %collective-permute-start.3 = (bf16[1,2,16,1024]{3,2,1,0:T(8,128)(2,1)S(1)}, bf16[1,2,16,1024]{3,2,1,0:T(8,128)(2,1)S(1)}, u32[]{:S(2)}, u32[]{:S(2)}) collective-permute-start(bf16[1,2,16,1024]{3,2,1,0:T(8,128)(2,1)S(1)} %get-tuple-element.19), channel_id=1, source_target_pairs={{0,2},{1,3},{2,0},{3,1},{4,6},{5,7},{6,4},{7,5},{8,10},{9,11},{10,... | collective-permute-start | bytes 196616 | tf_op jit(solution)/shard_map/ppermute | solution.py:205
  5.7 5.3 %collective-permute-start = (bf16[1,2,64,256]{3,2,1,0:T(8,128)(2,1)S(1)}, bf16[1,2,64,256]{3,2,1,0:T(8,128)(2,1)S(1)}, u32[]{:S(2)}, u32[]{:S(2)}) collective-permute-start(bf16[1,2,64,256]{3,2,1,0:T(8,128)(2,1)S(1)} %pad_maximum_fusion.2), channel_id=1, source_target_pairs={{0,24},{4,28},{8,16},{12,20},{16,8},{20,12},{24,0},{28,4},{1,25},{... | collective-permute-start | bytes 196616 | tf_op jit(solution)/shard_map/ppermute | solution.py:209
  8.2 4.3 %collective-permute-start.1 = (bf16[1,2,64,256]{3,2,1,0:T(8,128)(2,1)S(1)}, bf16[1,2,64,256]{3,2,1,0:T(8,128)(2,1)S(1)}, u32[]{:S(2)}, u32[]{:S(2)}) collective-permute-start(bf16[1,2,64,256]{3,2,1,0:T(8,128)(2,1)S(1)} %pad_maximum_fusion.2), channel_id=1, source_target_pairs={{0,16},{4,20},{8,24},{12,28},{16,0},{20,4},{24,8},{28,12},{1,17},{... | collective-permute-start | bytes 196616 | tf_op jit(solution)/shard_map/ppermute | solution.py:209
  8.7 4.3 %collective-permute-start.2 = (bf16[1,2,64,256]{3,2,1,0:T(8,128)(2,1)S(1)}, bf16[1,2,64,256]{3,2,1,0:T(8,128)(2,1)S(1)}, u32[]{:S(2)}, u32[]{:S(2)}) collective-permute-start(bf16[1,2,64,256]{3,2,1,0:T(8,128)(2,1)S(1)} %pad_maximum_fusion.2), channel_id=1, source_target_pairs={{0,8},{4,12},{8,0},{12,4},{16,24},{20,28},{24,16},{28,20},{1,9},{5... | collective-permute-start | bytes 196616 | tf_op jit(solution)/shard_map/ppermute | solution.py:209
  9.3 5.0 %collective-permute-start.6 = (bf16[2,2,16,512]{3,2,1,0:T(8,128)(2,1)S(1)}, bf16[2,2,16,512]{3,2,1,0:T(8,128)(2,1)S(1)}, u32[]{:S(2)}, u32[]{:S(2)}) collective-permute-start(bf16[2,2,16,512]{3,2,1,0:T(8,128)(2,1)S(1)} %pad_maximum_fusion.3), channel_id=1, source_target_pairs={{0,1},{1,0},{2,3},{3,2},{4,5},{5,4},{6,7},{7,6},{8,9},{9,8},{10,11... | collective-permute-start | bytes 196616 | tf_op jit(solution)/shard_map/ppermute | solution.py:219
  13.0 1.9 %collective-permute-start.5 = (bf16[4,2,64,128]{3,2,1,0:T(8,128)(2,1)S(1)}, bf16[4,2,64,128]{3,2,1,0:T(8,128)(2,1)S(1)}, u32[]{:S(2)}, u32[]{:S(2)}) collective-permute-start(bf16[4,2,64,128]{3,2,1,0:T(8,128)(2,1)S(1)} %pad_maximum_fusion.1.near_v), channel_id=1, source_target_pairs={{0,4},{4,0},{8,12},{12,8},{16,20},{20,16},{24,28},{28,24},{1,5},{5... | collective-permute-start | bytes 393224 | tf_op jit(solution)/shard_map/ppermute | solution.py:223
  13.1 1.8 %collective-permute-start.4 = (bf16[4,2,64,128]{3,2,1,0:T(8,128)(2,1)S(1)}, bf16[4,2,64,128]{3,2,1,0:T(8,128)(2,1)S(1)}, u32[]{:S(2)}, u32[]{:S(2)}) collective-permute-start(bf16[4,2,64,128]{3,2,1,0:T(8,128)(2,1)S(1)} %pad_maximum_fusion.near_k), channel_id=1, source_target_pairs={{0,4},{4,0},{8,12},{12,8},{16,20},{20,16},{24,28},{28,24},{1,5},{5... | collective-permute-start | bytes 393224 | tf_op jit(solution)/shard_map/ppermute | solution.py:223

commit v13 on v12

--- a/solution.py
+++ b/solution.py
@@ -75,15 +75,15 @@
     return jnp.concatenate([rows[m : m + 1] for m in range(chips)], axis=1)
 
 
-def place_pages(targets, keys, values, slot_count):
-    rows = jnp.concatenate([keys[...].reshape(-1, HEAD_DIM), values[...].reshape(-1, HEAD_DIM)], axis=1)
+def place_pages(targets, pairs, slot_count):
+    rows = pairs[...].reshape(-1, pairs.shape[-1])
     row = lax.broadcasted_iota(jnp.int32, (slot_count * PAGE, rows.shape[0]), 0)
     chosen = jnp.where(row == targets, 1.0, 0.0).astype(jnp.bfloat16)
     return jnp.dot(chosen, rows, preferred_element_type=jnp.float32)
 
 
-def score_part(queries, keys, half):
-    keys = keys[:, : half + 1].reshape(-1, HEAD_DIM)
+def score_part(queries, pairs, half):
+    keys = pairs[:, : half + 1].reshape(-1, 2 * HEAD_DIM)[:, :HEAD_DIM]
     return lax.dot_general(keys, queries, (((1,), (1,)), ((), ())), preferred_element_type=jnp.float32)
 
 
@@ -95,8 +95,8 @@
     return top, jnp.sum(weights, axis=0, keepdims=True), weights.astype(jnp.bfloat16)
 
 
-def weigh_part(weights, values, half):
-    values = values[:, : half + 1].reshape(-1, HEAD_DIM)
+def weigh_part(weights, pairs, half):
+    values = pairs[:, : half + 1].reshape(-1, 2 * HEAD_DIM)[:, HEAD_DIM:]
     return lax.dot_general(values, weights, (((0,), (0,)), ((), ())), preferred_element_type=jnp.float32)
 
 
@@ -116,14 +116,14 @@
 
 
 def plan_kernel(
-    lengths, page_slot, near_k, near_v, bias_a, bias_b, far_bias_a, far_bias_b, far_targets, pages_ref
+    lengths, page_slot, near, bias_a, bias_b, far_bias_a, far_bias_b, far_targets, pages_ref
 ):
-    chips, _, block_tok, _ = near_k.shape
+    chips, _, block_tok, _ = near.shape
     slot_count = pages_ref.shape[0] // PAGE
     sub_tok = block_tok // lax.axis_size("head")
     my_blk = lax.axis_index("blk")
     targets = functools.partial(page_targets, my_blk, page_slot, chips, slot_count)
-    pages_ref[...] = place_pages(targets(0), near_k, near_v, slot_count).astype(jnp.bfloat16)
+    pages_ref[...] = place_pages(targets(0), near, slot_count).astype(jnp.bfloat16)
     far_targets[...] = targets(1)
     bias = functools.partial(key_bias, my_blk, lengths[...], chips, block_tok, sub_tok)
     for half in range(2):
@@ -131,34 +131,34 @@
         (far_bias_a, far_bias_b)[half][...] = bias(half, 1)
 
 
-def near_kernel(own, across, beside, near_k, near_v, bias_a, bias_b, q_rows, top_ref, total_ref, out_ref):
+def near_kernel(own, across, beside, near, bias_a, bias_b, q_rows, top_ref, total_ref, out_ref):
     scores = {}
     for half in (1, 0):
         queries = gather_queries(own, across, beside, half)
         q_rows[half] = queries
-        scores[half] = score_part(queries, near_k, half)
+        scores[half] = score_part(queries, near, half)
     for half in (1, 0):
         top_ref[half], total_ref[half], weights = soften(scores[half], (bias_a, bias_b)[half][...])
-        out_ref[half] = weigh_part(weights, near_v, half)
+        out_ref[half] = weigh_part(weights, near, half)
 
 
 def far_kernel(
-    far_k, far_v, bias_a, bias_b, far_targets, pages_ref, q_rows, top_ref, total_ref, out_ref, attended, kv_cache,
+    far, bias_a, bias_b, far_targets, pages_ref, q_rows, top_ref, total_ref, out_ref, attended, kv_cache,
     pages, result, sems,
 ):
-    block_tok = far_k.shape[2]
+    block_tok = far.shape[2]
     slot_count = kv_cache.shape[0]
     my_head = lax.axis_index("head")
     sub_tok = block_tok // lax.axis_size("head")
-    scores = {half: score_part(q_rows[half], far_k, half) for half in (1, 0)}
-    moved = place_pages(far_targets[...], far_k, far_v, slot_count) + pages_ref[...].astype(jnp.float32)
+    scores = {half: score_part(q_rows[half], far, half) for half in (1, 0)}
+    moved = place_pages(far_targets[...], far, slot_count) + pages_ref[...].astype(jnp.float32)
     pages[...] = moved.astype(jnp.bfloat16).reshape(pages.shape)
     writes = [pltpu.make_async_copy(pages, kv_cache, sems.at[2])]
     writes[0].start()
     parts = {}
     for half in (1, 0):
         top, total, weights = soften(scores[half], (bias_a, bias_b)[half][...])
-        parts[half] = (top, total, weigh_part(weights, far_v, half))
+        parts[half] = (top, total, weigh_part(weights, far, half))
     for half in (1, 0):
         top, total, out = parts[half]
         best = jnp.maximum(top, top_ref[half])
@@ -217,10 +217,8 @@
     )
     near = lax.optimization_barrier((near[::-1], beside))[0][::-1]
     beside = lax.ppermute(beside, "head", [(i, i ^ 1) for i in range(head_count)])
-    near = [pair] + near
-    near_k = jnp.concatenate([p[..., :HEAD_DIM] for p in near], axis=0)
-    near_v = jnp.concatenate([p[..., HEAD_DIM:] for p in near], axis=0)
-    far_k, far_v = (lax.ppermute(x, "blk", [(i, i ^ 1) for i in range(blk_count)]) for x in (near_k, near_v))
+    near = jnp.concatenate([pair] + near, axis=0)
+    far = lax.ppermute(near, "blk", [(i, i ^ 1) for i in range(blk_count)])
 
     params = pltpu.CompilerParams(vmem_limit_bytes=32 * 1024 * 1024)
     cost = pl.CostEstimate(flops=4_000_000_000, bytes_accessed=1_000_000, transcendentals=200_000)
@@ -236,11 +234,11 @@
             jax.ShapeDtypeStruct((1, 2 * half_cols), jnp.int32),
             jax.ShapeDtypeStruct((slot_count * PAGE, 2 * HEAD_DIM), jnp.bfloat16),
         ),
-        in_specs=[vmem] * 4,
+        in_specs=[vmem] * 3,
         out_specs=(vmem,) * 6,
         compiler_params=params,
         cost_estimate=cost,
-    )(lengths, slots, near_k, near_v)
+    )(lengths, slots, near)
     stats = pl.pallas_call(
         near_kernel,
         out_shape=(
@@ -249,18 +247,18 @@
             jax.ShapeDtypeStruct((2, 1, rows), jnp.float32),
             jax.ShapeDtypeStruct((2, HEAD_DIM, rows), jnp.float32),
         ),
-        in_specs=[vmem] * 7,
+        in_specs=[vmem] * 6,
         out_specs=(vmem,) * 4,
         compiler_params=params,
         cost_estimate=cost,
-    )(query_states, across, beside, near_k, near_v, *bias)
+    )(query_states, across, beside, near, *bias)
     return pl.pallas_call(
         far_kernel,
         out_shape=(
             jax.ShapeDtypeStruct((1, 2, block_tok, width), jnp.bfloat16),
             jax.ShapeDtypeStruct((slot_count, 1, PAGE, 2 * HEAD_DIM), jnp.bfloat16),
         ),
-        in_specs=[vmem] * 10,
+        in_specs=[vmem] * 9,
         out_specs=(hbm, hbm),
         scratch_shapes=[
             pltpu.VMEM((slot_count, 1, PAGE, 2 * HEAD_DIM), jnp.bfloat16),
@@ -269,7 +267,7 @@
         ],
         compiler_params=params,
         cost_estimate=cost,
-    )(far_k, far_v, far_bias_a, far_bias_b, far_targets, pages, *stats)
+    )(far, far_bias_a, far_bias_b, far_targets, pages, *stats)
 
 
 def per_device_long(query_states, key_states, value_states, doc_lengths, page_slot):

time: 16.5 us -> 16.1 us (0.976)
  starting transfers between devices: 9.92 us -> 9.35 us
  waiting for transfers between devices: 2.01 us -> 2.37 us
    ppermute x2 -> x1, starting transfers between devices: 0.63 us -> 0.07 us  [per_device(): far = lax.ppermute(near, 'blk', [(i, i ^ 1) for i in range(blk_count)])]
    ppermute x2 -> x1, waiting for transfers between devices: 0.01 us -> 0.31 us  [per_device(): far = lax.ppermute(near, 'blk', [(i, i ^ 1) for i in range(blk_count)])]
  transfers between devices with their start and end apart: 7 -> 6, of which waited for: 2 -> 4; matrix products, arithmetic and copies ran while one was open for 1% -> 0% of each run, Pallas kernels for 7% -> 7%
where the time goes in v13:
time: 16.1 us; the launch traced here: 15.9 us
  starting transfers between devices  9.35 us (58%)
  Pallas kernels  3.42 us (21%)
  waiting for transfers between devices  2.37 us (15%)
  between operations  0.73 us (5%)
    ppermute x1, starting transfers between devices, per_device(): across = lax.ppermute(part, 'head', [(i, i ^ 2) for i in range(head_count)])  4.1 us
    ppermute x3, starting transfers between devices, per_device(): lax.ppermute(pair, 'blk', [(i, i ^ d) for i in range(blk_count)])  3.55 us
    ppermute x3, waiting for transfers between devices, per_device(): lax.ppermute(pair, 'blk', [(i, i ^ d) for i in range(blk_count)])  2.01 us
    ppermute x1, starting transfers between devices, per_device(): lax.ppermute(beside, 'head', [(i, i ^ 1) for i in range(head_count)])  1.63 us
    pallas_call x1, Pallas kernels, per_device(): pl.pallas_call(far_kernel, out_shape=(jax.ShapeDtypeStruct((1, 2, block_t...  1.37 us
    pallas_call x1, Pallas kernels, per_device(): pl.pallas_call(fetch_kernel, out_shape=(jax.ShapeDtypeStruct((*query_stat...  0.86 us
    pallas_call x1, Pallas kernels, per_device(): pl.pallas_call(near_kernel, out_shape=(jax.ShapeDtypeStruct((2, rows, HEA...  0.6 us
    pallas_call x1, Pallas kernels, per_device(): pl.pallas_call(plan_kernel, out_shape=(jax.ShapeDtypeStruct((half_cols, L...  0.58 us
  transfers between devices with their start and end apart: 6, of which 4 were waited for; matrix products, arithmetic and copies ran while one was open for 0% of the time, Pallas kernels for 7%

profile of v13, /device:TPU:0, one launch (start us, length us, event | category | flops | bytes accessed | tf_op | source)
XLA Modules:
  0.0 15.9 jit_solution(4590056465614660607)
XLA Ops:
  0.6 0.0 copy-start.1
  0.6 0.0 copy-start.2
  0.7 0.9 %shard_map.68 = (bf16[1,2,16,1024]{3,2,1,0:T(8,128)(2,1)S(1)}, s32[1,3]{1,0:T(1,128)S(1)}, s32[2,4,8]{2,1,0:T(4,128)S(1)}) custom-call(bf16[1,2,16,2048]{3,2,1,0:T(8,128)(2,1)} %own.1, s32[1,3]{1,0:T(1,128)} %bitcast.3, s32[2,4,8]{2,1,0:T(4,128)} %bitcast.2), custom_call_target="tpu_custom_call" | custom-call | bytes 200000 | tf_op jit(solution)/shard_map/pallas_call | solution.py:193
  1.5 0.0 copy-start
  1.5 4.1 %collective-permute-start.3 = (bf16[1,2,16,1024]{3,2,1,0:T(8,128)(2,1)S(1)}, bf16[1,2,16,1024]{3,2,1,0:T(8,128)(2,1)S(1)}, u32[]{:S(2)}, u32[]{:S(2)}) collective-permute-start(bf16[1,2,16,1024]{3,2,1,0:T(8,128)(2,1)S(1)} %get-tuple-element.19), channel_id=1, source_target_pairs={{0,2},{1,3},{2,0},{3,1},{4,6},{5,7},{6,4},{7,5},{8,10},{9,11},{10,... | collective-permute-start | bytes 196616 | tf_op jit(solution)/shard_map/ppermute | solution.py:205
  5.6 0.0 copy-done.1
  5.6 0.0 copy-done.2
  5.7 2.5 %collective-permute-start = (bf16[1,2,64,256]{3,2,1,0:T(8,128)(2,1)S(1)}, bf16[1,2,64,256]{3,2,1,0:T(8,128)(2,1)S(1)}, u32[]{:S(2)}, u32[]{:S(2)}) collective-permute-start(bf16[1,2,64,256]{3,2,1,0:T(8,128)(2,1)S(1)} %pad_maximum_fusion), channel_id=1, source_target_pairs={{0,24},{4,28},{8,16},{12,20},{16,8},{20,12},{24,0},{28,4},{1,25},{... | collective-permute-start | bytes 196616 | tf_op jit(solution)/shard_map/ppermute | solution.py:209
  8.2 0.5 %collective-permute-start.1 = (bf16[1,2,64,256]{3,2,1,0:T(8,128)(2,1)S(1)}, bf16[1,2,64,256]{3,2,1,0:T(8,128)(2,1)S(1)}, u32[]{:S(2)}, u32[]{:S(2)}) collective-permute-start(bf16[1,2,64,256]{3,2,1,0:T(8,128)(2,1)S(1)} %pad_maximum_fusion), channel_id=1, source_target_pairs={{0,16},{4,20},{8,24},{12,28},{16,0},{20,4},{24,8},{28,12},{1,17},{... | collective-permute-start | bytes 196616 | tf_op jit(solution)/shard_map/ppermute | solution.py:209
  8.7 0.5 %collective-permute-start.2 = (bf16[1,2,64,256]{3,2,1,0:T(8,128)(2,1)S(1)}, bf16[1,2,64,256]{3,2,1,0:T(8,128)(2,1)S(1)}, u32[]{:S(2)}, u32[]{:S(2)}) collective-permute-start(bf16[1,2,64,256]{3,2,1,0:T(8,128)(2,1)S(1)} %pad_maximum_fusion), channel_id=1, source_target_pairs={{0,8},{4,12},{8,0},{12,4},{16,24},{20,28},{24,16},{28,20},{1,9},{5... | collective-permute-start | bytes 196616 | tf_op jit(solution)/shard_map/ppermute | solution.py:209
  9.2 0.0 copy-done
  9.2 0.0 collective-permute-done.3.across
  9.3 1.6 %collective-permute-start.5 = (bf16[2,2,16,512]{3,2,1,0:T(8,128)(2,1)S(1)}, bf16[2,2,16,512]{3,2,1,0:T(8,128)(2,1)S(1)}, u32[]{:S(2)}, u32[]{:S(2)}) collective-permute-start(bf16[2,2,16,512]{3,2,1,0:T(8,128)(2,1)S(1)} %pad_maximum_fusion.1), channel_id=1, source_target_pairs={{0,1},{1,0},{2,3},{3,2},{4,5},{5,4},{6,7},{7,6},{8,9},{9,8},{10,11... | collective-permute-start | bytes 196616 | tf_op jit(solution)/shard_map/ppermute | solution.py:219
  10.9 0.1 collective-permute-done
  11.0 1.4 %collective-permute-done.1 = bf16[1,2,64,256]{3,2,1,0:T(8,128)(2,1)S(1)} collective-permute-done((bf16[1,2,64,256]{3,2,1,0:T(8,128)(2,1)S(1)}, bf16[1,2,64,256]{3,2,1,0:T(8,128)(2,1)S(1)}, u32[]{:S(2)}, u32[]{:S(2)}) %collective-permute-start.1) | collective-permute-done | bytes 65568 | tf_op jit(solution)/shard_map/ppermute | solution.py:209
  12.4 0.5 %collective-permute-done.2 = bf16[1,2,64,256]{3,2,1,0:T(8,128)(2,1)S(1)} collective-permute-done((bf16[1,2,64,256]{3,2,1,0:T(8,128)(2,1)S(1)}, bf16[1,2,64,256]{3,2,1,0:T(8,128)(2,1)S(1)}, u32[]{:S(2)}, u32[]{:S(2)}) %collective-permute-start.2) | collective-permute-done | bytes 65568 | tf_op jit(solution)/shard_map/ppermute | solution.py:209
  13.0 0.1 collective-permute-start.4
  13.1 0.6 %shard_map.69 = (f32[256,128]{1,0:T(8,128)S(1)}, f32[512,128]{1,0:T(8,128)S(1)}, f32[256,128]{1,0:T(8,128)S(1)}, f32[512,128]{1,0:T(8,128)S(1)}, s32[1,512]{1,0:T(1,128)S(1)}, /*index=5*/bf16[256,256]{1,0:T(8,128)(2,1)S(1)}) custom-call(s32[1,3]{1,0:T(1,128)S(1)} %get-tuple-element.24.lengths, s32[2,4,8]{2,1,0:T(4,128)S(1)} %get-tuple-element.25.page_slot, ...), custom_call_target="tpu_custom_call" | custom-call | flops 4000000000 | bytes 1000000 | tf_op jit(solution)/shard_map/pallas_call | solution.py:226
  13.6 0.0 collective-permute-done.5.beside
  13.6 0.6 %shard_map.70 = (bf16[2,256,128]{2,1,0:T(8,128)(2,1)S(1)}, f32[2,1,256]{2,1,0:T(1,128)S(1)}, f32[2,1,256]{2,1,0:T(1,128)S(1)}, f32[2,128,256]{2,1,0:T(8,128)S(1)}) custom-call(bf16[1,2,16,2048]{3,2,1,0:T(8,128)(2,1)S(1)} %copy-done, bf16[1,2,16,1024]{3,2,1,0:T(8,128)(2,1)S(1)} %collective-permute-done.3.across, ...), custom_call_target="tpu_custom_call" | custom-call | flops 4000000000 | bytes 1000000 | tf_op jit(solution)/shard_map/pallas_call | solution.py:242
  14.3 0.3 %collective-permute-done.4.far = bf16[4,2,64,256]{3,2,1,0:T(8,128)(2,1)S(1)} collective-permute-done((bf16[4,2,64,256]{3,2,1,0:T(8,128)(2,1)S(1)}, bf16[4,2,64,256]{3,2,1,0:T(8,128)(2,1)S(1)}, u32[]{:S(2)}, u32[]{:S(2)}) %collective-permute-start.4) | collective-permute-done | bytes 262176 | tf_op jit(solution)/shard_map/ppermute | solution.py:221
  14.6 1.4 %shard_map.71 = (bf16[1,2,64,512]{3,2,1,0:T(8,128)(2,1)}, bf16[16,1,16,256]{3,2,1,0:T(8,128)(2,1)}) custom-call(bf16[4,2,64,256]{3,2,1,0:T(8,128)(2,1)S(1)} %collective-permute-done.4.far, f32[256,128]{1,0:T(8,128)S(1)} %get-tuple-element.26.bias_a, f32[512,128]{1,0:T(8,128)S(1)} %get-tuple-element.27.bias_b, s32[1,512]{1,0:T(1,128)S(1)} %get-tuple-element.28.far_targets, ...), custom_call_target="tpu_custom_call" | custom-call | flops 4000000000 | bytes 1000000 | tf_op jit(solution)/shard_map/pallas_call | solution.py:255
  (8 shorter events, 0.1 us)
Async XLA Ops:
  0.6 5.0 %copy-start.1 = (bf16[1,2,64,128]{3,2,1,0:T(8,128)(2,1)S(1)}, bf16[1,2,64,128]{3,2,1,0:T(8,128)(2,1)}, u32[]{:S(2)}) copy-start(bf16[1,2,64,128]{3,2,1,0:T(8,128)(2,1)} %param.7) | copy-start | bytes 98308
  0.6 5.0 %copy-start.2 = (bf16[1,2,64,128]{3,2,1,0:T(8,128)(2,1)S(1)}, bf16[1,2,64,128]{3,2,1,0:T(8,128)(2,1)}, u32[]{:S(2)}) copy-start(bf16[1,2,64,128]{3,2,1,0:T(8,128)(2,1)} %param.6) | copy-start | bytes 98308
  1.5 7.7 %copy-start = (bf16[1,2,16,2048]{3,2,1,0:T(8,128)(2,1)S(1)}, bf16[1,2,16,2048]{3,2,1,0:T(8,128)(2,1)}, u32[]{:S(2)}) copy-start(bf16[1,2,16,2048]{3,2,1,0:T(8,128)(2,1)} %own.1) | copy-start | bytes 393220
  1.5 7.8 %collective-permute-start.3 = (bf16[1,2,16,1024]{3,2,1,0:T(8,128)(2,1)S(1)}, bf16[1,2,16,1024]{3,2,1,0:T(8,128)(2,1)S(1)}, u32[]{:S(2)}, u32[]{:S(2)}) collective-permute-start(bf16[1,2,16,1024]{3,2,1,0:T(8,128)(2,1)S(1)} %get-tuple-element.19), channel_id=1, source_target_pairs={{0,2},{1,3},{2,0},{3,1},{4,6},{5,7},{6,4},{7,5},{8,10},{9,11},{10,... | collective-permute-start | bytes 196616 | tf_op jit(solution)/shard_map/ppermute | solution.py:205
  5.7 5.3 %collective-permute-start = (bf16[1,2,64,256]{3,2,1,0:T(8,128)(2,1)S(1)}, bf16[1,2,64,256]{3,2,1,0:T(8,128)(2,1)S(1)}, u32[]{:S(2)}, u32[]{:S(2)}) collective-permute-start(bf16[1,2,64,256]{3,2,1,0:T(8,128)(2,1)S(1)} %pad_maximum_fusion), channel_id=1, source_target_pairs={{0,24},{4,28},{8,16},{12,20},{16,8},{20,12},{24,0},{28,4},{1,25},{... | collective-permute-start | bytes 196616 | tf_op jit(solution)/shard_map/ppermute | solution.py:209
  8.2 4.3 %collective-permute-start.1 = (bf16[1,2,64,256]{3,2,1,0:T(8,128)(2,1)S(1)}, bf16[1,2,64,256]{3,2,1,0:T(8,128)(2,1)S(1)}, u32[]{:S(2)}, u32[]{:S(2)}) collective-permute-start(bf16[1,2,64,256]{3,2,1,0:T(8,128)(2,1)S(1)} %pad_maximum_fusion), channel_id=1, source_target_pairs={{0,16},{4,20},{8,24},{12,28},{16,0},{20,4},{24,8},{28,12},{1,17},{... | collective-permute-start | bytes 196616 | tf_op jit(solution)/shard_map/ppermute | solution.py:209
  8.7 4.3 %collective-permute-start.2 = (bf16[1,2,64,256]{3,2,1,0:T(8,128)(2,1)S(1)}, bf16[1,2,64,256]{3,2,1,0:T(8,128)(2,1)S(1)}, u32[]{:S(2)}, u32[]{:S(2)}) collective-permute-start(bf16[1,2,64,256]{3,2,1,0:T(8,128)(2,1)S(1)} %pad_maximum_fusion), channel_id=1, source_target_pairs={{0,8},{4,12},{8,0},{12,4},{16,24},{20,28},{24,16},{28,20},{1,9},{5... | collective-permute-start | bytes 196616 | tf_op jit(solution)/shard_map/ppermute | solution.py:209
  9.3 4.3 %collective-permute-start.5 = (bf16[2,2,16,512]{3,2,1,0:T(8,128)(2,1)S(1)}, bf16[2,2,16,512]{3,2,1,0:T(8,128)(2,1)S(1)}, u32[]{:S(2)}, u32[]{:S(2)}) collective-permute-start(bf16[2,2,16,512]{3,2,1,0:T(8,128)(2,1)S(1)} %pad_maximum_fusion.1), channel_id=1, source_target_pairs={{0,1},{1,0},{2,3},{3,2},{4,5},{5,4},{6,7},{7,6},{8,9},{9,8},{10,11... | collective-permute-start | bytes 196616 | tf_op jit(solution)/shard_map/ppermute | solution.py:219
  13.0 1.6 %collective-permute-start.4 = (bf16[4,2,64,256]{3,2,1,0:T(8,128)(2,1)S(1)}, bf16[4,2,64,256]{3,2,1,0:T(8,128)(2,1)S(1)}, u32[]{:S(2)}, u32[]{:S(2)}) collective-permute-start(bf16[4,2,64,256]{3,2,1,0:T(8,128)(2,1)S(1)} %constant_dynamic-update-slice_fusion.near), channel_id=1, source_target_pairs={{0,4},{4,0},{8,12},{12,8},{16,20},{20,16},{24,28},{28,24},{1,5},{5... | collective-permute-start | bytes 786440 | tf_op jit(solution)/shard_map/ppermute | solution.py:221

commit v14 on v13

--- a/solution.py
+++ b/solution.py
@@ -75,11 +75,13 @@
     return jnp.concatenate([rows[m : m + 1] for m in range(chips)], axis=1)
 
 
-def place_pages(targets, pairs, slot_count):
-    rows = pairs[...].reshape(-1, pairs.shape[-1])
-    row = lax.broadcasted_iota(jnp.int32, (slot_count * PAGE, rows.shape[0]), 0)
-    chosen = jnp.where(row == targets, 1.0, 0.0).astype(jnp.bfloat16)
-    return jnp.dot(chosen, rows, preferred_element_type=jnp.float32)
+def choose_pages(targets, slot_count):
+    row = lax.broadcasted_iota(jnp.int32, (slot_count * PAGE, targets.shape[1]), 0)
+    return jnp.where(row == targets, 1.0, 0.0).astype(jnp.bfloat16)
+
+
+def place_pages(chosen, pairs):
+    return jnp.dot(chosen, pairs[...].reshape(-1, pairs.shape[-1]), preferred_element_type=jnp.float32)
 
 
 def score_part(queries, pairs, half):
@@ -116,15 +118,15 @@
 
 
 def plan_kernel(
-    lengths, page_slot, near, bias_a, bias_b, far_bias_a, far_bias_b, far_targets, pages_ref
+    lengths, page_slot, near, bias_a, bias_b, far_bias_a, far_bias_b, far_chosen, pages_ref
 ):
     chips, _, block_tok, _ = near.shape
     slot_count = pages_ref.shape[0] // PAGE
     sub_tok = block_tok // lax.axis_size("head")
     my_blk = lax.axis_index("blk")
     targets = functools.partial(page_targets, my_blk, page_slot, chips, slot_count)
-    pages_ref[...] = place_pages(targets(0), near, slot_count).astype(jnp.bfloat16)
-    far_targets[...] = targets(1)
+    pages_ref[...] = place_pages(choose_pages(targets(0), slot_count), near).astype(jnp.bfloat16)
+    far_chosen[...] = choose_pages(targets(1), slot_count)
     bias = functools.partial(key_bias, my_blk, lengths[...], chips, block_tok, sub_tok)
     for half in range(2):
         (bias_a, bias_b)[half][...] = bias(half, 0)
@@ -143,7 +145,7 @@
 
 
 def far_kernel(
-    far, bias_a, bias_b, far_targets, pages_ref, q_rows, top_ref, total_ref, out_ref, attended, kv_cache,
+    far, bias_a, bias_b, far_chosen, pages_ref, q_rows, top_ref, total_ref, out_ref, attended, kv_cache,
     pages, result, sems,
 ):
     block_tok = far.shape[2]
@@ -151,7 +153,7 @@
     my_head = lax.axis_index("head")
     sub_tok = block_tok // lax.axis_size("head")
     scores = {half: score_part(q_rows[half], far, half) for half in (1, 0)}
-    moved = place_pages(far_targets[...], far, slot_count) + pages_ref[...].astype(jnp.float32)
+    moved = place_pages(far_chosen[...], far) + pages_ref[...].astype(jnp.float32)
     pages[...] = moved.astype(jnp.bfloat16).reshape(pages.shape)
     writes = [pltpu.make_async_copy(pages, kv_cache, sems.at[2])]
     writes[0].start()
@@ -165,7 +167,7 @@
         here = jnp.exp2(top - best)
         there = jnp.exp2(top_ref[half] - best)
         inverse = 1.0 / (total * here + total_ref[half] * there)
-        out = (out * (here * inverse) + out_ref[half] * (there * inverse)).T.astype(jnp.bfloat16)
+        out = (out * (here * inverse) + out_ref[half] * (there * inverse)).astype(jnp.bfloat16).T
         for g in range(out.shape[0] // block_tok):
             for d in range(block_tok // sub_tok):
                 row = pl.multiple_of((my_head ^ d) * sub_tok, sub_tok)
@@ -223,7 +225,7 @@
     params = pltpu.CompilerParams(vmem_limit_bytes=32 * 1024 * 1024)
     cost = pl.CostEstimate(flops=4_000_000_000, bytes_accessed=1_000_000, transcendentals=200_000)
     half_cols = blk_count // 2 * block_tok
-    *bias, far_bias_a, far_bias_b, far_targets, pages = pl.pallas_call(
+    *bias, far_bias_a, far_bias_b, far_chosen, pages = pl.pallas_call(
         plan_kernel,
         out_shape=(
             jax.ShapeDtypeStruct((half_cols, LANES), jnp.float32),
@@ -231,7 +233,7 @@
         )
         * 2
         + (
-            jax.ShapeDtypeStruct((1, 2 * half_cols), jnp.int32),
+            jax.ShapeDtypeStruct((slot_count * PAGE, 2 * half_cols), jnp.bfloat16),
             jax.ShapeDtypeStruct((slot_count * PAGE, 2 * HEAD_DIM), jnp.bfloat16),
         ),
         in_specs=[vmem] * 3,
@@ -267,7 +269,7 @@
         ],
         compiler_params=params,
         cost_estimate=cost,
-    )(far, far_bias_a, far_bias_b, far_targets, pages, *stats)
+    )(far, far_bias_a, far_bias_b, far_chosen, pages, *stats)
 
 
 def per_device_long(query_states, key_states, value_states, doc_lengths, page_slot):

time: 16.1 us -> 16.1 us (level)
  transfers between devices with their start and end apart: 6 -> 6, of which waited for: 4 -> 4; matrix products, arithmetic and copies ran while one was open for 0% -> 0% of each run, Pallas kernels for 7% -> 8%
where the time goes in v14:
time: 16.1 us; the launch traced here: 15.9 us
  starting transfers between devices  9.35 us (58%)
  Pallas kernels  3.53 us (22%)
  waiting for transfers between devices  2.23 us (14%)
  between operations  0.73 us (5%)
    ppermute x1, starting transfers between devices, per_device(): across = lax.ppermute(part, 'head', [(i, i ^ 2) for i in range(head_count)])  4.1 us
    ppermute x3, starting transfers between devices, per_device(): lax.ppermute(pair, 'blk', [(i, i ^ d) for i in range(blk_count)])  3.55 us
    ppermute x3, waiting for transfers between devices, per_device(): lax.ppermute(pair, 'blk', [(i, i ^ d) for i in range(blk_count)])  2.01 us
    ppermute x1, starting transfers between devices, per_device(): lax.ppermute(beside, 'head', [(i, i ^ 1) for i in range(head_count)])  1.63 us
    pallas_call x1, Pallas kernels, per_device(): pl.pallas_call(far_kernel, out_shape=(jax.ShapeDtypeStruct((1, 2, block_t...  1.34 us
    pallas_call x1, Pallas kernels, per_device(): pl.pallas_call(fetch_kernel, out_shape=(jax.ShapeDtypeStruct((*query_stat...  0.86 us
    pallas_call x1, Pallas kernels, per_device(): pl.pallas_call(plan_kernel, out_shape=(jax.ShapeDtypeStruct((half_cols, L...  0.72 us
    pallas_call x1, Pallas kernels, per_device(): pl.pallas_call(near_kernel, out_shape=(jax.ShapeDtypeStruct((2, rows, HEA...  0.61 us
  transfers between devices with their start and end apart: 6, of which 4 were waited for; matrix products, arithmetic and copies ran while one was open for 0% of the time, Pallas kernels for 8%

profile of v14, /device:TPU:0, one launch (start us, length us, event | category | flops | bytes accessed | tf_op | source)
XLA Modules:
  0.0 15.9 jit_solution(16789872593898046133)
XLA Ops:
  0.6 0.0 copy-start.1
  0.6 0.0 copy-start.2
  0.7 0.9 %shard_map.68 = (bf16[1,2,16,1024]{3,2,1,0:T(8,128)(2,1)S(1)}, s32[1,3]{1,0:T(1,128)S(1)}, s32[2,4,8]{2,1,0:T(4,128)S(1)}) custom-call(bf16[1,2,16,2048]{3,2,1,0:T(8,128)(2,1)} %own.1, s32[1,3]{1,0:T(1,128)} %bitcast.3, s32[2,4,8]{2,1,0:T(4,128)} %bitcast.2), custom_call_target="tpu_custom_call" | custom-call | bytes 200000 | tf_op jit(solution)/shard_map/pallas_call | solution.py:195
  1.5 0.0 copy-start
  1.5 4.1 %collective-permute-start.3 = (bf16[1,2,16,1024]{3,2,1,0:T(8,128)(2,1)S(1)}, bf16[1,2,16,1024]{3,2,1,0:T(8,128)(2,1)S(1)}, u32[]{:S(2)}, u32[]{:S(2)}) collective-permute-start(bf16[1,2,16,1024]{3,2,1,0:T(8,128)(2,1)S(1)} %get-tuple-element.19), channel_id=1, source_target_pairs={{0,2},{1,3},{2,0},{3,1},{4,6},{5,7},{6,4},{7,5},{8,10},{9,11},{10,... | collective-permute-start | bytes 196616 | tf_op jit(solution)/shard_map/ppermute | solution.py:207
  5.6 0.0 copy-done.1
  5.6 0.0 copy-done.2
  5.7 2.5 %collective-permute-start = (bf16[1,2,64,256]{3,2,1,0:T(8,128)(2,1)S(1)}, bf16[1,2,64,256]{3,2,1,0:T(8,128)(2,1)S(1)}, u32[]{:S(2)}, u32[]{:S(2)}) collective-permute-start(bf16[1,2,64,256]{3,2,1,0:T(8,128)(2,1)S(1)} %pad_maximum_fusion), channel_id=1, source_target_pairs={{0,24},{4,28},{8,16},{12,20},{16,8},{20,12},{24,0},{28,4},{1,25},{... | collective-permute-start | bytes 196616 | tf_op jit(solution)/shard_map/ppermute | solution.py:211
  8.2 0.5 %collective-permute-start.1 = (bf16[1,2,64,256]{3,2,1,0:T(8,128)(2,1)S(1)}, bf16[1,2,64,256]{3,2,1,0:T(8,128)(2,1)S(1)}, u32[]{:S(2)}, u32[]{:S(2)}) collective-permute-start(bf16[1,2,64,256]{3,2,1,0:T(8,128)(2,1)S(1)} %pad_maximum_fusion), channel_id=1, source_target_pairs={{0,16},{4,20},{8,24},{12,28},{16,0},{20,4},{24,8},{28,12},{1,17},{... | collective-permute-start | bytes 196616 | tf_op jit(solution)/shard_map/ppermute | solution.py:211
  8.7 0.5 %collective-permute-start.2 = (bf16[1,2,64,256]{3,2,1,0:T(8,128)(2,1)S(1)}, bf16[1,2,64,256]{3,2,1,0:T(8,128)(2,1)S(1)}, u32[]{:S(2)}, u32[]{:S(2)}) collective-permute-start(bf16[1,2,64,256]{3,2,1,0:T(8,128)(2,1)S(1)} %pad_maximum_fusion), channel_id=1, source_target_pairs={{0,8},{4,12},{8,0},{12,4},{16,24},{20,28},{24,16},{28,20},{1,9},{5... | collective-permute-start | bytes 196616 | tf_op jit(solution)/shard_map/ppermute | solution.py:211
  9.2 0.0 copy-done
  9.2 0.0 collective-permute-done.3.across
  9.3 1.6 %collective-permute-start.5 = (bf16[2,2,16,512]{3,2,1,0:T(8,128)(2,1)S(1)}, bf16[2,2,16,512]{3,2,1,0:T(8,128)(2,1)S(1)}, u32[]{:S(2)}, u32[]{:S(2)}) collective-permute-start(bf16[2,2,16,512]{3,2,1,0:T(8,128)(2,1)S(1)} %pad_maximum_fusion.1), channel_id=1, source_target_pairs={{0,1},{1,0},{2,3},{3,2},{4,5},{5,4},{6,7},{7,6},{8,9},{9,8},{10,11... | collective-permute-start | bytes 196616 | tf_op jit(solution)/shard_map/ppermute | solution.py:221
  10.9 0.1 collective-permute-done
  11.0 1.4 %collective-permute-done.1 = bf16[1,2,64,256]{3,2,1,0:T(8,128)(2,1)S(1)} collective-permute-done((bf16[1,2,64,256]{3,2,1,0:T(8,128)(2,1)S(1)}, bf16[1,2,64,256]{3,2,1,0:T(8,128)(2,1)S(1)}, u32[]{:S(2)}, u32[]{:S(2)}) %collective-permute-start.1) | collective-permute-done | bytes 65568 | tf_op jit(solution)/shard_map/ppermute | solution.py:211
  12.4 0.5 %collective-permute-done.2 = bf16[1,2,64,256]{3,2,1,0:T(8,128)(2,1)S(1)} collective-permute-done((bf16[1,2,64,256]{3,2,1,0:T(8,128)(2,1)S(1)}, bf16[1,2,64,256]{3,2,1,0:T(8,128)(2,1)S(1)}, u32[]{:S(2)}, u32[]{:S(2)}) %collective-permute-start.2) | collective-permute-done | bytes 65568 | tf_op jit(solution)/shard_map/ppermute | solution.py:211
  13.0 0.1 collective-permute-start.4
  13.1 0.7 %shard_map.69 = (f32[256,128]{1,0:T(8,128)S(1)}, f32[512,128]{1,0:T(8,128)S(1)}, f32[256,128]{1,0:T(8,128)S(1)}, f32[512,128]{1,0:T(8,128)S(1)}, bf16[256,512]{1...) custom-call(s32[1,3]{1,0:T(1,128)S(1)} %get-tuple-element.24.lengths, s32[2,4,8]{2,1,0:T(4,128)S(1)} %get-tuple-element.25.page_slot, ...), custom_call_target="tpu_custom_call" | custom-call | flops 4000000000 | bytes 1000000 | tf_op jit(solution)/shard_map/pallas_call | solution.py:228
  13.8 0.0 collective-permute-done.5.beside
  13.8 0.6 %shard_map.70 = (bf16[2,256,128]{2,1,0:T(8,128)(2,1)S(1)}, f32[2,1,256]{2,1,0:T(1,128)S(1)}, f32[2,1,256]{2,1,0:T(1,128)S(1)}, f32[2,128,256]{2,1,0:T(8,128)S(1)}) custom-call(bf16[1,2,16,2048]{3,2,1,0:T(8,128)(2,1)S(1)} %copy-done, bf16[1,2,16,1024]{3,2,1,0:T(8,128)(2,1)S(1)} %collective-permute-done.3.across, ...), custom_call_target="tpu_custom_call" | custom-call | flops 4000000000 | bytes 1000000 | tf_op jit(solution)/shard_map/pallas_call | solution.py:244
  14.4 0.2 %collective-permute-done.4.far = bf16[4,2,64,256]{3,2,1,0:T(8,128)(2,1)S(1)} collective-permute-done((bf16[4,2,64,256]{3,2,1,0:T(8,128)(2,1)S(1)}, bf16[4,2,64,256]{3,2,1,0:T(8,128)(2,1)S(1)}, u32[]{:S(2)}, u32[]{:S(2)}) %collective-permute-start.4) | collective-permute-done | bytes 262176 | tf_op jit(solution)/shard_map/ppermute | solution.py:223
  14.6 1.3 %shard_map.71 = (bf16[1,2,64,512]{3,2,1,0:T(8,128)(2,1)}, bf16[16,1,16,256]{3,2,1,0:T(8,128)(2,1)}) custom-call(bf16[4,2,64,256]{3,2,1,0:T(8,128)(2,1)S(1)} %collective-permute-done.4.far, f32[256,128]{1,0:T(8,128)S(1)} %get-tuple-element.26.bias_a, f32[512,128]{1,0:T(8,128)S(1)} %get-tuple-element.27.bias_b, ...), custom_call_target="tpu_custom_call" | custom-call | flops 4000000000 | bytes 1000000 | tf_op jit(solution)/shard_map/pallas_call | solution.py:257
  (8 shorter events, 0.1 us)
Async XLA Ops:
  0.6 5.0 %copy-start.1 = (bf16[1,2,64,128]{3,2,1,0:T(8,128)(2,1)S(1)}, bf16[1,2,64,128]{3,2,1,0:T(8,128)(2,1)}, u32[]{:S(2)}) copy-start(bf16[1,2,64,128]{3,2,1,0:T(8,128)(2,1)} %param.7) | copy-start | bytes 98308
  0.6 5.0 %copy-start.2 = (bf16[1,2,64,128]{3,2,1,0:T(8,128)(2,1)S(1)}, bf16[1,2,64,128]{3,2,1,0:T(8,128)(2,1)}, u32[]{:S(2)}) copy-start(bf16[1,2,64,128]{3,2,1,0:T(8,128)(2,1)} %param.6) | copy-start | bytes 98308
  1.5 7.7 %copy-start = (bf16[1,2,16,2048]{3,2,1,0:T(8,128)(2,1)S(1)}, bf16[1,2,16,2048]{3,2,1,0:T(8,128)(2,1)}, u32[]{:S(2)}) copy-start(bf16[1,2,16,2048]{3,2,1,0:T(8,128)(2,1)} %own.1) | copy-start | bytes 393220
  1.5 7.8 %collective-permute-start.3 = (bf16[1,2,16,1024]{3,2,1,0:T(8,128)(2,1)S(1)}, bf16[1,2,16,1024]{3,2,1,0:T(8,128)(2,1)S(1)}, u32[]{:S(2)}, u32[]{:S(2)}) collective-permute-start(bf16[1,2,16,1024]{3,2,1,0:T(8,128)(2,1)S(1)} %get-tuple-element.19), channel_id=1, source_target_pairs={{0,2},{1,3},{2,0},{3,1},{4,6},{5,7},{6,4},{7,5},{8,10},{9,11},{10,... | collective-permute-start | bytes 196616 | tf_op jit(solution)/shard_map/ppermute | solution.py:207
  5.7 5.3 %collective-permute-start = (bf16[1,2,64,256]{3,2,1,0:T(8,128)(2,1)S(1)}, bf16[1,2,64,256]{3,2,1,0:T(8,128)(2,1)S(1)}, u32[]{:S(2)}, u32[]{:S(2)}) collective-permute-start(bf16[1,2,64,256]{3,2,1,0:T(8,128)(2,1)S(1)} %pad_maximum_fusion), channel_id=1, source_target_pairs={{0,24},{4,28},{8,16},{12,20},{16,8},{20,12},{24,0},{28,4},{1,25},{... | collective-permute-start | bytes 196616 | tf_op jit(solution)/shard_map/ppermute | solution.py:211
  8.2 4.3 %collective-permute-start.1 = (bf16[1,2,64,256]{3,2,1,0:T(8,128)(2,1)S(1)}, bf16[1,2,64,256]{3,2,1,0:T(8,128)(2,1)S(1)}, u32[]{:S(2)}, u32[]{:S(2)}) collective-permute-start(bf16[1,2,64,256]{3,2,1,0:T(8,128)(2,1)S(1)} %pad_maximum_fusion), channel_id=1, source_target_pairs={{0,16},{4,20},{8,24},{12,28},{16,0},{20,4},{24,8},{28,12},{1,17},{... | collective-permute-start | bytes 196616 | tf_op jit(solution)/shard_map/ppermute | solution.py:211
  8.7 4.3 %collective-permute-start.2 = (bf16[1,2,64,256]{3,2,1,0:T(8,128)(2,1)S(1)}, bf16[1,2,64,256]{3,2,1,0:T(8,128)(2,1)S(1)}, u32[]{:S(2)}, u32[]{:S(2)}) collective-permute-start(bf16[1,2,64,256]{3,2,1,0:T(8,128)(2,1)S(1)} %pad_maximum_fusion), channel_id=1, source_target_pairs={{0,8},{4,12},{8,0},{12,4},{16,24},{20,28},{24,16},{28,20},{1,9},{5... | collective-permute-start | bytes 196616 | tf_op jit(solution)/shard_map/ppermute | solution.py:211
  9.3 4.5 %collective-permute-start.5 = (bf16[2,2,16,512]{3,2,1,0:T(8,128)(2,1)S(1)}, bf16[2,2,16,512]{3,2,1,0:T(8,128)(2,1)S(1)}, u32[]{:S(2)}, u32[]{:S(2)}) collective-permute-start(bf16[2,2,16,512]{3,2,1,0:T(8,128)(2,1)S(1)} %pad_maximum_fusion.1), channel_id=1, source_target_pairs={{0,1},{1,0},{2,3},{3,2},{4,5},{5,4},{6,7},{7,6},{8,9},{9,8},{10,11... | collective-permute-start | bytes 196616 | tf_op jit(solution)/shard_map/ppermute | solution.py:221
  13.0 1.6 %collective-permute-start.4 = (bf16[4,2,64,256]{3,2,1,0:T(8,128)(2,1)S(1)}, bf16[4,2,64,256]{3,2,1,0:T(8,128)(2,1)S(1)}, u32[]{:S(2)}, u32[]{:S(2)}) collective-permute-start(bf16[4,2,64,256]{3,2,1,0:T(8,128)(2,1)S(1)} %constant_dynamic-update-slice_fusion.near), channel_id=1, source_target_pairs={{0,4},{4,0},{8,12},{12,8},{16,20},{20,16},{24,28},{28,24},{1,5},{5... | collective-permute-start | bytes 786440 | tf_op jit(solution)/shard_map/ppermute | solution.py:223

commit v15 on v14

--- a/solution.py
+++ b/solution.py
@@ -152,11 +152,11 @@
     slot_count = kv_cache.shape[0]
     my_head = lax.axis_index("head")
     sub_tok = block_tok // lax.axis_size("head")
-    scores = {half: score_part(q_rows[half], far, half) for half in (1, 0)}
     moved = place_pages(far_chosen[...], far) + pages_ref[...].astype(jnp.float32)
     pages[...] = moved.astype(jnp.bfloat16).reshape(pages.shape)
     writes = [pltpu.make_async_copy(pages, kv_cache, sems.at[2])]
     writes[0].start()
+    scores = {half: score_part(q_rows[half], far, half) for half in (1, 0)}
     parts = {}
     for half in (1, 0):
         top, total, weights = soften(scores[half], (bias_a, bias_b)[half][...])
@@ -217,7 +217,9 @@
         ],
         axis=0,
     )
-    near = lax.optimization_barrier((near[::-1], beside))[0][::-1]
+    order = (2, 0, 1)
+    sent = lax.optimization_barrier(([near[k] for k in order], beside))[0]
+    near = [sent[order.index(k)] for k in range(len(near))]
     beside = lax.ppermute(beside, "head", [(i, i ^ 1) for i in range(head_count)])
     near = jnp.concatenate([pair] + near, axis=0)
     far = lax.ppermute(near, "blk", [(i, i ^ 1) for i in range(blk_count)])

time: 16.1 us -> 16.1 us (level)
  no operation moved by 1% of the time
where the time goes in v15:
time: 16.1 us; the launch traced here: 16 us
  starting transfers between devices  9.35 us (58%)
  Pallas kernels  3.54 us (22%)
  waiting for transfers between devices  2.26 us (14%)
  between operations  0.73 us (5%)
    ppermute x1, starting transfers between devices, per_device(): across = lax.ppermute(part, 'head', [(i, i ^ 2) for i in range(head_count)])  4.1 us
    ppermute x3, starting transfers between devices, per_device(): lax.ppermute(pair, 'blk', [(i, i ^ d) for i in range(blk_count)])  3.55 us
    ppermute x3, waiting for transfers between devices, per_device(): lax.ppermute(pair, 'blk', [(i, i ^ d) for i in range(blk_count)])  2.04 us
    ppermute x1, starting transfers between devices, per_device(): lax.ppermute(beside, 'head', [(i, i ^ 1) for i in range(head_count)])  1.63 us
    pallas_call x1, Pallas kernels, per_device(): pl.pallas_call(far_kernel, out_shape=(jax.ShapeDtypeStruct((1, 2, block_t...  1.35 us
    pallas_call x1, Pallas kernels, per_device(): pl.pallas_call(fetch_kernel, out_shape=(jax.ShapeDtypeStruct((*query_stat...  0.86 us
    pallas_call x1, Pallas kernels, per_device(): pl.pallas_call(plan_kernel, out_shape=(jax.ShapeDtypeStruct((half_cols, L...  0.72 us
    pallas_call x1, Pallas kernels, per_device(): pl.pallas_call(near_kernel, out_shape=(jax.ShapeDtypeStruct((2, rows, HEA...  0.6 us
  transfers between devices with their start and end apart: 6, of which 4 were waited for; matrix products, arithmetic and copies ran while one was open for 0% of the time, Pallas kernels for 8%

profile of v15, /device:TPU:0, one launch (start us, length us, event | category | flops | bytes accessed | tf_op | source)
XLA Modules:
  0.0 16.0 jit_solution(7780376082115848983)
XLA Ops:
  0.6 0.0 copy-start.1
  0.6 0.0 copy-start.2
  0.7 0.9 %shard_map.68 = (bf16[1,2,16,1024]{3,2,1,0:T(8,128)(2,1)S(1)}, s32[1,3]{1,0:T(1,128)S(1)}, s32[2,4,8]{2,1,0:T(4,128)S(1)}) custom-call(bf16[1,2,16,2048]{3,2,1,0:T(8,128)(2,1)} %own.1, s32[1,3]{1,0:T(1,128)} %bitcast.3, s32[2,4,8]{2,1,0:T(4,128)} %bitcast.2), custom_call_target="tpu_custom_call" | custom-call | bytes 200000 | tf_op jit(solution)/shard_map/pallas_call | solution.py:195
  1.5 0.0 copy-start
  1.5 4.1 %collective-permute-start.3 = (bf16[1,2,16,1024]{3,2,1,0:T(8,128)(2,1)S(1)}, bf16[1,2,16,1024]{3,2,1,0:T(8,128)(2,1)S(1)}, u32[]{:S(2)}, u32[]{:S(2)}) collective-permute-start(bf16[1,2,16,1024]{3,2,1,0:T(8,128)(2,1)S(1)} %get-tuple-element.19), channel_id=1, source_target_pairs={{0,2},{1,3},{2,0},{3,1},{4,6},{5,7},{6,4},{7,5},{8,10},{9,11},{10,... | collective-permute-start | bytes 196616 | tf_op jit(solution)/shard_map/ppermute | solution.py:207
  5.6 0.0 copy-done.1
  5.6 0.0 copy-done.2
  5.7 2.5 %collective-permute-start = (bf16[1,2,64,256]{3,2,1,0:T(8,128)(2,1)S(1)}, bf16[1,2,64,256]{3,2,1,0:T(8,128)(2,1)S(1)}, u32[]{:S(2)}, u32[]{:S(2)}) collective-permute-start(bf16[1,2,64,256]{3,2,1,0:T(8,128)(2,1)S(1)} %pad_maximum_fusion), channel_id=1, source_target_pairs={{0,24},{4,28},{8,16},{12,20},{16,8},{20,12},{24,0},{28,4},{1,25},{... | collective-permute-start | bytes 196616 | tf_op jit(solution)/shard_map/ppermute | solution.py:211
  8.2 0.5 %collective-permute-start.1 = (bf16[1,2,64,256]{3,2,1,0:T(8,128)(2,1)S(1)}, bf16[1,2,64,256]{3,2,1,0:T(8,128)(2,1)S(1)}, u32[]{:S(2)}, u32[]{:S(2)}) collective-permute-start(bf16[1,2,64,256]{3,2,1,0:T(8,128)(2,1)S(1)} %pad_maximum_fusion), channel_id=1, source_target_pairs={{0,8},{4,12},{8,0},{12,4},{16,24},{20,28},{24,16},{28,20},{1,9},{5... | collective-permute-start | bytes 196616 | tf_op jit(solution)/shard_map/ppermute | solution.py:211
  8.7 0.5 %collective-permute-start.2 = (bf16[1,2,64,256]{3,2,1,0:T(8,128)(2,1)S(1)}, bf16[1,2,64,256]{3,2,1,0:T(8,128)(2,1)S(1)}, u32[]{:S(2)}, u32[]{:S(2)}) collective-permute-start(bf16[1,2,64,256]{3,2,1,0:T(8,128)(2,1)S(1)} %pad_maximum_fusion), channel_id=1, source_target_pairs={{0,16},{4,20},{8,24},{12,28},{16,0},{20,4},{24,8},{28,12},{1,17},{... | collective-permute-start | bytes 196616 | tf_op jit(solution)/shard_map/ppermute | solution.py:211
  9.2 0.0 copy-done
  9.2 0.0 collective-permute-done.3.across
  9.3 1.6 %collective-permute-start.5 = (bf16[2,2,16,512]{3,2,1,0:T(8,128)(2,1)S(1)}, bf16[2,2,16,512]{3,2,1,0:T(8,128)(2,1)S(1)}, u32[]{:S(2)}, u32[]{:S(2)}) collective-permute-start(bf16[2,2,16,512]{3,2,1,0:T(8,128)(2,1)S(1)} %pad_maximum_fusion.1), channel_id=1, source_target_pairs={{0,1},{1,0},{2,3},{3,2},{4,5},{5,4},{6,7},{7,6},{8,9},{9,8},{10,11... | collective-permute-start | bytes 196616 | tf_op jit(solution)/shard_map/ppermute | solution.py:223
  10.9 0.6 %collective-permute-done = bf16[1,2,64,256]{3,2,1,0:T(8,128)(2,1)S(1)} collective-permute-done((bf16[1,2,64,256]{3,2,1,0:T(8,128)(2,1)S(1)}, bf16[1,2,64,256]{3,2,1,0:T(8,128)(2,1)S(1)}, u32[]{:S(2)}, u32[]{:S(2)}) %collective-permute-start) | collective-permute-done | bytes 65568 | tf_op jit(solution)/shard_map/ppermute | solution.py:211
  11.5 0.9 %collective-permute-done.1 = bf16[1,2,64,256]{3,2,1,0:T(8,128)(2,1)S(1)} collective-permute-done((bf16[1,2,64,256]{3,2,1,0:T(8,128)(2,1)S(1)}, bf16[1,2,64,256]{3,2,1,0:T(8,128)(2,1)S(1)}, u32[]{:S(2)}, u32[]{:S(2)}) %collective-permute-start.1) | collective-permute-done | bytes 65568 | tf_op jit(solution)/shard_map/ppermute | solution.py:211
  12.4 0.5 %collective-permute-done.2 = bf16[1,2,64,256]{3,2,1,0:T(8,128)(2,1)S(1)} collective-permute-done((bf16[1,2,64,256]{3,2,1,0:T(8,128)(2,1)S(1)}, bf16[1,2,64,256]{3,2,1,0:T(8,128)(2,1)S(1)}, u32[]{:S(2)}, u32[]{:S(2)}) %collective-permute-start.2) | collective-permute-done | bytes 65568 | tf_op jit(solution)/shard_map/ppermute | solution.py:211
  13.0 0.1 collective-permute-start.4
  13.1 0.7 %shard_map.69 = (f32[256,128]{1,0:T(8,128)S(1)}, f32[512,128]{1,0:T(8,128)S(1)}, f32[256,128]{1,0:T(8,128)S(1)}, f32[512,128]{1,0:T(8,128)S(1)}, bf16[256,512]{1...) custom-call(s32[1,3]{1,0:T(1,128)S(1)} %get-tuple-element.24.lengths, s32[2,4,8]{2,1,0:T(4,128)S(1)} %get-tuple-element.25.page_slot, ...), custom_call_target="tpu_custom_call" | custom-call | flops 4000000000 | bytes 1000000 | tf_op jit(solution)/shard_map/pallas_call | solution.py:230
  13.8 0.0 collective-permute-done.5.beside
  13.8 0.6 %shard_map.70 = (bf16[2,256,128]{2,1,0:T(8,128)(2,1)S(1)}, f32[2,1,256]{2,1,0:T(1,128)S(1)}, f32[2,1,256]{2,1,0:T(1,128)S(1)}, f32[2,128,256]{2,1,0:T(8,128)S(1)}) custom-call(bf16[1,2,16,2048]{3,2,1,0:T(8,128)(2,1)S(1)} %copy-done, bf16[1,2,16,1024]{3,2,1,0:T(8,128)(2,1)S(1)} %collective-permute-done.3.across, ...), custom_call_target="tpu_custom_call" | custom-call | flops 4000000000 | bytes 1000000 | tf_op jit(solution)/shard_map/pallas_call | solution.py:246
  14.4 0.2 %collective-permute-done.4.far = bf16[4,2,64,256]{3,2,1,0:T(8,128)(2,1)S(1)} collective-permute-done((bf16[4,2,64,256]{3,2,1,0:T(8,128)(2,1)S(1)}, bf16[4,2,64,256]{3,2,1,0:T(8,128)(2,1)S(1)}, u32[]{:S(2)}, u32[]{:S(2)}) %collective-permute-start.4) | collective-permute-done | bytes 262176 | tf_op jit(solution)/shard_map/ppermute | solution.py:225
  14.6 1.3 %shard_map.71 = (bf16[1,2,64,512]{3,2,1,0:T(8,128)(2,1)}, bf16[16,1,16,256]{3,2,1,0:T(8,128)(2,1)}) custom-call(bf16[4,2,64,256]{3,2,1,0:T(8,128)(2,1)S(1)} %collective-permute-done.4.far, f32[256,128]{1,0:T(8,128)S(1)} %get-tuple-element.26.bias_a, f32[512,128]{1,0:T(8,128)S(1)} %get-tuple-element.27.bias_b, ...), custom_call_target="tpu_custom_call" | custom-call | flops 4000000000 | bytes 1000000 | tf_op jit(solution)/shard_map/pallas_call | solution.py:259
  (8 shorter events, 0.1 us)
Async XLA Ops:
  0.6 5.0 %copy-start.1 = (bf16[1,2,64,128]{3,2,1,0:T(8,128)(2,1)S(1)}, bf16[1,2,64,128]{3,2,1,0:T(8,128)(2,1)}, u32[]{:S(2)}) copy-start(bf16[1,2,64,128]{3,2,1,0:T(8,128)(2,1)} %param.7) | copy-start | bytes 98308
  0.6 5.0 %copy-start.2 = (bf16[1,2,64,128]{3,2,1,0:T(8,128)(2,1)S(1)}, bf16[1,2,64,128]{3,2,1,0:T(8,128)(2,1)}, u32[]{:S(2)}) copy-start(bf16[1,2,64,128]{3,2,1,0:T(8,128)(2,1)} %param.6) | copy-start | bytes 98308
  1.5 7.7 %copy-start = (bf16[1,2,16,2048]{3,2,1,0:T(8,128)(2,1)S(1)}, bf16[1,2,16,2048]{3,2,1,0:T(8,128)(2,1)}, u32[]{:S(2)}) copy-start(bf16[1,2,16,2048]{3,2,1,0:T(8,128)(2,1)} %own.1) | copy-start | bytes 393220
  1.5 7.8 %collective-permute-start.3 = (bf16[1,2,16,1024]{3,2,1,0:T(8,128)(2,1)S(1)}, bf16[1,2,16,1024]{3,2,1,0:T(8,128)(2,1)S(1)}, u32[]{:S(2)}, u32[]{:S(2)}) collective-permute-start(bf16[1,2,16,1024]{3,2,1,0:T(8,128)(2,1)S(1)} %get-tuple-element.19), channel_id=1, source_target_pairs={{0,2},{1,3},{2,0},{3,1},{4,6},{5,7},{6,4},{7,5},{8,10},{9,11},{10,... | collective-permute-start | bytes 196616 | tf_op jit(solution)/shard_map/ppermute | solution.py:207
  5.7 5.8 %collective-permute-start = (bf16[1,2,64,256]{3,2,1,0:T(8,128)(2,1)S(1)}, bf16[1,2,64,256]{3,2,1,0:T(8,128)(2,1)S(1)}, u32[]{:S(2)}, u32[]{:S(2)}) collective-permute-start(bf16[1,2,64,256]{3,2,1,0:T(8,128)(2,1)S(1)} %pad_maximum_fusion), channel_id=1, source_target_pairs={{0,24},{4,28},{8,16},{12,20},{16,8},{20,12},{24,0},{28,4},{1,25},{... | collective-permute-start | bytes 196616 | tf_op jit(solution)/shard_map/ppermute | solution.py:211
  8.2 4.3 %collective-permute-start.1 = (bf16[1,2,64,256]{3,2,1,0:T(8,128)(2,1)S(1)}, bf16[1,2,64,256]{3,2,1,0:T(8,128)(2,1)S(1)}, u32[]{:S(2)}, u32[]{:S(2)}) collective-permute-start(bf16[1,2,64,256]{3,2,1,0:T(8,128)(2,1)S(1)} %pad_maximum_fusion), channel_id=1, source_target_pairs={{0,8},{4,12},{8,0},{12,4},{16,24},{20,28},{24,16},{28,20},{1,9},{5... | collective-permute-start | bytes 196616 | tf_op jit(solution)/shard_map/ppermute | solution.py:211
  8.7 4.3 %collective-permute-start.2 = (bf16[1,2,64,256]{3,2,1,0:T(8,128)(2,1)S(1)}, bf16[1,2,64,256]{3,2,1,0:T(8,128)(2,1)S(1)}, u32[]{:S(2)}, u32[]{:S(2)}) collective-permute-start(bf16[1,2,64,256]{3,2,1,0:T(8,128)(2,1)S(1)} %pad_maximum_fusion), channel_id=1, source_target_pairs={{0,16},{4,20},{8,24},{12,28},{16,0},{20,4},{24,8},{28,12},{1,17},{... | collective-permute-start | bytes 196616 | tf_op jit(solution)/shard_map/ppermute | solution.py:211
  9.3 4.5 %collective-permute-start.5 = (bf16[2,2,16,512]{3,2,1,0:T(8,128)(2,1)S(1)}, bf16[2,2,16,512]{3,2,1,0:T(8,128)(2,1)S(1)}, u32[]{:S(2)}, u32[]{:S(2)}) collective-permute-start(bf16[2,2,16,512]{3,2,1,0:T(8,128)(2,1)S(1)} %pad_maximum_fusion.1), channel_id=1, source_target_pairs={{0,1},{1,0},{2,3},{3,2},{4,5},{5,4},{6,7},{7,6},{8,9},{9,8},{10,11... | collective-permute-start | bytes 196616 | tf_op jit(solution)/shard_map/ppermute | solution.py:223
  13.0 1.6 %collective-permute-start.4 = (bf16[4,2,64,256]{3,2,1,0:T(8,128)(2,1)S(1)}, bf16[4,2,64,256]{3,2,1,0:T(8,128)(2,1)S(1)}, u32[]{:S(2)}, u32[]{:S(2)}) collective-permute-start(bf16[4,2,64,256]{3,2,1,0:T(8,128)(2,1)S(1)} %constant_dynamic-update-slice_fusion.near), channel_id=1, source_target_pairs={{0,4},{4,0},{8,12},{12,8},{16,20},{20,16},{24,28},{28,24},{1,5},{5... | collective-permute-start | bytes 786440 | tf_op jit(solution)/shard_map/ppermute | solution.py:225

commit v16 on v14

--- a/solution.py
+++ b/solution.py
@@ -130,7 +130,13 @@
     bias = functools.partial(key_bias, my_blk, lengths[...], chips, block_tok, sub_tok)
     for half in range(2):
         (bias_a, bias_b)[half][...] = bias(half, 0)
-        (far_bias_a, far_bias_b)[half][...] = bias(half, 1)
+    first, second = bias(0, 1), bias(1, 1)
+    for m in range(chips):
+        rows = slice(m * block_tok, (m + 1) * block_tok)
+        far_bias_a[rows] = second[2 * m * block_tok : (2 * m + 1) * block_tok]
+        far_bias_b[rows] = jnp.where(
+            (my_blk ^ 1 ^ (2 * m)) < my_blk, first[rows], second[(2 * m + 1) * block_tok : (2 * m + 2) * block_tok]
+        )
 
 
 def near_kernel(own, across, beside, near, bias_a, bias_b, q_rows, top_ref, total_ref, out_ref):
@@ -157,10 +163,47 @@
     pages[...] = moved.astype(jnp.bfloat16).reshape(pages.shape)
     writes = [pltpu.make_async_copy(pages, kv_cache, sems.at[2])]
     writes[0].start()
-    parts = {}
-    for half in (1, 0):
-        top, total, weights = soften(scores[half], (bias_a, bias_b)[half][...])
-        parts[half] = (top, total, weigh_part(weights, far, half))
+    my_blk = lax.axis_index("blk")
+    chips = far.shape[0]
+    early = [(my_blk ^ 1 ^ (2 * m)) < my_blk for m in range(chips)]
+    scale = HEAD_DIM**-0.5 * LOG2E
+    wide = scores[1].shape[1] // LANES
+
+    def block(array, k):
+        return array[k * block_tok : (k + 1) * block_tok]
+
+    def masked(rows, bias):
+        return rows * scale + jnp.concatenate([bias] * wide, axis=1)
+
+    base = [masked(block(scores[1], 2 * m), bias_a[m * block_tok : (m + 1) * block_tok]) for m in range(chips)]
+    pick = [
+        masked(
+            jnp.where(early[m], block(scores[0], m), block(scores[1], 2 * m + 1)),
+            bias_b[m * block_tok : (m + 1) * block_tok],
+        )
+        for m in range(chips)
+    ]
+    peak = [jnp.max(x, axis=0, keepdims=True) for x in pick]
+    none = jnp.full_like(peak[0], -1e30)
+    tops = [none, functools.reduce(jnp.maximum, [jnp.max(x, axis=0, keepdims=True) for x in base])]
+    for m in range(chips):
+        tops[0] = jnp.maximum(tops[0], jnp.where(early[m], peak[m], none))
+        tops[1] = jnp.maximum(tops[1], jnp.where(early[m], none, peak[m]))
+    sums = [jnp.zeros_like(none), jnp.zeros_like(none)]
+    weights = [[], []]
+    for m in range(chips):
+        low = jnp.exp2(base[m] - tops[1])
+        one = jnp.exp2(pick[m] - jnp.where(early[m], tops[0], tops[1]))
+        part = jnp.sum(one, axis=0, keepdims=True)
+        sums[0] = sums[0] + jnp.where(early[m], part, 0.0)
+        sums[1] = sums[1] + jnp.sum(low, axis=0, keepdims=True) + jnp.where(early[m], 0.0, part)
+        one = one.astype(jnp.bfloat16)
+        zero = jnp.zeros_like(one)
+        weights[0].append(jnp.where(early[m], one, zero))
+        weights[1] += [low.astype(jnp.bfloat16), jnp.where(early[m], zero, one)]
+    parts = {
+        half: (tops[half], sums[half], weigh_part(jnp.concatenate(weights[half], axis=0), far, half)) for half in (1, 0)
+    }
     for half in (1, 0):
         top, total, out = parts[half]
         best = jnp.maximum(top, top_ref[half])
@@ -230,8 +273,9 @@
         out_shape=(
             jax.ShapeDtypeStruct((half_cols, LANES), jnp.float32),
             jax.ShapeDtypeStruct((2 * half_cols, LANES), jnp.float32),
-        )
-        * 2
+            jax.ShapeDtypeStruct((half_cols, LANES), jnp.float32),
+            jax.ShapeDtypeStruct((half_cols, LANES), jnp.float32),
+        )
         + (
             jax.ShapeDtypeStruct((slot_count * PAGE, 2 * half_cols), jnp.bfloat16),
             jax.ShapeDtypeStruct((slot_count * PAGE, 2 * HEAD_DIM), jnp.bfloat16),

time: 16.1 us -> 16.1 us (level)
  no operation moved by 1% of the time
where the time goes in v16:
time: 16.1 us; the launch traced here: 15.9 us
  starting transfers between devices  9.35 us (58%)
  Pallas kernels  3.53 us (22%)
  waiting for transfers between devices  2.22 us (14%)
  between operations  0.73 us (5%)
    ppermute x1, starting transfers between devices, per_device(): across = lax.ppermute(part, 'head', [(i, i ^ 2) for i in range(head_count)])  4.1 us
    ppermute x3, starting transfers between devices, per_device(): lax.ppermute(pair, 'blk', [(i, i ^ d) for i in range(blk_count)])  3.55 us
    ppermute x3, waiting for transfers between devices, per_device(): lax.ppermute(pair, 'blk', [(i, i ^ d) for i in range(blk_count)])  2.01 us
    ppermute x1, starting transfers between devices, per_device(): lax.ppermute(beside, 'head', [(i, i ^ 1) for i in range(head_count)])  1.63 us
    pallas_call x1, Pallas kernels, per_device(): pl.pallas_call(far_kernel, out_shape=(jax.ShapeDtypeStruct((1, 2, block_t...  1.33 us
    pallas_call x1, Pallas kernels, per_device(): pl.pallas_call(fetch_kernel, out_shape=(jax.ShapeDtypeStruct((*query_stat...  0.86 us
    pallas_call x1, Pallas kernels, per_device(): pl.pallas_call(plan_kernel, out_shape=(jax.ShapeDtypeStruct((half_cols, L...  0.73 us
    pallas_call x1, Pallas kernels, per_device(): pl.pallas_call(near_kernel, out_shape=(jax.ShapeDtypeStruct((2, rows, HEA...  0.61 us
  transfers between devices with their start and end apart: 6, of which 4 were waited for; matrix products, arithmetic and copies ran while one was open for 0% of the time, Pallas kernels for 8%

profile of v16, /device:TPU:0, one launch (start us, length us, event | category | flops | bytes accessed | tf_op | source)
XLA Modules:
  0.0 15.9 jit_solution(5435440097756042651)
XLA Ops:
  0.6 0.0 copy-start.1
  0.6 0.0 copy-start.2
  0.7 0.9 %shard_map.68 = (bf16[1,2,16,1024]{3,2,1,0:T(8,128)(2,1)S(1)}, s32[1,3]{1,0:T(1,128)S(1)}, s32[2,4,8]{2,1,0:T(4,128)S(1)}) custom-call(bf16[1,2,16,2048]{3,2,1,0:T(8,128)(2,1)} %own.1, s32[1,3]{1,0:T(1,128)} %bitcast.3, s32[2,4,8]{2,1,0:T(4,128)} %bitcast.2), custom_call_target="tpu_custom_call" | custom-call | bytes 200000 | tf_op jit(solution)/shard_map/pallas_call | solution.py:238
  1.5 0.0 copy-start
  1.5 4.1 %collective-permute-start.3 = (bf16[1,2,16,1024]{3,2,1,0:T(8,128)(2,1)S(1)}, bf16[1,2,16,1024]{3,2,1,0:T(8,128)(2,1)S(1)}, u32[]{:S(2)}, u32[]{:S(2)}) collective-permute-start(bf16[1,2,16,1024]{3,2,1,0:T(8,128)(2,1)S(1)} %get-tuple-element.19), channel_id=1, source_target_pairs={{0,2},{1,3},{2,0},{3,1},{4,6},{5,7},{6,4},{7,5},{8,10},{9,11},{10,... | collective-permute-start | bytes 196616 | tf_op jit(solution)/shard_map/ppermute | solution.py:250
  5.6 0.0 copy-done.1
  5.6 0.0 copy-done.2
  5.7 2.5 %collective-permute-start = (bf16[1,2,64,256]{3,2,1,0:T(8,128)(2,1)S(1)}, bf16[1,2,64,256]{3,2,1,0:T(8,128)(2,1)S(1)}, u32[]{:S(2)}, u32[]{:S(2)}) collective-permute-start(bf16[1,2,64,256]{3,2,1,0:T(8,128)(2,1)S(1)} %pad_maximum_fusion), channel_id=1, source_target_pairs={{0,24},{4,28},{8,16},{12,20},{16,8},{20,12},{24,0},{28,4},{1,25},{... | collective-permute-start | bytes 196616 | tf_op jit(solution)/shard_map/ppermute | solution.py:254
  8.2 0.5 %collective-permute-start.1 = (bf16[1,2,64,256]{3,2,1,0:T(8,128)(2,1)S(1)}, bf16[1,2,64,256]{3,2,1,0:T(8,128)(2,1)S(1)}, u32[]{:S(2)}, u32[]{:S(2)}) collective-permute-start(bf16[1,2,64,256]{3,2,1,0:T(8,128)(2,1)S(1)} %pad_maximum_fusion), channel_id=1, source_target_pairs={{0,16},{4,20},{8,24},{12,28},{16,0},{20,4},{24,8},{28,12},{1,17},{... | collective-permute-start | bytes 196616 | tf_op jit(solution)/shard_map/ppermute | solution.py:254
  8.7 0.5 %collective-permute-start.2 = (bf16[1,2,64,256]{3,2,1,0:T(8,128)(2,1)S(1)}, bf16[1,2,64,256]{3,2,1,0:T(8,128)(2,1)S(1)}, u32[]{:S(2)}, u32[]{:S(2)}) collective-permute-start(bf16[1,2,64,256]{3,2,1,0:T(8,128)(2,1)S(1)} %pad_maximum_fusion), channel_id=1, source_target_pairs={{0,8},{4,12},{8,0},{12,4},{16,24},{20,28},{24,16},{28,20},{1,9},{5... | collective-permute-start | bytes 196616 | tf_op jit(solution)/shard_map/ppermute | solution.py:254
  9.2 0.0 copy-done
  9.2 0.0 collective-permute-done.3.across
  9.3 1.6 %collective-permute-start.5 = (bf16[2,2,16,512]{3,2,1,0:T(8,128)(2,1)S(1)}, bf16[2,2,16,512]{3,2,1,0:T(8,128)(2,1)S(1)}, u32[]{:S(2)}, u32[]{:S(2)}) collective-permute-start(bf16[2,2,16,512]{3,2,1,0:T(8,128)(2,1)S(1)} %pad_maximum_fusion.1), channel_id=1, source_target_pairs={{0,1},{1,0},{2,3},{3,2},{4,5},{5,4},{6,7},{7,6},{8,9},{9,8},{10,11... | collective-permute-start | bytes 196616 | tf_op jit(solution)/shard_map/ppermute | solution.py:264
  10.9 0.1 collective-permute-done
  11.0 1.4 %collective-permute-done.1 = bf16[1,2,64,256]{3,2,1,0:T(8,128)(2,1)S(1)} collective-permute-done((bf16[1,2,64,256]{3,2,1,0:T(8,128)(2,1)S(1)}, bf16[1,2,64,256]{3,2,1,0:T(8,128)(2,1)S(1)}, u32[]{:S(2)}, u32[]{:S(2)}) %collective-permute-start.1) | collective-permute-done | bytes 65568 | tf_op jit(solution)/shard_map/ppermute | solution.py:254
  12.4 0.5 %collective-permute-done.2 = bf16[1,2,64,256]{3,2,1,0:T(8,128)(2,1)S(1)} collective-permute-done((bf16[1,2,64,256]{3,2,1,0:T(8,128)(2,1)S(1)}, bf16[1,2,64,256]{3,2,1,0:T(8,128)(2,1)S(1)}, u32[]{:S(2)}, u32[]{:S(2)}) %collective-permute-start.2) | collective-permute-done | bytes 65568 | tf_op jit(solution)/shard_map/ppermute | solution.py:254
  13.0 0.1 collective-permute-start.4
  13.1 0.7 %shard_map.69 = (f32[256,128]{1,0:T(8,128)S(1)}, f32[512,128]{1,0:T(8,128)S(1)}, f32[256,128]{1,0:T(8,128)S(1)}, f32[256,128]{1,0:T(8,128)S(1)}, bf16[256,512]{1...) custom-call(s32[1,3]{1,0:T(1,128)S(1)} %get-tuple-element.24.lengths, s32[2,4,8]{2,1,0:T(4,128)S(1)} %get-tuple-element.25.page_slot, ...), custom_call_target="tpu_custom_call" | custom-call | flops 4000000000 | bytes 1000000 | tf_op jit(solution)/shard_map/pallas_call | solution.py:271
  13.8 0.0 collective-permute-done.5.beside
  13.8 0.6 %shard_map.70 = (bf16[2,256,128]{2,1,0:T(8,128)(2,1)S(1)}, f32[2,1,256]{2,1,0:T(1,128)S(1)}, f32[2,1,256]{2,1,0:T(1,128)S(1)}, f32[2,128,256]{2,1,0:T(8,128)S(1)}) custom-call(bf16[1,2,16,2048]{3,2,1,0:T(8,128)(2,1)S(1)} %copy-done, bf16[1,2,16,1024]{3,2,1,0:T(8,128)(2,1)S(1)} %collective-permute-done.3.across, ...), custom_call_target="tpu_custom_call" | custom-call | flops 4000000000 | bytes 1000000 | tf_op jit(solution)/shard_map/pallas_call | solution.py:288
  14.4 0.2 %collective-permute-done.4.far = bf16[4,2,64,256]{3,2,1,0:T(8,128)(2,1)S(1)} collective-permute-done((bf16[4,2,64,256]{3,2,1,0:T(8,128)(2,1)S(1)}, bf16[4,2,64,256]{3,2,1,0:T(8,128)(2,1)S(1)}, u32[]{:S(2)}, u32[]{:S(2)}) %collective-permute-start.4) | collective-permute-done | bytes 262176 | tf_op jit(solution)/shard_map/ppermute | solution.py:266
  14.6 1.3 %shard_map.71 = (bf16[1,2,64,512]{3,2,1,0:T(8,128)(2,1)}, bf16[16,1,16,256]{3,2,1,0:T(8,128)(2,1)}) custom-call(bf16[4,2,64,256]{3,2,1,0:T(8,128)(2,1)S(1)} %collective-permute-done.4.far, f32[256,128]{1,0:T(8,128)S(1)} %get-tuple-element.26.bias_a, f32[256,128]{1,0:T(8,128)S(1)} %get-tuple-element.27.bias_b, ...), custom_call_target="tpu_custom_call" | custom-call | flops 4000000000 | bytes 1000000 | tf_op jit(solution)/shard_map/pallas_call | solution.py:301
  (8 shorter events, 0.1 us)
Async XLA Ops:
  0.6 5.0 %copy-start.1 = (bf16[1,2,64,128]{3,2,1,0:T(8,128)(2,1)S(1)}, bf16[1,2,64,128]{3,2,1,0:T(8,128)(2,1)}, u32[]{:S(2)}) copy-start(bf16[1,2,64,128]{3,2,1,0:T(8,128)(2,1)} %param.7) | copy-start | bytes 98308
  0.6 5.0 %copy-start.2 = (bf16[1,2,64,128]{3,2,1,0:T(8,128)(2,1)S(1)}, bf16[1,2,64,128]{3,2,1,0:T(8,128)(2,1)}, u32[]{:S(2)}) copy-start(bf16[1,2,64,128]{3,2,1,0:T(8,128)(2,1)} %param.6) | copy-start | bytes 98308
  1.5 7.7 %copy-start = (bf16[1,2,16,2048]{3,2,1,0:T(8,128)(2,1)S(1)}, bf16[1,2,16,2048]{3,2,1,0:T(8,128)(2,1)}, u32[]{:S(2)}) copy-start(bf16[1,2,16,2048]{3,2,1,0:T(8,128)(2,1)} %own.1) | copy-start | bytes 393220
  1.5 7.8 %collective-permute-start.3 = (bf16[1,2,16,1024]{3,2,1,0:T(8,128)(2,1)S(1)}, bf16[1,2,16,1024]{3,2,1,0:T(8,128)(2,1)S(1)}, u32[]{:S(2)}, u32[]{:S(2)}) collective-permute-start(bf16[1,2,16,1024]{3,2,1,0:T(8,128)(2,1)S(1)} %get-tuple-element.19), channel_id=1, source_target_pairs={{0,2},{1,3},{2,0},{3,1},{4,6},{5,7},{6,4},{7,5},{8,10},{9,11},{10,... | collective-permute-start | bytes 196616 | tf_op jit(solution)/shard_map/ppermute | solution.py:250
  5.7 5.3 %collective-permute-start = (bf16[1,2,64,256]{3,2,1,0:T(8,128)(2,1)S(1)}, bf16[1,2,64,256]{3,2,1,0:T(8,128)(2,1)S(1)}, u32[]{:S(2)}, u32[]{:S(2)}) collective-permute-start(bf16[1,2,64,256]{3,2,1,0:T(8,128)(2,1)S(1)} %pad_maximum_fusion), channel_id=1, source_target_pairs={{0,24},{4,28},{8,16},{12,20},{16,8},{20,12},{24,0},{28,4},{1,25},{... | collective-permute-start | bytes 196616 | tf_op jit(solution)/shard_map/ppermute | solution.py:254
  8.2 4.3 %collective-permute-start.1 = (bf16[1,2,64,256]{3,2,1,0:T(8,128)(2,1)S(1)}, bf16[1,2,64,256]{3,2,1,0:T(8,128)(2,1)S(1)}, u32[]{:S(2)}, u32[]{:S(2)}) collective-permute-start(bf16[1,2,64,256]{3,2,1,0:T(8,128)(2,1)S(1)} %pad_maximum_fusion), channel_id=1, source_target_pairs={{0,16},{4,20},{8,24},{12,28},{16,0},{20,4},{24,8},{28,12},{1,17},{... | collective-permute-start | bytes 196616 | tf_op jit(solution)/shard_map/ppermute | solution.py:254
  8.7 4.3 %collective-permute-start.2 = (bf16[1,2,64,256]{3,2,1,0:T(8,128)(2,1)S(1)}, bf16[1,2,64,256]{3,2,1,0:T(8,128)(2,1)S(1)}, u32[]{:S(2)}, u32[]{:S(2)}) collective-permute-start(bf16[1,2,64,256]{3,2,1,0:T(8,128)(2,1)S(1)} %pad_maximum_fusion), channel_id=1, source_target_pairs={{0,8},{4,12},{8,0},{12,4},{16,24},{20,28},{24,16},{28,20},{1,9},{5... | collective-permute-start | bytes 196616 | tf_op jit(solution)/shard_map/ppermute | solution.py:254
  9.3 4.5 %collective-permute-start.5 = (bf16[2,2,16,512]{3,2,1,0:T(8,128)(2,1)S(1)}, bf16[2,2,16,512]{3,2,1,0:T(8,128)(2,1)S(1)}, u32[]{:S(2)}, u32[]{:S(2)}) collective-permute-start(bf16[2,2,16,512]{3,2,1,0:T(8,128)(2,1)S(1)} %pad_maximum_fusion.1), channel_id=1, source_target_pairs={{0,1},{1,0},{2,3},{3,2},{4,5},{5,4},{6,7},{7,6},{8,9},{9,8},{10,11... | collective-permute-start | bytes 196616 | tf_op jit(solution)/shard_map/ppermute | solution.py:264
  13.0 1.6 %collective-permute-start.4 = (bf16[4,2,64,256]{3,2,1,0:T(8,128)(2,1)S(1)}, bf16[4,2,64,256]{3,2,1,0:T(8,128)(2,1)S(1)}, u32[]{:S(2)}, u32[]{:S(2)}) collective-permute-start(bf16[4,2,64,256]{3,2,1,0:T(8,128)(2,1)S(1)} %constant_dynamic-update-slice_fusion.near), channel_id=1, source_target_pairs={{0,4},{4,0},{8,12},{12,8},{16,20},{20,16},{24,28},{28,24},{1,5},{5... | collective-permute-start | bytes 786440 | tf_op jit(solution)/shard_map/ppermute | solution.py:266

commit v17 on v16

--- a/solution.py
+++ b/solution.py
@@ -105,11 +105,12 @@
 def fetch_kernel(queries, lengths, page_slot, part, lengths_out, slots_out, sems):
     _, halves, _, width = part.shape
     start = ((lax.axis_index("head") & 2) ^ 2) * (width // 2)
-    pairs = [(lengths, lengths_out), (page_slot, slots_out)]
+    pairs = []
     for half in range(halves):
         for lane in range(0, width, width // 2):
             lanes = pl.ds(pl.multiple_of(start + lane, width // 2), width // 2)
             pairs.append((queries.at[0, half, :, lanes], part.at[0, half, :, lane : lane + width // 2]))
+    pairs += [(lengths, lengths_out), (page_slot, slots_out)]
     copies = [pltpu.make_async_copy(a, b, sems.at[k]) for k, (a, b) in enumerate(pairs)]
     for copy in copies:
         copy.start()
@@ -202,9 +203,9 @@
         weights[0].append(jnp.where(early[m], one, zero))
         weights[1] += [low.astype(jnp.bfloat16), jnp.where(early[m], zero, one)]
     parts = {
-        half: (tops[half], sums[half], weigh_part(jnp.concatenate(weights[half], axis=0), far, half)) for half in (1, 0)
+        half: (tops[half], sums[half], weigh_part(jnp.concatenate(weights[half], axis=0), far, half)) for half in range(2)
     }
-    for half in (1, 0):
+    for half in range(2):
         top, total, out = parts[half]
         best = jnp.maximum(top, top_ref[half])
         here = jnp.exp2(top - best)

time: 16.1 us -> 16.1 us (level)
  no operation moved by 1% of the time
where the time goes in v17:
time: 16.1 us; the launch traced here: 15.9 us
  starting transfers between devices  9.35 us (58%)
  Pallas kernels  3.52 us (22%)
  waiting for transfers between devices  2.22 us (14%)
  between operations  0.73 us (5%)
    ppermute x1, starting transfers between devices, per_device(): across = lax.ppermute(part, 'head', [(i, i ^ 2) for i in range(head_count)])  4.1 us
    ppermute x3, starting transfers between devices, per_device(): lax.ppermute(pair, 'blk', [(i, i ^ d) for i in range(blk_count)])  3.55 us
    ppermute x3, waiting for transfers between devices, per_device(): lax.ppermute(pair, 'blk', [(i, i ^ d) for i in range(blk_count)])  2.01 us
    ppermute x1, starting transfers between devices, per_device(): lax.ppermute(beside, 'head', [(i, i ^ 1) for i in range(head_count)])  1.63 us
    pallas_call x1, Pallas kernels, per_device(): pl.pallas_call(far_kernel, out_shape=(jax.ShapeDtypeStruct((1, 2, block_t...  1.35 us
    pallas_call x1, Pallas kernels, per_device(): pl.pallas_call(fetch_kernel, out_shape=(jax.ShapeDtypeStruct((*query_stat...  0.84 us
    pallas_call x1, Pallas kernels, per_device(): pl.pallas_call(plan_kernel, out_shape=(jax.ShapeDtypeStruct((half_cols, L...  0.73 us
    pallas_call x1, Pallas kernels, per_device(): pl.pallas_call(near_kernel, out_shape=(jax.ShapeDtypeStruct((2, rows, HEA...  0.61 us
  transfers between devices with their start and end apart: 6, of which 4 were waited for; matrix products, arithmetic and copies ran while one was open for 0% of the time, Pallas kernels for 8%

profile of v17, /device:TPU:0, one launch (start us, length us, event | category | flops | bytes accessed | tf_op | source)
XLA Modules:
  0.0 15.9 jit_solution(7756904531500943634)
XLA Ops:
  0.6 0.0 copy-start.1
  0.6 0.0 copy-start.2
  0.7 0.8 %shard_map.68 = (bf16[1,2,16,1024]{3,2,1,0:T(8,128)(2,1)S(1)}, s32[1,3]{1,0:T(1,128)S(1)}, s32[2,4,8]{2,1,0:T(4,128)S(1)}) custom-call(bf16[1,2,16,2048]{3,2,1,0:T(8,128)(2,1)} %own.1, s32[1,3]{1,0:T(1,128)} %bitcast.3, s32[2,4,8]{2,1,0:T(4,128)} %bitcast.2), custom_call_target="tpu_custom_call" | custom-call | bytes 200000 | tf_op jit(solution)/shard_map/pallas_call | solution.py:239
  1.5 0.0 copy-start
  1.5 4.1 %collective-permute-start.3 = (bf16[1,2,16,1024]{3,2,1,0:T(8,128)(2,1)S(1)}, bf16[1,2,16,1024]{3,2,1,0:T(8,128)(2,1)S(1)}, u32[]{:S(2)}, u32[]{:S(2)}) collective-permute-start(bf16[1,2,16,1024]{3,2,1,0:T(8,128)(2,1)S(1)} %get-tuple-element.19), channel_id=1, source_target_pairs={{0,2},{1,3},{2,0},{3,1},{4,6},{5,7},{6,4},{7,5},{8,10},{9,11},{10,... | collective-permute-start | bytes 196616 | tf_op jit(solution)/shard_map/ppermute | solution.py:251
  5.6 0.0 copy-done.1
  5.6 0.0 copy-done.2
  5.6 2.5 %collective-permute-start = (bf16[1,2,64,256]{3,2,1,0:T(8,128)(2,1)S(1)}, bf16[1,2,64,256]{3,2,1,0:T(8,128)(2,1)S(1)}, u32[]{:S(2)}, u32[]{:S(2)}) collective-permute-start(bf16[1,2,64,256]{3,2,1,0:T(8,128)(2,1)S(1)} %pad_maximum_fusion), channel_id=1, source_target_pairs={{0,24},{4,28},{8,16},{12,20},{16,8},{20,12},{24,0},{28,4},{1,25},{... | collective-permute-start | bytes 196616 | tf_op jit(solution)/shard_map/ppermute | solution.py:255
  8.1 0.5 %collective-permute-start.1 = (bf16[1,2,64,256]{3,2,1,0:T(8,128)(2,1)S(1)}, bf16[1,2,64,256]{3,2,1,0:T(8,128)(2,1)S(1)}, u32[]{:S(2)}, u32[]{:S(2)}) collective-permute-start(bf16[1,2,64,256]{3,2,1,0:T(8,128)(2,1)S(1)} %pad_maximum_fusion), channel_id=1, source_target_pairs={{0,16},{4,20},{8,24},{12,28},{16,0},{20,4},{24,8},{28,12},{1,17},{... | collective-permute-start | bytes 196616 | tf_op jit(solution)/shard_map/ppermute | solution.py:255
  8.6 0.5 %collective-permute-start.2 = (bf16[1,2,64,256]{3,2,1,0:T(8,128)(2,1)S(1)}, bf16[1,2,64,256]{3,2,1,0:T(8,128)(2,1)S(1)}, u32[]{:S(2)}, u32[]{:S(2)}) collective-permute-start(bf16[1,2,64,256]{3,2,1,0:T(8,128)(2,1)S(1)} %pad_maximum_fusion), channel_id=1, source_target_pairs={{0,8},{4,12},{8,0},{12,4},{16,24},{20,28},{24,16},{28,20},{1,9},{5... | collective-permute-start | bytes 196616 | tf_op jit(solution)/shard_map/ppermute | solution.py:255
  9.2 0.0 copy-done
  9.2 0.0 collective-permute-done.3.across
  9.3 1.6 %collective-permute-start.5 = (bf16[2,2,16,512]{3,2,1,0:T(8,128)(2,1)S(1)}, bf16[2,2,16,512]{3,2,1,0:T(8,128)(2,1)S(1)}, u32[]{:S(2)}, u32[]{:S(2)}) collective-permute-start(bf16[2,2,16,512]{3,2,1,0:T(8,128)(2,1)S(1)} %pad_maximum_fusion.1), channel_id=1, source_target_pairs={{0,1},{1,0},{2,3},{3,2},{4,5},{5,4},{6,7},{7,6},{8,9},{9,8},{10,11... | collective-permute-start | bytes 196616 | tf_op jit(solution)/shard_map/ppermute | solution.py:265
  10.9 0.1 collective-permute-done
  11.0 1.4 %collective-permute-done.1 = bf16[1,2,64,256]{3,2,1,0:T(8,128)(2,1)S(1)} collective-permute-done((bf16[1,2,64,256]{3,2,1,0:T(8,128)(2,1)S(1)}, bf16[1,2,64,256]{3,2,1,0:T(8,128)(2,1)S(1)}, u32[]{:S(2)}, u32[]{:S(2)}) %collective-permute-start.1) | collective-permute-done | bytes 65568 | tf_op jit(solution)/shard_map/ppermute | solution.py:255
  12.4 0.5 %collective-permute-done.2 = bf16[1,2,64,256]{3,2,1,0:T(8,128)(2,1)S(1)} collective-permute-done((bf16[1,2,64,256]{3,2,1,0:T(8,128)(2,1)S(1)}, bf16[1,2,64,256]{3,2,1,0:T(8,128)(2,1)S(1)}, u32[]{:S(2)}, u32[]{:S(2)}) %collective-permute-start.2) | collective-permute-done | bytes 65568 | tf_op jit(solution)/shard_map/ppermute | solution.py:255
  12.9 0.1 collective-permute-start.4
  13.0 0.7 %shard_map.69 = (f32[256,128]{1,0:T(8,128)S(1)}, f32[512,128]{1,0:T(8,128)S(1)}, f32[256,128]{1,0:T(8,128)S(1)}, f32[256,128]{1,0:T(8,128)S(1)}, bf16[256,512]{1...) custom-call(s32[1,3]{1,0:T(1,128)S(1)} %get-tuple-element.24.lengths, s32[2,4,8]{2,1,0:T(4,128)S(1)} %get-tuple-element.25.page_slot, ...), custom_call_target="tpu_custom_call" | custom-call | flops 4000000000 | bytes 1000000 | tf_op jit(solution)/shard_map/pallas_call | solution.py:272
  13.8 0.0 collective-permute-done.5.beside
  13.8 0.6 %shard_map.70 = (bf16[2,256,128]{2,1,0:T(8,128)(2,1)S(1)}, f32[2,1,256]{2,1,0:T(1,128)S(1)}, f32[2,1,256]{2,1,0:T(1,128)S(1)}, f32[2,128,256]{2,1,0:T(8,128)S(1)}) custom-call(bf16[1,2,16,2048]{3,2,1,0:T(8,128)(2,1)S(1)} %copy-done, bf16[1,2,16,1024]{3,2,1,0:T(8,128)(2,1)S(1)} %collective-permute-done.3.across, ...), custom_call_target="tpu_custom_call" | custom-call | flops 4000000000 | bytes 1000000 | tf_op jit(solution)/shard_map/pallas_call | solution.py:289
  14.4 0.2 collective-permute-done.4.far
  14.5 1.3 %shard_map.71 = (bf16[1,2,64,512]{3,2,1,0:T(8,128)(2,1)}, bf16[16,1,16,256]{3,2,1,0:T(8,128)(2,1)}) custom-call(bf16[4,2,64,256]{3,2,1,0:T(8,128)(2,1)S(1)} %collective-permute-done.4.far, f32[256,128]{1,0:T(8,128)S(1)} %get-tuple-element.26.bias_a, f32[256,128]{1,0:T(8,128)S(1)} %get-tuple-element.27.bias_b, ...), custom_call_target="tpu_custom_call" | custom-call | flops 4000000000 | bytes 1000000 | tf_op jit(solution)/shard_map/pallas_call | solution.py:302
  (8 shorter events, 0.1 us)
Async XLA Ops:
  0.6 5.0 %copy-start.1 = (bf16[1,2,64,128]{3,2,1,0:T(8,128)(2,1)S(1)}, bf16[1,2,64,128]{3,2,1,0:T(8,128)(2,1)}, u32[]{:S(2)}) copy-start(bf16[1,2,64,128]{3,2,1,0:T(8,128)(2,1)} %param.7) | copy-start | bytes 98308
  0.6 5.0 %copy-start.2 = (bf16[1,2,64,128]{3,2,1,0:T(8,128)(2,1)S(1)}, bf16[1,2,64,128]{3,2,1,0:T(8,128)(2,1)}, u32[]{:S(2)}) copy-start(bf16[1,2,64,128]{3,2,1,0:T(8,128)(2,1)} %param.6) | copy-start | bytes 98308
  1.5 7.7 %copy-start = (bf16[1,2,16,2048]{3,2,1,0:T(8,128)(2,1)S(1)}, bf16[1,2,16,2048]{3,2,1,0:T(8,128)(2,1)}, u32[]{:S(2)}) copy-start(bf16[1,2,16,2048]{3,2,1,0:T(8,128)(2,1)} %own.1) | copy-start | bytes 393220
  1.5 7.8 %collective-permute-start.3 = (bf16[1,2,16,1024]{3,2,1,0:T(8,128)(2,1)S(1)}, bf16[1,2,16,1024]{3,2,1,0:T(8,128)(2,1)S(1)}, u32[]{:S(2)}, u32[]{:S(2)}) collective-permute-start(bf16[1,2,16,1024]{3,2,1,0:T(8,128)(2,1)S(1)} %get-tuple-element.19), channel_id=1, source_target_pairs={{0,2},{1,3},{2,0},{3,1},{4,6},{5,7},{6,4},{7,5},{8,10},{9,11},{10,... | collective-permute-start | bytes 196616 | tf_op jit(solution)/shard_map/ppermute | solution.py:251
  5.6 5.3 %collective-permute-start = (bf16[1,2,64,256]{3,2,1,0:T(8,128)(2,1)S(1)}, bf16[1,2,64,256]{3,2,1,0:T(8,128)(2,1)S(1)}, u32[]{:S(2)}, u32[]{:S(2)}) collective-permute-start(bf16[1,2,64,256]{3,2,1,0:T(8,128)(2,1)S(1)} %pad_maximum_fusion), channel_id=1, source_target_pairs={{0,24},{4,28},{8,16},{12,20},{16,8},{20,12},{24,0},{28,4},{1,25},{... | collective-permute-start | bytes 196616 | tf_op jit(solution)/shard_map/ppermute | solution.py:255
  8.1 4.3 %collective-permute-start.1 = (bf16[1,2,64,256]{3,2,1,0:T(8,128)(2,1)S(1)}, bf16[1,2,64,256]{3,2,1,0:T(8,128)(2,1)S(1)}, u32[]{:S(2)}, u32[]{:S(2)}) collective-permute-start(bf16[1,2,64,256]{3,2,1,0:T(8,128)(2,1)S(1)} %pad_maximum_fusion), channel_id=1, source_target_pairs={{0,16},{4,20},{8,24},{12,28},{16,0},{20,4},{24,8},{28,12},{1,17},{... | collective-permute-start | bytes 196616 | tf_op jit(solution)/shard_map/ppermute | solution.py:255
  8.6 4.3 %collective-permute-start.2 = (bf16[1,2,64,256]{3,2,1,0:T(8,128)(2,1)S(1)}, bf16[1,2,64,256]{3,2,1,0:T(8,128)(2,1)S(1)}, u32[]{:S(2)}, u32[]{:S(2)}) collective-permute-start(bf16[1,2,64,256]{3,2,1,0:T(8,128)(2,1)S(1)} %pad_maximum_fusion), channel_id=1, source_target_pairs={{0,8},{4,12},{8,0},{12,4},{16,24},{20,28},{24,16},{28,20},{1,9},{5... | collective-permute-start | bytes 196616 | tf_op jit(solution)/shard_map/ppermute | solution.py:255
  9.3 4.5 %collective-permute-start.5 = (bf16[2,2,16,512]{3,2,1,0:T(8,128)(2,1)S(1)}, bf16[2,2,16,512]{3,2,1,0:T(8,128)(2,1)S(1)}, u32[]{:S(2)}, u32[]{:S(2)}) collective-permute-start(bf16[2,2,16,512]{3,2,1,0:T(8,128)(2,1)S(1)} %pad_maximum_fusion.1), channel_id=1, source_target_pairs={{0,1},{1,0},{2,3},{3,2},{4,5},{5,4},{6,7},{7,6},{8,9},{9,8},{10,11... | collective-permute-start | bytes 196616 | tf_op jit(solution)/shard_map/ppermute | solution.py:265
  12.9 1.6 %collective-permute-start.4 = (bf16[4,2,64,256]{3,2,1,0:T(8,128)(2,1)S(1)}, bf16[4,2,64,256]{3,2,1,0:T(8,128)(2,1)S(1)}, u32[]{:S(2)}, u32[]{:S(2)}) collective-permute-start(bf16[4,2,64,256]{3,2,1,0:T(8,128)(2,1)S(1)} %constant_dynamic-update-slice_fusion.near), channel_id=1, source_target_pairs={{0,4},{4,0},{8,12},{12,8},{16,20},{20,16},{24,28},{28,24},{1,5},{5... | collective-permute-start | bytes 786440 | tf_op jit(solution)/shard_map/ppermute | solution.py:267

commit v18 on v17

--- a/solution.py
+++ b/solution.py
@@ -160,10 +160,6 @@
     my_head = lax.axis_index("head")
     sub_tok = block_tok // lax.axis_size("head")
     scores = {half: score_part(q_rows[half], far, half) for half in (1, 0)}
-    moved = place_pages(far_chosen[...], far) + pages_ref[...].astype(jnp.float32)
-    pages[...] = moved.astype(jnp.bfloat16).reshape(pages.shape)
-    writes = [pltpu.make_async_copy(pages, kv_cache, sems.at[2])]
-    writes[0].start()
     my_blk = lax.axis_index("blk")
     chips = far.shape[0]
     early = [(my_blk ^ 1 ^ (2 * m)) < my_blk for m in range(chips)]
@@ -205,6 +201,13 @@
     parts = {
         half: (tops[half], sums[half], weigh_part(jnp.concatenate(weights[half], axis=0), far, half)) for half in range(2)
     }
+    moved = place_pages(far_chosen[...], far) + pages_ref[...].astype(jnp.float32)
+    pages[...] = moved.astype(jnp.bfloat16).reshape(pages.shape)
+    writes = []
+    for k, slot in enumerate(range(0, slot_count, slot_count // 4)):
+        some = pl.ds(slot, slot_count // 4)
+        writes.append(pltpu.make_async_copy(pages.at[some], kv_cache.at[some], sems.at[2 + k]))
+        writes[-1].start()
     for half in range(2):
         top, total, out = parts[half]
         best = jnp.maximum(top, top_ref[half])
@@ -310,7 +313,7 @@
         scratch_shapes=[
             pltpu.VMEM((slot_count, 1, PAGE, 2 * HEAD_DIM), jnp.bfloat16),
             pltpu.VMEM((2, block_tok, width), jnp.bfloat16),
-            pltpu.SemaphoreType.DMA((3,)),
+            pltpu.SemaphoreType.DMA((6,)),
         ],
         compiler_params=params,
         cost_estimate=cost,

time: 16.1 us -> 16.1 us (level)
  no operation moved by 1% of the time
where the time goes in v18:
time: 16.1 us; the launch traced here: 15.9 us
  starting transfers between devices  9.35 us (58%)
  Pallas kernels  3.53 us (22%)
  waiting for transfers between devices  2.22 us (14%)
  between operations  0.73 us (5%)
    ppermute x1, starting transfers between devices, per_device(): across = lax.ppermute(part, 'head', [(i, i ^ 2) for i in range(head_count)])  4.1 us
    ppermute x3, starting transfers between devices, per_device(): lax.ppermute(pair, 'blk', [(i, i ^ d) for i in range(blk_count)])  3.55 us
    ppermute x3, waiting for transfers between devices, per_device(): lax.ppermute(pair, 'blk', [(i, i ^ d) for i in range(blk_count)])  2.01 us
    ppermute x1, starting transfers between devices, per_device(): lax.ppermute(beside, 'head', [(i, i ^ 1) for i in range(head_count)])  1.63 us
    pallas_call x1, Pallas kernels, per_device(): pl.pallas_call(far_kernel, out_shape=(jax.ShapeDtypeStruct((1, 2, block_t...  1.36 us
    pallas_call x1, Pallas kernels, per_device(): pl.pallas_call(fetch_kernel, out_shape=(jax.ShapeDtypeStruct((*query_stat...  0.84 us
    pallas_call x1, Pallas kernels, per_device(): pl.pallas_call(plan_kernel, out_shape=(jax.ShapeDtypeStruct((half_cols, L...  0.73 us
    pallas_call x1, Pallas kernels, per_device(): pl.pallas_call(near_kernel, out_shape=(jax.ShapeDtypeStruct((2, rows, HEA...  0.61 us
  transfers between devices with their start and end apart: 6, of which 4 were waited for; matrix products, arithmetic and copies ran while one was open for 0% of the time, Pallas kernels for 8%

profile of v18, /device:TPU:0, one launch (start us, length us, event | category | flops | bytes accessed | tf_op | source)
XLA Modules:
  0.0 15.9 jit_solution(17340366595784808862)
XLA Ops:
  0.6 0.0 copy-start.1
  0.6 0.0 copy-start.2
  0.7 0.8 %shard_map.68 = (bf16[1,2,16,1024]{3,2,1,0:T(8,128)(2,1)S(1)}, s32[1,3]{1,0:T(1,128)S(1)}, s32[2,4,8]{2,1,0:T(4,128)S(1)}) custom-call(bf16[1,2,16,2048]{3,2,1,0:T(8,128)(2,1)} %own.1, s32[1,3]{1,0:T(1,128)} %bitcast.3, s32[2,4,8]{2,1,0:T(4,128)} %bitcast.2), custom_call_target="tpu_custom_call" | custom-call | bytes 200000 | tf_op jit(solution)/shard_map/pallas_call | solution.py:242
  1.5 0.0 copy-start
  1.5 4.1 %collective-permute-start.3 = (bf16[1,2,16,1024]{3,2,1,0:T(8,128)(2,1)S(1)}, bf16[1,2,16,1024]{3,2,1,0:T(8,128)(2,1)S(1)}, u32[]{:S(2)}, u32[]{:S(2)}) collective-permute-start(bf16[1,2,16,1024]{3,2,1,0:T(8,128)(2,1)S(1)} %get-tuple-element.19), channel_id=1, source_target_pairs={{0,2},{1,3},{2,0},{3,1},{4,6},{5,7},{6,4},{7,5},{8,10},{9,11},{10,... | collective-permute-start | bytes 196616 | tf_op jit(solution)/shard_map/ppermute | solution.py:254
  5.6 0.0 copy-done.1
  5.6 0.0 copy-done.2
  5.6 2.5 %collective-permute-start = (bf16[1,2,64,256]{3,2,1,0:T(8,128)(2,1)S(1)}, bf16[1,2,64,256]{3,2,1,0:T(8,128)(2,1)S(1)}, u32[]{:S(2)}, u32[]{:S(2)}) collective-permute-start(bf16[1,2,64,256]{3,2,1,0:T(8,128)(2,1)S(1)} %pad_maximum_fusion), channel_id=1, source_target_pairs={{0,24},{4,28},{8,16},{12,20},{16,8},{20,12},{24,0},{28,4},{1,25},{... | collective-permute-start | bytes 196616 | tf_op jit(solution)/shard_map/ppermute | solution.py:258
  8.1 0.5 %collective-permute-start.1 = (bf16[1,2,64,256]{3,2,1,0:T(8,128)(2,1)S(1)}, bf16[1,2,64,256]{3,2,1,0:T(8,128)(2,1)S(1)}, u32[]{:S(2)}, u32[]{:S(2)}) collective-permute-start(bf16[1,2,64,256]{3,2,1,0:T(8,128)(2,1)S(1)} %pad_maximum_fusion), channel_id=1, source_target_pairs={{0,16},{4,20},{8,24},{12,28},{16,0},{20,4},{24,8},{28,12},{1,17},{... | collective-permute-start | bytes 196616 | tf_op jit(solution)/shard_map/ppermute | solution.py:258
  8.6 0.5 %collective-permute-start.2 = (bf16[1,2,64,256]{3,2,1,0:T(8,128)(2,1)S(1)}, bf16[1,2,64,256]{3,2,1,0:T(8,128)(2,1)S(1)}, u32[]{:S(2)}, u32[]{:S(2)}) collective-permute-start(bf16[1,2,64,256]{3,2,1,0:T(8,128)(2,1)S(1)} %pad_maximum_fusion), channel_id=1, source_target_pairs={{0,8},{4,12},{8,0},{12,4},{16,24},{20,28},{24,16},{28,20},{1,9},{5... | collective-permute-start | bytes 196616 | tf_op jit(solution)/shard_map/ppermute | solution.py:258
  9.2 0.0 copy-done
  9.2 0.0 collective-permute-done.3.across
  9.3 1.6 %collective-permute-start.5 = (bf16[2,2,16,512]{3,2,1,0:T(8,128)(2,1)S(1)}, bf16[2,2,16,512]{3,2,1,0:T(8,128)(2,1)S(1)}, u32[]{:S(2)}, u32[]{:S(2)}) collective-permute-start(bf16[2,2,16,512]{3,2,1,0:T(8,128)(2,1)S(1)} %pad_maximum_fusion.1), channel_id=1, source_target_pairs={{0,1},{1,0},{2,3},{3,2},{4,5},{5,4},{6,7},{7,6},{8,9},{9,8},{10,11... | collective-permute-start | bytes 196616 | tf_op jit(solution)/shard_map/ppermute | solution.py:268
  10.9 0.1 collective-permute-done
  11.0 1.4 %collective-permute-done.1 = bf16[1,2,64,256]{3,2,1,0:T(8,128)(2,1)S(1)} collective-permute-done((bf16[1,2,64,256]{3,2,1,0:T(8,128)(2,1)S(1)}, bf16[1,2,64,256]{3,2,1,0:T(8,128)(2,1)S(1)}, u32[]{:S(2)}, u32[]{:S(2)}) %collective-permute-start.1) | collective-permute-done | bytes 65568 | tf_op jit(solution)/shard_map/ppermute | solution.py:258
  12.4 0.5 %collective-permute-done.2 = bf16[1,2,64,256]{3,2,1,0:T(8,128)(2,1)S(1)} collective-permute-done((bf16[1,2,64,256]{3,2,1,0:T(8,128)(2,1)S(1)}, bf16[1,2,64,256]{3,2,1,0:T(8,128)(2,1)S(1)}, u32[]{:S(2)}, u32[]{:S(2)}) %collective-permute-start.2) | collective-permute-done | bytes 65568 | tf_op jit(solution)/shard_map/ppermute | solution.py:258
  12.9 0.1 collective-permute-start.4
  13.0 0.7 %shard_map.69 = (f32[256,128]{1,0:T(8,128)S(1)}, f32[512,128]{1,0:T(8,128)S(1)}, f32[256,128]{1,0:T(8,128)S(1)}, f32[256,128]{1,0:T(8,128)S(1)}, bf16[256,512]{1...) custom-call(s32[1,3]{1,0:T(1,128)S(1)} %get-tuple-element.24.lengths, s32[2,4,8]{2,1,0:T(4,128)S(1)} %get-tuple-element.25.page_slot, ...), custom_call_target="tpu_custom_call" | custom-call | flops 4000000000 | bytes 1000000 | tf_op jit(solution)/shard_map/pallas_call | solution.py:275
  13.8 0.0 collective-permute-done.5.beside
  13.8 0.6 %shard_map.70 = (bf16[2,256,128]{2,1,0:T(8,128)(2,1)S(1)}, f32[2,1,256]{2,1,0:T(1,128)S(1)}, f32[2,1,256]{2,1,0:T(1,128)S(1)}, f32[2,128,256]{2,1,0:T(8,128)S(1)}) custom-call(bf16[1,2,16,2048]{3,2,1,0:T(8,128)(2,1)S(1)} %copy-done, bf16[1,2,16,1024]{3,2,1,0:T(8,128)(2,1)S(1)} %collective-permute-done.3.across, ...), custom_call_target="tpu_custom_call" | custom-call | flops 4000000000 | bytes 1000000 | tf_op jit(solution)/shard_map/pallas_call | solution.py:292
  14.4 0.2 collective-permute-done.4.far
  14.5 1.4 %shard_map.71 = (bf16[1,2,64,512]{3,2,1,0:T(8,128)(2,1)}, bf16[16,1,16,256]{3,2,1,0:T(8,128)(2,1)}) custom-call(bf16[4,2,64,256]{3,2,1,0:T(8,128)(2,1)S(1)} %collective-permute-done.4.far, f32[256,128]{1,0:T(8,128)S(1)} %get-tuple-element.26.bias_a, f32[256,128]{1,0:T(8,128)S(1)} %get-tuple-element.27.bias_b, ...), custom_call_target="tpu_custom_call" | custom-call | flops 4000000000 | bytes 1000000 | tf_op jit(solution)/shard_map/pallas_call | solution.py:305
  (8 shorter events, 0.1 us)
Async XLA Ops:
  0.6 5.0 %copy-start.1 = (bf16[1,2,64,128]{3,2,1,0:T(8,128)(2,1)S(1)}, bf16[1,2,64,128]{3,2,1,0:T(8,128)(2,1)}, u32[]{:S(2)}) copy-start(bf16[1,2,64,128]{3,2,1,0:T(8,128)(2,1)} %param.7) | copy-start | bytes 98308
  0.6 5.0 %copy-start.2 = (bf16[1,2,64,128]{3,2,1,0:T(8,128)(2,1)S(1)}, bf16[1,2,64,128]{3,2,1,0:T(8,128)(2,1)}, u32[]{:S(2)}) copy-start(bf16[1,2,64,128]{3,2,1,0:T(8,128)(2,1)} %param.6) | copy-start | bytes 98308
  1.5 7.7 %copy-start = (bf16[1,2,16,2048]{3,2,1,0:T(8,128)(2,1)S(1)}, bf16[1,2,16,2048]{3,2,1,0:T(8,128)(2,1)}, u32[]{:S(2)}) copy-start(bf16[1,2,16,2048]{3,2,1,0:T(8,128)(2,1)} %own.1) | copy-start | bytes 393220
  1.5 7.8 %collective-permute-start.3 = (bf16[1,2,16,1024]{3,2,1,0:T(8,128)(2,1)S(1)}, bf16[1,2,16,1024]{3,2,1,0:T(8,128)(2,1)S(1)}, u32[]{:S(2)}, u32[]{:S(2)}) collective-permute-start(bf16[1,2,16,1024]{3,2,1,0:T(8,128)(2,1)S(1)} %get-tuple-element.19), channel_id=1, source_target_pairs={{0,2},{1,3},{2,0},{3,1},{4,6},{5,7},{6,4},{7,5},{8,10},{9,11},{10,... | collective-permute-start | bytes 196616 | tf_op jit(solution)/shard_map/ppermute | solution.py:254
  5.6 5.3 %collective-permute-start = (bf16[1,2,64,256]{3,2,1,0:T(8,128)(2,1)S(1)}, bf16[1,2,64,256]{3,2,1,0:T(8,128)(2,1)S(1)}, u32[]{:S(2)}, u32[]{:S(2)}) collective-permute-start(bf16[1,2,64,256]{3,2,1,0:T(8,128)(2,1)S(1)} %pad_maximum_fusion), channel_id=1, source_target_pairs={{0,24},{4,28},{8,16},{12,20},{16,8},{20,12},{24,0},{28,4},{1,25},{... | collective-permute-start | bytes 196616 | tf_op jit(solution)/shard_map/ppermute | solution.py:258
  8.1 4.3 %collective-permute-start.1 = (bf16[1,2,64,256]{3,2,1,0:T(8,128)(2,1)S(1)}, bf16[1,2,64,256]{3,2,1,0:T(8,128)(2,1)S(1)}, u32[]{:S(2)}, u32[]{:S(2)}) collective-permute-start(bf16[1,2,64,256]{3,2,1,0:T(8,128)(2,1)S(1)} %pad_maximum_fusion), channel_id=1, source_target_pairs={{0,16},{4,20},{8,24},{12,28},{16,0},{20,4},{24,8},{28,12},{1,17},{... | collective-permute-start | bytes 196616 | tf_op jit(solution)/shard_map/ppermute | solution.py:258
  8.6 4.3 %collective-permute-start.2 = (bf16[1,2,64,256]{3,2,1,0:T(8,128)(2,1)S(1)}, bf16[1,2,64,256]{3,2,1,0:T(8,128)(2,1)S(1)}, u32[]{:S(2)}, u32[]{:S(2)}) collective-permute-start(bf16[1,2,64,256]{3,2,1,0:T(8,128)(2,1)S(1)} %pad_maximum_fusion), channel_id=1, source_target_pairs={{0,8},{4,12},{8,0},{12,4},{16,24},{20,28},{24,16},{28,20},{1,9},{5... | collective-permute-start | bytes 196616 | tf_op jit(solution)/shard_map/ppermute | solution.py:258
  9.3 4.5 %collective-permute-start.5 = (bf16[2,2,16,512]{3,2,1,0:T(8,128)(2,1)S(1)}, bf16[2,2,16,512]{3,2,1,0:T(8,128)(2,1)S(1)}, u32[]{:S(2)}, u32[]{:S(2)}) collective-permute-start(bf16[2,2,16,512]{3,2,1,0:T(8,128)(2,1)S(1)} %pad_maximum_fusion.1), channel_id=1, source_target_pairs={{0,1},{1,0},{2,3},{3,2},{4,5},{5,4},{6,7},{7,6},{8,9},{9,8},{10,11... | collective-permute-start | bytes 196616 | tf_op jit(solution)/shard_map/ppermute | solution.py:268
  12.9 1.6 %collective-permute-start.4 = (bf16[4,2,64,256]{3,2,1,0:T(8,128)(2,1)S(1)}, bf16[4,2,64,256]{3,2,1,0:T(8,128)(2,1)S(1)}, u32[]{:S(2)}, u32[]{:S(2)}) collective-permute-start(bf16[4,2,64,256]{3,2,1,0:T(8,128)(2,1)S(1)} %constant_dynamic-update-slice_fusion.near), channel_id=1, source_target_pairs={{0,4},{4,0},{8,12},{12,8},{16,20},{20,16},{24,28},{28,24},{1,5},{5... | collective-permute-start | bytes 786440 | tf_op jit(solution)/shard_map/ppermute | solution.py:270

commit v19 on v14

--- a/solution.py
+++ b/solution.py
@@ -105,11 +105,12 @@
 def fetch_kernel(queries, lengths, page_slot, part, lengths_out, slots_out, sems):
     _, halves, _, width = part.shape
     start = ((lax.axis_index("head") & 2) ^ 2) * (width // 2)
-    pairs = [(lengths, lengths_out), (page_slot, slots_out)]
+    pairs = []
     for half in range(halves):
         for lane in range(0, width, width // 2):
             lanes = pl.ds(pl.multiple_of(start + lane, width // 2), width // 2)
             pairs.append((queries.at[0, half, :, lanes], part.at[0, half, :, lane : lane + width // 2]))
+    pairs += [(lengths, lengths_out), (page_slot, slots_out)]
     copies = [pltpu.make_async_copy(a, b, sems.at[k]) for k, (a, b) in enumerate(pairs)]
     for copy in copies:
         copy.start()

time: 16.1 us -> 16.1 us (level)
  no operation moved by 1% of the time
where the time goes in v19:
time: 16.1 us; the launch traced here: 15.9 us
  starting transfers between devices  9.35 us (58%)
  Pallas kernels  3.5 us (22%)
  waiting for transfers between devices  2.23 us (14%)
  between operations  0.73 us (5%)
    ppermute x1, starting transfers between devices, per_device(): across = lax.ppermute(part, 'head', [(i, i ^ 2) for i in range(head_count)])  4.1 us
    ppermute x3, starting transfers between devices, per_device(): lax.ppermute(pair, 'blk', [(i, i ^ d) for i in range(blk_count)])  3.55 us
    ppermute x3, waiting for transfers between devices, per_device(): lax.ppermute(pair, 'blk', [(i, i ^ d) for i in range(blk_count)])  2.01 us
    ppermute x1, starting transfers between devices, per_device(): lax.ppermute(beside, 'head', [(i, i ^ 1) for i in range(head_count)])  1.63 us
    pallas_call x1, Pallas kernels, per_device(): pl.pallas_call(far_kernel, out_shape=(jax.ShapeDtypeStruct((1, 2, block_t...  1.34 us
    pallas_call x1, Pallas kernels, per_device(): pl.pallas_call(fetch_kernel, out_shape=(jax.ShapeDtypeStruct((*query_stat...  0.84 us
    pallas_call x1, Pallas kernels, per_device(): pl.pallas_call(plan_kernel, out_shape=(jax.ShapeDtypeStruct((half_cols, L...  0.72 us
    pallas_call x1, Pallas kernels, per_device(): pl.pallas_call(near_kernel, out_shape=(jax.ShapeDtypeStruct((2, rows, HEA...  0.61 us
  transfers between devices with their start and end apart: 6, of which 4 were waited for; matrix products, arithmetic and copies ran while one was open for 0% of the time, Pallas kernels for 8%

profile of v19, /device:TPU:0, one launch (start us, length us, event | category | flops | bytes accessed | tf_op | source)
XLA Modules:
  0.0 15.9 jit_solution(9535264671494769483)
XLA Ops:
  0.6 0.0 copy-start.1
  0.6 0.0 copy-start.2
  0.7 0.8 %shard_map.68 = (bf16[1,2,16,1024]{3,2,1,0:T(8,128)(2,1)S(1)}, s32[1,3]{1,0:T(1,128)S(1)}, s32[2,4,8]{2,1,0:T(4,128)S(1)}) custom-call(bf16[1,2,16,2048]{3,2,1,0:T(8,128)(2,1)} %own.1, s32[1,3]{1,0:T(1,128)} %bitcast.3, s32[2,4,8]{2,1,0:T(4,128)} %bitcast.2), custom_call_target="tpu_custom_call" | custom-call | bytes 200000 | tf_op jit(solution)/shard_map/pallas_call | solution.py:196
  1.5 0.0 copy-start
  1.5 4.1 %collective-permute-start.3 = (bf16[1,2,16,1024]{3,2,1,0:T(8,128)(2,1)S(1)}, bf16[1,2,16,1024]{3,2,1,0:T(8,128)(2,1)S(1)}, u32[]{:S(2)}, u32[]{:S(2)}) collective-permute-start(bf16[1,2,16,1024]{3,2,1,0:T(8,128)(2,1)S(1)} %get-tuple-element.19), channel_id=1, source_target_pairs={{0,2},{1,3},{2,0},{3,1},{4,6},{5,7},{6,4},{7,5},{8,10},{9,11},{10,... | collective-permute-start | bytes 196616 | tf_op jit(solution)/shard_map/ppermute | solution.py:208
  5.6 0.0 copy-done.1
  5.6 0.0 copy-done.2
  5.6 2.5 %collective-permute-start = (bf16[1,2,64,256]{3,2,1,0:T(8,128)(2,1)S(1)}, bf16[1,2,64,256]{3,2,1,0:T(8,128)(2,1)S(1)}, u32[]{:S(2)}, u32[]{:S(2)}) collective-permute-start(bf16[1,2,64,256]{3,2,1,0:T(8,128)(2,1)S(1)} %pad_maximum_fusion), channel_id=1, source_target_pairs={{0,24},{4,28},{8,16},{12,20},{16,8},{20,12},{24,0},{28,4},{1,25},{... | collective-permute-start | bytes 196616 | tf_op jit(solution)/shard_map/ppermute | solution.py:212
  8.1 0.5 %collective-permute-start.1 = (bf16[1,2,64,256]{3,2,1,0:T(8,128)(2,1)S(1)}, bf16[1,2,64,256]{3,2,1,0:T(8,128)(2,1)S(1)}, u32[]{:S(2)}, u32[]{:S(2)}) collective-permute-start(bf16[1,2,64,256]{3,2,1,0:T(8,128)(2,1)S(1)} %pad_maximum_fusion), channel_id=1, source_target_pairs={{0,16},{4,20},{8,24},{12,28},{16,0},{20,4},{24,8},{28,12},{1,17},{... | collective-permute-start | bytes 196616 | tf_op jit(solution)/shard_map/ppermute | solution.py:212
  8.6 0.5 %collective-permute-start.2 = (bf16[1,2,64,256]{3,2,1,0:T(8,128)(2,1)S(1)}, bf16[1,2,64,256]{3,2,1,0:T(8,128)(2,1)S(1)}, u32[]{:S(2)}, u32[]{:S(2)}) collective-permute-start(bf16[1,2,64,256]{3,2,1,0:T(8,128)(2,1)S(1)} %pad_maximum_fusion), channel_id=1, source_target_pairs={{0,8},{4,12},{8,0},{12,4},{16,24},{20,28},{24,16},{28,20},{1,9},{5... | collective-permute-start | bytes 196616 | tf_op jit(solution)/shard_map/ppermute | solution.py:212
  9.2 0.0 copy-done
  9.2 0.0 collective-permute-done.3.across
  9.3 1.6 %collective-permute-start.5 = (bf16[2,2,16,512]{3,2,1,0:T(8,128)(2,1)S(1)}, bf16[2,2,16,512]{3,2,1,0:T(8,128)(2,1)S(1)}, u32[]{:S(2)}, u32[]{:S(2)}) collective-permute-start(bf16[2,2,16,512]{3,2,1,0:T(8,128)(2,1)S(1)} %pad_maximum_fusion.1), channel_id=1, source_target_pairs={{0,1},{1,0},{2,3},{3,2},{4,5},{5,4},{6,7},{7,6},{8,9},{9,8},{10,11... | collective-permute-start | bytes 196616 | tf_op jit(solution)/shard_map/ppermute | solution.py:222
  10.9 0.1 collective-permute-done
  11.0 1.4 %collective-permute-done.1 = bf16[1,2,64,256]{3,2,1,0:T(8,128)(2,1)S(1)} collective-permute-done((bf16[1,2,64,256]{3,2,1,0:T(8,128)(2,1)S(1)}, bf16[1,2,64,256]{3,2,1,0:T(8,128)(2,1)S(1)}, u32[]{:S(2)}, u32[]{:S(2)}) %collective-permute-start.1) | collective-permute-done | bytes 65568 | tf_op jit(solution)/shard_map/ppermute | solution.py:212
  12.4 0.5 %collective-permute-done.2 = bf16[1,2,64,256]{3,2,1,0:T(8,128)(2,1)S(1)} collective-permute-done((bf16[1,2,64,256]{3,2,1,0:T(8,128)(2,1)S(1)}, bf16[1,2,64,256]{3,2,1,0:T(8,128)(2,1)S(1)}, u32[]{:S(2)}, u32[]{:S(2)}) %collective-permute-start.2) | collective-permute-done | bytes 65568 | tf_op jit(solution)/shard_map/ppermute | solution.py:212
  12.9 0.1 collective-permute-start.4
  13.0 0.7 %shard_map.69 = (f32[256,128]{1,0:T(8,128)S(1)}, f32[512,128]{1,0:T(8,128)S(1)}, f32[256,128]{1,0:T(8,128)S(1)}, f32[512,128]{1,0:T(8,128)S(1)}, bf16[256,512]{1...) custom-call(s32[1,3]{1,0:T(1,128)S(1)} %get-tuple-element.24.lengths, s32[2,4,8]{2,1,0:T(4,128)S(1)} %get-tuple-element.25.page_slot, ...), custom_call_target="tpu_custom_call" | custom-call | flops 4000000000 | bytes 1000000 | tf_op jit(solution)/shard_map/pallas_call | solution.py:229
  13.8 0.0 collective-permute-done.5.beside
  13.8 0.6 %shard_map.70 = (bf16[2,256,128]{2,1,0:T(8,128)(2,1)S(1)}, f32[2,1,256]{2,1,0:T(1,128)S(1)}, f32[2,1,256]{2,1,0:T(1,128)S(1)}, f32[2,128,256]{2,1,0:T(8,128)S(1)}) custom-call(bf16[1,2,16,2048]{3,2,1,0:T(8,128)(2,1)S(1)} %copy-done, bf16[1,2,16,1024]{3,2,1,0:T(8,128)(2,1)S(1)} %collective-permute-done.3.across, ...), custom_call_target="tpu_custom_call" | custom-call | flops 4000000000 | bytes 1000000 | tf_op jit(solution)/shard_map/pallas_call | solution.py:245
  14.4 0.2 %collective-permute-done.4.far = bf16[4,2,64,256]{3,2,1,0:T(8,128)(2,1)S(1)} collective-permute-done((bf16[4,2,64,256]{3,2,1,0:T(8,128)(2,1)S(1)}, bf16[4,2,64,256]{3,2,1,0:T(8,128)(2,1)S(1)}, u32[]{:S(2)}, u32[]{:S(2)}) %collective-permute-start.4) | collective-permute-done | bytes 262176 | tf_op jit(solution)/shard_map/ppermute | solution.py:224
  14.5 1.3 %shard_map.71 = (bf16[1,2,64,512]{3,2,1,0:T(8,128)(2,1)}, bf16[16,1,16,256]{3,2,1,0:T(8,128)(2,1)}) custom-call(bf16[4,2,64,256]{3,2,1,0:T(8,128)(2,1)S(1)} %collective-permute-done.4.far, f32[256,128]{1,0:T(8,128)S(1)} %get-tuple-element.26.bias_a, f32[512,128]{1,0:T(8,128)S(1)} %get-tuple-element.27.bias_b, ...), custom_call_target="tpu_custom_call" | custom-call | flops 4000000000 | bytes 1000000 | tf_op jit(solution)/shard_map/pallas_call | solution.py:258
  (8 shorter events, 0.1 us)
Async XLA Ops:
  0.6 5.0 %copy-start.1 = (bf16[1,2,64,128]{3,2,1,0:T(8,128)(2,1)S(1)}, bf16[1,2,64,128]{3,2,1,0:T(8,128)(2,1)}, u32[]{:S(2)}) copy-start(bf16[1,2,64,128]{3,2,1,0:T(8,128)(2,1)} %param.7) | copy-start | bytes 98308
  0.6 5.0 %copy-start.2 = (bf16[1,2,64,128]{3,2,1,0:T(8,128)(2,1)S(1)}, bf16[1,2,64,128]{3,2,1,0:T(8,128)(2,1)}, u32[]{:S(2)}) copy-start(bf16[1,2,64,128]{3,2,1,0:T(8,128)(2,1)} %param.6) | copy-start | bytes 98308
  1.5 7.7 %copy-start = (bf16[1,2,16,2048]{3,2,1,0:T(8,128)(2,1)S(1)}, bf16[1,2,16,2048]{3,2,1,0:T(8,128)(2,1)}, u32[]{:S(2)}) copy-start(bf16[1,2,16,2048]{3,2,1,0:T(8,128)(2,1)} %own.1) | copy-start | bytes 393220
  1.5 7.8 %collective-permute-start.3 = (bf16[1,2,16,1024]{3,2,1,0:T(8,128)(2,1)S(1)}, bf16[1,2,16,1024]{3,2,1,0:T(8,128)(2,1)S(1)}, u32[]{:S(2)}, u32[]{:S(2)}) collective-permute-start(bf16[1,2,16,1024]{3,2,1,0:T(8,128)(2,1)S(1)} %get-tuple-element.19), channel_id=1, source_target_pairs={{0,2},{1,3},{2,0},{3,1},{4,6},{5,7},{6,4},{7,5},{8,10},{9,11},{10,... | collective-permute-start | bytes 196616 | tf_op jit(solution)/shard_map/ppermute | solution.py:208
  5.6 5.3 %collective-permute-start = (bf16[1,2,64,256]{3,2,1,0:T(8,128)(2,1)S(1)}, bf16[1,2,64,256]{3,2,1,0:T(8,128)(2,1)S(1)}, u32[]{:S(2)}, u32[]{:S(2)}) collective-permute-start(bf16[1,2,64,256]{3,2,1,0:T(8,128)(2,1)S(1)} %pad_maximum_fusion), channel_id=1, source_target_pairs={{0,24},{4,28},{8,16},{12,20},{16,8},{20,12},{24,0},{28,4},{1,25},{... | collective-permute-start | bytes 196616 | tf_op jit(solution)/shard_map/ppermute | solution.py:212
  8.1 4.3 %collective-permute-start.1 = (bf16[1,2,64,256]{3,2,1,0:T(8,128)(2,1)S(1)}, bf16[1,2,64,256]{3,2,1,0:T(8,128)(2,1)S(1)}, u32[]{:S(2)}, u32[]{:S(2)}) collective-permute-start(bf16[1,2,64,256]{3,2,1,0:T(8,128)(2,1)S(1)} %pad_maximum_fusion), channel_id=1, source_target_pairs={{0,16},{4,20},{8,24},{12,28},{16,0},{20,4},{24,8},{28,12},{1,17},{... | collective-permute-start | bytes 196616 | tf_op jit(solution)/shard_map/ppermute | solution.py:212
  8.6 4.3 %collective-permute-start.2 = (bf16[1,2,64,256]{3,2,1,0:T(8,128)(2,1)S(1)}, bf16[1,2,64,256]{3,2,1,0:T(8,128)(2,1)S(1)}, u32[]{:S(2)}, u32[]{:S(2)}) collective-permute-start(bf16[1,2,64,256]{3,2,1,0:T(8,128)(2,1)S(1)} %pad_maximum_fusion), channel_id=1, source_target_pairs={{0,8},{4,12},{8,0},{12,4},{16,24},{20,28},{24,16},{28,20},{1,9},{5... | collective-permute-start | bytes 196616 | tf_op jit(solution)/shard_map/ppermute | solution.py:212
  9.3 4.5 %collective-permute-start.5 = (bf16[2,2,16,512]{3,2,1,0:T(8,128)(2,1)S(1)}, bf16[2,2,16,512]{3,2,1,0:T(8,128)(2,1)S(1)}, u32[]{:S(2)}, u32[]{:S(2)}) collective-permute-start(bf16[2,2,16,512]{3,2,1,0:T(8,128)(2,1)S(1)} %pad_maximum_fusion.1), channel_id=1, source_target_pairs={{0,1},{1,0},{2,3},{3,2},{4,5},{5,4},{6,7},{7,6},{8,9},{9,8},{10,11... | collective-permute-start | bytes 196616 | tf_op jit(solution)/shard_map/ppermute | solution.py:222
  12.9 1.6 %collective-permute-start.4 = (bf16[4,2,64,256]{3,2,1,0:T(8,128)(2,1)S(1)}, bf16[4,2,64,256]{3,2,1,0:T(8,128)(2,1)S(1)}, u32[]{:S(2)}, u32[]{:S(2)}) collective-permute-start(bf16[4,2,64,256]{3,2,1,0:T(8,128)(2,1)S(1)} %constant_dynamic-update-slice_fusion.near), channel_id=1, source_target_pairs={{0,4},{4,0},{8,12},{12,8},{16,20},{20,16},{24,28},{28,24},{1,5},{5... | collective-permute-start | bytes 786440 | tf_op jit(solution)/shard_map/ppermute | solution.py:224
